TPU v7x, 32 devices: a whole 2x2x4 slice. The times are simulated.
32 devices in a mesh: groups: 2 (over y), row: 4 (over x, core), col: 4 (over z).
Axes of the slice: x: 2, y: 2, z: 4, core: 2. Of those that a mesh axis runs over, the one named last changes fastest.
Arguments:
- pair_act: bfloat16 [768, 384, 128], P(('groups', 'row'), 'col'), parts along dimension 0, may hold values from -6 to 6
- pair_mask: int32 [768, 384], P(('groups', 'row'), 'col'), parts along dimension 0, may hold values 0 or 1
- input_gain: float32 [2, 128], replicated, may hold values from 0.5 to 1.5
- input_bias: float32 [2, 128], replicated, may hold values from -3 to 3
- project_weight: bfloat16 [2, 128, 512], replicated, may hold values from -0.5 to 0.5
- gate_weight: bfloat16 [2, 128, 128], replicated, may hold values from -0.5 to 0.5
- output_gain: float32 [2, 128], replicated, may hold values from 0.5 to 1.5
- output_bias: float32 [2, 128], replicated, may hold values from -3 to 3
- output_weight: bfloat16 [2, 128, 128], replicated, may hold values from -0.5 to 0.5
Outputs:
- updated_pair: bfloat16 [768, 384, 128], P(('groups', 'row'), 'col'), parts along dimension 0
There are 2 independent parts, one for each index of `groups`. A program takes and returns all parts, laid end to end along the dimension named above; an argument that names none is the same for every part. Nothing has to cross between parts.
Inputs may be any that keep to these rules, and one draw needn't show every extreme that they name: `pair_mask`: 1 marks a valid residue pair.
All inputs are finite; a program needn't handle non-finite values. No bound on the sum of `pair_mask` on one device may be relied on, other than what follows from the above.
Results may differ from a plain program's by a relative error of at most 0.0075.
Values may be sent and summed in bfloat16 or wider, within the bound.
No kernel may reach another device: no remote copies, remote signals or barrier semaphores. Data moves between devices by JAX's collectives and lax.ppermute only.
A program may use at most 128 MiB of HBM per device.

v0:
```python
import jax
import jax.numpy as jnp
from jax import lax
from jax.sharding import PartitionSpec as P


def from_root(block, axis, owner):
    block = jnp.where(lax.axis_index(axis) == owner, block, jnp.zeros_like(block))
    return lax.psum(block, axis)


def layer_norm(values, gain, bias):
    average = jnp.mean(values, axis=-1, keepdims=True)
    centred = values - average
    spread_sq = jnp.mean(centred * centred, axis=-1, keepdims=True)
    return centred * lax.rsqrt(spread_sq + 1e-05) * gain + bias


def outgoing_sum(left_proj, right_proj):
    rows_here, cols_here, width = left_proj.shape
    col_ratio = lax.axis_size("col") // lax.axis_size("row")
    stripe = lax.all_gather(right_proj, "col", axis=1, tiled=True)
    col_index = lax.axis_index("col")
    picked = lax.dynamic_slice_in_dim(stripe, col_index % col_ratio * cols_here, cols_here, 0)
    mirror = from_root(picked, "row", col_index // col_ratio)
    return jnp.einsum(
        "ikc,jkc->ijc",
        lax.all_gather(left_proj, "col", axis=1, tiled=True),
        mirror,
        preferred_element_type=jnp.float32,
    )


def incoming_sum(left_proj, right_proj):
    stripe = lax.all_gather(left_proj, "col", axis=1, tiled=True)
    return lax.psum_scatter(
        jnp.einsum("kic,kjc->ijc", stripe, right_proj, preferred_element_type=jnp.float32).astype(
            jnp.bfloat16
        ),
        "row",
        scatter_dimension=0,
        tiled=True,
    ).astype(jnp.float32)


def triangle_update(
    pair_act,
    mask_float,
    layer_index,
    input_gain,
    input_bias,
    project_weight,
    gate_weight,
    output_gain,
    output_bias,
    output_weight,
    incoming,
):
    rows_here, cols_here, channels_here = pair_act.shape
    width = output_weight.shape[1]
    pair_float = pair_act.astype(jnp.float32)
    normed = layer_norm(pair_float, input_gain[layer_index], input_bias[layer_index]).astype(
        jnp.bfloat16
    )
    flattened = normed.reshape(-1, channels_here)
    projected = jnp.dot(flattened, project_weight[layer_index], preferred_element_type=jnp.float32)
    projected = projected.reshape(rows_here, cols_here, 4 * width)
    left_proj = (
        jax.nn.sigmoid(projected[..., :width]) * projected[..., width : 2 * width] * mask_float
    )
    right_proj = (
        jax.nn.sigmoid(projected[..., 2 * width : 3 * width])
        * projected[..., 3 * width :]
        * mask_float
    )
    left_proj = left_proj.astype(jnp.bfloat16)
    right_proj = right_proj.astype(jnp.bfloat16)
    gate_value = jax.nn.sigmoid(
        jnp.dot(flattened, gate_weight[layer_index], preferred_element_type=jnp.float32)
    )
    gate_value = gate_value.reshape(rows_here, cols_here, channels_here)
    if incoming:
        triangle = incoming_sum(left_proj, right_proj)
    else:
        triangle = outgoing_sum(left_proj, right_proj)
    normed_sum = layer_norm(triangle, output_gain[layer_index], output_bias[layer_index]).astype(
        jnp.bfloat16
    )
    mapped = jnp.dot(
        normed_sum.reshape(-1, width),
        output_weight[layer_index],
        preferred_element_type=jnp.float32,
    )
    mapped = mapped.reshape(rows_here, cols_here, channels_here)
    return (pair_float + gate_value * mapped).astype(jnp.bfloat16)


def shards(
    pair_act,
    pair_mask,
    input_gain,
    input_bias,
    project_weight,
    gate_weight,
    output_gain,
    output_bias,
    output_weight,
):
    mask_float = pair_mask.astype(jnp.float32)[..., None]
    after_outgoing = triangle_update(
        pair_act,
        mask_float,
        0,
        input_gain,
        input_bias,
        project_weight,
        gate_weight,
        output_gain,
        output_bias,
        output_weight,
        False,
    )
    return triangle_update(
        after_outgoing,
        mask_float,
        1,
        input_gain,
        input_bias,
        project_weight,
        gate_weight,
        output_gain,
        output_bias,
        output_weight,
        True,
    )


def solution(mesh):
    return jax.shard_map(
        shards,
        mesh=mesh,
        in_specs=(
            P(("groups", "row"), "col", None),
            P(("groups", "row"), "col"),
            P(),
            P(),
            P(),
            P(),
            P(),
            P(),
            P(),
        ),
        out_specs=P(("groups", "row"), "col", None),
        check_vma=False,
    )
```

profile of v0, /device:TPU:20, one launch (start us, length us, event | category | flops | bytes accessed | tf_op | source)
XLA Modules:
  0.0 887.3 jit_solution(6741432868803370864)
XLA Ops:
  9.3 4.4 fusion.16
  19.4 4.2 fusion.37
  24.3 165.3 %all-gather.4.cloned.1.call-done = bf16[96,384,128]{2,1,0:T(8,128)(2,1)} async-done(((bf16[96,96,128]{2,1,0:T(8,128)(2,1)}), bf16[96,384,128]{2,1,0:T(8,128)(2,1)}) %all-gather.4.cloned.1.call-update) | async-done | bytes 9437200 | tf_op jit(solution)/shard_map/all_gather | solution.py:22
  189.7 4.3 broadcast_select_fusion
  194.9 5.4 fusion.4
  200.3 156.0 %all-gather.6.cloned.1.call-done = bf16[96,384,128]{2,1,0:T(8,128)(2,1)} async-done(((bf16[96,96,128]{2,1,0:T(8,128)(2,1)}), bf16[96,384,128]{2,1,0:T(8,128)(2,1)}) %all-gather.6.cloned.1.call-update) | async-done | bytes 9437200 | tf_op jit(solution)/shard_map/all_gather | solution.py:28
  356.3 13.1 %copy.29 = bf16[96,384,128]{1,0,2:T(8,128)(2,1)} copy(bf16[96,384,128]{2,1,0:T(8,128)(2,1)} %all-gather.6.cloned.1.call-done) | data formatting | bytes 18874368 | tf_op jit(solution)/shard_map/all_gather | solution.py:28
  369.3 159.3 %all-reduce.2.cloned.1.call-done = bf16[96,384,128]{2,1,0:T(8,128)(2,1)} async-done(((bf16[96,384,128]{2,1,0:T(8,128)(2,1)}), bf16[96,384,128]{2,1,0:T(8,128)(2,1)}) %all-reduce.2.cloned.1.call-update) | async-done | bytes 9437200 | tf_op jit(solution)/shard_map/psum | solution.py:9
  528.6 12.8 %copy.28 = bf16[96,384,128]{1,0,2:T(8,128)(2,1)} copy(bf16[96,384,128]{2,1,0:T(8,128)(2,1)} %all-reduce.2.cloned.1.call-done) | data formatting | bytes 18874368 | tf_op jit(solution)/shard_map/psum | solution.py:9
  541.4 12.5 %bitcast_reduce_fusion = (f32[96,96]{0,1:T(8,128)S(1)}, f32[128,96,96]{2,1,0:T(8,128)}) fusion(bf16[96,384,128]{1,0,2:T(8,128)(2,1)} %copy.28, bf16[96,384,128]{1,0,2:T(8,128)(2,1)} %copy.29), kind=kOutput, calls=%fused_computation.17 | convolution fusion | flops 907140096 | bytes 23629824 | tf_op jit(solution)/shard_map/ikc,jkc->ijc/dot_general | solution.py:26
  554.1 3.7 multiply_reduce_fusion
  558.0 4.6 add_convert_fusion
  562.6 5.2 copy.34
  567.8 4.9 convert_reduce_fusion
  581.5 4.4 fusion.27
  585.9 4.2 copy.35
  590.1 161.1 %all-gather.8.cloned.1.call-done = bf16[96,384,128]{2,1,0:T(8,128)(2,1)} async-done(((bf16[96,96,128]{2,1,0:T(8,128)(2,1)}), bf16[96,384,128]{2,1,0:T(8,128)(2,1)}) %all-gather.8.cloned.1.call-update) | async-done | bytes 9437200 | tf_op jit(solution)/shard_map/all_gather | solution.py:35
  751.2 12.8 %copy.36 = bf16[96,384,128]{1,0,2:T(8,128)(2,1)} copy(bf16[96,384,128]{2,1,0:T(8,128)(2,1)} %all-gather.8.cloned.1.call-done) | data formatting | bytes 18874368 | tf_op jit(solution)/shard_map/all_gather | solution.py:35
  764.0 10.0 %convert_bitcast_fusion = bf16[384,96,128]{0,1,2:T(8,128)(2,1)} fusion(bf16[96,96,128]{0,1,2:T(8,128)(2,1)S(1)} %copy.35, bf16[96,384,128]{1,0,2:T(8,128)(2,1)} %copy.36), kind=kOutput, calls=%fused_computation.8 | convolution fusion | flops 910688256 | bytes 21233664 | tf_op jit(solution)/shard_map/kic,kjc->ijc/dot_general | solution.py:37
  774.0 13.9 %copy.37 = bf16[384,96,128]{2,1,0:T(8,128)(2,1)} copy(bf16[384,96,128]{0,1,2:T(8,128)(2,1)} %convert_bitcast_fusion) | data formatting | bytes 18874368 | tf_op jit(solution)/shard_map/convert_element_type | solution.py:37
  789.6 3.6 fusion.5
  793.2 73.3 %reduce-scatter.2.cloned.1.call-done = bf16[96,96,128]{2,1,0:T(8,128)(2,1)} async-done(((bf16[384,96,128]{2,1,0:T(8,128)(2,1)}), bf16[96,96,128]{2,1,0:T(8,128)(2,1)}) %reduce-scatter.2.cloned.1.call-update) | async-done | bytes 2359312 | tf_op jit(solution)/shard_map/reduce_scatter | solution.py:36
  869.2 4.4 fusion.20
  873.7 7.1 fusion.25
  (62 shorter events, 23.5 us)
Async XLA Ops:
  6.5 7.3 copy-start
  6.5 7.2 copy-start.9
  6.5 7.2 copy-start.11
  6.5 7.2 copy-start.10
  6.5 10.2 %copy-start.7 = (bf16[2,128,512]{2,1,0:T(8,128)(2,1)S(1)}, bf16[2,128,512]{2,1,0:T(8,128)(2,1)}, u32[]{:S(2)}) copy-start(bf16[2,128,512]{2,1,0:T(8,128)(2,1)} %param.13) | copy-start | bytes 786436
  6.5 183.1 %all-gather.4.cloned.1.call-start = ((), (), s32[]{:S(2)}) async-start(), calls=%async_computation.1 | async-start | bytes 11796480 | tf_op jit(solution)/shard_map/all_gather | solution.py:22
  16.7 2.6 copy-start.4
  23.5 332.7 %all-gather.6.cloned.1.call-start = ((), (), s32[]{:S(2)}) async-start(), calls=%async_computation.3 | async-start | bytes 11796480 | tf_op jit(solution)/shard_map/all_gather | solution.py:28
  24.3 504.3 %all-reduce.2.cloned.1.call-start = ((), (), s32[]{:S(2)}) async-start(), calls=%async_computation.2 | async-start | bytes 18874368 | tf_op jit(solution)/shard_map/psum | solution.py:9
  194.0 0.7 copy-start.12
  194.0 0.7 copy-start.13
  194.0 0.9 copy-start.14
  194.1 557.1 %all-gather.8.cloned.1.call-start = ((), (), s32[]{:S(2)}) async-start(), calls=%async_computation.4 | async-start | bytes 11796480 | tf_op jit(solution)/shard_map/all_gather | solution.py:35
  562.6 5.2 copy-start.8
  572.7 3.2 copy-start.1
  578.9 2.6 copy-start.5
  585.9 280.6 %reduce-scatter.2.cloned.1.call-start = ((), (), s32[]{:S(2)}) async-start(), calls=%async_computation.5 | async-start | bytes 11796480 | tf_op jit(solution)/shard_map/reduce_scatter | solution.py:36
  787.9 1.7 copy-start.6
  793.2 80.4 %copy-start.2 = (bf16[96,96,128]{2,1,0:T(8,128)(2,1)S(1)}, bf16[96,96,128]{2,1,0:T(8,128)(2,1)}, u32[]{:S(2)}) copy-start(bf16[96,96,128]{2,1,0:T(8,128)(2,1)} %copy-done.1) | copy-start | bytes 7077892
  866.5 7.2 copy-start.3
Sparse Core Ops, SparseCore 0:
  23.7 165.9 all-gather.3
  191.3 164.9 all-gather.5
  358.8 169.7 all-reduce.1
  586.0 165.1 all-gather.7
  788.1 78.3 reduce-scatter.1
where the time goes:
time: 891 us; the launch traced here: 887 us
  waiting for transfers between devices  716 us (80%)
  local copies, waits for them, and re-layouts  64.8 us (7%)
  matrix products  48.7 us (5%)
  other arithmetic  44.4 us (5%)
  between operations  13.4 us (2%)
    all_gather x1, waiting for transfers between devices, outgoing_sum(): stripe = lax.all_gather(right_proj, 'col', axis=1, tiled=True)  165 us
    all_gather x1, waiting for transfers between devices, incoming_sum(): stripe = lax.all_gather(left_proj, 'col', axis=1, tiled=True)  161 us
    psum x1, waiting for transfers between devices, from_root(): return lax.psum(block, axis)  159 us
    all_gather x1, waiting for transfers between devices, outgoing_sum(): lax.all_gather(left_proj, 'col', axis=1, tiled=True)  156 us
    reduce_scatter x1, waiting for transfers between devices, incoming_sum(): lax.psum_scatter(jnp.einsum('kic,kjc->ijc', stripe, right_proj, preferred...  73.3 us
  transfers between devices with their start and end apart: 5, of which 5 were waited for; matrix products, arithmetic and copies ran while one was open for 3% of the time, Pallas kernels for 0%

commit v1 on v0

v1 whole, which is shorter than its diff:
```python
import jax
import jax.numpy as jnp
from jax import lax
from jax.sharding import PartitionSpec as P

GRID = ("row", "col")


def layer_norm(values, gain, bias, axis):
    average = jnp.mean(values, axis=axis, keepdims=True)
    centred = values - average
    spread_sq = jnp.mean(centred * centred, axis=axis, keepdims=True)
    return centred * lax.rsqrt(spread_sq + 1e-05) * gain + bias


def triangle_update(
    pair_act,
    mask_float,
    layer_index,
    input_gain,
    input_bias,
    project_weight,
    gate_weight,
    output_gain,
    output_bias,
    output_weight,
    incoming,
):
    rows, cols = lax.axis_size("row"), lax.axis_size("col")
    peers = rows * cols
    rows_here, cols_here, channels_here = pair_act.shape
    width = output_weight.shape[1]
    own = width // peers
    pixels = rows_here * cols_here
    pair_float = pair_act.astype(jnp.float32).reshape(pixels, channels_here)
    normed = layer_norm(
        pair_float, input_gain[layer_index], input_bias[layer_index], -1
    ).astype(jnp.bfloat16)
    projected = lax.dot_general(
        project_weight[layer_index],
        normed,
        (((0,), (1,)), ((), ())),
        preferred_element_type=jnp.float32,
    ).reshape(4, peers, own, pixels)
    mask_row = mask_float.reshape(1, 1, pixels)
    left_proj = (jax.nn.sigmoid(projected[0]) * projected[1] * mask_row).astype(jnp.bfloat16)
    right_proj = (jax.nn.sigmoid(projected[2]) * projected[3] * mask_row).astype(jnp.bfloat16)
    both = jnp.concatenate([left_proj, right_proj], axis=1)
    both = lax.all_to_all(both, GRID, 0, 0)
    both = both.reshape(rows, cols, 2, own, rows_here, cols_here)
    both = both.transpose(2, 3, 0, 4, 1, 5).reshape(2, own, rows * rows_here, cols * cols_here)
    spec = "cki,ckj->cij" if incoming else "cik,cjk->cij"
    triangle = jnp.einsum(spec, both[0], both[1], preferred_element_type=jnp.float32)
    triangle = triangle.astype(jnp.bfloat16).reshape(own, rows, rows_here, cols, cols_here)
    triangle = triangle.transpose(1, 3, 0, 2, 4).reshape(peers, own, pixels)
    triangle = lax.all_to_all(triangle, GRID, 0, 0).reshape(width, pixels)
    normed_sum = layer_norm(
        triangle.astype(jnp.float32),
        output_gain[layer_index][:, None],
        output_bias[layer_index][:, None],
        0,
    ).astype(jnp.bfloat16)
    gate_value = jax.nn.sigmoid(
        jnp.dot(normed, gate_weight[layer_index], preferred_element_type=jnp.float32)
    )
    mapped = lax.dot_general(
        normed_sum,
        output_weight[layer_index],
        (((0,), (0,)), ((), ())),
        preferred_element_type=jnp.float32,
    )
    return (
        (pair_float + gate_value * mapped)
        .astype(jnp.bfloat16)
        .reshape(rows_here, cols_here, channels_here)
    )


def shards(pair_act, pair_mask, *params):
    mask_float = pair_mask.astype(jnp.float32)
    for index in range(2):
        pair_act = triangle_update(pair_act, mask_float, index, *params, index == 1)
    return pair_act


def solution(mesh):
    return jax.shard_map(
        shards,
        mesh=mesh,
        in_specs=(P(("groups", "row"), "col", None), P(("groups", "row"), "col"))
        + (P(),) * 7,
        out_specs=P(("groups", "row"), "col", None),
        check_vma=False,
    )
```

time: 891 us -> 499 us (0.56)
  the two profiles are of different devices: /device:TPU:20 before, /device:TPU:0 now
where the time goes in v1:
time: 499 us; the launch traced here: 493 us
  blocking collectives  222 us (44%)
  local copies, waits for them, and re-layouts  102 us (20%)
  waiting for transfers between devices  97.8 us (20%)
  matrix products  38.5 us (8%)
  other arithmetic  24.6 us (5%)
  starting transfers between devices  7.45 us (1%)
    all_to_all x2, blocking collectives, triangle_update(): both = lax.all_to_all(both, GRID, 0, 0)  222 us
    all_to_all x2, waiting for transfers between devices, triangle_update(): triangle = lax.all_to_all(triangle, GRID, 0, 0).reshape(width, pixels)  97.8 us
    reshape x4, local copies, waits for them, and re-layouts, triangle_update(): both = both.reshape(rows, cols, 2, own, rows_here, cols_here)  41.8 us
    reshape x4, local copies, waits for them, and re-layouts, triangle_update(): triangle.astype(jnp.bfloat16).reshape(own, rows, rows_here, cols, cols_here)  16 us
    reshape x2, local copies, waits for them, and re-layouts, triangle_update(): triangle = triangle.transpose(1, 3, 0, 2, 4).reshape(peers, own, pixels)  13.4 us
    squeeze x2, local copies, waits for them, and re-layouts, triangle_update(): both[0]  12.2 us
    dot_general x2, matrix products, triangle_update(): jnp.dot(normed, gate_weight[layer_index], preferred_element_type=jnp.floa...  11.8 us
    dot_general x2, matrix products, triangle_update(): jnp.einsum(spec, both[0], both[1], preferred_element_type=jnp.float32)  10.9 us
  transfers between devices with their start and end apart: 2, of which 2 were waited for; matrix products, arithmetic and copies ran while one was open for 2% of the time, Pallas kernels for 0%

profile of v1, /device:TPU:0, one launch (start us, length us, event | category | flops | bytes accessed | tf_op | source)
XLA Modules:
  0.0 493.1 jit_solution(12431824600717459531)
XLA Ops:
  2.8 4.4 multiply_reduce_fusion.1
  15.9 113.2 %all_to_all.20 = bf16[16,16,9216]{2,1,0:T(8,128)(2,1)} all-to-all(bf16[16,16,9216]{2,1,0:T(8,128)(2,1)S(1)} %pad_maximum_fusion), channel_id=1, replica_groups=mesh['groups'=2,'row'=4,'col'=4] {'row','col'}, dimensions={0} | all-to-all | bytes 9437184 | tf_op jit(solution)/shard_map/all_to_all | solution.py:49
  129.0 10.0 %reshape.241 = bf16[4,4,2,8,96,96]{5,4,3,2,1,0:T(8,128)(2,1)} reshape(bf16[16,16,9216]{2,1,0:T(8,128)(2,1)} %all_to_all.20) | data formatting | bytes 9437184 | tf_op jit(solution)/shard_map/reshape | solution.py:50
  139.1 10.9 %copy.24 = bf16[4,4,2,8,96,96]{5,1,4,0,3,2:T(4,128)(2,1)S(1)} copy(bf16[4,4,2,8,96,96]{5,4,3,2,1,0:T(8,128)(2,1)} %reshape.241) | data formatting | bytes 9437184 | tf_op jit(solution)/shard_map/reshape | solution.py:50
  149.9 4.4 fusion.72
  154.4 6.1 %squeeze.50 = bf16[8,384,384]{2,1,0:T(8,128)(2,1)} reshape(bf16[1,8,4,96,4,96]{5,4,3,2,1,0:T(4,128)(2,1)} %get-tuple-element.16) | data formatting | bytes 4718592 | tf_op jit(solution)/shard_map/squeeze | solution.py:53
  164.1 5.5 %convolution_convert_fusion.1 = bf16[8,384,384]{2,1,0:T(8,128)(2,1)} fusion(bf16[8,384,384]{2,1,0:T(8,128)(2,1)} %squeeze.50, bf16[8,384,384]{2,1,0:T(8,128)(2,1)} %squeeze.51), kind=kOutput, calls=%fused_computation.87 | convolution fusion | flops 907149312 | bytes 7077888 | tf_op jit(solution)/shard_map/cik,cjk->cij/dot_general | solution.py:53
  169.6 5.8 %reshape.242 = bf16[8,4,96,4,96]{4,3,2,1,0:T(4,128)(2,1)S(1)} reshape(bf16[8,384,384]{2,1,0:T(8,128)(2,1)} %convolution_convert_fusion.1) | data formatting | bytes 4718592 | tf_op jit(solution)/shard_map/reshape | solution.py:54
  177.6 6.7 %reshape.243 = bf16[16,8,9216]{2,1,0:T(8,128)(2,1)} reshape(bf16[4,4,8,96,96]{4,3,2,1,0:T(8,128)(2,1)} %bitcast.93) | data formatting | bytes 4718592 | tf_op jit(solution)/shard_map/reshape | solution.py:55
  188.3 5.2 %fusion.9 = f32[9216,128]{1,0:T(8,128)} fusion(bf16[9216,128]{1,0:T(8,128)(2,1)} %bitcast.96, bf16[2,128,128]{2,1,0:T(8,128)(2,1)S(1)} %copy-done.15), kind=kOutput, calls=%fused_computation.15 | convolution fusion | flops 305528832 | bytes 7110656 | tf_op jit(solution)/shard_map/dot_general | solution.py:64
  193.5 49.6 %all-to-all-done.1 = bf16[16,8,9216]{2,1,0:T(8,128)(2,1)S(1)} async-done(((bf16[16,8,9216]{2,1,0:T(8,128)(2,1)}), bf16[16,8,9216]{2,1,0:T(8,128)(2,1)S(1)}, u32[]{:S(2)}, u32[]{:S(2)}) %all-to-all-start.1) | async-done | bytes 2359328 | tf_op jit(solution)/shard_map/all_to_all | solution.py:56
  244.7 4.8 fusion.73
  255.2 4.0 fusion.31
  261.9 109.3 %all_to_all.21 = bf16[16,16,9216]{2,1,0:T(8,128)(2,1)} all-to-all(bf16[16,16,9216]{2,1,0:T(8,128)(2,1)S(1)} %pad_maximum_fusion.1), channel_id=1, replica_groups=mesh['groups'=2,'row'=4,'col'=4] {'row','col'}, dimensions={0} | all-to-all | bytes 9437184 | tf_op jit(solution)/shard_map/all_to_all | solution.py:49
  371.2 10.0 %reshape.244 = bf16[4,4,2,8,96,96]{5,4,3,2,1,0:T(8,128)(2,1)} reshape(bf16[16,16,9216]{2,1,0:T(8,128)(2,1)} %all_to_all.21) | data formatting | bytes 9437184 | tf_op jit(solution)/shard_map/reshape | solution.py:50
  381.2 10.9 %copy.23 = bf16[4,4,2,8,96,96]{5,1,4,0,3,2:T(4,128)(2,1)S(1)} copy(bf16[4,4,2,8,96,96]{5,4,3,2,1,0:T(8,128)(2,1)} %reshape.244) | data formatting | bytes 9437184 | tf_op jit(solution)/shard_map/reshape | solution.py:50
  392.1 4.4 fusion.71
  396.5 6.1 %reshape.252 = bf16[8,384,384]{2,1,0:T(8,128)(2,1)} reshape(bf16[1,8,4,96,4,96]{5,4,3,2,1,0:T(4,128)(2,1)} %get-tuple-element.14) | data formatting | bytes 4718592 | tf_op jit(solution)/shard_map/squeeze | solution.py:53
  406.1 5.4 %convolution_convert_fusion = bf16[8,384,384]{2,1,0:T(8,128)(2,1)} fusion(bf16[8,384,384]{2,1,0:T(8,128)(2,1)} %reshape.252, bf16[8,384,384]{2,1,0:T(8,128)(2,1)} %squeeze.58), kind=kOutput, calls=%fused_computation.86 | convolution fusion | flops 907149312 | bytes 7077888 | tf_op jit(solution)/shard_map/cki,ckj->cij/dot_general | solution.py:53
  411.5 5.8 %reshape.245 = bf16[8,4,96,4,96]{4,3,2,1,0:T(4,128)(2,1)S(1)} reshape(bf16[8,384,384]{2,1,0:T(8,128)(2,1)} %convolution_convert_fusion) | data formatting | bytes 4718592 | tf_op jit(solution)/shard_map/reshape | solution.py:54
  419.5 6.7 %reshape.246 = bf16[16,8,9216]{2,1,0:T(8,128)(2,1)} reshape(bf16[4,4,8,96,96]{4,3,2,1,0:T(8,128)(2,1)} %bitcast.94) | data formatting | bytes 4718592 | tf_op jit(solution)/shard_map/reshape | solution.py:55
  430.1 6.6 %fusion.10 = f32[9216,128]{1,0:T(8,128)} fusion(bf16[2,128,128]{2,1,0:T(8,128)(2,1)S(1)} %copy-done.16, f32[9216,128]{1,0:T(8,128)} %copy-done, f32[128]{0:T(128)S(1)} %get-tuple-element.19, f32[128]{0:T(128)S(1)} %get-tuple-element.24, f32[9216]{0:T(1024)S(1)} %add_rsqrt_fusion.2, f32[9216]{0:T(1024)S(1)} %broadcast_multiply_fusion.2), kind=kOutput, calls=%fused_computation.16 | convolution fusion | flops 311427072 | bytes 9544704 | tf_op jit(solution)/shard_map/dot_general | solution.py:64
  436.7 48.2 %all-to-all-done.3 = bf16[16,8,9216]{2,1,0:T(8,128)(2,1)S(1)} async-done(((bf16[16,8,9216]{2,1,0:T(8,128)(2,1)}), bf16[16,8,9216]{2,1,0:T(8,128)(2,1)S(1)}, u32[]{:S(2)}, u32[]{:S(2)}) %all-to-all-start.3) | async-done | bytes 2359328 | tf_op jit(solution)/shard_map/all_to_all | solution.py:56
  487.3 5.6 %fusion.7 = bf16[9216,128]{1,0:T(8,128)(2,1)} fusion(f32[9216,128]{1,0:T(8,128)} %copy-done, f32[9216,128]{1,0:T(8,128)S(1)} %copy-done.6, bf16[16,8,9216]{2,1,0:T(8,128)(2,1)S(1)} %all-to-all-done.3, f32[16,8]{1,0:T(8,128)S(1)} %add.124, f32[16,8]{1,0:T(8,128)S(1)} %mul.173, f32[9216]{0:T(1024)S(1)} %add_rsqrt_fusion.1, ...), kind=kOutput, calls=%fused_computation.13 | convolution fusion | flops 312606720 | bytes 14278656 | tf_op jit(solution)/shard_map/dot_general | solution.py:66
  (68 shorter events, 43.0 us)
Async XLA Ops:
  0.0 7.3 %copy-start.1 = (bf16[96,96,128]{2,1,0:T(8,128)(2,1)S(1)}, bf16[96,96,128]{2,1,0:T(8,128)(2,1)}, u32[]{:S(2)}) copy-start(bf16[96,96,128]{2,1,0:T(8,128)(2,1)} %param.9) | copy-start | bytes 7077892
  0.0 7.2 %copy-start.10 = (s32[96,96]{1,0:T(8,128)S(1)}, s32[96,96]{1,0:T(8,128)}, u32[]{:S(2)}) copy-start(s32[96,96]{1,0:T(8,128)} %param.10) | copy-start | bytes 110596
  0.0 7.3 %copy-start.12 = (f32[2,128]{1,0:T(2,128)S(1)}, f32[2,128]{1,0:T(2,128)}, u32[]{:S(2)}) copy-start(f32[2,128]{1,0:T(2,128)} %param.11) | copy-start | bytes 3076
  0.0 7.3 %copy-start.11 = (f32[2,128]{1,0:T(2,128)S(1)}, f32[2,128]{1,0:T(2,128)}, u32[]{:S(2)}) copy-start(f32[2,128]{1,0:T(2,128)} %param.12) | copy-start | bytes 3076
  0.0 10.2 %copy-start.7 = (bf16[2,128,512]{2,1,0:T(8,128)(2,1)S(1)}, bf16[2,128,512]{2,1,0:T(8,128)(2,1)}, u32[]{:S(2)}) copy-start(bf16[2,128,512]{2,1,0:T(8,128)(2,1)} %param.13) | copy-start | bytes 786436
  10.2 2.7 copy-start.5
  154.4 6.1 %copy-start.3 = (bf16[1,8,4,96,4,96]{5,4,3,2,1,0:T(4,128)(2,1)S(1)}, bf16[1,8,4,96,4,96]{5,4,3,2,1,0:T(4,128)(2,1)}, u32[]{:S(2)}) copy-start(bf16[1,8,4,96,4,96]{5,4,3,2,1,0:T(4,128)(2,1)} %get-tuple-element.15) | copy-start | bytes 7077892
  177.6 10.5 %copy-start.13 = (f32[2,128]{1,0:T(2,128)S(1)}, f32[2,128]{1,0:T(2,128)}, u32[]{:S(2)}) copy-start(f32[2,128]{1,0:T(2,128)} %param.16) | copy-start | bytes 3076
  177.6 10.5 %copy-start.14 = (f32[2,128]{1,0:T(2,128)S(1)}, f32[2,128]{1,0:T(2,128)}, u32[]{:S(2)}) copy-start(f32[2,128]{1,0:T(2,128)} %param.15) | copy-start | bytes 3076
  177.6 10.7 %copy-start.15 = (bf16[2,128,128]{2,1,0:T(8,128)(2,1)S(1)}, bf16[2,128,128]{2,1,0:T(8,128)(2,1)}, u32[]{:S(2)}) copy-start(bf16[2,128,128]{2,1,0:T(8,128)(2,1)} %param.14) | copy-start | bytes 196612
  184.3 58.7 %all-to-all-start.1 = ((bf16[16,8,9216]{2,1,0:T(8,128)(2,1)}), bf16[16,8,9216]{2,1,0:T(8,128)(2,1)S(1)}, u32[]{:S(2)}, u32[]{:S(2)}) async-start(bf16[16,8,9216]{2,1,0:T(8,128)(2,1)} %reshape.243), calls=%async_computation.1 | async-start | bytes 4718592 | tf_op jit(solution)/shard_map/all_to_all | solution.py:56
  193.5 50.7 %copy-start.8 = (bf16[2,128,128]{2,1,0:T(8,128)(2,1)S(1)}, bf16[2,128,128]{2,1,0:T(8,128)(2,1)}, u32[]{:S(2)}) copy-start(bf16[2,128,128]{2,1,0:T(8,128)(2,1)} %param.17) | copy-start | bytes 196612
  243.1 1.7 copy-start.2
  249.5 5.6 %copy-start = (f32[9216,128]{1,0:T(8,128)}, f32[9216,128]{1,0:T(8,128)S(1)}, u32[]{:S(2)}) copy-start(f32[9216,128]{1,0:T(8,128)S(1)} %get-tuple-element.22) | copy-start | bytes 14155780
  396.5 6.1 %copy-start.4 = (bf16[1,8,4,96,4,96]{5,4,3,2,1,0:T(4,128)(2,1)S(1)}, bf16[1,8,4,96,4,96]{5,4,3,2,1,0:T(4,128)(2,1)}, u32[]{:S(2)}) copy-start(bf16[1,8,4,96,4,96]{5,4,3,2,1,0:T(4,128)(2,1)} %get-tuple-element.13) | copy-start | bytes 7077892
  419.5 10.6 %copy-start.16 = (bf16[2,128,128]{2,1,0:T(8,128)(2,1)S(1)}, bf16[2,128,128]{2,1,0:T(8,128)(2,1)}, u32[]{:S(2)}) copy-start(bf16[2,128,128]{2,1,0:T(8,128)(2,1)} %param.14) | copy-start | bytes 196612
  426.2 58.7 %all-to-all-start.3 = ((bf16[16,8,9216]{2,1,0:T(8,128)(2,1)}), bf16[16,8,9216]{2,1,0:T(8,128)(2,1)S(1)}, u32[]{:S(2)}, u32[]{:S(2)}) async-start(bf16[16,8,9216]{2,1,0:T(8,128)(2,1)} %reshape.246), calls=%async_computation.3 | async-start | bytes 4718592 | tf_op jit(solution)/shard_map/all_to_all | solution.py:56
  436.7 49.4 %copy-start.9 = (bf16[2,128,128]{2,1,0:T(8,128)(2,1)S(1)}, bf16[2,128,128]{2,1,0:T(8,128)(2,1)}, u32[]{:S(2)}) copy-start(bf16[2,128,128]{2,1,0:T(8,128)(2,1)} %param.17) | copy-start | bytes 196612
  484.9 2.3 copy-start.6

commit v2 on v1

--- a/solution.py
+++ b/solution.py
@@ -1,9 +1,303 @@
+import functools
+
 import jax
 import jax.numpy as jnp
 from jax import lax
+from jax.experimental import pallas as pl
+from jax.experimental.pallas import tpu as pltpu
 from jax.sharding import PartitionSpec as P
 
 GRID = ("row", "col")
+LANES = 128
+
+
+def logistic(values):
+    return 0.5 * jnp.tanh(0.5 * values) + 0.5
+
+
+def channel_norm(values, gain, bias):
+    average = jnp.mean(values, axis=0, keepdims=True)
+    centred = values - average
+    spread_sq = jnp.mean(centred * centred, axis=0, keepdims=True)
+    return centred * lax.rsqrt(spread_sq + 1e-05) * gain + bias
+
+
+def dot(left, right):
+    return jnp.dot(left, right, preferred_element_type=jnp.float32)
+
+
+def emit_projections(peers, zt, mask, gain, bias, weight_t, lr_ref):
+    width = weight_t.shape[0] // 4
+    own = width // peers
+    normed = channel_norm(zt, gain, bias).astype(jnp.bfloat16)
+    projected = dot(weight_t, normed)
+    tile = projected.shape[1]
+    left = logistic(projected[:width]) * projected[width : 2 * width] * mask
+    right = logistic(projected[2 * width : 3 * width]) * projected[3 * width :] * mask
+    both = jnp.concatenate(
+        [left.reshape(peers, own, tile), right.reshape(peers, own, tile)], axis=1
+    )
+    lr_ref[...] = both.reshape(2 * width, tile).astype(jnp.bfloat16)
+
+
+def first_kernel(peers, z_ref, mask_ref, gain_ref, bias_ref, weight_ref, lr_ref, zt_ref):
+    zt = z_ref[...].astype(jnp.float32).T
+    zt_ref[...] = zt.astype(jnp.bfloat16)
+    emit_projections(
+        peers, zt, mask_ref[...], gain_ref[...], bias_ref[...], weight_ref[...], lr_ref
+    )
+
+
+def gate_kernel(zt_ref, gain_ref, bias_ref, weight_ref, gate_ref):
+    normed = channel_norm(
+        zt_ref[...].astype(jnp.float32), gain_ref[...], bias_ref[...]
+    ).astype(jnp.bfloat16)
+    gate_ref[...] = logistic(dot(weight_ref[...], normed)).astype(jnp.bfloat16)
+
+
+def updated(t_ref, zt_ref, gate_ref, ogain_ref, obias_ref, oweight_ref):
+    normed_sum = channel_norm(
+        t_ref[...].astype(jnp.float32), ogain_ref[...], obias_ref[...]
+    ).astype(jnp.bfloat16)
+    mapped = dot(oweight_ref[...], normed_sum)
+    return zt_ref[...].astype(jnp.float32) + gate_ref[...].astype(jnp.float32) * mapped
+
+
+def middle_kernel(
+    peers, t_ref, zt_ref, gate_ref, ogain_ref, obias_ref, oweight_ref,
+    mask_ref, gain_ref, bias_ref, weight_ref, lr_ref, out_ref,
+):
+    fresh = updated(t_ref, zt_ref, gate_ref, ogain_ref, obias_ref, oweight_ref).astype(jnp.bfloat16)
+    out_ref[...] = fresh
+    emit_projections(
+        peers, fresh.astype(jnp.float32), mask_ref[...], gain_ref[...], bias_ref[...],
+        weight_ref[...], lr_ref,
+    )
+
+
+def last_kernel(t_ref, zt_ref, gate_ref, ogain_ref, obias_ref, oweight_ref, out_ref):
+    fresh = updated(t_ref, zt_ref, gate_ref, ogain_ref, obias_ref, oweight_ref)
+    out_ref[...] = fresh.T.astype(jnp.bfloat16)
+
+
+def triangle_kernel(
+    blocks, side, own, incoming, x_ref, y_ref, left_ref, right_ref, rows_ref, tiles_ref
+):
+    step = pl.program_id(0)
+    pair = 2 * own
+    span = 4 * side
+    lane = lax.broadcasted_iota(jnp.int32, (pair, LANES), 1)
+    inside = lane < side
+
+    @pl.when(step < blocks)
+    def _unpack():
+        for col in range(blocks):
+
+            def split(group, carry, col=col):
+                x = x_ref[
+                    pl.ds(col * pair, pair), pl.ds(pl.multiple_of(group * span, LANES), span)
+                ].astype(jnp.float32)
+                a, b, c = x[:, :LANES], x[:, LANES : 2 * LANES], x[:, 2 * LANES :]
+                picked = (
+                    a,
+                    pltpu.roll(jnp.where(lane >= 96, a, b), 32, 1),
+                    pltpu.roll(jnp.where(lane >= 64, b, c), 64, 1),
+                    pltpu.roll(c, 96, 1),
+                )
+                for k, row in enumerate(picked):
+                    rows_ref[
+                        pl.ds(pl.multiple_of((group * 4 + k) * pair, pair), pair), :
+                    ] = jnp.where(inside, row, 0.0)
+                return carry
+
+            lax.fori_loop(0, side // 4, split, 0, unroll=4)
+            at = pl.multiple_of(step * side, 16)
+            at_right = at if incoming else pl.multiple_of(step * LANES, 16)
+            for ch in range(own):
+                left_ref[ch, pl.ds(at, side), col * LANES : (col + 1) * LANES] = rows_ref[
+                    pl.ds(ch, side, stride=pair), :
+                ].astype(jnp.bfloat16)
+                right_ref[ch, pl.ds(at_right, side), col * LANES : (col + 1) * LANES] = rows_ref[
+                    pl.ds(own + ch, side, stride=pair), :
+                ].astype(jnp.bfloat16)
+
+    @pl.when(step >= blocks)
+    def _multiply():
+        block = step - blocks
+        for ch in range(own):
+            if incoming:
+                left = left_ref[ch, :, pl.ds(pl.multiple_of(block * LANES, LANES), LANES)]
+                product = lax.dot_general(
+                    left, right_ref[ch], (((0,), (0,)), ((), ())), preferred_element_type=jnp.float32
+                )[:side]
+            else:
+                left = left_ref[ch, pl.ds(pl.multiple_of(block * side, 16), side), :]
+                product = lax.dot_general(
+                    left, right_ref[ch], (((1,), (1,)), ((), ())), preferred_element_type=jnp.float32
+                )
+            for col in range(blocks):
+                tiles_ref[
+                    pl.ds((col // 2) * side * pair + (col % 2) * own + ch, side, stride=pair), :
+                ] = product[:, col * LANES : (col + 1) * LANES]
+        for half in range(blocks // 2):
+
+            def join(group, carry, half=half):
+                p, q, r, s = (
+                    tiles_ref[
+                        pl.ds(
+                            pl.multiple_of(half * side * pair + (group * 4 + k) * pair, pair), pair
+                        ),
+                        :,
+                    ]
+                    for k in range(4)
+                )
+                q, r, s = pltpu.roll(q, 96, 1), pltpu.roll(r, 64, 1), pltpu.roll(s, 32, 1)
+                flat = jnp.concatenate(
+                    [
+                        jnp.where(inside, p, q),
+                        jnp.where(lane < 64, q, r),
+                        jnp.where(lane < 32, r, s),
+                    ],
+                    axis=1,
+                )
+                y_ref[
+                    pl.ds(half * pair, pair), pl.ds(pl.multiple_of(group * span, LANES), span)
+                ] = flat.astype(jnp.bfloat16)
+                return carry
+
+            lax.fori_loop(0, side // 4, join, 0, unroll=4)
+
+
+def fits(rows, cols, rows_here, cols_here, width):
+    return (
+        rows == cols
+        and rows % 2 == 0
+        and rows_here == cols_here
+        and 4 * cols_here == 3 * LANES
+        and 16 * rows * cols == 2 * width
+    )
+
+
+def whole_spec(array):
+    return pl.BlockSpec(array.shape, lambda i: (0,) * array.ndim)
+
+
+def triangle_call(received, blocks, side, own, incoming):
+    pair = 2 * own
+    pixels = side * side
+    padded = blocks * LANES
+    left_rows = blocks * side
+    right_rows = left_rows if incoming else padded
+    return pl.pallas_call(
+        functools.partial(triangle_kernel, blocks, side, own, incoming),
+        grid=(2 * blocks,),
+        in_specs=[
+            pl.BlockSpec((blocks * pair, pixels), lambda i: (jnp.minimum(i, blocks - 1), 0))
+        ],
+        out_specs=pl.BlockSpec((blocks * own, pixels), lambda i: (jnp.maximum(i - blocks, 0), 0)),
+        out_shape=jax.ShapeDtypeStruct((blocks * blocks * own, pixels), jnp.bfloat16),
+        scratch_shapes=[
+            pltpu.VMEM((own, left_rows, padded), jnp.bfloat16),
+            pltpu.VMEM((own, right_rows, padded), jnp.bfloat16),
+            pltpu.VMEM((side * pair, LANES), jnp.float32),
+            pltpu.VMEM((blocks // 2 * side * pair, LANES), jnp.float32),
+        ],
+        compiler_params=pltpu.CompilerParams(vmem_limit_bytes=48 * 1024 * 1024),
+        cost_estimate=pl.CostEstimate(
+            flops=2 * own * (blocks * side) ** 3, bytes_accessed=6 * received.size, transcendentals=0
+        ),
+    )(received)
+
+
+def pixel_call(body, tiled, fixed, outs, pixels, tile, flops, row_major_in=(), row_major_out=()):
+    def spec(channels, row_major):
+        if row_major:
+            return pl.BlockSpec((tile, channels), lambda i: (i, 0))
+        return pl.BlockSpec((channels, tile), lambda i: (0, i))
+
+    in_specs = [
+        spec(a.shape[1] if k in row_major_in else a.shape[0], k in row_major_in)
+        for k, a in enumerate(tiled)
+    ] + [whole_spec(a) for a in fixed]
+    out_specs = [spec(ch, k in row_major_out) for k, ch in enumerate(outs)]
+    out_shape = [
+        jax.ShapeDtypeStruct((pixels, ch) if k in row_major_out else (ch, pixels), jnp.bfloat16)
+        for k, ch in enumerate(outs)
+    ]
+    return pl.pallas_call(
+        body,
+        grid=(pixels // tile,),
+        in_specs=in_specs,
+        out_specs=out_specs,
+        out_shape=out_shape,
+        compiler_params=pltpu.CompilerParams(vmem_limit_bytes=48 * 1024 * 1024),
+        cost_estimate=pl.CostEstimate(
+            flops=flops, bytes_accessed=2 * pixels * (sum(outs) + 256), transcendentals=0
+        ),
+    )(*tiled, *fixed)
+
+
+def by_kernels(
+    pair_act,
+    mask_float,
+    input_gain,
+    input_bias,
+    project_weight,
+    gate_weight,
+    output_gain,
+    output_bias,
+    output_weight,
+):
+    rows, cols = lax.axis_size("row"), lax.axis_size("col")
+    peers = rows * cols
+    side, _, channels = pair_act.shape
+    width = output_weight.shape[1]
+    own = width // peers
+    pixels = side * side
+    tile = 9 * LANES
+    mask = mask_float.reshape(1, pixels)
+    column = [a[:, :, None] for a in (input_gain, input_bias, output_gain, output_bias)]
+    project_t, gate_t, output_t = (
+        a.transpose(0, 2, 1) for a in (project_weight, gate_weight, output_weight)
+    )
+    arriving = lambda u: (column[0][u], column[1][u], project_t[u])
+    leaving = lambda u: (column[2][u], column[3][u], output_t[u])
+    mult = 2 * pixels * channels
+
+    def gate_of(zt, u):
+        return pixel_call(
+            gate_kernel, (zt,), (column[0][u], column[1][u], gate_t[u]), (channels,),
+            pixels, tile, mult * channels,
+        )[0]
+
+    def triangle_of(sent, incoming):
+        received = lax.all_to_all(sent.reshape(peers, 2 * own, pixels), GRID, 0, 0)
+        product = triangle_call(
+            received.reshape(2 * width, pixels), rows, side, own, incoming
+        )
+        return lax.all_to_all(product.reshape(peers, own, pixels), GRID, 0, 0).reshape(width, pixels)
+
+    sent, zt = pixel_call(
+        functools.partial(first_kernel, peers),
+        (pair_act.reshape(pixels, channels), mask), arriving(0), (2 * width, channels),
+        pixels, tile, mult * 4 * width, row_major_in=(0,),
+    )
+    gate = gate_of(zt, 0)
+    triangle = triangle_of(sent, False)
+
+    def middle(t, z, g, m, og, ob, ow, ig, ib, pw, lr, out):
+        middle_kernel(peers, t, z, g, og, ob, ow, m, ig, ib, pw, lr, out)
+
+    sent, zt = pixel_call(
+        middle, (triangle, zt, gate, mask), leaving(0) + arriving(1), (2 * width, channels),
+        pixels, tile, mult * 5 * width,
+    )
+    gate = gate_of(zt, 1)
+    triangle = triangle_of(sent, True)
+    return pixel_call(
+        last_kernel, (triangle, zt, gate), leaving(1), (channels,),
+        pixels, tile, mult * channels, row_major_out=(0,),
+    )[0].reshape(side, side, channels)
 
 
 def layer_norm(values, gain, bias, axis):
@@ -78,6 +372,9 @@
 
 def shards(pair_act, pair_mask, *params):
     mask_float = pair_mask.astype(jnp.float32)
+    rows, cols = lax.axis_size("row"), lax.axis_size("col")
+    if fits(rows, cols, *pair_act.shape[:2], params[-1].shape[1]):
+        return by_kernels(pair_act, mask_float, *params)
     for index in range(2):
         pair_act = triangle_update(pair_act, mask_float, index, *params, index == 1)
     return pair_act

time: 499 us -> 423 us (0.85)
  the two profiles are of different devices: /device:TPU:0 before, /device:TPU:20 now
where the time goes in v2:
time: 423 us; the launch traced here: 417 us
  blocking collectives  220 us (52%)
  waiting for transfers between devices  91.4 us (22%)
  Pallas kernels  80.5 us (19%)
  starting transfers between devices  15 us (4%)
  local copies, waits for them, and re-layouts  9.9 us (2%)
    all_to_all x2, blocking collectives, triangle_of(): received = lax.all_to_all(sent.reshape(peers, 2 * own, pixels), GRID, 0, 0)  220 us
    all_to_all x2, waiting for transfers between devices, triangle_of(): lax.all_to_all(product.reshape(peers, own, pixels), GRID, 0, 0)  91.4 us
    pallas_call x2, Pallas kernels, triangle_call(): pl.pallas_call(functools.partial(triangle_kernel, blocks, side, own, inco...  46.8 us
    pallas_call x5, Pallas kernels, pixel_call(): pl.pallas_call(body, grid=(pixels // tile,), in_specs=in_specs, out_specs...  33.7 us
    all_to_all x2, starting transfers between devices, triangle_of(): lax.all_to_all(product.reshape(peers, own, pixels), GRID, 0, 0)  15 us
  transfers between devices with their start and end apart: 2, of which 2 were waited for; matrix products, arithmetic and copies ran while one was open for 0% of the time, Pallas kernels for 2%

profile of v2, /device:TPU:20, one launch (start us, length us, event | category | flops | bytes accessed | tf_op | source)
XLA Modules:
  0.0 417.5 jit_solution(2323370722559818500)
XLA Ops:
  0.0 0.8 slice_bitcast_fusion.9
  0.8 0.1 copy.11.gain_ref
  0.9 0.8 slice_bitcast_fusion.8
  1.7 1.1 copy.10
  2.9 0.8 convert_element_type.3
  3.8 1.7 copy-done.4
  5.5 6.8 %shard_map.91 = (bf16[256,9216]{1,0:T(8,128)(2,1)}, bf16[128,9216]{1,0:T(8,128)(2,1)S(1)}) custom-call(bf16[9216,128]{1,0:T(8,128)(2,1)S(1)} %bitcast.42, f32[1,9216]{1,0:T(1,128)S(1)} %reshape.50.mask_ref.m, f32[128,1]{1,0:T(8,128)S(1)} %copy.11.gain_ref, f32[128,1]{1,0:T(8,128)S(1)} %copy.12.bias_ref, bf16[512,128]{1,0:T(8,128)(2,1)S(1)} %get-tuple-element.14.weight_ref), custom_call_target="tpu_custom_call" | custom-call | flops 1207959552 | bytes 11796480 | tf_op jit(solution)/shard_map/pallas_call | solution.py:227
  12.3 108.8 %all_to_all.20 = bf16[16,16,9216]{2,1,0:T(8,128)(2,1)} all-to-all(bf16[16,16,9216]{2,1,0:T(8,128)(2,1)} %bitcast.46), channel_id=1, replica_groups=mesh['groups'=2,'row'=4,'col'=4] {'row','col'}, dimensions={0} | all-to-all | bytes 9437184 | tf_op jit(solution)/shard_map/all_to_all | solution.py:274
  121.1 24.2 %shard_map.92 = bf16[128,9216]{1,0:T(8,128)(2,1)S(1)} custom-call(bf16[256,9216]{1,0:T(8,128)(2,1)} %bitcast.43), custom_call_target="tpu_custom_call" | custom-call | flops 905969664 | bytes 14155776 | tf_op jit(solution)/shard_map/pallas_call | solution.py:191
  145.3 1.4 copy-done.1
  146.7 7.6 %all-to-all-start.1 = ((bf16[16,8,9216]{2,1,0:T(8,128)(2,1)}), bf16[16,8,9216]{2,1,0:T(8,128)(2,1)}, u32[]{:S(2)}, u32[]{:S(2)}) async-start(bf16[16,8,9216]{2,1,0:T(8,128)(2,1)} %bitcast.41), calls=%async_computation.1 | async-start | bytes 4718592 | tf_op jit(solution)/shard_map/all_to_all | solution.py:278
  154.3 0.1 copy.13
  154.6 0.1 copy.16
  155.0 3.8 shard_map.93.g
  158.9 1.5 copy-done.2
  160.3 45.4 %all-to-all-done.1 = bf16[16,8,9216]{2,1,0:T(8,128)(2,1)} async-done(((bf16[16,8,9216]{2,1,0:T(8,128)(2,1)}), bf16[16,8,9216]{2,1,0:T(8,128)(2,1)}, u32[]{:S(2)}, u32[]{:S(2)}) %all-to-all-start.1) | async-done | bytes 2359328 | tf_op jit(solution)/shard_map/all_to_all | solution.py:278
  205.7 11.3 %shard_map.94 = (bf16[256,9216]{1,0:T(8,128)(2,1)}, bf16[128,9216]{1,0:T(8,128)(2,1)S(1)}) custom-call(bf16[128,9216]{1,0:T(8,128)(2,1)} %bitcast.8.t, bf16[128,9216]{1,0:T(8,128)(2,1)} %copy-done, bf16[128,9216]{1,0:T(8,128)(2,1)} %copy-done.2, f32[1,9216]{1,0:T(1,128)S(1)} %reshape.50.mask_ref.m, f32[128,1]{1,0:T(8,128)S(1)} %copy.17.og, ...), custom_call_target="tpu_custom_call" | custom-call | flops 1509949440 | bytes 11796480 | tf_op jit(solution)/shard_map/pallas_call | solution.py:227
  217.0 110.9 %all_to_all.21 = bf16[16,16,9216]{2,1,0:T(8,128)(2,1)} all-to-all(bf16[16,16,9216]{2,1,0:T(8,128)(2,1)} %bitcast.45), channel_id=1, replica_groups=mesh['groups'=2,'row'=4,'col'=4] {'row','col'}, dimensions={0} | all-to-all | bytes 9437184 | tf_op jit(solution)/shard_map/all_to_all | solution.py:274
  327.9 22.6 %shard_map.95 = bf16[128,9216]{1,0:T(8,128)(2,1)} custom-call(bf16[256,9216]{1,0:T(8,128)(2,1)} %bitcast.44), custom_call_target="tpu_custom_call" | custom-call | flops 905969664 | bytes 14155776 | tf_op jit(solution)/shard_map/pallas_call | solution.py:191
  350.5 7.5 %all-to-all-start.3 = ((bf16[16,8,9216]{2,1,0:T(8,128)(2,1)}), bf16[16,8,9216]{2,1,0:T(8,128)(2,1)}, u32[]{:S(2)}, u32[]{:S(2)}) async-start(bf16[16,8,9216]{2,1,0:T(8,128)(2,1)} %bitcast.20), calls=%async_computation.3 | async-start | bytes 4718592 | tf_op jit(solution)/shard_map/all_to_all | solution.py:278
  358.2 3.8 shard_map.96.gate_ref
  362.1 1.4 copy-done.3
  363.5 46.0 %all-to-all-done.3 = bf16[16,8,9216]{2,1,0:T(8,128)(2,1)} async-done(((bf16[16,8,9216]{2,1,0:T(8,128)(2,1)}), bf16[16,8,9216]{2,1,0:T(8,128)(2,1)}, u32[]{:S(2)}, u32[]{:S(2)}) %all-to-all-start.3) | async-done | bytes 2359328 | tf_op jit(solution)/shard_map/all_to_all | solution.py:278
  409.5 8.0 %shard_map.97 = bf16[9216,128]{1,0:T(8,128)(2,1)} custom-call(bf16[128,9216]{1,0:T(8,128)(2,1)} %bitcast.21.t_ref, bf16[128,9216]{1,0:T(8,128)(2,1)S(1)} %get-tuple-element.12.zt_ref, bf16[128,9216]{1,0:T(8,128)(2,1)} %copy-done.3, f32[128,1]{1,0:T(8,128)S(1)} %copy.23.ogain_ref, f32[128,1]{1,0:T(8,128)S(1)} %copy.24.obias_ref, ...), custom_call_target="tpu_custom_call" | custom-call | flops 301989888 | bytes 7077888 | tf_op jit(solution)/shard_map/pallas_call | solution.py:227
  (27 shorter events, 1.0 us)
Async XLA Ops:
  3.8 1.7 copy-start.4
  12.3 142.8 %copy-start = (bf16[128,9216]{1,0:T(8,128)(2,1)}, bf16[128,9216]{1,0:T(8,128)(2,1)S(1)}, u32[]{:S(2)}) copy-start(bf16[128,9216]{1,0:T(8,128)(2,1)S(1)} %get-tuple-element.10.zt_ref.z) | copy-start | bytes 7077892
  145.3 1.4 copy-start.1
  146.7 7.6 %copy-start.5 = (bf16[2,128,128]{2,1,0:T(8,128)(2,1)S(1)}, bf16[2,128,128]{2,1,0:T(8,128)(2,1)}, u32[]{:S(2)}) copy-start(bf16[2,128,128]{2,1,0:T(8,128)(2,1)} %param.14) | copy-start | bytes 196612
  146.7 7.9 %copy-start.6 = (bf16[2,128,128]{2,1,0:T(8,128)(2,1)S(1)}, bf16[2,128,128]{2,1,0:T(8,128)(2,1)}, u32[]{:S(2)}) copy-start(bf16[2,128,128]{2,1,0:T(8,128)(2,1)} %param.17) | copy-start | bytes 196612
  146.7 8.1 %copy-start.7 = (f32[2,128]{1,0:T(2,128)S(1)}, f32[2,128]{1,0:T(2,128)}, u32[]{:S(2)}) copy-start(f32[2,128]{1,0:T(2,128)} %param.15) | copy-start | bytes 3076
  146.7 8.2 %copy-start.8 = (f32[2,128]{1,0:T(2,128)S(1)}, f32[2,128]{1,0:T(2,128)}, u32[]{:S(2)}) copy-start(f32[2,128]{1,0:T(2,128)} %param.16) | copy-start | bytes 3076
  146.7 59.0 %all-to-all-start.1 = ((bf16[16,8,9216]{2,1,0:T(8,128)(2,1)}), bf16[16,8,9216]{2,1,0:T(8,128)(2,1)}, u32[]{:S(2)}, u32[]{:S(2)}) async-start(bf16[16,8,9216]{2,1,0:T(8,128)(2,1)} %bitcast.41), calls=%async_computation.1 | async-start | bytes 4718592 | tf_op jit(solution)/shard_map/all_to_all | solution.py:278
  158.9 1.5 copy-start.2
  350.5 58.9 %all-to-all-start.3 = ((bf16[16,8,9216]{2,1,0:T(8,128)(2,1)}), bf16[16,8,9216]{2,1,0:T(8,128)(2,1)}, u32[]{:S(2)}, u32[]{:S(2)}) async-start(bf16[16,8,9216]{2,1,0:T(8,128)(2,1)} %bitcast.20), calls=%async_computation.3 | async-start | bytes 4718592 | tf_op jit(solution)/shard_map/all_to_all | solution.py:278
  362.0 1.4 copy-start.3

commit v3 on v2

--- a/solution.py
+++ b/solution.py
@@ -86,6 +86,7 @@
     step = pl.program_id(0)
     pair = 2 * own
     span = 4 * side
+    pitch_rows = pair + 1
     lane = lax.broadcasted_iota(jnp.int32, (pair, LANES), 1)
     inside = lane < side
 
@@ -106,46 +107,50 @@
                 )
                 for k, row in enumerate(picked):
                     rows_ref[
-                        pl.ds(pl.multiple_of((group * 4 + k) * pair, pair), pair), :
+                        pl.ds((group * 4 + k) * pitch_rows, pair), :
                     ] = jnp.where(inside, row, 0.0)
                 return carry
 
-            lax.fori_loop(0, side // 4, split, 0, unroll=4)
+            lax.fori_loop(0, side // 4, split, 0, unroll=24)
             at = pl.multiple_of(step * side, 16)
             at_right = at if incoming else pl.multiple_of(step * LANES, 16)
             for ch in range(own):
                 left_ref[ch, pl.ds(at, side), col * LANES : (col + 1) * LANES] = rows_ref[
-                    pl.ds(ch, side, stride=pair), :
+                    pl.ds(ch, side, stride=pitch_rows), :
                 ].astype(jnp.bfloat16)
                 right_ref[ch, pl.ds(at_right, side), col * LANES : (col + 1) * LANES] = rows_ref[
-                    pl.ds(own + ch, side, stride=pair), :
+                    pl.ds(own + ch, side, stride=pitch_rows), :
                 ].astype(jnp.bfloat16)
 
+    @pl.when(step == blocks - 1)
+    def _multiply():
+        contract = ((0,), (0,)) if incoming else ((1,), (1,))
+        for ch in range(own):
+            product = lax.dot_general(
+                left_ref[ch], right_ref[ch], (contract, ((), ())), preferred_element_type=jnp.float32
+            )
+            pitch = LANES if incoming else side
+            for row in range(blocks):
+                for col in range(blocks):
+                    tiles_ref[
+                        row,
+                        pl.ds((col // 2) * side * pitch_rows + (col % 2) * own + ch, side, stride=pitch_rows),
+                        :,
+                    ] = product[
+                        row * pitch : row * pitch + side, col * LANES : (col + 1) * LANES
+                    ]
+
     @pl.when(step >= blocks)
-    def _multiply():
+    def _repack():
         block = step - blocks
-        for ch in range(own):
-            if incoming:
-                left = left_ref[ch, :, pl.ds(pl.multiple_of(block * LANES, LANES), LANES)]
-                product = lax.dot_general(
-                    left, right_ref[ch], (((0,), (0,)), ((), ())), preferred_element_type=jnp.float32
-                )[:side]
-            else:
-                left = left_ref[ch, pl.ds(pl.multiple_of(block * side, 16), side), :]
-                product = lax.dot_general(
-                    left, right_ref[ch], (((1,), (1,)), ((), ())), preferred_element_type=jnp.float32
-                )
-            for col in range(blocks):
-                tiles_ref[
-                    pl.ds((col // 2) * side * pair + (col % 2) * own + ch, side, stride=pair), :
-                ] = product[:, col * LANES : (col + 1) * LANES]
         for half in range(blocks // 2):
 
             def join(group, carry, half=half):
                 p, q, r, s = (
                     tiles_ref[
+                        block,
                         pl.ds(
-                            pl.multiple_of(half * side * pair + (group * 4 + k) * pair, pair), pair
+                            half * side * pitch_rows + (group * 4 + k) * pitch_rows, pair
                         ),
                         :,
                     ]
@@ -165,7 +170,7 @@
                 ] = flat.astype(jnp.bfloat16)
                 return carry
 
-            lax.fori_loop(0, side // 4, join, 0, unroll=4)
+            lax.fori_loop(0, side // 4, join, 0, unroll=24)
 
 
 def fits(rows, cols, rows_here, cols_here, width):
@@ -199,8 +204,8 @@
         scratch_shapes=[
             pltpu.VMEM((own, left_rows, padded), jnp.bfloat16),
             pltpu.VMEM((own, right_rows, padded), jnp.bfloat16),
-            pltpu.VMEM((side * pair, LANES), jnp.float32),
-            pltpu.VMEM((blocks // 2 * side * pair, LANES), jnp.float32),
+            pltpu.VMEM((side * (pair + 1), LANES), jnp.float32),
+            pltpu.VMEM((blocks, blocks // 2 * side * (pair + 1), LANES), jnp.float32),
         ],
         compiler_params=pltpu.CompilerParams(vmem_limit_bytes=48 * 1024 * 1024),
         cost_estimate=pl.CostEstimate(

time: 423 us -> 394 us (0.931)
  Pallas kernels: 80.5 us -> 51.5 us
    pallas_call x2, Pallas kernels: 46.8 us -> 17.7 us  [triangle_call(): pl.pallas_call(functools.partial(triangle_kernel, blocks, side, own, inco...]
where the time goes in v3:
time: 394 us; the launch traced here: 388 us
  blocking collectives  220 us (56%)
  waiting for transfers between devices  91.4 us (23%)
  Pallas kernels  51.5 us (13%)
  starting transfers between devices  15 us (4%)
  local copies, waits for them, and re-layouts  9.9 us (3%)
    all_to_all x2, blocking collectives, triangle_of(): received = lax.all_to_all(sent.reshape(peers, 2 * own, pixels), GRID, 0, 0)  220 us
    all_to_all x2, waiting for transfers between devices, triangle_of(): lax.all_to_all(product.reshape(peers, own, pixels), GRID, 0, 0)  91.4 us
    pallas_call x5, Pallas kernels, pixel_call(): pl.pallas_call(body, grid=(pixels // tile,), in_specs=in_specs, out_specs...  33.7 us
    pallas_call x2, Pallas kernels, triangle_call(): pl.pallas_call(functools.partial(triangle_kernel, blocks, side, own, inco...  17.7 us
    all_to_all x2, starting transfers between devices, triangle_of(): lax.all_to_all(product.reshape(peers, own, pixels), GRID, 0, 0)  15 us
  transfers between devices with their start and end apart: 2, of which 2 were waited for; matrix products, arithmetic and copies ran while one was open for 0% of the time, Pallas kernels for 2%

profile of v3, /device:TPU:20, one launch (start us, length us, event | category | flops | bytes accessed | tf_op | source)
XLA Modules:
  0.0 388.4 jit_solution(14656292510247031899)
XLA Ops:
  0.0 0.8 slice_bitcast_fusion.9
  0.8 0.1 copy.11.gain_ref
  0.9 0.8 slice_bitcast_fusion.8
  1.7 1.1 copy.10
  2.9 0.8 convert_element_type.3
  3.8 1.7 copy-done.4
  5.5 6.8 %shard_map.91 = (bf16[256,9216]{1,0:T(8,128)(2,1)}, bf16[128,9216]{1,0:T(8,128)(2,1)S(1)}) custom-call(bf16[9216,128]{1,0:T(8,128)(2,1)S(1)} %bitcast.42, f32[1,9216]{1,0:T(1,128)S(1)} %reshape.50.mask_ref.m, f32[128,1]{1,0:T(8,128)S(1)} %copy.11.gain_ref, f32[128,1]{1,0:T(8,128)S(1)} %copy.12.bias_ref, bf16[512,128]{1,0:T(8,128)(2,1)S(1)} %get-tuple-element.14.weight_ref), custom_call_target="tpu_custom_call" | custom-call | flops 1207959552 | bytes 11796480 | tf_op jit(solution)/shard_map/pallas_call | solution.py:232
  12.3 108.8 %all_to_all.20 = bf16[16,16,9216]{2,1,0:T(8,128)(2,1)} all-to-all(bf16[16,16,9216]{2,1,0:T(8,128)(2,1)} %bitcast.46), channel_id=1, replica_groups=mesh['groups'=2,'row'=4,'col'=4] {'row','col'}, dimensions={0} | all-to-all | bytes 9437184 | tf_op jit(solution)/shard_map/all_to_all | solution.py:279
  121.1 7.9 %shard_map.92 = bf16[128,9216]{1,0:T(8,128)(2,1)S(1)} custom-call(bf16[256,9216]{1,0:T(8,128)(2,1)} %bitcast.43), custom_call_target="tpu_custom_call" | custom-call | flops 905969664 | bytes 14155776 | tf_op jit(solution)/shard_map/pallas_call | solution.py:196
  129.0 1.4 copy-done.1
  130.4 7.6 %all-to-all-start.1 = ((bf16[16,8,9216]{2,1,0:T(8,128)(2,1)}), bf16[16,8,9216]{2,1,0:T(8,128)(2,1)}, u32[]{:S(2)}, u32[]{:S(2)}) async-start(bf16[16,8,9216]{2,1,0:T(8,128)(2,1)} %bitcast.41), calls=%async_computation.1 | async-start | bytes 4718592 | tf_op jit(solution)/shard_map/all_to_all | solution.py:283
  138.0 0.1 copy.13
  138.4 0.1 copy.16
  138.8 3.8 shard_map.93.g
  142.6 1.5 copy-done.2
  144.1 45.4 %all-to-all-done.1 = bf16[16,8,9216]{2,1,0:T(8,128)(2,1)} async-done(((bf16[16,8,9216]{2,1,0:T(8,128)(2,1)}), bf16[16,8,9216]{2,1,0:T(8,128)(2,1)}, u32[]{:S(2)}, u32[]{:S(2)}) %all-to-all-start.1) | async-done | bytes 2359328 | tf_op jit(solution)/shard_map/all_to_all | solution.py:283
  189.5 11.3 %shard_map.94 = (bf16[256,9216]{1,0:T(8,128)(2,1)}, bf16[128,9216]{1,0:T(8,128)(2,1)S(1)}) custom-call(bf16[128,9216]{1,0:T(8,128)(2,1)} %bitcast.8.t, bf16[128,9216]{1,0:T(8,128)(2,1)} %copy-done, bf16[128,9216]{1,0:T(8,128)(2,1)} %copy-done.2, f32[1,9216]{1,0:T(1,128)S(1)} %reshape.50.mask_ref.m, f32[128,1]{1,0:T(8,128)S(1)} %copy.17.og, ...), custom_call_target="tpu_custom_call" | custom-call | flops 1509949440 | bytes 11796480 | tf_op jit(solution)/shard_map/pallas_call | solution.py:232
  200.8 110.9 %all_to_all.21 = bf16[16,16,9216]{2,1,0:T(8,128)(2,1)} all-to-all(bf16[16,16,9216]{2,1,0:T(8,128)(2,1)} %bitcast.45), channel_id=1, replica_groups=mesh['groups'=2,'row'=4,'col'=4] {'row','col'}, dimensions={0} | all-to-all | bytes 9437184 | tf_op jit(solution)/shard_map/all_to_all | solution.py:279
  311.6 9.8 %shard_map.95 = bf16[128,9216]{1,0:T(8,128)(2,1)} custom-call(bf16[256,9216]{1,0:T(8,128)(2,1)} %bitcast.44), custom_call_target="tpu_custom_call" | custom-call | flops 905969664 | bytes 14155776 | tf_op jit(solution)/shard_map/pallas_call | solution.py:196
  321.5 7.5 %all-to-all-start.3 = ((bf16[16,8,9216]{2,1,0:T(8,128)(2,1)}), bf16[16,8,9216]{2,1,0:T(8,128)(2,1)}, u32[]{:S(2)}, u32[]{:S(2)}) async-start(bf16[16,8,9216]{2,1,0:T(8,128)(2,1)} %bitcast.20), calls=%async_computation.3 | async-start | bytes 4718592 | tf_op jit(solution)/shard_map/all_to_all | solution.py:283
  329.1 3.8 shard_map.96.gate_ref
  333.0 1.4 copy-done.3
  334.4 46.0 %all-to-all-done.3 = bf16[16,8,9216]{2,1,0:T(8,128)(2,1)} async-done(((bf16[16,8,9216]{2,1,0:T(8,128)(2,1)}), bf16[16,8,9216]{2,1,0:T(8,128)(2,1)}, u32[]{:S(2)}, u32[]{:S(2)}) %all-to-all-start.3) | async-done | bytes 2359328 | tf_op jit(solution)/shard_map/all_to_all | solution.py:283
  380.4 8.0 %shard_map.97 = bf16[9216,128]{1,0:T(8,128)(2,1)} custom-call(bf16[128,9216]{1,0:T(8,128)(2,1)} %bitcast.21.t_ref, bf16[128,9216]{1,0:T(8,128)(2,1)S(1)} %get-tuple-element.12.zt_ref, bf16[128,9216]{1,0:T(8,128)(2,1)} %copy-done.3, f32[128,1]{1,0:T(8,128)S(1)} %copy.23.ogain_ref, f32[128,1]{1,0:T(8,128)S(1)} %copy.24.obias_ref, ...), custom_call_target="tpu_custom_call" | custom-call | flops 301989888 | bytes 7077888 | tf_op jit(solution)/shard_map/pallas_call | solution.py:232
  (27 shorter events, 1.0 us)
Async XLA Ops:
  3.8 1.7 copy-start.4
  12.3 126.5 %copy-start = (bf16[128,9216]{1,0:T(8,128)(2,1)}, bf16[128,9216]{1,0:T(8,128)(2,1)S(1)}, u32[]{:S(2)}) copy-start(bf16[128,9216]{1,0:T(8,128)(2,1)S(1)} %get-tuple-element.10.zt_ref.z) | copy-start | bytes 7077892
  129.0 1.4 copy-start.1
  130.4 7.6 %copy-start.5 = (bf16[2,128,128]{2,1,0:T(8,128)(2,1)S(1)}, bf16[2,128,128]{2,1,0:T(8,128)(2,1)}, u32[]{:S(2)}) copy-start(bf16[2,128,128]{2,1,0:T(8,128)(2,1)} %param.14) | copy-start | bytes 196612
  130.4 8.0 %copy-start.6 = (bf16[2,128,128]{2,1,0:T(8,128)(2,1)S(1)}, bf16[2,128,128]{2,1,0:T(8,128)(2,1)}, u32[]{:S(2)}) copy-start(bf16[2,128,128]{2,1,0:T(8,128)(2,1)} %param.17) | copy-start | bytes 196612
  130.4 8.1 %copy-start.7 = (f32[2,128]{1,0:T(2,128)S(1)}, f32[2,128]{1,0:T(2,128)}, u32[]{:S(2)}) copy-start(f32[2,128]{1,0:T(2,128)} %param.15) | copy-start | bytes 3076
  130.4 8.2 %copy-start.8 = (f32[2,128]{1,0:T(2,128)S(1)}, f32[2,128]{1,0:T(2,128)}, u32[]{:S(2)}) copy-start(f32[2,128]{1,0:T(2,128)} %param.16) | copy-start | bytes 3076
  130.4 59.0 %all-to-all-start.1 = ((bf16[16,8,9216]{2,1,0:T(8,128)(2,1)}), bf16[16,8,9216]{2,1,0:T(8,128)(2,1)}, u32[]{:S(2)}, u32[]{:S(2)}) async-start(bf16[16,8,9216]{2,1,0:T(8,128)(2,1)} %bitcast.41), calls=%async_computation.1 | async-start | bytes 4718592 | tf_op jit(solution)/shard_map/all_to_all | solution.py:283
  142.6 1.5 copy-start.2
  321.5 58.9 %all-to-all-start.3 = ((bf16[16,8,9216]{2,1,0:T(8,128)(2,1)}), bf16[16,8,9216]{2,1,0:T(8,128)(2,1)}, u32[]{:S(2)}, u32[]{:S(2)}) async-start(bf16[16,8,9216]{2,1,0:T(8,128)(2,1)} %bitcast.20), calls=%async_computation.3 | async-start | bytes 4718592 | tf_op jit(solution)/shard_map/all_to_all | solution.py:283
  333.0 1.4 copy-start.3

commit v4 on v3

--- a/solution.py
+++ b/solution.py
@@ -80,47 +80,60 @@
     out_ref[...] = fresh.T.astype(jnp.bfloat16)
 
 
-def triangle_kernel(
-    blocks, side, own, incoming, x_ref, y_ref, left_ref, right_ref, rows_ref, tiles_ref
-):
+def triangle_kernel(blocks, side, own, incoming, n_in, *refs):
+    x_refs, y_refs, (left_ref, right_ref, rows_ref, tiles_ref) = refs[:n_in], refs[n_in:-4], refs[-4:]
     step = pl.program_id(0)
+    zh = lax.axis_index("zh")
     pair = 2 * own
     span = 4 * side
+    strip = side // 2
+    half = blocks // 2
     pitch_rows = pair + 1
     lane = lax.broadcasted_iota(jnp.int32, (pair, LANES), 1)
     inside = lane < side
 
+    def piece_of(piece_refs, piece):
+        if len(piece_refs) == 1:
+            return piece_refs[0], piece * strip * side
+        return piece_refs[piece], 0
+
     @pl.when(step < blocks)
     def _unpack():
-        for col in range(blocks):
-
-            def split(group, carry, col=col):
-                x = x_ref[
-                    pl.ds(col * pair, pair), pl.ds(pl.multiple_of(group * span, LANES), span)
-                ].astype(jnp.float32)
-                a, b, c = x[:, :LANES], x[:, LANES : 2 * LANES], x[:, 2 * LANES :]
-                picked = (
-                    a,
-                    pltpu.roll(jnp.where(lane >= 96, a, b), 32, 1),
-                    pltpu.roll(jnp.where(lane >= 64, b, c), 64, 1),
-                    pltpu.roll(c, 96, 1),
-                )
-                for k, row in enumerate(picked):
-                    rows_ref[
-                        pl.ds((group * 4 + k) * pitch_rows, pair), :
-                    ] = jnp.where(inside, row, 0.0)
-                return carry
-
-            lax.fori_loop(0, side // 4, split, 0, unroll=24)
-            at = pl.multiple_of(step * side, 16)
-            at_right = at if incoming else pl.multiple_of(step * LANES, 16)
-            for ch in range(own):
-                left_ref[ch, pl.ds(at, side), col * LANES : (col + 1) * LANES] = rows_ref[
-                    pl.ds(ch, side, stride=pitch_rows), :
-                ].astype(jnp.bfloat16)
-                right_ref[ch, pl.ds(at_right, side), col * LANES : (col + 1) * LANES] = rows_ref[
-                    pl.ds(own + ch, side, stride=pitch_rows), :
-                ].astype(jnp.bfloat16)
+        upper, row_pair = step // half, lax.rem(step, half)
+        mirror = lax.rem(row_pair + zh, 2)
+        for r in range(2):
+            at = pl.multiple_of((row_pair * 2 + r) * side + upper * strip, 16)
+            if incoming:
+                at_right = at
+            else:
+                at_right = pl.multiple_of((mirror * 2 + r) * LANES + upper * strip, 16)
+            for zl in range(half):
+                for piece in range(2):
+                    x_ref, first = piece_of(x_refs, piece)
+                    for group in range(strip // 4):
+                        x = x_ref[
+                            (r * half + zl) * pair : (r * half + zl + 1) * pair,
+                            first + group * span : first + (group + 1) * span,
+                        ].astype(jnp.float32)
+                        a, b, c = x[:, :LANES], x[:, LANES : 2 * LANES], x[:, 2 * LANES :]
+                        picked = (
+                            a,
+                            pltpu.roll(jnp.where(lane >= 96, a, b), 32, 1),
+                            pltpu.roll(jnp.where(lane >= 64, b, c), 64, 1),
+                            pltpu.roll(c, 96, 1),
+                        )
+                        for k, row in enumerate(picked):
+                            rows_ref[pl.ds((group * 4 + k) * pitch_rows, pair), :] = jnp.where(
+                                inside, row, 0.0
+                            )
+                    lanes = slice((piece * half + zl) * LANES, (piece * half + zl + 1) * LANES)
+                    for ch in range(own):
+                        left_ref[ch, pl.ds(at, strip), lanes] = rows_ref[
+                            pl.ds(ch, strip, stride=pitch_rows), :
+                        ].astype(jnp.bfloat16)
+                        right_ref[ch, pl.ds(at_right, strip), lanes] = rows_ref[
+                            pl.ds(own + ch, strip, stride=pitch_rows), :
+                        ].astype(jnp.bfloat16)
 
     @pl.when(step == blocks - 1)
     def _multiply():
@@ -129,57 +142,56 @@
             product = lax.dot_general(
                 left_ref[ch], right_ref[ch], (contract, ((), ())), preferred_element_type=jnp.float32
             )
-            pitch = LANES if incoming else side
-            for row in range(blocks):
-                for col in range(blocks):
-                    tiles_ref[
-                        row,
-                        pl.ds((col // 2) * side * pitch_rows + (col % 2) * own + ch, side, stride=pitch_rows),
-                        :,
-                    ] = product[
-                        row * pitch : row * pitch + side, col * LANES : (col + 1) * LANES
-                    ]
+            for place in range(blocks):
+                if incoming:
+                    row, pitch = lax.rem(place // 2 + zh, 2) * 2 + place % 2, LANES
+                else:
+                    row, pitch = place, side
+                for upper in range(2):
+                    for col in range(blocks):
+                        tiles_ref[
+                            col // half,
+                            upper * blocks + row,
+                            pl.ds((col % half) * own + ch, strip, stride=pitch_rows),
+                            :,
+                        ] = product[
+                            place * pitch + upper * strip : place * pitch + (upper + 1) * strip,
+                            col * LANES : (col + 1) * LANES,
+                        ]
 
     @pl.when(step >= blocks)
     def _repack():
-        block = step - blocks
-        for half in range(blocks // 2):
-
-            def join(group, carry, half=half):
-                p, q, r, s = (
-                    tiles_ref[
-                        block,
-                        pl.ds(
-                            half * side * pitch_rows + (group * 4 + k) * pitch_rows, pair
-                        ),
-                        :,
-                    ]
-                    for k in range(4)
-                )
-                q, r, s = pltpu.roll(q, 96, 1), pltpu.roll(r, 64, 1), pltpu.roll(s, 32, 1)
-                flat = jnp.concatenate(
-                    [
-                        jnp.where(inside, p, q),
-                        jnp.where(lane < 64, q, r),
-                        jnp.where(lane < 32, r, s),
-                    ],
-                    axis=1,
-                )
-                y_ref[
-                    pl.ds(half * pair, pair), pl.ds(pl.multiple_of(group * span, LANES), span)
-                ] = flat.astype(jnp.bfloat16)
-                return carry
-
-            lax.fori_loop(0, side // 4, join, 0, unroll=24)
-
-
-def fits(rows, cols, rows_here, cols_here, width):
+        for r in range(2):
+            place = (step - blocks) * 2 + r
+            for piece in range(2):
+                y_ref, first = piece_of(y_refs, piece)
+                for group in range(strip // 4):
+                    p, q, t, s = (
+                        tiles_ref[piece, place, pl.ds((group * 4 + k) * pitch_rows, pair), :]
+                        for k in range(4)
+                    )
+                    q, t, s = pltpu.roll(q, 96, 1), pltpu.roll(t, 64, 1), pltpu.roll(s, 32, 1)
+                    flat = jnp.concatenate(
+                        [
+                            jnp.where(inside, p, q),
+                            jnp.where(lane < 64, q, t),
+                            jnp.where(lane < 32, t, s),
+                        ],
+                        axis=1,
+                    )
+                    y_ref[
+                        r * pair : (r + 1) * pair, first + group * span : first + (group + 1) * span
+                    ] = flat.astype(jnp.bfloat16)
+
+
+def fits(mesh, residues, width):
+    rows, cols = mesh.shape["row"], mesh.shape["col"]
     return (
-        rows == cols
-        and rows % 2 == 0
-        and rows_here == cols_here
-        and 4 * cols_here == 3 * LANES
-        and 16 * rows * cols == 2 * width
+        mesh.shape["groups"] == 2
+        and rows == 4
+        and cols == 4
+        and 4 * residues == 3 * LANES * cols
+        and width == 8 * rows * cols
     )
 
 
@@ -187,31 +199,39 @@
     return pl.BlockSpec(array.shape, lambda i: (0,) * array.ndim)
 
 
-def triangle_call(received, blocks, side, own, incoming):
+def triangle_call(received, n_out, blocks, side, own, incoming):
     pair = 2 * own
     pixels = side * side
     padded = blocks * LANES
+    strip = side // 2
     left_rows = blocks * side
     right_rows = left_rows if incoming else padded
     return pl.pallas_call(
-        functools.partial(triangle_kernel, blocks, side, own, incoming),
+        functools.partial(triangle_kernel, blocks, side, own, incoming, len(received)),
         grid=(2 * blocks,),
         in_specs=[
-            pl.BlockSpec((blocks * pair, pixels), lambda i: (jnp.minimum(i, blocks - 1), 0))
+            pl.BlockSpec((blocks * pair, a.shape[1]), lambda i: (jnp.minimum(i, blocks - 1), 0))
+            for a in received
         ],
-        out_specs=pl.BlockSpec((blocks * own, pixels), lambda i: (jnp.maximum(i - blocks, 0), 0)),
-        out_shape=jax.ShapeDtypeStruct((blocks * blocks * own, pixels), jnp.bfloat16),
+        out_specs=[
+            pl.BlockSpec((2 * pair, pixels // n_out), lambda i: (jnp.maximum(i - blocks, 0), 0))
+        ] * n_out,
+        out_shape=[
+            jax.ShapeDtypeStruct((blocks * blocks * own, pixels // n_out), jnp.bfloat16)
+        ] * n_out,
         scratch_shapes=[
             pltpu.VMEM((own, left_rows, padded), jnp.bfloat16),
             pltpu.VMEM((own, right_rows, padded), jnp.bfloat16),
-            pltpu.VMEM((side * (pair + 1), LANES), jnp.float32),
-            pltpu.VMEM((blocks, blocks // 2 * side * (pair + 1), LANES), jnp.float32),
+            pltpu.VMEM((strip * (pair + 1), LANES), jnp.float32),
+            pltpu.VMEM((2, 2 * blocks, strip * (pair + 1), LANES), jnp.float32),
         ],
         compiler_params=pltpu.CompilerParams(vmem_limit_bytes=48 * 1024 * 1024),
         cost_estimate=pl.CostEstimate(
-            flops=2 * own * (blocks * side) ** 3, bytes_accessed=6 * received.size, transcendentals=0
+            flops=2 * own * (blocks * side) ** 3,
+            bytes_accessed=12 * blocks * blocks * pair * pixels // 2,
+            transcendentals=0,
         ),
-    )(received)
+    )(*received)
 
 
 def pixel_call(body, tiled, fixed, outs, pixels, tile, flops, row_major_in=(), row_major_out=()):
@@ -242,9 +262,26 @@
     )(*tiled, *fixed)
 
 
+SWAP = ((0, 1), (1, 0))
+LINE = ("groups", "zh")
+CUBE = ("groups", "row", "zl")
+
+
+def gather_group(own_half, other_half, home, chunks):
+    early = lax.ppermute(own_half, LINE, ((1, 0), (2, 3)))
+    size = own_half.shape[0] // chunks
+    over, late = [], []
+    for k in range(chunks):
+        part = lax.ppermute(other_half[k * size : (k + 1) * size], "groups", SWAP)
+        over.append(part)
+        late.append(lax.ppermute(part, LINE, ((0, 1), (3, 2))))
+    over, late = (jnp.concatenate(parts) if chunks > 1 else parts[0] for parts in (over, late))
+    return jnp.where(home, own_half, over), jnp.where(home, early, late)
+
+
 def by_kernels(
     pair_act,
-    mask_float,
+    pair_mask,
     input_gain,
     input_bias,
     project_weight,
@@ -253,56 +290,89 @@
     output_bias,
     output_weight,
 ):
-    rows, cols = lax.axis_size("row"), lax.axis_size("col")
-    peers = rows * cols
+    blocks = lax.axis_size("row")
+    peers = blocks * blocks
     side, _, channels = pair_act.shape
     width = output_weight.shape[1]
     own = width // peers
     pixels = side * side
+    strip = side // 2
     tile = 9 * LANES
-    mask = mask_float.reshape(1, pixels)
+    upper = lax.axis_index("groups")
+    home = upper == lax.axis_index("zh")
     column = [a[:, :, None] for a in (input_gain, input_bias, output_gain, output_bias)]
     project_t, gate_t, output_t = (
         a.transpose(0, 2, 1) for a in (project_weight, gate_weight, output_weight)
     )
     arriving = lambda u: (column[0][u], column[1][u], project_t[u])
     leaving = lambda u: (column[2][u], column[3][u], output_t[u])
-    mult = 2 * pixels * channels
+    mult = 2 * channels
+
+    def halves(array):
+        return (
+            lax.dynamic_slice_in_dim(array, upper * strip, strip),
+            lax.dynamic_slice_in_dim(array, (1 - upper) * strip, strip),
+        )
+
+    z_pieces = gather_group(*halves(pair_act), home, 2)
+    m_pieces = gather_group(
+        *(h.reshape(-1, LANES) for h in halves(pair_mask.astype(jnp.bfloat16))), home, 1
+    )
+    m_pieces = [m.reshape(1, -1) for m in m_pieces]
 
     def gate_of(zt, u):
         return pixel_call(
             gate_kernel, (zt,), (column[0][u], column[1][u], gate_t[u]), (channels,),
-            pixels, tile, mult * channels,
+            zt.shape[1], tile, zt.shape[1] * mult * channels,
         )[0]
 
-    def triangle_of(sent, incoming):
-        received = lax.all_to_all(sent.reshape(peers, 2 * own, pixels), GRID, 0, 0)
-        product = triangle_call(
-            received.reshape(2 * width, pixels), rows, side, own, incoming
+    def exchange(array):
+        there = lax.all_to_all(array.reshape(peers, -1, array.shape[1]), CUBE, 0, 0)
+        return there.reshape(array.shape)
+
+    received, zts = [], []
+    for z, m in zip(z_pieces, m_pieces):
+        sent, zt = pixel_call(
+            functools.partial(first_kernel, peers),
+            (z.reshape(-1, channels), m), arriving(0), (2 * width, channels),
+            pixels // 2, tile, pixels // 2 * mult * 4 * width, row_major_in=(0,),
         )
-        return lax.all_to_all(product.reshape(peers, own, pixels), GRID, 0, 0).reshape(width, pixels)
-
-    sent, zt = pixel_call(
-        functools.partial(first_kernel, peers),
-        (pair_act.reshape(pixels, channels), mask), arriving(0), (2 * width, channels),
-        pixels, tile, mult * 4 * width, row_major_in=(0,),
-    )
+        received.append(exchange(sent))
+        zts.append(zt)
+    zt = jnp.concatenate(zts, axis=1)
+    mask = jnp.concatenate(m_pieces, axis=1)
     gate = gate_of(zt, 0)
-    triangle = triangle_of(sent, False)
+    triangle = exchange(*triangle_call(received, 1, blocks, side, own, False))
 
     def middle(t, z, g, m, og, ob, ow, ig, ib, pw, lr, out):
         middle_kernel(peers, t, z, g, og, ob, ow, m, ig, ib, pw, lr, out)
 
     sent, zt = pixel_call(
         middle, (triangle, zt, gate, mask), leaving(0) + arriving(1), (2 * width, channels),
-        pixels, tile, mult * 5 * width,
+        pixels, tile, pixels * mult * 5 * width,
     )
     gate = gate_of(zt, 1)
-    triangle = triangle_of(sent, True)
-    return pixel_call(
-        last_kernel, (triangle, zt, gate), leaving(1), (channels,),
-        pixels, tile, mult * channels, row_major_out=(0,),
-    )[0].reshape(side, side, channels)
+    products = triangle_call([exchange(sent)], 2, blocks, side, own, True)
+
+    def finish(piece, triangle):
+        part = slice(piece * strip * side, (piece + 1) * strip * side)
+        return pixel_call(
+            last_kernel, (triangle, zt[:, part], gate[:, part]), leaving(1), (channels,),
+            pixels // 2, tile, pixels // 2 * mult * channels, row_major_out=(0,),
+        )[0]
+
+    there = finish(1, exchange(products[1]))
+    beside, across = (
+        lax.ppermute(there, LINE, pairs) for pairs in (((0, 1), (3, 2)), ((1, 2), (2, 1)))
+    )
+    there, waiting = lax.optimization_barrier((there, products[0]))
+    here = finish(0, exchange(waiting))
+    back = lax.ppermute(here, LINE, ((1, 3), (2, 0)))
+    mine, others = jnp.where(home, here, beside), jnp.where(home, back, across)
+    first = upper == 0
+    return jnp.concatenate(
+        [jnp.where(first, mine, others), jnp.where(first, others, mine)]
+    ).reshape(side, side, channels)
 
 
 def layer_norm(values, gain, bias, axis):
@@ -377,20 +447,27 @@
 
 def shards(pair_act, pair_mask, *params):
     mask_float = pair_mask.astype(jnp.float32)
-    rows, cols = lax.axis_size("row"), lax.axis_size("col")
-    if fits(rows, cols, *pair_act.shape[:2], params[-1].shape[1]):
-        return by_kernels(pair_act, mask_float, *params)
     for index in range(2):
         pair_act = triangle_update(pair_act, mask_float, index, *params, index == 1)
     return pair_act
 
 
 def solution(mesh):
-    return jax.shard_map(
-        shards,
-        mesh=mesh,
-        in_specs=(P(("groups", "row"), "col", None), P(("groups", "row"), "col"))
-        + (P(),) * 7,
-        out_specs=P(("groups", "row"), "col", None),
-        check_vma=False,
-    )
+    def updates(pair_act, pair_mask, *params):
+        body, grid, cols = shards, mesh, "col"
+        if fits(mesh, pair_act.shape[1], params[-1].shape[1]):
+            sizes = mesh.devices.shape
+            grid = jax.sharding.Mesh(
+                mesh.devices.reshape(*sizes[:2], 2, sizes[2] // 2), ("groups", "row", "zh", "zl")
+            )
+            body, cols = by_kernels, ("zh", "zl")
+        pixels = (("groups", "row"), cols)
+        return jax.shard_map(
+            body,
+            mesh=grid,
+            in_specs=(P(*pixels, None), P(*pixels)) + (P(),) * 7,
+            out_specs=P(*pixels, None),
+            check_vma=False,
+        )(pair_act, pair_mask, *params)
+
+    return updates

time: 394 us -> 383 us (0.972)
  blocking collectives: 220 us -> 92.1 us
  waiting for transfers between devices: 91.4 us -> 138 us
  starting transfers between devices: 15 us -> 46.3 us
  local copies, waits for them, and re-layouts: 9.9 us -> 35.9 us
  other arithmetic: 0.81 us -> 14.5 us
    all_to_all x2, blocking collectives: 220 us -> 92.1 us  [exchange(): there = lax.all_to_all(array.reshape(peers, -1, array.shape[1]), CUBE, 0, 0)]
    ppermute x0 -> x11, waiting for transfers between devices: none -> 94.9 us  [the longest x2 40.1 us: gather_group(): early = lax.ppermute(own_half, LINE, ((1, 0), (2, 3)))]
    all_to_all x2 -> x4, waiting for transfers between devices: 91.4 us -> 43.4 us  [exchange(): there = lax.all_to_all(array.reshape(peers, -1, array.shape[1]), CUBE, 0, 0)]
    ppermute x0 -> x11, starting transfers between devices: none -> 26.3 us  [the longest x3 12.3 us: gather_group(): late.append(lax.ppermute(part, LINE, ((0, 1), (3, 2))))]
    unnamed x21 -> x110, local copies, waits for them, and re-layouts: 7.33 us -> 25.3 us
    concatenate x0 -> x2, other arithmetic: none -> 9.91 us  [the longest x1 9.26 us: by_kernels(): jnp.concatenate([jnp.where(first, mine, others), jnp.where(first, others,...]
    all_to_all x2 -> x4, starting transfers between devices: 15 us -> 20 us  [exchange(): there = lax.all_to_all(array.reshape(peers, -1, array.shape[1]), CUBE, 0, 0)]
    select_n x0 -> x3, other arithmetic: none -> 4.57 us  [the longest x2 3.04 us: gather_group(): return (jnp.where(home, own_half, over), jnp.where(home, early, late))]
  transfers between devices with their start and end apart: 2 -> 15, of which waited for: 2 -> 8; matrix products, arithmetic and copies ran while one was open for 0% -> 3% of each run, Pallas kernels for 2% -> 4%
where the time goes in v4:
time: 383 us; the launch traced here: 376 us
  waiting for transfers between devices  138 us (36%)
  blocking collectives  92.1 us (24%)
  Pallas kernels  48.6 us (13%)
  starting transfers between devices  46.3 us (12%)
  local copies, waits for them, and re-layouts  35.9 us (9%)
  other arithmetic  14.5 us (4%)
    all_to_all x2, blocking collectives, exchange(): there = lax.all_to_all(array.reshape(peers, -1, array.shape[1]), CUBE, 0, 0)  92.1 us
    all_to_all x4, waiting for transfers between devices, exchange(): there = lax.all_to_all(array.reshape(peers, -1, array.shape[1]), CUBE, 0, 0)  43.4 us
    ppermute x2, waiting for transfers between devices, gather_group(): early = lax.ppermute(own_half, LINE, ((1, 0), (2, 3)))  40.1 us
    pallas_call x7, Pallas kernels, pixel_call(): pl.pallas_call(body, grid=(pixels // tile,), in_specs=in_specs, out_specs...  31.4 us
    ppermute x2, waiting for transfers between devices, by_kernels(): lax.ppermute(there, LINE, pairs)  26.3 us
    unnamed x110, local copies, waits for them, and re-layouts  25.3 us
    ppermute x3, waiting for transfers between devices, gather_group(): part = lax.ppermute(other_half[k * size:(k + 1) * size], 'groups', SWAP)  23.5 us
    all_to_all x4, starting transfers between devices, exchange(): there = lax.all_to_all(array.reshape(peers, -1, array.shape[1]), CUBE, 0, 0)  20 us
  transfers between devices with their start and end apart: 15, of which 8 were waited for; matrix products, arithmetic and copies ran while one was open for 3% of the time, Pallas kernels for 4%

profile of v4, /device:TPU:20, one launch (start us, length us, event | category | flops | bytes accessed | tf_op | source)
XLA Modules:
  0.0 376.2 jit_solution(18128947940890483779)
XLA Ops:
  5.9 23.5 %collective-permute-done.2 = bf16[36,128]{1,0:T(8,128)(2,1)S(1)} collective-permute-done((bf16[36,128]{1,0:T(8,128)(2,1)S(1)}, bf16[36,128]{1,0:T(8,128)(2,1)S(1)}, u32[]{:S(2)}, u32[]{:S(2)}) %collective-permute-start.2) | collective-permute-done | bytes 9248 | tf_op jit(solution)/shard_map/ppermute | solution.py:275
  36.7 5.3 %all-to-all-start = ((bf16[16,16,4608]{2,1,0:T(8,128)(2,1)}), bf16[16,16,4608]{2,1,0:T(8,128)(2,1)S(1)}, u32[]{:S(2)}, u32[]{:S(2)}) async-start(bf16[16,16,4608]{2,1,0:T(8,128)(2,1)} %bitcast.61), calls=%async_computation | async-start | bytes 4718592 | tf_op jit(solution)/shard_map/all_to_all | solution.py:330
  43.3 5.6 %collective-permute-start.4 = (bf16[24,96,128]{2,1,0:T(8,128)(2,1)}, bf16[24,96,128]{2,1,0:T(8,128)(2,1)S(1)}, u32[]{:S(2)}, u32[]{:S(2)}) collective-permute-start(bf16[24,96,128]{2,1,0:T(8,128)(2,1)} %copy-done.40), channel_id=1, source_target_pairs={{0,2},{18,16},{1,3},{19,17},{4,6},{22,20},{5,7},{23,21},{8,10},{26... | collective-permute-start | bytes 1769480 | tf_op jit(solution)/shard_map/ppermute | solution.py:277
  51.5 5.4 %collective-permute-start.7 = (bf16[36,128]{1,0:T(8,128)(2,1)}, bf16[36,128]{1,0:T(8,128)(2,1)S(1)}, u32[]{:S(2)}, u32[]{:S(2)}) collective-permute-start(bf16[36,128]{1,0:T(8,128)(2,1)} %copy-done.46), channel_id=1, source_target_pairs={{0,2},{18,16},{1,3},{19,17},{4,6},{22,20},{5,7},{23,21},{8,10},{26... | collective-permute-start | bytes 27656 | tf_op jit(solution)/shard_map/ppermute | solution.py:277
  56.9 40.1 %collective-permute-done.6 = bf16[36,128]{1,0:T(8,128)(2,1)S(1)} collective-permute-done((bf16[36,128]{1,0:T(8,128)(2,1)S(1)}, bf16[36,128]{1,0:T(8,128)(2,1)S(1)}, u32[]{:S(2)}, u32[]{:S(2)}) %collective-permute-start.6) | collective-permute-done | bytes 9248 | tf_op jit(solution)/shard_map/ppermute | solution.py:271
  97.0 3.0 collective-permute-done.7
  106.4 33.6 %all_to_all.30 = bf16[16,16,4608]{2,1,0:T(8,128)(2,1)} all-to-all(bf16[16,16,4608]{2,1,0:T(8,128)(2,1)} %bitcast.62), channel_id=1, replica_groups=mesh['groups'=2,'row'=4,'zh'=2,'zl'=2] {'groups','row','zl'}, dimensions={0} | all-to-all | bytes 4718592 | tf_op jit(solution)/shard_map/all_to_all | solution.py:330
  140.0 7.6 %shard_map.93 = bf16[128,9216]{1,0:T(8,128)(2,1)S(1)} custom-call(bf16[256,4608]{1,0:T(8,128)(2,1)S(1)} %bitcast.58, bf16[256,4608]{1,0:T(8,128)(2,1)} %bitcast.71), custom_call_target="tpu_custom_call" | custom-call | flops 905969664 | bytes 14155776 | tf_op jit(solution)/shard_map/pallas_call | solution.py:209
  149.0 4.9 %all-to-all-start.2 = ((bf16[16,8,9216]{2,1,0:T(8,128)(2,1)}), bf16[16,8,9216]{2,1,0:T(8,128)(2,1)}, u32[]{:S(2)}, u32[]{:S(2)}) async-start(bf16[16,8,9216]{2,1,0:T(8,128)(2,1)} %bitcast.59), calls=%async_computation.2 | async-start | bytes 4718592 | tf_op jit(solution)/shard_map/all_to_all | solution.py:330
  161.2 3.8 %shard_map.94.g = bf16[128,9216]{1,0:T(8,128)(2,1)S(1)} custom-call(bf16[128,9216]{1,0:T(8,128)(2,1)S(1)} %constant_dynamic-update-slice_fusion.zt_ref.z, f32[128,1]{1,0:T(8,128)S(1)} %copy-done.25, f32[128,1]{1,0:T(8,128)S(1)} %copy-done.28, bf16[128,128]{1,0:T(8,128)(2,1)S(1)} %get-tuple-element.38.weight_ref), custom_call_target="tpu_custom_call" | custom-call | flops 301989888 | bytes 7077888 | tf_op jit(solution)/shard_map/pallas_call | solution.py:252
  166.5 17.8 %all-to-all-done.2 = bf16[16,8,9216]{2,1,0:T(8,128)(2,1)} async-done(((bf16[16,8,9216]{2,1,0:T(8,128)(2,1)}), bf16[16,8,9216]{2,1,0:T(8,128)(2,1)}, u32[]{:S(2)}, u32[]{:S(2)}) %all-to-all-start.2) | async-done | bytes 2359328 | tf_op jit(solution)/shard_map/all_to_all | solution.py:330
  190.1 11.3 %shard_map.95 = (bf16[256,9216]{1,0:T(8,128)(2,1)}, bf16[128,9216]{1,0:T(8,128)(2,1)S(1)}) custom-call(bf16[128,9216]{1,0:T(8,128)(2,1)} %bitcast.11.t, bf16[128,9216]{1,0:T(8,128)(2,1)} %copy-done, bf16[128,9216]{1,0:T(8,128)(2,1)} %copy-done.2, bf16[1,9216]{1,0:T(2,128)(2,1)S(1)} %copy-done.31, f32[128,1]{1,0:T(8,128)S(1)} %copy-done.29, ...), custom_call_target="tpu_custom_call" | custom-call | flops 1509949440 | bytes 11796480 | tf_op jit(solution)/shard_map/pallas_call | solution.py:252
  201.4 58.5 %all_to_all.31 = bf16[16,16,9216]{2,1,0:T(8,128)(2,1)} all-to-all(bf16[16,16,9216]{2,1,0:T(8,128)(2,1)} %bitcast.72), channel_id=1, replica_groups=mesh['groups'=2,'row'=4,'zh'=2,'zl'=2] {'groups','row','zl'}, dimensions={0} | all-to-all | bytes 9437184 | tf_op jit(solution)/shard_map/all_to_all | solution.py:330
  259.9 9.7 %shard_map.96 = (bf16[128,4608]{1,0:T(8,128)(2,1)S(1)}, bf16[128,4608]{1,0:T(8,128)(2,1)}) custom-call(bf16[256,9216]{1,0:T(8,128)(2,1)} %bitcast.70), custom_call_target="tpu_custom_call" | custom-call | flops 905969664 | bytes 14155776 | tf_op jit(solution)/shard_map/pallas_call | solution.py:209
  270.7 4.9 %all-to-all-start.4 = ((bf16[16,8,4608]{2,1,0:T(8,128)(2,1)}), bf16[16,8,4608]{2,1,0:T(8,128)(2,1)}, u32[]{:S(2)}, u32[]{:S(2)}) async-start(bf16[16,8,4608]{2,1,0:T(8,128)(2,1)} %bitcast.23), calls=%async_computation.4 | async-start | bytes 2359296 | tf_op jit(solution)/shard_map/all_to_all | solution.py:330
  277.0 3.8 %shard_map.97 = bf16[128,9216]{1,0:T(8,128)(2,1)S(1)} custom-call(bf16[128,9216]{1,0:T(8,128)(2,1)S(1)} %get-tuple-element.20.zt_ref, f32[128,1]{1,0:T(8,128)S(1)} %copy-done.13, f32[128,1]{1,0:T(8,128)S(1)} %copy-done.15, bf16[128,128]{1,0:T(8,128)(2,1)S(1)} %copy-done.32), custom_call_target="tpu_custom_call" | custom-call | flops 301989888 | bytes 7077888 | tf_op jit(solution)/shard_map/pallas_call | solution.py:252
  282.7 8.6 %all-to-all-done.4 = bf16[16,8,4608]{2,1,0:T(8,128)(2,1)} async-done(((bf16[16,8,4608]{2,1,0:T(8,128)(2,1)}), bf16[16,8,4608]{2,1,0:T(8,128)(2,1)}, u32[]{:S(2)}, u32[]{:S(2)}) %all-to-all-start.4) | async-done | bytes 1179680 | tf_op jit(solution)/shard_map/all_to_all | solution.py:330
  296.3 3.5 shard_map.98
  300.9 4.9 %all-to-all-start.5 = ((bf16[16,8,4608]{2,1,0:T(8,128)(2,1)}), bf16[16,8,4608]{2,1,0:T(8,128)(2,1)S(1)}, u32[]{:S(2)}, u32[]{:S(2)}) async-start(bf16[16,8,4608]{2,1,0:T(8,128)(2,1)} %bitcast.64), calls=%async_computation.5 | async-start | bytes 2359296 | tf_op jit(solution)/shard_map/all_to_all | solution.py:330
  307.5 5.7 %collective-permute-start.8 = (bf16[4608,128]{1,0:T(8,128)(2,1)}, bf16[4608,128]{1,0:T(8,128)(2,1)}, u32[]{:S(2)}, u32[]{:S(2)}) collective-permute-start(bf16[4608,128]{1,0:T(8,128)(2,1)} %copy-done.11), channel_id=1, source_target_pairs={{0,2},{18,16},{1,3},{19,17},{4,6},{22,20},{5,7},{23,21},{8,10},{26... | collective-permute-start | bytes 3538952 | tf_op jit(solution)/shard_map/ppermute | solution.py:366
  313.2 16.9 %all-to-all-done.5 = bf16[16,8,4608]{2,1,0:T(8,128)(2,1)S(1)} async-done(((bf16[16,8,4608]{2,1,0:T(8,128)(2,1)}), bf16[16,8,4608]{2,1,0:T(8,128)(2,1)S(1)}, u32[]{:S(2)}, u32[]{:S(2)}) %all-to-all-start.5) | async-done | bytes 1179680 | tf_op jit(solution)/shard_map/all_to_all | solution.py:330
  332.6 3.2 shard_map.99
  337.1 26.3 %collective-permute-done.8 = bf16[4608,128]{1,0:T(8,128)(2,1)} collective-permute-done((bf16[4608,128]{1,0:T(8,128)(2,1)}, bf16[4608,128]{1,0:T(8,128)(2,1)}, u32[]{:S(2)}, u32[]{:S(2)}) %collective-permute-start.8) | collective-permute-done | bytes 1179680 | tf_op jit(solution)/shard_map/ppermute | solution.py:366
  366.9 9.3 %pad_maximum_fusion = bf16[9216,128]{1,0:T(8,128)(2,1)} fusion(bf16[4608,128]{1,0:T(8,128)(2,1)S(1)} %get-tuple-element.26, bf16[4608,128]{1,0:T(8,128)(2,1)S(1)} %get-tuple-element.25), kind=kLoop, calls=%fused_computation | loop fusion | flops 4718592 | bytes 4718592 | tf_op jit(solution)/shard_map/concatenate | solution.py:373
  (156 shorter events, 58.5 us)
Async XLA Ops:
  1.4 28.0 %collective-permute-start = (bf16[24,96,128]{2,1,0:T(8,128)(2,1)S(1)}, bf16[24,96,128]{2,1,0:T(8,128)(2,1)S(1)}, u32[]{:S(2)}, u32[]{:S(2)}) collective-permute-start(bf16[24,96,128]{2,1,0:T(8,128)(2,1)S(1)} %get-tuple-element.31), channel_id=1, source_target_pairs={{0,16},{16,0},{1,17},{17,1},{2,18},{18,2},{3,19},{19,3},{4,20},{20... | collective-permute-start | bytes 1769480 | tf_op jit(solution)/shard_map/ppermute | solution.py:275
  2.0 27.5 %collective-permute-start.1 = (bf16[24,96,128]{2,1,0:T(8,128)(2,1)S(1)}, bf16[24,96,128]{2,1,0:T(8,128)(2,1)S(1)}, u32[]{:S(2)}, u32[]{:S(2)}) collective-permute-start(bf16[24,96,128]{2,1,0:T(8,128)(2,1)S(1)} %get-tuple-element.32), channel_id=1, source_target_pairs={{0,16},{16,0},{1,17},{17,1},{2,18},{18,2},{3,19},{19,3},{4,20},{20... | collective-permute-start | bytes 1769480 | tf_op jit(solution)/shard_map/ppermute | solution.py:275
  3.6 25.8 %collective-permute-start.2 = (bf16[36,128]{1,0:T(8,128)(2,1)S(1)}, bf16[36,128]{1,0:T(8,128)(2,1)S(1)}, u32[]{:S(2)}, u32[]{:S(2)}) collective-permute-start(bf16[36,128]{1,0:T(8,128)(2,1)S(1)} %reshape.75), channel_id=1, source_target_pairs={{0,16},{16,0},{1,17},{17,1},{2,18},{18,2},{3,19},{19,3},{4,20},{20... | collective-permute-start | bytes 27656 | tf_op jit(solution)/shard_map/ppermute | solution.py:275
  5.0 27.3 %copy-start.34 = (bf16[512,128]{1,0:T(8,128)(2,1)}, bf16[512,128]{1,0:T(8,128)(2,1)S(1)}, u32[]{:S(2)}) copy-start(bf16[512,128]{1,0:T(8,128)(2,1)S(1)} %get-tuple-element.34.weight_ref) | copy-start | bytes 393220
  5.8 26.6 %copy-start.23 = (f32[128,1]{1,0:T(8,128)}, f32[128,1]{1,0:T(8,128)S(1)}, u32[]{:S(2)}) copy-start(f32[128,1]{1,0:T(8,128)S(1)} %copy.11.gain_ref) | copy-start | bytes 1540
  5.9 26.5 %copy-start.26 = (f32[128,1]{1,0:T(8,128)}, f32[128,1]{1,0:T(8,128)S(1)}, u32[]{:S(2)}) copy-start(f32[128,1]{1,0:T(8,128)S(1)} %copy.12.bias_ref) | copy-start | bytes 1540
  36.7 69.7 %all-to-all-start = ((bf16[16,16,4608]{2,1,0:T(8,128)(2,1)}), bf16[16,16,4608]{2,1,0:T(8,128)(2,1)S(1)}, u32[]{:S(2)}, u32[]{:S(2)}) async-start(bf16[16,16,4608]{2,1,0:T(8,128)(2,1)} %bitcast.61), calls=%async_computation | async-start | bytes 4718592 | tf_op jit(solution)/shard_map/all_to_all | solution.py:330
  42.0 58.1 %collective-permute-start.3 = (bf16[48,96,128]{2,1,0:T(8,128)(2,1)}, bf16[48,96,128]{2,1,0:T(8,128)(2,1)S(1)}, u32[]{:S(2)}, u32[]{:S(2)}) collective-permute-start(bf16[48,96,128]{2,1,0:T(8,128)(2,1)} %get-tuple-element.24), channel_id=1, source_target_pairs={{2,0},{16,18},{3,1},{17,19},{6,4},{20,22},{7,5},{21,23},{10,8},{24... | collective-permute-start | bytes 3538952 | tf_op jit(solution)/shard_map/ppermute | solution.py:271
  43.3 56.8 %collective-permute-start.4 = (bf16[24,96,128]{2,1,0:T(8,128)(2,1)}, bf16[24,96,128]{2,1,0:T(8,128)(2,1)S(1)}, u32[]{:S(2)}, u32[]{:S(2)}) collective-permute-start(bf16[24,96,128]{2,1,0:T(8,128)(2,1)} %copy-done.40), channel_id=1, source_target_pairs={{0,2},{18,16},{1,3},{19,17},{4,6},{22,20},{5,7},{23,21},{8,10},{26... | collective-permute-start | bytes 1769480 | tf_op jit(solution)/shard_map/ppermute | solution.py:277
  48.8 51.3 %collective-permute-start.5 = (bf16[24,96,128]{2,1,0:T(8,128)(2,1)}, bf16[24,96,128]{2,1,0:T(8,128)(2,1)S(1)}, u32[]{:S(2)}, u32[]{:S(2)}) collective-permute-start(bf16[24,96,128]{2,1,0:T(8,128)(2,1)} %copy-done.41), channel_id=1, source_target_pairs={{0,2},{18,16},{1,3},{19,17},{4,6},{22,20},{5,7},{23,21},{8,10},{26... | collective-permute-start | bytes 1769480 | tf_op jit(solution)/shard_map/ppermute | solution.py:277
  50.2 46.8 %collective-permute-start.6 = (bf16[36,128]{1,0:T(8,128)(2,1)S(1)}, bf16[36,128]{1,0:T(8,128)(2,1)S(1)}, u32[]{:S(2)}, u32[]{:S(2)}) collective-permute-start(bf16[36,128]{1,0:T(8,128)(2,1)S(1)} %reshape.74), channel_id=1, source_target_pairs={{2,0},{16,18},{3,1},{17,19},{6,4},{20,22},{7,5},{21,23},{10,8},{24... | collective-permute-start | bytes 27656 | tf_op jit(solution)/shard_map/ppermute | solution.py:271
  51.5 48.5 %collective-permute-start.7 = (bf16[36,128]{1,0:T(8,128)(2,1)}, bf16[36,128]{1,0:T(8,128)(2,1)S(1)}, u32[]{:S(2)}, u32[]{:S(2)}) collective-permute-start(bf16[36,128]{1,0:T(8,128)(2,1)} %copy-done.46), channel_id=1, source_target_pairs={{0,2},{18,16},{1,3},{19,17},{4,6},{22,20},{5,7},{23,21},{8,10},{26... | collective-permute-start | bytes 27656 | tf_op jit(solution)/shard_map/ppermute | solution.py:277
  149.0 6.6 %copy-start.44 = (bf16[2,128,128]{2,1,0:T(8,128)(2,1)S(1)}, bf16[2,128,128]{2,1,0:T(8,128)(2,1)}, u32[]{:S(2)}) copy-start(bf16[2,128,128]{2,1,0:T(8,128)(2,1)} %param.17) | copy-start | bytes 196612
  149.0 6.7 %copy-start.50 = (f32[2,128]{1,0:T(2,128)S(1)}, f32[2,128]{1,0:T(2,128)}, u32[]{:S(2)}) copy-start(f32[2,128]{1,0:T(2,128)} %param.15) | copy-start | bytes 3076
  149.0 7.5 %copy-start.51 = (f32[2,128]{1,0:T(2,128)S(1)}, f32[2,128]{1,0:T(2,128)}, u32[]{:S(2)}) copy-start(f32[2,128]{1,0:T(2,128)} %param.16) | copy-start | bytes 3076
  149.0 9.5 %copy-start.37 = (bf16[1,1,36,128]{3,1,2,0:T(2,128)(2,1)S(1)}, bf16[1,1,36,128]{3,1,2,0:T(2,128)(2,1)}, u32[]{:S(2)}) copy-start(bf16[1,1,36,128]{3,1,2,0:T(2,128)(2,1)} %copy-done.36) | copy-start | bytes 27652
  149.0 9.4 %copy-start.39 = (bf16[1,1,36,128]{3,1,2,0:T(2,128)(2,1)S(1)}, bf16[1,1,36,128]{3,1,2,0:T(2,128)(2,1)}, u32[]{:S(2)}) copy-start(bf16[1,1,36,128]{3,1,2,0:T(2,128)(2,1)} %copy-done.38) | copy-start | bytes 27652
  149.0 35.3 %all-to-all-start.2 = ((bf16[16,8,9216]{2,1,0:T(8,128)(2,1)}), bf16[16,8,9216]{2,1,0:T(8,128)(2,1)}, u32[]{:S(2)}, u32[]{:S(2)}) async-start(bf16[16,8,9216]{2,1,0:T(8,128)(2,1)} %bitcast.59), calls=%async_computation.2 | async-start | bytes 4718592 | tf_op jit(solution)/shard_map/all_to_all | solution.py:330
  270.7 20.7 %all-to-all-start.4 = ((bf16[16,8,4608]{2,1,0:T(8,128)(2,1)}), bf16[16,8,4608]{2,1,0:T(8,128)(2,1)}, u32[]{:S(2)}, u32[]{:S(2)}) async-start(bf16[16,8,4608]{2,1,0:T(8,128)(2,1)} %bitcast.23), calls=%async_computation.4 | async-start | bytes 2359296 | tf_op jit(solution)/shard_map/all_to_all | solution.py:330
  300.9 29.3 %copy-start.3 = (bf16[128,4608]{1,0:T(8,128)(2,1)S(1)}, bf16[128,4608]{1,0:T(8,128)(2,1)}, u32[]{:S(2)}) copy-start(bf16[128,4608]{1,0:T(8,128)(2,1)} %get-tuple-element.50.zt_ref) | copy-start | bytes 3538948
  300.9 29.3 %all-to-all-start.5 = ((bf16[16,8,4608]{2,1,0:T(8,128)(2,1)}), bf16[16,8,4608]{2,1,0:T(8,128)(2,1)S(1)}, u32[]{:S(2)}, u32[]{:S(2)}) async-start(bf16[16,8,4608]{2,1,0:T(8,128)(2,1)} %bitcast.64), calls=%async_computation.5 | async-start | bytes 2359296 | tf_op jit(solution)/shard_map/all_to_all | solution.py:330
  305.8 31.3 %collective-permute-start.10 = (bf16[4608,128]{1,0:T(8,128)(2,1)}, bf16[4608,128]{1,0:T(8,128)(2,1)}, u32[]{:S(2)}, u32[]{:S(2)}) collective-permute-start(bf16[4608,128]{1,0:T(8,128)(2,1)} %copy-done.11), channel_id=1, source_target_pairs={{2,16},{16,2},{3,17},{17,3},{6,20},{20,6},{7,21},{21,7},{10,24},{2... | collective-permute-start | bytes 3538952 | tf_op jit(solution)/shard_map/ppermute | solution.py:366
  307.5 55.9 %collective-permute-start.8 = (bf16[4608,128]{1,0:T(8,128)(2,1)}, bf16[4608,128]{1,0:T(8,128)(2,1)}, u32[]{:S(2)}, u32[]{:S(2)}) collective-permute-start(bf16[4608,128]{1,0:T(8,128)(2,1)} %copy-done.11), channel_id=1, source_target_pairs={{0,2},{18,16},{1,3},{19,17},{4,6},{22,20},{5,7},{23,21},{8,10},{26... | collective-permute-start | bytes 3538952 | tf_op jit(solution)/shard_map/ppermute | solution.py:366
  335.8 29.6 %collective-permute-start.9 = (bf16[4608,128]{1,0:T(8,128)(2,1)}, bf16[4608,128]{1,0:T(8,128)(2,1)S(1)}, u32[]{:S(2)}, u32[]{:S(2)}) collective-permute-start(bf16[4608,128]{1,0:T(8,128)(2,1)} %shard_map.99), channel_id=1, source_target_pairs={{2,18},{16,0},{3,19},{17,1},{6,22},{20,4},{7,23},{21,5},{10,26},{2... | collective-permute-start | bytes 3538952 | tf_op jit(solution)/shard_map/ppermute | solution.py:370
  (43 other events, 89.5 us)

commit v5 on v4

--- a/solution.py
+++ b/solution.py
@@ -11,8 +11,7 @@
 LANES = 128
 
 
-def logistic(values):
-    return 0.5 * jnp.tanh(0.5 * values) + 0.5
+IN_GAIN, IN_BIAS, OUT_GAIN, OUT_BIAS = range(4)
 
 
 def channel_norm(values, gain, bias):
@@ -26,58 +25,96 @@
     return jnp.dot(left, right, preferred_element_type=jnp.float32)
 
 
-def emit_projections(peers, zt, mask, gain, bias, weight_t, lr_ref):
-    width = weight_t.shape[0] // 4
+def norm_of(values, small_ref, update, which):
+    at = 4 * update + which
+    return channel_norm(values, small_ref[:, at : at + 1], small_ref[:, at + 1 : at + 2])
+
+
+def emit_projections(peers, update, zt, mask_ref, small_ref, weight_ref, lr_ref):
+    width = lr_ref.shape[0] // 2
     own = width // peers
-    normed = channel_norm(zt, gain, bias).astype(jnp.bfloat16)
-    projected = dot(weight_t, normed)
-    tile = projected.shape[1]
-    left = logistic(projected[:width]) * projected[width : 2 * width] * mask
-    right = logistic(projected[2 * width : 3 * width]) * projected[3 * width :] * mask
+    tile = zt.shape[1]
+    normed = norm_of(zt, small_ref, update, IN_GAIN) * mask_ref[...].astype(jnp.float32)
+    projected = dot(weight_ref[update, : 4 * width], normed.astype(jnp.bfloat16))
+    left = (jnp.tanh(projected[:width]) + 1.0) * projected[width : 2 * width]
+    right = (jnp.tanh(projected[2 * width : 3 * width]) + 1.0) * projected[3 * width :]
     both = jnp.concatenate(
         [left.reshape(peers, own, tile), right.reshape(peers, own, tile)], axis=1
     )
     lr_ref[...] = both.reshape(2 * width, tile).astype(jnp.bfloat16)
 
 
-def first_kernel(peers, z_ref, mask_ref, gain_ref, bias_ref, weight_ref, lr_ref, zt_ref):
-    zt = z_ref[...].astype(jnp.float32).T
+def first_kernel(peers, n_far, own_ref, *refs):
+    far_refs, (mask_ref, small_ref, weight_ref), (lr_ref, zt_ref, z_ref) = (
+        refs[:n_far], refs[n_far : n_far + 3], refs[-3:],
+    )
+    home = lax.axis_index("groups") == lax.axis_index("zh")
+    per_part = pl.num_programs(0) // n_far
+
+    @pl.when(home)
+    def _own():
+        z_ref[...] = own_ref[...].astype(jnp.float32)
+
+    for k, far_ref in enumerate(far_refs):
+
+        @pl.when(jnp.logical_and(jnp.logical_not(home), pl.program_id(0) // per_part == k))
+        def _far(far_ref=far_ref):
+            z_ref[...] = far_ref[...].astype(jnp.float32)
+
+    zt = z_ref[...].T
     zt_ref[...] = zt.astype(jnp.bfloat16)
-    emit_projections(
-        peers, zt, mask_ref[...], gain_ref[...], bias_ref[...], weight_ref[...], lr_ref
-    )
-
-
-def gate_kernel(zt_ref, gain_ref, bias_ref, weight_ref, gate_ref):
-    normed = channel_norm(
-        zt_ref[...].astype(jnp.float32), gain_ref[...], bias_ref[...]
-    ).astype(jnp.bfloat16)
-    gate_ref[...] = logistic(dot(weight_ref[...], normed)).astype(jnp.bfloat16)
-
-
-def updated(t_ref, zt_ref, gate_ref, ogain_ref, obias_ref, oweight_ref):
-    normed_sum = channel_norm(
-        t_ref[...].astype(jnp.float32), ogain_ref[...], obias_ref[...]
-    ).astype(jnp.bfloat16)
-    mapped = dot(oweight_ref[...], normed_sum)
+    emit_projections(peers, 0, zt, mask_ref, small_ref, weight_ref, lr_ref)
+
+
+def gate_kernel(update, zt_ref, small_ref, weight_ref, gate_ref):
+    channels = gate_ref.shape[0]
+    normed = norm_of(zt_ref[...].astype(jnp.float32), small_ref, update, IN_GAIN)
+    at = weight_ref.shape[1] - 2 * channels
+    gates = dot(weight_ref[update, at : at + channels], normed.astype(jnp.bfloat16))
+    gate_ref[...] = (0.5 * jnp.tanh(gates) + 0.5).astype(jnp.bfloat16)
+
+
+def updated(update, t_ref, zt_ref, gate_ref, small_ref, weight_ref):
+    normed_sum = norm_of(t_ref[...].astype(jnp.float32), small_ref, update, OUT_GAIN)
+    at = weight_ref.shape[1] - zt_ref.shape[0]
+    mapped = dot(weight_ref[update, at:], normed_sum.astype(jnp.bfloat16))
     return zt_ref[...].astype(jnp.float32) + gate_ref[...].astype(jnp.float32) * mapped
 
 
 def middle_kernel(
-    peers, t_ref, zt_ref, gate_ref, ogain_ref, obias_ref, oweight_ref,
-    mask_ref, gain_ref, bias_ref, weight_ref, lr_ref, out_ref,
+    peers, t_ref, zt_ref, gate_ref, mask_ref, small_ref, weight_ref, lr_ref, out_ref
 ):
-    fresh = updated(t_ref, zt_ref, gate_ref, ogain_ref, obias_ref, oweight_ref).astype(jnp.bfloat16)
+    fresh = updated(0, t_ref, zt_ref, gate_ref, small_ref, weight_ref).astype(jnp.bfloat16)
     out_ref[...] = fresh
-    emit_projections(
-        peers, fresh.astype(jnp.float32), mask_ref[...], gain_ref[...], bias_ref[...],
-        weight_ref[...], lr_ref,
-    )
-
-
-def last_kernel(t_ref, zt_ref, gate_ref, ogain_ref, obias_ref, oweight_ref, out_ref):
-    fresh = updated(t_ref, zt_ref, gate_ref, ogain_ref, obias_ref, oweight_ref)
+    emit_projections(peers, 1, fresh.astype(jnp.float32), mask_ref, small_ref, weight_ref, lr_ref)
+
+
+def last_kernel(t_ref, zt_ref, gate_ref, small_ref, weight_ref, out_ref):
+    fresh = updated(1, t_ref, zt_ref, gate_ref, small_ref, weight_ref)
     out_ref[...] = fresh.T.astype(jnp.bfloat16)
+
+
+def assemble_kernel(here_ref, beside_ref, back_ref, across_ref, out_ref, sems):
+    upper = lax.axis_index("groups")
+    home = upper == lax.axis_index("zh")
+
+    def put(mine_ref, others_ref):
+        copies = (
+            pltpu.make_async_copy(mine_ref, out_ref.at[upper], sems.at[0]),
+            pltpu.make_async_copy(others_ref, out_ref.at[1 - upper], sems.at[1]),
+        )
+        for copy in copies:
+            copy.start()
+        for copy in copies:
+            copy.wait()
+
+    @pl.when(home)
+    def _home():
+        put(here_ref, back_ref)
+
+    @pl.when(jnp.logical_not(home))
+    def _away():
+        put(beside_ref, across_ref)
 
 
 def triangle_kernel(blocks, side, own, incoming, n_in, *refs):
@@ -234,32 +271,43 @@
     )(*received)
 
 
-def pixel_call(body, tiled, fixed, outs, pixels, tile, flops, row_major_in=(), row_major_out=()):
-    def spec(channels, row_major):
+def pixel_call(body, tiled, fixed, outs, steps, tile, flops, start=0, pixels=None, kept=(), scratch=(), row_major_out=False):
+    pixels = pixels or steps * tile
+
+    def spec(channels, first, count, row_major):
         if row_major:
-            return pl.BlockSpec((tile, channels), lambda i: (i, 0))
-        return pl.BlockSpec((channels, tile), lambda i: (0, i))
+            return pl.BlockSpec(
+                (tile, channels), lambda i: (jnp.clip(i + first, 0, count - 1), 0)
+            )
+        return pl.BlockSpec((channels, tile), lambda i: (0, jnp.clip(i + first, 0, count - 1)))
 
     in_specs = [
-        spec(a.shape[1] if k in row_major_in else a.shape[0], k in row_major_in)
-        for k, a in enumerate(tiled)
-    ] + [whole_spec(a) for a in fixed]
-    out_specs = [spec(ch, k in row_major_out) for k, ch in enumerate(outs)]
-    out_shape = [
-        jax.ShapeDtypeStruct((pixels, ch) if k in row_major_out else (ch, pixels), jnp.bfloat16)
-        for k, ch in enumerate(outs)
+        spec(a.shape[1] if row_major else a.shape[0], first, count, row_major)
+        for a, first, count, row_major in tiled
     ]
+    in_specs += [whole_spec(a) for a in fixed]
+    in_specs += [pl.BlockSpec(memory_space=pl.ANY)] * len(kept)
+    n_in, n_kept = len(in_specs), len(kept)
+
+    def kernel(*refs):
+        body(*refs[: n_in - n_kept], *refs[n_in:])
+
     return pl.pallas_call(
-        body,
-        grid=(pixels // tile,),
+        kernel,
+        grid=(steps,),
         in_specs=in_specs,
-        out_specs=out_specs,
-        out_shape=out_shape,
+        out_specs=[spec(ch, start, pixels // tile, row_major_out) for ch in outs],
+        out_shape=[
+            jax.ShapeDtypeStruct((pixels, ch) if row_major_out else (ch, pixels), jnp.bfloat16)
+            for ch in outs
+        ],
+        input_output_aliases={n_in - n_kept + k: k for k in range(n_kept)},
+        scratch_shapes=list(scratch),
         compiler_params=pltpu.CompilerParams(vmem_limit_bytes=48 * 1024 * 1024),
         cost_estimate=pl.CostEstimate(
-            flops=flops, bytes_accessed=2 * pixels * (sum(outs) + 256), transcendentals=0
+            flops=flops, bytes_accessed=2 * steps * tile * (sum(outs) + 256), transcendentals=0
         ),
-    )(*tiled, *fixed)
+    )(*(a for a, *_ in tiled), *fixed, *kept)
 
 
 SWAP = ((0, 1), (1, 0))
@@ -267,7 +315,7 @@
 CUBE = ("groups", "row", "zl")
 
 
-def gather_group(own_half, other_half, home, chunks):
+def gather_group(own_half, other_half, chunks):
     early = lax.ppermute(own_half, LINE, ((1, 0), (2, 3)))
     size = own_half.shape[0] // chunks
     over, late = [], []
@@ -275,8 +323,7 @@
         part = lax.ppermute(other_half[k * size : (k + 1) * size], "groups", SWAP)
         over.append(part)
         late.append(lax.ppermute(part, LINE, ((0, 1), (3, 2))))
-    over, late = (jnp.concatenate(parts) if chunks > 1 else parts[0] for parts in (over, late))
-    return jnp.where(home, own_half, over), jnp.where(home, early, late)
+    return early, over, late
 
 
 def by_kernels(
@@ -298,15 +345,10 @@
     pixels = side * side
     strip = side // 2
     tile = 9 * LANES
+    steps = pixels // tile
     upper = lax.axis_index("groups")
     home = upper == lax.axis_index("zh")
-    column = [a[:, :, None] for a in (input_gain, input_bias, output_gain, output_bias)]
-    project_t, gate_t, output_t = (
-        a.transpose(0, 2, 1) for a in (project_weight, gate_weight, output_weight)
-    )
-    arriving = lambda u: (column[0][u], column[1][u], project_t[u])
-    leaving = lambda u: (column[2][u], column[3][u], output_t[u])
-    mult = 2 * channels
+    mult = 2 * channels * tile
 
     def halves(array):
         return (
@@ -314,51 +356,63 @@
             lax.dynamic_slice_in_dim(array, (1 - upper) * strip, strip),
         )
 
-    z_pieces = gather_group(*halves(pair_act), home, 2)
-    m_pieces = gather_group(
-        *(h.reshape(-1, LANES) for h in halves(pair_mask.astype(jnp.bfloat16))), home, 1
-    )
-    m_pieces = [m.reshape(1, -1) for m in m_pieces]
+    z_own, z_other = (h.reshape(-1, channels) for h in halves(pair_act))
+    z_early, z_over, z_late = gather_group(z_own, z_other, 2)
+    m_own, m_other = (
+        h.reshape(-1, LANES) for h in halves(pair_mask.astype(jnp.bfloat16))
+    )
+    m_early, (m_over,), (m_late,) = gather_group(m_own, m_other, 1)
+    m_pieces = [
+        jnp.where(home, a, b).reshape(1, -1) for a, b in ((m_own, m_over), (m_early, m_late))
+    ]
+    small = jnp.stack([input_gain, input_bias, output_gain, output_bias], axis=1)
+    small = small.reshape(-1, channels).T
+    weights = jnp.concatenate(
+        [project_weight * 0.5, gate_weight * 0.5, output_weight], axis=2
+    ).transpose(0, 2, 1)
+    fixed = (small, weights)
+
+    def first(piece, ours, far, mask, kept):
+        per_part = steps // 2 // len(far)
+        tiled = [(ours, 0, steps // 2, True)]
+        tiled += [(part, -k * per_part, per_part, True) for k, part in enumerate(far)]
+        tiled += [(mask, 0, steps // 2, False)]
+        return pixel_call(
+            functools.partial(first_kernel, peers, len(far)),
+            tiled, fixed, (2 * width, channels), steps // 2, tile, steps // 2 * mult * 4 * width,
+            start=piece * steps // 2, pixels=pixels, kept=kept,
+            scratch=(pltpu.VMEM((tile, channels), jnp.float32),),
+        )
 
     def gate_of(zt, u):
         return pixel_call(
-            gate_kernel, (zt,), (column[0][u], column[1][u], gate_t[u]), (channels,),
-            zt.shape[1], tile, zt.shape[1] * mult * channels,
+            functools.partial(gate_kernel, u), [(zt, 0, steps, False)], fixed, (channels,),
+            steps, tile, steps * mult * channels,
         )[0]
 
     def exchange(array):
         there = lax.all_to_all(array.reshape(peers, -1, array.shape[1]), CUBE, 0, 0)
         return there.reshape(array.shape)
 
-    received, zts = [], []
-    for z, m in zip(z_pieces, m_pieces):
-        sent, zt = pixel_call(
-            functools.partial(first_kernel, peers),
-            (z.reshape(-1, channels), m), arriving(0), (2 * width, channels),
-            pixels // 2, tile, pixels // 2 * mult * 4 * width, row_major_in=(0,),
-        )
-        received.append(exchange(sent))
-        zts.append(zt)
-    zt = jnp.concatenate(zts, axis=1)
+    begun = first(0, z_own, z_over, m_pieces[0], ())
+    sent, zt = first(1, z_early, z_late, m_pieces[1], begun)
+    gate = gate_of(zt, 0)
+    triangle = exchange(*triangle_call([exchange(sent)], 1, blocks, side, own, False))
     mask = jnp.concatenate(m_pieces, axis=1)
-    gate = gate_of(zt, 0)
-    triangle = exchange(*triangle_call(received, 1, blocks, side, own, False))
-
-    def middle(t, z, g, m, og, ob, ow, ig, ib, pw, lr, out):
-        middle_kernel(peers, t, z, g, og, ob, ow, m, ig, ib, pw, lr, out)
-
     sent, zt = pixel_call(
-        middle, (triangle, zt, gate, mask), leaving(0) + arriving(1), (2 * width, channels),
-        pixels, tile, pixels * mult * 5 * width,
+        functools.partial(middle_kernel, peers),
+        [(a, 0, steps, False) for a in (triangle, zt, gate, mask)], fixed, (2 * width, channels),
+        steps, tile, steps * mult * 5 * width,
     )
     gate = gate_of(zt, 1)
     products = triangle_call([exchange(sent)], 2, blocks, side, own, True)
 
     def finish(piece, triangle):
-        part = slice(piece * strip * side, (piece + 1) * strip * side)
+        at = piece * steps // 2
         return pixel_call(
-            last_kernel, (triangle, zt[:, part], gate[:, part]), leaving(1), (channels,),
-            pixels // 2, tile, pixels // 2 * mult * channels, row_major_out=(0,),
+            last_kernel,
+            [(triangle, 0, steps // 2, False), (zt, at, steps, False), (gate, at, steps, False)],
+            fixed, (channels,), steps // 2, tile, steps // 2 * mult * channels, row_major_out=True,
         )[0]
 
     there = finish(1, exchange(products[1]))
@@ -368,11 +422,13 @@
     there, waiting = lax.optimization_barrier((there, products[0]))
     here = finish(0, exchange(waiting))
     back = lax.ppermute(here, LINE, ((1, 3), (2, 0)))
-    mine, others = jnp.where(home, here, beside), jnp.where(home, back, across)
-    first = upper == 0
-    return jnp.concatenate(
-        [jnp.where(first, mine, others), jnp.where(first, others, mine)]
-    ).reshape(side, side, channels)
+    return pl.pallas_call(
+        assemble_kernel,
+        in_specs=[pl.BlockSpec(memory_space=pl.ANY)] * 4,
+        out_specs=pl.BlockSpec(memory_space=pl.ANY),
+        out_shape=jax.ShapeDtypeStruct((2, *here.shape), here.dtype),
+        scratch_shapes=[pltpu.SemaphoreType.DMA((2,))],
+    )(here, beside, back, across).reshape(side, side, channels)
 
 
 def layer_norm(values, gain, bias, axis):

time: 383 us -> 448 us (1.17); the launches traced: 376 us -> 446 us
  Pallas kernels: 48.6 us -> 127 us
  blocking collectives: 92.1 us -> 120 us
  local copies, waits for them, and re-layouts: 35.9 us -> 14.5 us
  other arithmetic: 14.5 us -> 1.08 us
  starting transfers between devices: 46.3 us -> 35.6 us
  waiting for transfers between devices: 138 us -> 148 us
    pallas_call x7 -> x8, Pallas kernels: 31.4 us -> 110 us  [the longest x1 72.6 us: by_kernels(): pl.pallas_call(assemble_kernel, in_specs=[pl.BlockSpec(memory_space=pl.AN...]
    ppermute x2, waiting for transfers between devices: 40.1 us -> 0.01 us  [gather_group(): early = lax.ppermute(own_half, LINE, ((1, 0), (2, 3)))]
    ppermute x3, waiting for transfers between devices: 3.04 us -> 35 us  [gather_group(): late.append(lax.ppermute(part, LINE, ((0, 1), (3, 2))))]
    all_to_all x2, blocking collectives: 92.1 us -> 120 us  [exchange(): there = lax.all_to_all(array.reshape(peers, -1, array.shape[1]), CUBE, 0, 0)]
    all_to_all x4 -> x3, waiting for transfers between devices: 43.4 us -> 66.8 us  [exchange(): there = lax.all_to_all(array.reshape(peers, -1, array.shape[1]), CUBE, 0, 0)]
    unnamed x110 -> x37, local copies, waits for them, and re-layouts: 25.3 us -> 10.8 us
    ppermute x1, waiting for transfers between devices: 2.05 us -> 15.9 us  [by_kernels(): back = lax.ppermute(here, LINE, ((1, 3), (2, 0)))]
    ppermute x2, waiting for transfers between devices: 26.3 us -> 12.5 us  [by_kernels(): lax.ppermute(there, LINE, pairs)]
  transfers between devices with their start and end apart: 15 -> 14, of which waited for: 8 -> 8; matrix products, arithmetic and copies ran while one was open for 3% -> 1% of each run, Pallas kernels for 4% -> 4%
where the time goes in v5:
time: 448 us; the launch traced here: 446 us
  waiting for transfers between devices  148 us (33%)
  Pallas kernels  127 us (28%)
  blocking collectives  120 us (27%)
  starting transfers between devices  35.6 us (8%)
  local copies, waits for them, and re-layouts  14.5 us (3%)
    all_to_all x2, blocking collectives, exchange(): there = lax.all_to_all(array.reshape(peers, -1, array.shape[1]), CUBE, 0, 0)  120 us
    pallas_call x1, Pallas kernels, by_kernels(): pl.pallas_call(assemble_kernel, in_specs=[pl.BlockSpec(memory_space=pl.AN...  72.6 us
    all_to_all x3, waiting for transfers between devices, exchange(): there = lax.all_to_all(array.reshape(peers, -1, array.shape[1]), CUBE, 0, 0)  66.8 us
    pallas_call x7, Pallas kernels, pixel_call(): pl.pallas_call(kernel, grid=(steps,), in_specs=in_specs, out_specs=[spec(...  37.7 us
    ppermute x3, waiting for transfers between devices, gather_group(): late.append(lax.ppermute(part, LINE, ((0, 1), (3, 2))))  35 us
    ppermute x3, waiting for transfers between devices, gather_group(): part = lax.ppermute(other_half[k * size:(k + 1) * size], 'groups', SWAP)  17.9 us
    pallas_call x2, Pallas kernels, triangle_call(): pl.pallas_call(functools.partial(triangle_kernel, blocks, side, own, inco...  16.6 us
    ppermute x1, waiting for transfers between devices, by_kernels(): back = lax.ppermute(here, LINE, ((1, 3), (2, 0)))  15.9 us
  transfers between devices with their start and end apart: 14, of which 8 were waited for; matrix products, arithmetic and copies ran while one was open for 1% of the time, Pallas kernels for 4%

profile of v5, /device:TPU:20, one launch (start us, length us, event | category | flops | bytes accessed | tf_op | source)
XLA Modules:
  0.0 446.4 jit_solution(5480382452548189139)
XLA Ops:
  11.4 9.2 %collective-permute-done.1.refs_1_ = bf16[2304,128]{1,0:T(8,128)(2,1)S(1)} collective-permute-done((bf16[2304,128]{1,0:T(8,128)(2,1)}, bf16[2304,128]{1,0:T(8,128)(2,1)S(1)}, u32[]{:S(2)}, u32[]{:S(2)}) %collective-permute-start.1) | collective-permute-done | bytes 589856 | tf_op jit(solution)/shard_map/ppermute | solution.py:323
  23.1 8.7 %collective-permute-done.3.refs_2_ = bf16[2304,128]{1,0:T(8,128)(2,1)} collective-permute-done((bf16[2304,128]{1,0:T(8,128)(2,1)}, bf16[2304,128]{1,0:T(8,128)(2,1)}, u32[]{:S(2)}, u32[]{:S(2)}) %collective-permute-start.3) | collective-permute-done | bytes 589856 | tf_op jit(solution)/shard_map/ppermute | solution.py:323
  36.2 35.0 %collective-permute-done.7 = bf16[36,128]{1,0:T(8,128)(2,1)S(1)} collective-permute-done((bf16[36,128]{1,0:T(8,128)(2,1)S(1)}, bf16[36,128]{1,0:T(8,128)(2,1)S(1)}, u32[]{:S(2)}, u32[]{:S(2)}) %collective-permute-start.7) | collective-permute-done | bytes 9248 | tf_op jit(solution)/shard_map/ppermute | solution.py:325
  71.2 5.5 %shard_map.91 = (bf16[256,9216]{1,0:T(8,128)(2,1)}, bf16[128,9216]{1,0:T(8,128)(2,1)S(1)}) custom-call(bf16[4608,128]{1,0:T(8,128)(2,1)} %bitcast.refs_0_, bf16[2304,128]{1,0:T(8,128)(2,1)S(1)} %collective-permute-done.1.refs_1_, bf16[2304,128]{1,0:T(8,128)(2,1)} %collective-permute-done.3.refs_2_, bf16[1,4608]{1,0:T(2,128)(2,1)S(1)} %bitcast.44, ...), custom_call_target="tpu_custom_call" | custom-call | flops 603979776 | bytes 5898240 | tf_op jit(solution)/shard_map/pallas_call | solution.py:295
  76.7 5.6 %shard_map.92 = (bf16[256,9216]{1,0:T(8,128)(2,1)}, bf16[128,9216]{1,0:T(8,128)(2,1)S(1)}) custom-call(bf16[4608,128]{1,0:T(8,128)(2,1)} %collective-permute-done.refs_0_, bf16[2304,128]{1,0:T(8,128)(2,1)} %collective-permute-done.2.refs_1_, bf16[2304,128]{1,0:T(8,128)(2,1)} %collective-permute-done.4.refs_2_, ...), custom_call_target="tpu_custom_call", output_to_operand_aliasing={{0}: (6, {}), {1}: (7, {})} | custom-call | flops 603979776 | bytes 5898240 | tf_op jit(solution)/shard_map/pallas_call | solution.py:295
  82.4 61.4 %all_to_all.25 = bf16[16,16,9216]{2,1,0:T(8,128)(2,1)} all-to-all(bf16[16,16,9216]{2,1,0:T(8,128)(2,1)} %bitcast.50), channel_id=1, replica_groups=mesh['groups'=2,'row'=4,'zh'=2,'zl'=2] {'groups','row','zl'}, dimensions={0} | all-to-all | bytes 9437184 | tf_op jit(solution)/shard_map/all_to_all | solution.py:394
  143.8 8.0 %shard_map.93 = bf16[128,9216]{1,0:T(8,128)(2,1)S(1)} custom-call(bf16[256,9216]{1,0:T(8,128)(2,1)} %bitcast.49), custom_call_target="tpu_custom_call" | custom-call | flops 905969664 | bytes 14155776 | tf_op jit(solution)/shard_map/pallas_call | solution.py:246
  153.2 4.9 %all-to-all-start.1 = ((bf16[16,8,9216]{2,1,0:T(8,128)(2,1)}), bf16[16,8,9216]{2,1,0:T(8,128)(2,1)}, u32[]{:S(2)}, u32[]{:S(2)}) async-start(bf16[16,8,9216]{2,1,0:T(8,128)(2,1)} %bitcast.34), calls=%async_computation.1 | async-start | bytes 4718592 | tf_op jit(solution)/shard_map/all_to_all | solution.py:394
  158.2 3.9 shard_map.94.refs_2_
  163.5 24.9 %all-to-all-done.1 = bf16[16,8,9216]{2,1,0:T(8,128)(2,1)} async-done(((bf16[16,8,9216]{2,1,0:T(8,128)(2,1)}), bf16[16,8,9216]{2,1,0:T(8,128)(2,1)}, u32[]{:S(2)}, u32[]{:S(2)}) %all-to-all-start.1) | async-done | bytes 2359328 | tf_op jit(solution)/shard_map/all_to_all | solution.py:394
  188.5 11.3 %shard_map.95 = (bf16[256,9216]{1,0:T(8,128)(2,1)}, bf16[128,9216]{1,0:T(8,128)(2,1)S(1)}) custom-call(bf16[128,9216]{1,0:T(8,128)(2,1)} %bitcast.13.refs_0_, bf16[128,9216]{1,0:T(8,128)(2,1)} %copy-done.1, bf16[128,9216]{1,0:T(8,128)(2,1)} %copy-done.3, bf16[1,9216]{1,0:T(2,128)(2,1)S(1)} %pad_maximum_fusion.refs_3_, f32[128,8]{1,0:T(8,128)S(1)} %bitcast.38, ...), custom_call_target="tpu_custom_call" | custom-call | flops 1509949440 | bytes 11796480 | tf_op jit(solution)/shard_map/pallas_call | solution.py:295
  199.8 58.5 %all_to_all.26 = bf16[16,16,9216]{2,1,0:T(8,128)(2,1)} all-to-all(bf16[16,16,9216]{2,1,0:T(8,128)(2,1)} %bitcast.51), channel_id=1, replica_groups=mesh['groups'=2,'row'=4,'zh'=2,'zl'=2] {'groups','row','zl'}, dimensions={0} | all-to-all | bytes 9437184 | tf_op jit(solution)/shard_map/all_to_all | solution.py:394
  258.3 8.6 %shard_map.96 = (bf16[128,4608]{1,0:T(8,128)(2,1)S(1)}, bf16[128,4608]{1,0:T(8,128)(2,1)S(1)}) custom-call(bf16[256,9216]{1,0:T(8,128)(2,1)} %bitcast.48), custom_call_target="tpu_custom_call" | custom-call | flops 905969664 | bytes 14155776 | tf_op jit(solution)/shard_map/pallas_call | solution.py:246
  269.0 4.8 %all-to-all-start.3 = ((bf16[16,8,4608]{2,1,0:T(8,128)(2,1)}), bf16[16,8,4608]{2,1,0:T(8,128)(2,1)}, u32[]{:S(2)}, u32[]{:S(2)}) async-start(bf16[16,8,4608]{2,1,0:T(8,128)(2,1)} %bitcast.43), calls=%async_computation.3 | async-start | bytes 2359296 | tf_op jit(solution)/shard_map/all_to_all | solution.py:394
  273.7 3.8 shard_map.97.refs_2_
  279.0 10.5 %all-to-all-done.3 = bf16[16,8,4608]{2,1,0:T(8,128)(2,1)} async-done(((bf16[16,8,4608]{2,1,0:T(8,128)(2,1)}), bf16[16,8,4608]{2,1,0:T(8,128)(2,1)}, u32[]{:S(2)}, u32[]{:S(2)}) %all-to-all-start.3) | async-done | bytes 1179680 | tf_op jit(solution)/shard_map/all_to_all | solution.py:394
  289.5 3.7 shard_map.98
  294.3 5.3 %all-to-all-start.4 = ((bf16[16,8,4608]{2,1,0:T(8,128)(2,1)}), bf16[16,8,4608]{2,1,0:T(8,128)(2,1)}, u32[]{:S(2)}, u32[]{:S(2)}) async-start(bf16[16,8,4608]{2,1,0:T(8,128)(2,1)} %bitcast.42), calls=%async_computation.4 | async-start | bytes 2359296 | tf_op jit(solution)/shard_map/all_to_all | solution.py:394
  301.2 5.8 %collective-permute-start.8 = (bf16[4608,128]{1,0:T(8,128)(2,1)}, bf16[4608,128]{1,0:T(8,128)(2,1)}, u32[]{:S(2)}, u32[]{:S(2)}) collective-permute-start(bf16[4608,128]{1,0:T(8,128)(2,1)} %copy-done.5), channel_id=1, source_target_pairs={{0,2},{18,16},{1,3},{19,17},{4,6},{22,20},{5,7},{23,21},{8,10},{26... | collective-permute-start | bytes 3538952 | tf_op jit(solution)/shard_map/ppermute | solution.py:420
  307.0 31.4 %all-to-all-done.4 = bf16[16,8,4608]{2,1,0:T(8,128)(2,1)} async-done(((bf16[16,8,4608]{2,1,0:T(8,128)(2,1)}), bf16[16,8,4608]{2,1,0:T(8,128)(2,1)}, u32[]{:S(2)}, u32[]{:S(2)}) %all-to-all-start.4) | async-done | bytes 1179680 | tf_op jit(solution)/shard_map/all_to_all | solution.py:394
  338.3 3.8 shard_map.99.here_ref
  344.4 12.5 %collective-permute-done.8.beside_ref = bf16[4608,128]{1,0:T(8,128)(2,1)} collective-permute-done((bf16[4608,128]{1,0:T(8,128)(2,1)}, bf16[4608,128]{1,0:T(8,128)(2,1)}, u32[]{:S(2)}, u32[]{:S(2)}) %collective-permute-start.8) | collective-permute-done | bytes 1179680 | tf_op jit(solution)/shard_map/ppermute | solution.py:420
  356.9 15.9 %collective-permute-done.9.back_ref = bf16[4608,128]{1,0:T(8,128)(2,1)S(1)} collective-permute-done((bf16[4608,128]{1,0:T(8,128)(2,1)S(1)}, bf16[4608,128]{1,0:T(8,128)(2,1)S(1)}, u32[]{:S(2)}, u32[]{:S(2)}) %collective-permute-start.9) | collective-permute-done | bytes 1179680 | tf_op jit(solution)/shard_map/ppermute | solution.py:424
  373.8 72.6 %shard_map.100 = bf16[2,4608,128]{2,1,0:T(8,128)(2,1)} custom-call(bf16[4608,128]{1,0:T(8,128)(2,1)} %copy-done.4, bf16[4608,128]{1,0:T(8,128)(2,1)} %collective-permute-done.8.beside_ref, bf16[4608,128]{1,0:T(8,128)(2,1)} %copy-done.9, bf16[4608,128]{1,0:T(8,128)(2,1)} %collective-permute-done.10.across_ref), custom_call_target="tpu_custom_call" | custom-call | tf_op jit(solution)/shard_map/pallas_call | solution.py:425
  (68 shorter events, 30.5 us)
Async XLA Ops:
  0.0 7.5 %copy-start.8 = (bf16[96,96,128]{2,1,0:T(8,128)(2,1)S(1)}, bf16[96,96,128]{2,1,0:T(8,128)(2,1)}, u32[]{:S(2)}) copy-start(bf16[96,96,128]{2,1,0:T(8,128)(2,1)} %param.9) | copy-start | bytes 7077892
  1.1 33.8 %collective-permute-start.6 = (bf16[36,128]{1,0:T(8,128)(2,1)S(1)}, bf16[36,128]{1,0:T(8,128)(2,1)S(1)}, u32[]{:S(2)}, u32[]{:S(2)}) collective-permute-start(bf16[36,128]{1,0:T(8,128)(2,1)S(1)} %reshape.56), channel_id=1, source_target_pairs={{0,16},{16,0},{1,17},{17,1},{2,18},{18,2},{3,19},{19,3},{4,20},{20... | collective-permute-start | bytes 27656 | tf_op jit(solution)/shard_map/ppermute | solution.py:323
  1.6 9.4 %copy-start.10 = (bf16[2,128,128]{2,1,0:T(8,128)(2,1)S(1)}, bf16[2,128,128]{2,1,0:T(8,128)(2,1)}, u32[]{:S(2)}) copy-start(bf16[2,128,128]{2,1,0:T(8,128)(2,1)} %param.14) | copy-start | bytes 196612
  1.6 9.5 %copy-start.11 = (bf16[2,128,128]{2,1,0:T(8,128)(2,1)S(1)}, bf16[2,128,128]{2,1,0:T(8,128)(2,1)}, u32[]{:S(2)}) copy-start(bf16[2,128,128]{2,1,0:T(8,128)(2,1)} %param.17) | copy-start | bytes 196612
  4.0 30.7 %copy-start.12 = (f32[2,128]{1,0:T(2,128)S(1)}, f32[2,128]{1,0:T(2,128)}, u32[]{:S(2)}) copy-start(f32[2,128]{1,0:T(2,128)} %param.16) | copy-start | bytes 3076
  4.0 30.7 %copy-start.13 = (f32[2,128]{1,0:T(2,128)S(1)}, f32[2,128]{1,0:T(2,128)}, u32[]{:S(2)}) copy-start(f32[2,128]{1,0:T(2,128)} %param.15) | copy-start | bytes 3076
  4.0 30.7 %copy-start.14 = (f32[2,128]{1,0:T(2,128)S(1)}, f32[2,128]{1,0:T(2,128)}, u32[]{:S(2)}) copy-start(f32[2,128]{1,0:T(2,128)} %param.12) | copy-start | bytes 3076
  4.0 30.7 %copy-start.15 = (f32[2,128]{1,0:T(2,128)S(1)}, f32[2,128]{1,0:T(2,128)}, u32[]{:S(2)}) copy-start(f32[2,128]{1,0:T(2,128)} %param.11) | copy-start | bytes 3076
  4.0 16.5 %collective-permute-start.1 = (bf16[2304,128]{1,0:T(8,128)(2,1)}, bf16[2304,128]{1,0:T(8,128)(2,1)S(1)}, u32[]{:S(2)}, u32[]{:S(2)}) collective-permute-start(bf16[2304,128]{1,0:T(8,128)(2,1)} %bitcast.1), channel_id=1, source_target_pairs={{0,16},{16,0},{1,17},{17,1},{2,18},{18,2},{3,19},{19,3},{4,20},{20... | collective-permute-start | bytes 1769480 | tf_op jit(solution)/shard_map/ppermute | solution.py:323
  5.6 26.2 %collective-permute-start.3 = (bf16[2304,128]{1,0:T(8,128)(2,1)}, bf16[2304,128]{1,0:T(8,128)(2,1)}, u32[]{:S(2)}, u32[]{:S(2)}) collective-permute-start(bf16[2304,128]{1,0:T(8,128)(2,1)} %bitcast.2), channel_id=1, source_target_pairs={{0,16},{16,0},{1,17},{17,1},{2,18},{18,2},{3,19},{19,3},{4,20},{20... | collective-permute-start | bytes 1769480 | tf_op jit(solution)/shard_map/ppermute | solution.py:323
  6.2 30.0 %collective-permute-start.5 = (bf16[36,128]{1,0:T(8,128)(2,1)S(1)}, bf16[36,128]{1,0:T(8,128)(2,1)S(1)}, u32[]{:S(2)}, u32[]{:S(2)}) collective-permute-start(bf16[36,128]{1,0:T(8,128)(2,1)S(1)} %reshape.55), channel_id=1, source_target_pairs={{2,0},{16,18},{3,1},{17,19},{6,4},{20,22},{7,5},{21,23},{10,8},{24... | collective-permute-start | bytes 27656 | tf_op jit(solution)/shard_map/ppermute | solution.py:319
  8.6 68.2 %collective-permute-start = (bf16[4608,128]{1,0:T(8,128)(2,1)}, bf16[4608,128]{1,0:T(8,128)(2,1)}, u32[]{:S(2)}, u32[]{:S(2)}) collective-permute-start(bf16[4608,128]{1,0:T(8,128)(2,1)} %bitcast.refs_0_), channel_id=1, source_target_pairs={{2,0},{16,18},{3,1},{17,19},{6,4},{20,22},{7,5},{21,23},{10,8},{24... | collective-permute-start | bytes 3538952 | tf_op jit(solution)/shard_map/ppermute | solution.py:319
  20.5 56.2 %collective-permute-start.2 = (bf16[2304,128]{1,0:T(8,128)(2,1)S(1)}, bf16[2304,128]{1,0:T(8,128)(2,1)}, u32[]{:S(2)}, u32[]{:S(2)}) collective-permute-start(bf16[2304,128]{1,0:T(8,128)(2,1)S(1)} %collective-permute-done.1.refs_1_), channel_id=1, source_target_pairs={{0,2},{18,16},{1,3},{19,17},{4,6},{22,20},{5,7},{23,21},{8,10},{26... | collective-permute-start | bytes 1769480 | tf_op jit(solution)/shard_map/ppermute | solution.py:325
  31.8 44.9 %collective-permute-start.4 = (bf16[2304,128]{1,0:T(8,128)(2,1)}, bf16[2304,128]{1,0:T(8,128)(2,1)}, u32[]{:S(2)}, u32[]{:S(2)}) collective-permute-start(bf16[2304,128]{1,0:T(8,128)(2,1)} %collective-permute-done.3.refs_2_), channel_id=1, source_target_pairs={{0,2},{18,16},{1,3},{19,17},{4,6},{22,20},{5,7},{23,21},{8,10},{26... | collective-permute-start | bytes 1769480 | tf_op jit(solution)/shard_map/ppermute | solution.py:325
  34.8 36.3 %collective-permute-start.7 = (bf16[36,128]{1,0:T(8,128)(2,1)S(1)}, bf16[36,128]{1,0:T(8,128)(2,1)S(1)}, u32[]{:S(2)}, u32[]{:S(2)}) collective-permute-start(bf16[36,128]{1,0:T(8,128)(2,1)S(1)} %collective-permute-done.6), channel_id=1, source_target_pairs={{0,2},{18,16},{1,3},{19,17},{4,6},{22,20},{5,7},{23,21},{8,10},{26... | collective-permute-start | bytes 27656 | tf_op jit(solution)/shard_map/ppermute | solution.py:325
  82.4 75.8 %copy-start.1 = (bf16[128,9216]{1,0:T(8,128)(2,1)}, bf16[128,9216]{1,0:T(8,128)(2,1)S(1)}, u32[]{:S(2)}) copy-start(bf16[128,9216]{1,0:T(8,128)(2,1)S(1)} %get-tuple-element.17.refs_0_.refs_1_) | copy-start | bytes 7077892
  151.8 1.4 copy-start.2
  153.2 35.3 %all-to-all-start.1 = ((bf16[16,8,9216]{2,1,0:T(8,128)(2,1)}), bf16[16,8,9216]{2,1,0:T(8,128)(2,1)}, u32[]{:S(2)}, u32[]{:S(2)}) async-start(bf16[16,8,9216]{2,1,0:T(8,128)(2,1)} %bitcast.34), calls=%async_computation.1 | async-start | bytes 4718592 | tf_op jit(solution)/shard_map/all_to_all | solution.py:394
  162.1 1.5 copy-start.3
  269.0 20.5 %all-to-all-start.3 = ((bf16[16,8,4608]{2,1,0:T(8,128)(2,1)}), bf16[16,8,4608]{2,1,0:T(8,128)(2,1)}, u32[]{:S(2)}, u32[]{:S(2)}) async-start(bf16[16,8,4608]{2,1,0:T(8,128)(2,1)} %bitcast.43), calls=%async_computation.3 | async-start | bytes 2359296 | tf_op jit(solution)/shard_map/all_to_all | solution.py:394
  294.3 44.1 %all-to-all-start.4 = ((bf16[16,8,4608]{2,1,0:T(8,128)(2,1)}), bf16[16,8,4608]{2,1,0:T(8,128)(2,1)}, u32[]{:S(2)}, u32[]{:S(2)}) async-start(bf16[16,8,4608]{2,1,0:T(8,128)(2,1)} %bitcast.42), calls=%async_computation.4 | async-start | bytes 2359296 | tf_op jit(solution)/shard_map/all_to_all | solution.py:394
  299.5 44.9 %collective-permute-start.10 = (bf16[4608,128]{1,0:T(8,128)(2,1)}, bf16[4608,128]{1,0:T(8,128)(2,1)}, u32[]{:S(2)}, u32[]{:S(2)}) collective-permute-start(bf16[4608,128]{1,0:T(8,128)(2,1)} %copy-done.5), channel_id=1, source_target_pairs={{2,16},{16,2},{3,17},{17,3},{6,20},{20,6},{7,21},{21,7},{10,24},{2... | collective-permute-start | bytes 3538952 | tf_op jit(solution)/shard_map/ppermute | solution.py:420
  301.2 55.7 %collective-permute-start.8 = (bf16[4608,128]{1,0:T(8,128)(2,1)}, bf16[4608,128]{1,0:T(8,128)(2,1)}, u32[]{:S(2)}, u32[]{:S(2)}) collective-permute-start(bf16[4608,128]{1,0:T(8,128)(2,1)} %copy-done.5), channel_id=1, source_target_pairs={{0,2},{18,16},{1,3},{19,17},{4,6},{22,20},{5,7},{23,21},{8,10},{26... | collective-permute-start | bytes 3538952 | tf_op jit(solution)/shard_map/ppermute | solution.py:420
  343.1 29.7 %collective-permute-start.9 = (bf16[4608,128]{1,0:T(8,128)(2,1)S(1)}, bf16[4608,128]{1,0:T(8,128)(2,1)S(1)}, u32[]{:S(2)}, u32[]{:S(2)}) collective-permute-start(bf16[4608,128]{1,0:T(8,128)(2,1)S(1)} %shard_map.99.here_ref), channel_id=1, source_target_pairs={{2,18},{16,0},{3,19},{17,1},{6,22},{20,4},{7,23},{21,5},{10,26},{2... | collective-permute-start | bytes 3538952 | tf_op jit(solution)/shard_map/ppermute | solution.py:424
  (6 other events, 6.6 us)

commit v6 on v5

--- a/solution.py
+++ b/solution.py
@@ -44,25 +44,21 @@
     lr_ref[...] = both.reshape(2 * width, tile).astype(jnp.bfloat16)
 
 
-def first_kernel(peers, n_far, own_ref, *refs):
-    far_refs, (mask_ref, small_ref, weight_ref), (lr_ref, zt_ref, z_ref) = (
-        refs[:n_far], refs[n_far : n_far + 3], refs[-3:],
+def first_kernel(peers, parts, own_ref, *refs):
+    far_refs, (mask_ref, small_ref, weight_ref), (lr_ref, zt_ref) = (
+        refs[: len(parts)], refs[len(parts) : -2], refs[-2:],
     )
     home = lax.axis_index("groups") == lax.axis_index("zh")
-    per_part = pl.num_programs(0) // n_far
-
-    @pl.when(home)
-    def _own():
-        z_ref[...] = own_ref[...].astype(jnp.float32)
-
-    for k, far_ref in enumerate(far_refs):
-
-        @pl.when(jnp.logical_and(jnp.logical_not(home), pl.program_id(0) // per_part == k))
-        def _far(far_ref=far_ref):
-            z_ref[...] = far_ref[...].astype(jnp.float32)
-
-    zt = z_ref[...].T
-    zt_ref[...] = zt.astype(jnp.bfloat16)
+    step = pl.program_id(0)
+
+    def put(z_ref):
+        zt_ref[...] = z_ref[...].astype(jnp.float32).T.astype(jnp.bfloat16)
+
+    pl.when(home)(lambda: put(own_ref))
+    for (begin, end), far_ref in zip(parts, far_refs):
+        here = jnp.logical_and(step >= begin, step < end)
+        pl.when(jnp.logical_and(jnp.logical_not(home), here))(functools.partial(put, far_ref))
+    zt = zt_ref[...].astype(jnp.float32)
     emit_projections(peers, 0, zt, mask_ref, small_ref, weight_ref, lr_ref)
 
 
@@ -94,27 +90,19 @@
     out_ref[...] = fresh.T.astype(jnp.bfloat16)
 
 
-def assemble_kernel(here_ref, beside_ref, back_ref, across_ref, out_ref, sems):
-    upper = lax.axis_index("groups")
-    home = upper == lax.axis_index("zh")
-
-    def put(mine_ref, others_ref):
-        copies = (
-            pltpu.make_async_copy(mine_ref, out_ref.at[upper], sems.at[0]),
-            pltpu.make_async_copy(others_ref, out_ref.at[1 - upper], sems.at[1]),
-        )
-        for copy in copies:
-            copy.start()
-        for copy in copies:
-            copy.wait()
-
-    @pl.when(home)
-    def _home():
-        put(here_ref, back_ref)
-
-    @pl.when(jnp.logical_not(home))
-    def _away():
-        put(beside_ref, across_ref)
+def assemble_kernel(per_half, place_ref, here_ref, beside_ref, back_ref, across_ref, out_ref):
+    mine = pl.program_id(0) // per_half == place_ref[0]
+    home = place_ref[1] == 1
+    for side_of, whose, ref in (
+        (home, mine, here_ref),
+        (jnp.logical_not(home), mine, beside_ref),
+        (home, jnp.logical_not(mine), back_ref),
+        (jnp.logical_not(home), jnp.logical_not(mine), across_ref),
+    ):
+
+        @pl.when(jnp.logical_and(side_of, whose))
+        def _put(ref=ref):
+            out_ref[...] = ref[...]
 
 
 def triangle_kernel(blocks, side, own, incoming, n_in, *refs):
@@ -315,14 +303,16 @@
 CUBE = ("groups", "row", "zl")
 
 
-def gather_group(own_half, other_half, chunks):
+def gather_group(own_half, other_half, cuts):
     early = lax.ppermute(own_half, LINE, ((1, 0), (2, 3)))
-    size = own_half.shape[0] // chunks
     over, late = [], []
-    for k in range(chunks):
-        part = lax.ppermute(other_half[k * size : (k + 1) * size], "groups", SWAP)
+    for begin, end in zip((0, *cuts[:-2]), cuts[:-1]):
+        part = lax.ppermute(other_half[begin:end], "groups", SWAP)
         over.append(part)
         late.append(lax.ppermute(part, LINE, ((0, 1), (3, 2))))
+    rest = other_half[cuts[-2] :]
+    late.append(lax.ppermute(rest, LINE, ((1, 2), (2, 1))))
+    over.append(lax.ppermute(rest, LINE, ((0, 2), (3, 1))))
     return early, over, late
 
 
@@ -344,11 +334,9 @@
     own = width // peers
     pixels = side * side
     strip = side // 2
-    tile = 9 * LANES
-    steps = pixels // tile
     upper = lax.axis_index("groups")
     home = upper == lax.axis_index("zh")
-    mult = 2 * channels * tile
+    mult = 2 * channels
 
     def halves(array):
         return (
@@ -356,15 +344,21 @@
             lax.dynamic_slice_in_dim(array, (1 - upper) * strip, strip),
         )
 
-    z_own, z_other = (h.reshape(-1, channels) for h in halves(pair_act))
-    z_early, z_over, z_late = gather_group(z_own, z_other, 2)
     m_own, m_other = (
         h.reshape(-1, LANES) for h in halves(pair_mask.astype(jnp.bfloat16))
     )
-    m_early, (m_over,), (m_late,) = gather_group(m_own, m_other, 1)
+    m_next = lax.ppermute(
+        jnp.where(home, m_other, m_own), LINE, ((1, 0), (2, 3), (0, 2), (3, 1))
+    )
+    m_across = lax.ppermute(m_other, LINE, ((1, 2), (2, 1)))
     m_pieces = [
-        jnp.where(home, a, b).reshape(1, -1) for a, b in ((m_own, m_over), (m_early, m_late))
+        jnp.where(home, a, b).reshape(1, -1) for a, b in ((m_own, m_next), (m_next, m_across))
     ]
+    z_own, z_other = (h.reshape(-1, channels) for h in halves(pair_act))
+    tile = 9 * LANES
+    per_piece = pixels // 2 // tile
+    tiles = (1, per_piece - 1, per_piece)
+    z_early, z_over, z_late = gather_group(z_own, z_other, [n * tile for n in tiles])
     small = jnp.stack([input_gain, input_bias, output_gain, output_bias], axis=1)
     small = small.reshape(-1, channels).T
     weights = jnp.concatenate(
@@ -373,36 +367,40 @@
     fixed = (small, weights)
 
     def first(piece, ours, far, mask, kept):
-        per_part = steps // 2 // len(far)
-        tiled = [(ours, 0, steps // 2, True)]
-        tiled += [(part, -k * per_part, per_part, True) for k, part in enumerate(far)]
-        tiled += [(mask, 0, steps // 2, False)]
+        parts = list(zip((0, *tiles), tiles))
+        tiled = [(ours, 0, per_piece, True)]
+        tiled += [
+            (part, -begin, end - begin, True) for part, (begin, end) in zip(far, parts)
+        ]
+        tiled += [(mask, 0, per_piece, False)]
         return pixel_call(
-            functools.partial(first_kernel, peers, len(far)),
-            tiled, fixed, (2 * width, channels), steps // 2, tile, steps // 2 * mult * 4 * width,
-            start=piece * steps // 2, pixels=pixels, kept=kept,
-            scratch=(pltpu.VMEM((tile, channels), jnp.float32),),
+            functools.partial(first_kernel, peers, parts),
+            tiled, fixed, (2 * width, channels), per_piece, tile, pixels // 2 * mult * 4 * width,
+            start=piece * per_piece, pixels=pixels, kept=kept,
         )
+
+    begun = first(0, z_own, z_over, m_pieces[0], ())
+    sent, zt = first(1, z_early, z_late, m_pieces[1], begun)
+    wide = 2 * tile
+    steps = pixels // wide
 
     def gate_of(zt, u):
         return pixel_call(
             functools.partial(gate_kernel, u), [(zt, 0, steps, False)], fixed, (channels,),
-            steps, tile, steps * mult * channels,
+            steps, wide, pixels * mult * channels,
         )[0]
 
     def exchange(array):
         there = lax.all_to_all(array.reshape(peers, -1, array.shape[1]), CUBE, 0, 0)
         return there.reshape(array.shape)
 
-    begun = first(0, z_own, z_over, m_pieces[0], ())
-    sent, zt = first(1, z_early, z_late, m_pieces[1], begun)
     gate = gate_of(zt, 0)
     triangle = exchange(*triangle_call([exchange(sent)], 1, blocks, side, own, False))
     mask = jnp.concatenate(m_pieces, axis=1)
     sent, zt = pixel_call(
         functools.partial(middle_kernel, peers),
         [(a, 0, steps, False) for a in (triangle, zt, gate, mask)], fixed, (2 * width, channels),
-        steps, tile, steps * mult * 5 * width,
+        steps, wide, pixels * mult * 5 * width,
     )
     gate = gate_of(zt, 1)
     products = triangle_call([exchange(sent)], 2, blocks, side, own, True)
@@ -412,7 +410,7 @@
         return pixel_call(
             last_kernel,
             [(triangle, 0, steps // 2, False), (zt, at, steps, False), (gate, at, steps, False)],
-            fixed, (channels,), steps // 2, tile, steps // 2 * mult * channels, row_major_out=True,
+            fixed, (channels,), steps // 2, wide, pixels // 2 * mult * channels, row_major_out=True,
         )[0]
 
     there = finish(1, exchange(products[1]))
@@ -422,13 +420,28 @@
     there, waiting = lax.optimization_barrier((there, products[0]))
     here = finish(0, exchange(waiting))
     back = lax.ppermute(here, LINE, ((1, 3), (2, 0)))
+    place = jnp.stack([upper, home.astype(upper.dtype)])
+    per_half = steps // 2
+
+    def source(of_mine, at_home):
+        def index(i, place_ref):
+            wanted = jnp.logical_and(
+                (i // per_half == place_ref[0]) == of_mine, (place_ref[1] == 1) == at_home
+            )
+            return jnp.where(wanted, lax.rem(i, per_half), 0), 0
+
+        return pl.BlockSpec((wide, channels), index)
+
     return pl.pallas_call(
-        assemble_kernel,
-        in_specs=[pl.BlockSpec(memory_space=pl.ANY)] * 4,
-        out_specs=pl.BlockSpec(memory_space=pl.ANY),
-        out_shape=jax.ShapeDtypeStruct((2, *here.shape), here.dtype),
-        scratch_shapes=[pltpu.SemaphoreType.DMA((2,))],
-    )(here, beside, back, across).reshape(side, side, channels)
+        functools.partial(assemble_kernel, per_half),
+        grid_spec=pltpu.PrefetchScalarGridSpec(
+            num_scalar_prefetch=1,
+            grid=(steps,),
+            in_specs=[source(*w) for w in ((True, True), (True, False), (False, True), (False, False))],
+            out_specs=pl.BlockSpec((wide, channels), lambda i, place_ref: (i, 0)),
+        ),
+        out_shape=jax.ShapeDtypeStruct((pixels, channels), jnp.bfloat16),
+    )(place, here, beside, back, across).reshape(side, side, channels)
 
 
 def layer_norm(values, gain, bias, axis):

time: 448 us -> 374 us (0.83)
  the two profiles are of different devices: /device:TPU:20 before, /device:TPU:4 now
where the time goes in v6:
time: 374 us; the launch traced here: 373 us
  waiting for transfers between devices  135 us (36%)
  blocking collectives  127 us (34%)
  Pallas kernels  54.7 us (15%)
  starting transfers between devices  40.4 us (11%)
  local copies, waits for them, and re-layouts  15.1 us (4%)
    all_to_all x2, blocking collectives, exchange(): there = lax.all_to_all(array.reshape(peers, -1, array.shape[1]), CUBE, 0, 0)  127 us
    all_to_all x3, waiting for transfers between devices, exchange(): there = lax.all_to_all(array.reshape(peers, -1, array.shape[1]), CUBE, 0, 0)  59 us
    ppermute x2, waiting for transfers between devices, gather_group(): late.append(lax.ppermute(part, LINE, ((0, 1), (3, 2))))  33.4 us
    pallas_call x7, Pallas kernels, pixel_call(): pl.pallas_call(kernel, grid=(steps,), in_specs=in_specs, out_specs=[spec(...  33 us
    ppermute x2, waiting for transfers between devices, by_kernels(): lax.ppermute(there, LINE, pairs)  28.8 us
    pallas_call x2, Pallas kernels, triangle_call(): pl.pallas_call(functools.partial(triangle_kernel, blocks, side, own, inco...  16.6 us
    all_to_all x3, starting transfers between devices, exchange(): there = lax.all_to_all(array.reshape(peers, -1, array.shape[1]), CUBE, 0, 0)  15 us
    ppermute x1, waiting for transfers between devices, by_kernels(): lax.ppermute(jnp.where(home, m_other, m_own), LINE, ((1, 0), (2, 3), (0,...  13.7 us
  transfers between devices with their start and end apart: 15, of which 9 were waited for; matrix products, arithmetic and copies ran while one was open for 1% of the time, Pallas kernels for 4%

profile of v6, /device:TPU:4, one launch (start us, length us, event | category | flops | bytes accessed | tf_op | source)
XLA Modules:
  0.0 373.2 jit_solution(16683000613870853069)
XLA Ops:
  6.0 4.4 %collective-permute-start.5 = (bf16[1152,128]{1,0:T(8,128)(2,1)}, bf16[1152,128]{1,0:T(8,128)(2,1)}, u32[]{:S(2)}, u32[]{:S(2)}) collective-permute-start(bf16[1152,128]{1,0:T(8,128)(2,1)} %bitcast.5), channel_id=1, source_target_pairs={{2,16},{16,2},{3,17},{17,3},{6,20},{20,6},{7,21},{21,7},{10,24},{2... | collective-permute-start | bytes 884744 | tf_op jit(solution)/shard_map/ppermute | solution.py:314
  10.7 3.2 collective-permute-start.7
  16.8 13.7 %collective-permute-done.6 = bf16[36,128]{1,0:T(8,128)(2,1)S(1)} collective-permute-done((bf16[36,128]{1,0:T(8,128)(2,1)S(1)}, bf16[36,128]{1,0:T(8,128)(2,1)S(1)}, u32[]{:S(2)}, u32[]{:S(2)}) %collective-permute-start.6) | collective-permute-done | bytes 9248 | tf_op jit(solution)/shard_map/ppermute | solution.py:350
  31.8 5.7 %collective-permute-start = (bf16[4608,128]{1,0:T(8,128)(2,1)}, bf16[4608,128]{1,0:T(8,128)(2,1)S(1)}, u32[]{:S(2)}, u32[]{:S(2)}) collective-permute-start(bf16[4608,128]{1,0:T(8,128)(2,1)} %bitcast.2.refs_0_), channel_id=1, source_target_pairs={{2,0},{16,18},{3,1},{17,19},{6,4},{20,22},{7,5},{21,23},{10,8},{24... | collective-permute-start | bytes 3538952 | tf_op jit(solution)/shard_map/ppermute | solution.py:307
  40.4 5.6 %shard_map.91 = (bf16[256,9216]{1,0:T(8,128)(2,1)}, bf16[128,9216]{1,0:T(8,128)(2,1)S(1)}) custom-call(bf16[4608,128]{1,0:T(8,128)(2,1)} %bitcast.2.refs_0_, bf16[1152,128]{1,0:T(8,128)(2,1)} %collective-permute-done.1.refs_1_, bf16[2304,128]{1,0:T(8,128)(2,1)S(1)} %collective-permute-done.3.refs_2_, bf16[1152,128]{1,0:T(8,128)(2,1)S(1)} %collective-permute-done.8.refs_3_, ...), custom_call_target="tpu_custom_call" | custom-call | flops 603979776 | bytes 5898240 | tf_op jit(solution)/shard_map/pallas_call | solution.py:283
  46.0 22.0 %collective-permute-done.2.refs_1_ = bf16[1152,128]{1,0:T(8,128)(2,1)S(1)} collective-permute-done((bf16[1152,128]{1,0:T(8,128)(2,1)}, bf16[1152,128]{1,0:T(8,128)(2,1)S(1)}, u32[]{:S(2)}, u32[]{:S(2)}) %collective-permute-start.2) | collective-permute-done | bytes 294944 | tf_op jit(solution)/shard_map/ppermute | solution.py:312
  68.0 11.5 %collective-permute-done.4.refs_2_ = bf16[2304,128]{1,0:T(8,128)(2,1)S(1)} collective-permute-done((bf16[2304,128]{1,0:T(8,128)(2,1)S(1)}, bf16[2304,128]{1,0:T(8,128)(2,1)S(1)}, u32[]{:S(2)}, u32[]{:S(2)}) %collective-permute-start.4) | collective-permute-done | bytes 589856 | tf_op jit(solution)/shard_map/ppermute | solution.py:312
  79.4 5.2 %shard_map.92 = (bf16[256,9216]{1,0:T(8,128)(2,1)}, bf16[128,9216]{1,0:T(8,128)(2,1)S(1)}) custom-call(bf16[4608,128]{1,0:T(8,128)(2,1)S(1)} %collective-permute-done.refs_0_, bf16[1152,128]{1,0:T(8,128)(2,1)S(1)} %collective-permute-done.2.refs_1_, ...), custom_call_target="tpu_custom_call", output_to_operand_aliasing={{0}: (7, {}), {1}: (8, {})} | custom-call | flops 603979776 | bytes 5898240 | tf_op jit(solution)/shard_map/pallas_call | solution.py:283
  84.6 67.5 %all_to_all.25 = bf16[16,16,9216]{2,1,0:T(8,128)(2,1)} all-to-all(bf16[16,16,9216]{2,1,0:T(8,128)(2,1)} %bitcast.47), channel_id=1, replica_groups=mesh['groups'=2,'row'=4,'zh'=2,'zl'=2] {'groups','row','zl'}, dimensions={0} | all-to-all | bytes 9437184 | tf_op jit(solution)/shard_map/all_to_all | solution.py:394
  152.1 8.0 %shard_map.93 = bf16[128,9216]{1,0:T(8,128)(2,1)S(1)} custom-call(bf16[256,9216]{1,0:T(8,128)(2,1)} %bitcast.46), custom_call_target="tpu_custom_call" | custom-call | flops 905969664 | bytes 14155776 | tf_op jit(solution)/shard_map/pallas_call | solution.py:234
  161.5 4.7 %all-to-all-start.1 = ((bf16[16,8,9216]{2,1,0:T(8,128)(2,1)}), bf16[16,8,9216]{2,1,0:T(8,128)(2,1)}, u32[]{:S(2)}, u32[]{:S(2)}) async-start(bf16[16,8,9216]{2,1,0:T(8,128)(2,1)} %bitcast.35), calls=%async_computation.1 | async-start | bytes 4718592 | tf_op jit(solution)/shard_map/all_to_all | solution.py:394
  170.9 25.7 %all-to-all-done.1 = bf16[16,8,9216]{2,1,0:T(8,128)(2,1)} async-done(((bf16[16,8,9216]{2,1,0:T(8,128)(2,1)}), bf16[16,8,9216]{2,1,0:T(8,128)(2,1)}, u32[]{:S(2)}, u32[]{:S(2)}) %all-to-all-start.1) | async-done | bytes 2359328 | tf_op jit(solution)/shard_map/all_to_all | solution.py:394
  196.6 9.5 %shard_map.95 = (bf16[256,9216]{1,0:T(8,128)(2,1)}, bf16[128,9216]{1,0:T(8,128)(2,1)S(1)}) custom-call(bf16[128,9216]{1,0:T(8,128)(2,1)} %bitcast.16.refs_0_, bf16[128,9216]{1,0:T(8,128)(2,1)} %copy-done.1, bf16[128,9216]{1,0:T(8,128)(2,1)} %copy-done.3, bf16[1,9216]{1,0:T(2,128)(2,1)S(1)} %pad_maximum_fusion.refs_3_, f32[128,8]{1,0:T(8,128)S(1)} %bitcast.39, ...), custom_call_target="tpu_custom_call" | custom-call | flops 1509949440 | bytes 11796480 | tf_op jit(solution)/shard_map/pallas_call | solution.py:283
  206.1 59.1 %all_to_all.26 = bf16[16,16,9216]{2,1,0:T(8,128)(2,1)} all-to-all(bf16[16,16,9216]{2,1,0:T(8,128)(2,1)} %bitcast.48), channel_id=1, replica_groups=mesh['groups'=2,'row'=4,'zh'=2,'zl'=2] {'groups','row','zl'}, dimensions={0} | all-to-all | bytes 9437184 | tf_op jit(solution)/shard_map/all_to_all | solution.py:394
  265.2 8.6 %shard_map.96 = (bf16[128,4608]{1,0:T(8,128)(2,1)S(1)}, bf16[128,4608]{1,0:T(8,128)(2,1)S(1)}) custom-call(bf16[256,9216]{1,0:T(8,128)(2,1)} %bitcast.45), custom_call_target="tpu_custom_call" | custom-call | flops 905969664 | bytes 14155776 | tf_op jit(solution)/shard_map/pallas_call | solution.py:234
  275.9 5.0 %all-to-all-start.3 = ((bf16[16,8,4608]{2,1,0:T(8,128)(2,1)}), bf16[16,8,4608]{2,1,0:T(8,128)(2,1)}, u32[]{:S(2)}, u32[]{:S(2)}) async-start(bf16[16,8,4608]{2,1,0:T(8,128)(2,1)} %bitcast.44), calls=%async_computation.3 | async-start | bytes 2359296 | tf_op jit(solution)/shard_map/all_to_all | solution.py:394
  285.4 11.3 %all-to-all-done.3 = bf16[16,8,4608]{2,1,0:T(8,128)(2,1)} async-done(((bf16[16,8,4608]{2,1,0:T(8,128)(2,1)}), bf16[16,8,4608]{2,1,0:T(8,128)(2,1)}, u32[]{:S(2)}, u32[]{:S(2)}) %all-to-all-start.3) | async-done | bytes 1179680 | tf_op jit(solution)/shard_map/all_to_all | solution.py:394
  300.6 5.2 %all-to-all-start.4 = ((bf16[16,8,4608]{2,1,0:T(8,128)(2,1)}), bf16[16,8,4608]{2,1,0:T(8,128)(2,1)}, u32[]{:S(2)}, u32[]{:S(2)}) async-start(bf16[16,8,4608]{2,1,0:T(8,128)(2,1)} %bitcast.43), calls=%async_computation.4 | async-start | bytes 2359296 | tf_op jit(solution)/shard_map/all_to_all | solution.py:394
  307.1 3.5 collective-permute-start.11
  310.6 22.0 %all-to-all-done.4 = bf16[16,8,4608]{2,1,0:T(8,128)(2,1)} async-done(((bf16[16,8,4608]{2,1,0:T(8,128)(2,1)}), bf16[16,8,4608]{2,1,0:T(8,128)(2,1)}, u32[]{:S(2)}, u32[]{:S(2)}) %all-to-all-start.4) | async-done | bytes 1179680 | tf_op jit(solution)/shard_map/all_to_all | solution.py:394
  332.6 3.7 shard_map.99.here_ref
  338.2 24.0 %collective-permute-done.9.beside_ref = bf16[4608,128]{1,0:T(8,128)(2,1)} collective-permute-done((bf16[4608,128]{1,0:T(8,128)(2,1)}, bf16[4608,128]{1,0:T(8,128)(2,1)}, u32[]{:S(2)}, u32[]{:S(2)}) %collective-permute-start.9) | collective-permute-done | bytes 1179680 | tf_op jit(solution)/shard_map/ppermute | solution.py:418
  362.3 4.8 %collective-permute-done.11.across_ref = bf16[4608,128]{1,0:T(8,128)(2,1)} collective-permute-done((bf16[4608,128]{1,0:T(8,128)(2,1)}, bf16[4608,128]{1,0:T(8,128)(2,1)}, u32[]{:S(2)}, u32[]{:S(2)}) %collective-permute-start.11) | collective-permute-done | bytes 1179680 | tf_op jit(solution)/shard_map/ppermute | solution.py:418
  368.1 5.1 %shard_map.100 = bf16[9216,128]{1,0:T(8,128)(2,1)} custom-call(s32[2]{0:T(128)} %pad_add_fusion.place_ref, bf16[4608,128]{1,0:T(8,128)(2,1)} %shard_map.99.here_ref, bf16[4608,128]{1,0:T(8,128)(2,1)} %collective-permute-done.9.beside_ref, bf16[4608,128]{1,0:T(8,128)(2,1)} %copy-done.8, bf16[4608,128]{1,0:T(8,128)(2,1)} %collective-permute-done.11.across_ref), custom_call_target="tpu_custom_call" | custom-call | tf_op jit(solution)/shard_map/pallas_call | solution.py:435
  (71 shorter events, 33.8 us)
Async XLA Ops:
  0.0 10.5 %copy-start.11 = (s32[96,96]{1,0:T(8,128)S(1)}, s32[96,96]{1,0:T(8,128)}, u32[]{:S(2)}) copy-start(s32[96,96]{1,0:T(8,128)} %param.10) | copy-start | bytes 110596
  0.0 14.1 %copy-start.9 = (bf16[2,128,128]{2,1,0:T(8,128)(2,1)S(1)}, bf16[2,128,128]{2,1,0:T(8,128)(2,1)}, u32[]{:S(2)}) copy-start(bf16[2,128,128]{2,1,0:T(8,128)(2,1)} %param.17) | copy-start | bytes 196612
  0.0 14.2 %copy-start.10 = (bf16[2,128,128]{2,1,0:T(8,128)(2,1)S(1)}, bf16[2,128,128]{2,1,0:T(8,128)(2,1)}, u32[]{:S(2)}) copy-start(bf16[2,128,128]{2,1,0:T(8,128)(2,1)} %param.14) | copy-start | bytes 196612
  0.0 15.5 %copy-start.7 = (bf16[96,96,128]{2,1,0:T(8,128)(2,1)S(1)}, bf16[96,96,128]{2,1,0:T(8,128)(2,1)}, u32[]{:S(2)}) copy-start(bf16[96,96,128]{2,1,0:T(8,128)(2,1)} %param.9) | copy-start | bytes 7077892
  2.1 35.4 %collective-permute-start.1 = (bf16[1152,128]{1,0:T(8,128)(2,1)}, bf16[1152,128]{1,0:T(8,128)(2,1)}, u32[]{:S(2)}, u32[]{:S(2)}) collective-permute-start(bf16[1152,128]{1,0:T(8,128)(2,1)} %bitcast.3), channel_id=1, source_target_pairs={{0,16},{16,0},{1,17},{17,1},{2,18},{18,2},{3,19},{19,3},{4,20},{20... | collective-permute-start | bytes 884744 | tf_op jit(solution)/shard_map/ppermute | solution.py:310
  4.0 34.8 %collective-permute-start.3 = (bf16[2304,128]{1,0:T(8,128)(2,1)}, bf16[2304,128]{1,0:T(8,128)(2,1)S(1)}, u32[]{:S(2)}, u32[]{:S(2)}) collective-permute-start(bf16[2304,128]{1,0:T(8,128)(2,1)} %bitcast.4), channel_id=1, source_target_pairs={{0,16},{16,0},{1,17},{17,1},{2,18},{18,2},{3,19},{19,3},{4,20},{20... | collective-permute-start | bytes 1769480 | tf_op jit(solution)/shard_map/ppermute | solution.py:310
  6.0 40.0 %collective-permute-start.5 = (bf16[1152,128]{1,0:T(8,128)(2,1)}, bf16[1152,128]{1,0:T(8,128)(2,1)}, u32[]{:S(2)}, u32[]{:S(2)}) collective-permute-start(bf16[1152,128]{1,0:T(8,128)(2,1)} %bitcast.5), channel_id=1, source_target_pairs={{2,16},{16,2},{3,17},{17,3},{6,20},{20,6},{7,21},{21,7},{10,24},{2... | collective-permute-start | bytes 884744 | tf_op jit(solution)/shard_map/ppermute | solution.py:314
  10.5 6.1 %copy-start.12 = (f32[2,128]{1,0:T(2,128)S(1)}, f32[2,128]{1,0:T(2,128)}, u32[]{:S(2)}) copy-start(f32[2,128]{1,0:T(2,128)} %param.16) | copy-start | bytes 3076
  10.5 6.1 %copy-start.13 = (f32[2,128]{1,0:T(2,128)S(1)}, f32[2,128]{1,0:T(2,128)}, u32[]{:S(2)}) copy-start(f32[2,128]{1,0:T(2,128)} %param.15) | copy-start | bytes 3076
  10.5 6.1 %copy-start.14 = (f32[2,128]{1,0:T(2,128)S(1)}, f32[2,128]{1,0:T(2,128)}, u32[]{:S(2)}) copy-start(f32[2,128]{1,0:T(2,128)} %param.12) | copy-start | bytes 3076
  10.5 6.1 %copy-start.15 = (f32[2,128]{1,0:T(2,128)S(1)}, f32[2,128]{1,0:T(2,128)}, u32[]{:S(2)}) copy-start(f32[2,128]{1,0:T(2,128)} %param.11) | copy-start | bytes 3076
  10.7 21.1 %collective-permute-start.7 = (bf16[36,128]{1,0:T(8,128)(2,1)S(1)}, bf16[36,128]{1,0:T(8,128)(2,1)S(1)}, u32[]{:S(2)}, u32[]{:S(2)}) collective-permute-start(bf16[36,128]{1,0:T(8,128)(2,1)S(1)} %reshape.56), channel_id=1, source_target_pairs={{2,16},{16,2},{3,17},{17,3},{6,20},{20,6},{7,21},{21,7},{10,24},{2... | collective-permute-start | bytes 27656 | tf_op jit(solution)/shard_map/ppermute | solution.py:353
  14.0 16.5 %collective-permute-start.6 = (bf16[36,128]{1,0:T(8,128)(2,1)S(1)}, bf16[36,128]{1,0:T(8,128)(2,1)S(1)}, u32[]{:S(2)}, u32[]{:S(2)}) collective-permute-start(bf16[36,128]{1,0:T(8,128)(2,1)S(1)} %broadcast_select_fusion), channel_id=1, source_target_pairs={{2,0},{16,18},{0,16},{18,2},{3,1},{17,19},{1,17},{19,3},{6,4},{20,... | collective-permute-start | bytes 27656 | tf_op jit(solution)/shard_map/ppermute | solution.py:350
  30.5 10.0 %collective-permute-start.8 = (bf16[1152,128]{1,0:T(8,128)(2,1)}, bf16[1152,128]{1,0:T(8,128)(2,1)S(1)}, u32[]{:S(2)}, u32[]{:S(2)}) collective-permute-start(bf16[1152,128]{1,0:T(8,128)(2,1)} %bitcast.5), channel_id=1, source_target_pairs={{0,16},{18,2},{1,17},{19,3},{4,20},{22,6},{5,21},{23,7},{8,24},{26... | collective-permute-start | bytes 884744 | tf_op jit(solution)/shard_map/ppermute | solution.py:315
  31.8 36.2 %collective-permute-start = (bf16[4608,128]{1,0:T(8,128)(2,1)}, bf16[4608,128]{1,0:T(8,128)(2,1)S(1)}, u32[]{:S(2)}, u32[]{:S(2)}) collective-permute-start(bf16[4608,128]{1,0:T(8,128)(2,1)} %bitcast.2.refs_0_), channel_id=1, source_target_pairs={{2,0},{16,18},{3,1},{17,19},{6,4},{20,22},{7,5},{21,23},{10,8},{24... | collective-permute-start | bytes 3538952 | tf_op jit(solution)/shard_map/ppermute | solution.py:307
  37.5 30.5 %collective-permute-start.2 = (bf16[1152,128]{1,0:T(8,128)(2,1)}, bf16[1152,128]{1,0:T(8,128)(2,1)S(1)}, u32[]{:S(2)}, u32[]{:S(2)}) collective-permute-start(bf16[1152,128]{1,0:T(8,128)(2,1)} %collective-permute-done.1.refs_1_), channel_id=1, source_target_pairs={{0,2},{18,16},{1,3},{19,17},{4,6},{22,20},{5,7},{23,21},{8,10},{26... | collective-permute-start | bytes 884744 | tf_op jit(solution)/shard_map/ppermute | solution.py:312
  38.8 40.6 %collective-permute-start.4 = (bf16[2304,128]{1,0:T(8,128)(2,1)S(1)}, bf16[2304,128]{1,0:T(8,128)(2,1)S(1)}, u32[]{:S(2)}, u32[]{:S(2)}) collective-permute-start(bf16[2304,128]{1,0:T(8,128)(2,1)S(1)} %collective-permute-done.3.refs_2_), channel_id=1, source_target_pairs={{0,2},{18,16},{1,3},{19,17},{4,6},{22,20},{5,7},{23,21},{8,10},{26... | collective-permute-start | bytes 1769480 | tf_op jit(solution)/shard_map/ppermute | solution.py:312
  84.6 81.7 %copy-start.1 = (bf16[128,9216]{1,0:T(8,128)(2,1)}, bf16[128,9216]{1,0:T(8,128)(2,1)S(1)}, u32[]{:S(2)}) copy-start(bf16[128,9216]{1,0:T(8,128)(2,1)S(1)} %get-tuple-element.17.refs_0_.refs_1_) | copy-start | bytes 7077892
  161.5 35.1 %all-to-all-start.1 = ((bf16[16,8,9216]{2,1,0:T(8,128)(2,1)}), bf16[16,8,9216]{2,1,0:T(8,128)(2,1)}, u32[]{:S(2)}, u32[]{:S(2)}) async-start(bf16[16,8,9216]{2,1,0:T(8,128)(2,1)} %bitcast.35), calls=%async_computation.1 | async-start | bytes 4718592 | tf_op jit(solution)/shard_map/all_to_all | solution.py:394
  275.9 20.8 %all-to-all-start.3 = ((bf16[16,8,4608]{2,1,0:T(8,128)(2,1)}), bf16[16,8,4608]{2,1,0:T(8,128)(2,1)}, u32[]{:S(2)}, u32[]{:S(2)}) async-start(bf16[16,8,4608]{2,1,0:T(8,128)(2,1)} %bitcast.44), calls=%async_computation.3 | async-start | bytes 2359296 | tf_op jit(solution)/shard_map/all_to_all | solution.py:394
  300.6 32.0 %all-to-all-start.4 = ((bf16[16,8,4608]{2,1,0:T(8,128)(2,1)}), bf16[16,8,4608]{2,1,0:T(8,128)(2,1)}, u32[]{:S(2)}, u32[]{:S(2)}) async-start(bf16[16,8,4608]{2,1,0:T(8,128)(2,1)} %bitcast.43), calls=%async_computation.4 | async-start | bytes 2359296 | tf_op jit(solution)/shard_map/all_to_all | solution.py:394
  305.8 56.4 %collective-permute-start.9 = (bf16[4608,128]{1,0:T(8,128)(2,1)}, bf16[4608,128]{1,0:T(8,128)(2,1)}, u32[]{:S(2)}, u32[]{:S(2)}) collective-permute-start(bf16[4608,128]{1,0:T(8,128)(2,1)} %copy-done.4), channel_id=1, source_target_pairs={{0,2},{18,16},{1,3},{19,17},{4,6},{22,20},{5,7},{23,21},{8,10},{26... | collective-permute-start | bytes 3538952 | tf_op jit(solution)/shard_map/ppermute | solution.py:418
  307.1 59.9 %collective-permute-start.11 = (bf16[4608,128]{1,0:T(8,128)(2,1)}, bf16[4608,128]{1,0:T(8,128)(2,1)}, u32[]{:S(2)}, u32[]{:S(2)}) collective-permute-start(bf16[4608,128]{1,0:T(8,128)(2,1)} %copy-done.4), channel_id=1, source_target_pairs={{2,16},{16,2},{3,17},{17,3},{6,20},{20,6},{7,21},{21,7},{10,24},{2... | collective-permute-start | bytes 3538952 | tf_op jit(solution)/shard_map/ppermute | solution.py:418
  336.3 30.8 %collective-permute-start.10 = (bf16[4608,128]{1,0:T(8,128)(2,1)}, bf16[4608,128]{1,0:T(8,128)(2,1)S(1)}, u32[]{:S(2)}, u32[]{:S(2)}) collective-permute-start(bf16[4608,128]{1,0:T(8,128)(2,1)} %shard_map.99.here_ref), channel_id=1, source_target_pairs={{2,18},{16,0},{3,19},{17,1},{6,22},{20,4},{7,23},{21,5},{10,26},{2... | collective-permute-start | bytes 3538952 | tf_op jit(solution)/shard_map/ppermute | solution.py:422
  (7 other events, 8.4 us)

commit v7 on v6

--- a/solution.py
+++ b/solution.py
@@ -30,11 +30,11 @@
     return channel_norm(values, small_ref[:, at : at + 1], small_ref[:, at + 1 : at + 2])
 
 
-def emit_projections(peers, update, zt, mask_ref, small_ref, weight_ref, lr_ref):
+def emit_projections(peers, update, zt, mask, small_ref, weight_ref, lr_ref):
     width = lr_ref.shape[0] // 2
     own = width // peers
     tile = zt.shape[1]
-    normed = norm_of(zt, small_ref, update, IN_GAIN) * mask_ref[...].astype(jnp.float32)
+    normed = norm_of(zt, small_ref, update, IN_GAIN) * mask
     projected = dot(weight_ref[update, : 4 * width], normed.astype(jnp.bfloat16))
     left = (jnp.tanh(projected[:width]) + 1.0) * projected[width : 2 * width]
     right = (jnp.tanh(projected[2 * width : 3 * width]) + 1.0) * projected[3 * width :]
@@ -44,22 +44,45 @@
     lr_ref[...] = both.reshape(2 * width, tile).astype(jnp.bfloat16)
 
 
+def pack_kernel(cuts, place_ref, own_ref, own_mask_ref, other_ref, other_mask_ref, *out_refs):
+    part_refs, (own_out_ref, next_ref) = out_refs[:-2], out_refs[-2:]
+    step = pl.program_id(0)
+    size = own_ref.shape[0]
+
+    def put(out_ref, ref, mask_ref):
+        out_ref[0, :size] = ref[...]
+        out_ref[0, size:] = mask_ref[0]
+
+    put(own_out_ref, own_ref, own_mask_ref)
+    pl.when(place_ref[1] == 1)(lambda: put(next_ref, other_ref, other_mask_ref))
+    pl.when(place_ref[1] != 1)(lambda: put(next_ref, own_ref, own_mask_ref))
+    for begin, end, part_ref in zip((0, *cuts), cuts, part_refs):
+        pl.when(jnp.logical_and(step >= begin, step < end))(
+            functools.partial(put, part_ref, other_ref, other_mask_ref)
+        )
+
+
 def first_kernel(peers, parts, own_ref, *refs):
-    far_refs, (mask_ref, small_ref, weight_ref), (lr_ref, zt_ref) = (
-        refs[: len(parts)], refs[len(parts) : -2], refs[-2:],
+    far_refs, (small_ref, weight_ref), (lr_ref, zt_ref, mask_ref) = (
+        refs[: len(parts)], refs[len(parts) : -3], refs[-3:],
     )
     home = lax.axis_index("groups") == lax.axis_index("zh")
     step = pl.program_id(0)
+    tile = zt_ref.shape[1]
 
     def put(z_ref):
-        zt_ref[...] = z_ref[...].astype(jnp.float32).T.astype(jnp.bfloat16)
+        zt_ref[...] = z_ref[0, :tile].astype(jnp.float32).T.astype(jnp.bfloat16)
+        marks = z_ref[0, tile:].astype(jnp.float32)
+        flat = jnp.concatenate([marks[k : k + 1] for k in range(tile // LANES)], axis=1)
+        mask_ref[...] = jnp.broadcast_to(flat, mask_ref.shape).astype(jnp.bfloat16)
 
     pl.when(home)(lambda: put(own_ref))
     for (begin, end), far_ref in zip(parts, far_refs):
         here = jnp.logical_and(step >= begin, step < end)
         pl.when(jnp.logical_and(jnp.logical_not(home), here))(functools.partial(put, far_ref))
     zt = zt_ref[...].astype(jnp.float32)
-    emit_projections(peers, 0, zt, mask_ref, small_ref, weight_ref, lr_ref)
+    mask = mask_ref[...].astype(jnp.float32)[:1]
+    emit_projections(peers, 0, zt, mask, small_ref, weight_ref, lr_ref)
 
 
 def gate_kernel(update, zt_ref, small_ref, weight_ref, gate_ref):
@@ -82,7 +105,8 @@
 ):
     fresh = updated(0, t_ref, zt_ref, gate_ref, small_ref, weight_ref).astype(jnp.bfloat16)
     out_ref[...] = fresh
-    emit_projections(peers, 1, fresh.astype(jnp.float32), mask_ref, small_ref, weight_ref, lr_ref)
+    mask = mask_ref[...].astype(jnp.float32)[:1]
+    emit_projections(peers, 1, fresh.astype(jnp.float32), mask, small_ref, weight_ref, lr_ref)
 
 
 def last_kernel(t_ref, zt_ref, gate_ref, small_ref, weight_ref, out_ref):
@@ -242,7 +266,7 @@
             pl.BlockSpec((2 * pair, pixels // n_out), lambda i: (jnp.maximum(i - blocks, 0), 0))
         ] * n_out,
         out_shape=[
-            jax.ShapeDtypeStruct((blocks * blocks * own, pixels // n_out), jnp.bfloat16)
+            pltpu.HBM((blocks * blocks * own, pixels // n_out), jnp.bfloat16)
         ] * n_out,
         scratch_shapes=[
             pltpu.VMEM((own, left_rows, padded), jnp.bfloat16),
@@ -269,9 +293,14 @@
             )
         return pl.BlockSpec((channels, tile), lambda i: (0, jnp.clip(i + first, 0, count - 1)))
 
+    def packed(a, first, count):
+        return pl.BlockSpec(
+            (1, *a.shape[1:]), lambda i: (jnp.clip(i + first, 0, count - 1), 0, 0)
+        )
+
     in_specs = [
-        spec(a.shape[1] if row_major else a.shape[0], first, count, row_major)
-        for a, first, count, row_major in tiled
+        packed(a, first, count) if a.ndim == 3 else spec(a.shape[0], first, count, False)
+        for a, first, count in tiled
     ]
     in_specs += [whole_spec(a) for a in fixed]
     in_specs += [pl.BlockSpec(memory_space=pl.ANY)] * len(kept)
@@ -286,7 +315,7 @@
         in_specs=in_specs,
         out_specs=[spec(ch, start, pixels // tile, row_major_out) for ch in outs],
         out_shape=[
-            jax.ShapeDtypeStruct((pixels, ch) if row_major_out else (ch, pixels), jnp.bfloat16)
+            pltpu.HBM((pixels, ch) if row_major_out else (ch, pixels), jnp.bfloat16)
             for ch in outs
         ],
         input_output_aliases={n_in - n_kept + k: k for k in range(n_kept)},
@@ -298,22 +327,37 @@
     )(*(a for a, *_ in tiled), *fixed, *kept)
 
 
-SWAP = ((0, 1), (1, 0))
 LINE = ("groups", "zh")
 CUBE = ("groups", "row", "zl")
 
 
-def gather_group(own_half, other_half, cuts):
-    early = lax.ppermute(own_half, LINE, ((1, 0), (2, 3)))
-    over, late = [], []
-    for begin, end in zip((0, *cuts[:-2]), cuts[:-1]):
-        part = lax.ppermute(other_half[begin:end], "groups", SWAP)
-        over.append(part)
-        late.append(lax.ppermute(part, LINE, ((0, 1), (3, 2))))
-    rest = other_half[cuts[-2] :]
-    late.append(lax.ppermute(rest, LINE, ((1, 2), (2, 1))))
-    over.append(lax.ppermute(rest, LINE, ((0, 2), (3, 1))))
-    return early, over, late
+def pack(pair_act, mask, place, cuts, tile):
+    per_strip = cuts[-1]
+    channels = pair_act.shape[1]
+    rows = tile + mask.shape[1]
+
+    def strip(other, blocks):
+        index = lambda i, place_ref: jnp.abs(other - place_ref[0]) * per_strip + i
+        if blocks:
+            return pl.BlockSpec((1, *mask.shape[1:]), lambda i, p: (index(i, p), 0, 0))
+        return pl.BlockSpec((tile, channels), lambda i, p: (index(i, p), 0))
+
+    def part(begin, end):
+        return pl.BlockSpec(
+            (1, rows, channels), lambda i, p: (jnp.clip(i - begin, 0, end - begin - 1), 0, 0)
+        )
+
+    outs = [*zip((0, *cuts), cuts), (0, per_strip), (0, per_strip)]
+    return pl.pallas_call(
+        functools.partial(pack_kernel, cuts),
+        grid_spec=pltpu.PrefetchScalarGridSpec(
+            num_scalar_prefetch=1,
+            grid=(per_strip,),
+            in_specs=[strip(0, False), strip(0, True), strip(1, False), strip(1, True)],
+            out_specs=[part(*o) for o in outs],
+        ),
+        out_shape=[pltpu.HBM((end - begin, rows, channels), jnp.bfloat16) for begin, end in outs],
+    )(place, pair_act, mask, pair_act, mask)
 
 
 def by_kernels(
@@ -338,27 +382,19 @@
     home = upper == lax.axis_index("zh")
     mult = 2 * channels
 
-    def halves(array):
-        return (
-            lax.dynamic_slice_in_dim(array, upper * strip, strip),
-            lax.dynamic_slice_in_dim(array, (1 - upper) * strip, strip),
-        )
-
-    m_own, m_other = (
-        h.reshape(-1, LANES) for h in halves(pair_mask.astype(jnp.bfloat16))
-    )
-    m_next = lax.ppermute(
-        jnp.where(home, m_other, m_own), LINE, ((1, 0), (2, 3), (0, 2), (3, 1))
-    )
-    m_across = lax.ppermute(m_other, LINE, ((1, 2), (2, 1)))
-    m_pieces = [
-        jnp.where(home, a, b).reshape(1, -1) for a, b in ((m_own, m_next), (m_next, m_across))
-    ]
-    z_own, z_other = (h.reshape(-1, channels) for h in halves(pair_act))
+    place = jnp.stack([upper, home.astype(upper.dtype)])
     tile = 9 * LANES
     per_piece = pixels // 2 // tile
-    tiles = (1, per_piece - 1, per_piece)
-    z_early, z_over, z_late = gather_group(z_own, z_other, [n * tile for n in tiles])
+    cuts = (1, per_piece - 1, per_piece)
+    marks = pair_mask.astype(jnp.bfloat16).reshape(2 * per_piece, tile // LANES, LANES)
+    marks = jnp.pad(marks, ((0, 0), (0, 16 - tile // LANES), (0, 0)))
+    *z_parts, z_own, z_next = pack(pair_act.reshape(pixels, channels), marks, place, cuts, tile)
+    z_far = []
+    for part in z_parts[:-1]:
+        over = lax.ppermute(part, LINE, ((1, 3), (2, 0)))
+        z_far.append(lax.ppermute(over, LINE, ((0, 1), (3, 2))))
+    z_near = lax.ppermute(z_next, LINE, ((1, 0), (2, 3), (0, 2), (3, 1)))
+    z_far.append(lax.ppermute(z_parts[-1], LINE, ((1, 2), (2, 1))))
     small = jnp.stack([input_gain, input_bias, output_gain, output_bias], axis=1)
     small = small.reshape(-1, channels).T
     weights = jnp.concatenate(
@@ -366,27 +402,23 @@
     ).transpose(0, 2, 1)
     fixed = (small, weights)
 
-    def first(piece, ours, far, mask, kept):
-        parts = list(zip((0, *tiles), tiles))
-        tiled = [(ours, 0, per_piece, True)]
-        tiled += [
-            (part, -begin, end - begin, True) for part, (begin, end) in zip(far, parts)
-        ]
-        tiled += [(mask, 0, per_piece, False)]
+    def first(piece, ours, far, parts, kept):
+        tiled = [(ours, 0, per_piece)]
+        tiled += [(part, -begin, end - begin) for part, (begin, end) in zip(far, parts)]
         return pixel_call(
             functools.partial(first_kernel, peers, parts),
-            tiled, fixed, (2 * width, channels), per_piece, tile, pixels // 2 * mult * 4 * width,
+            tiled, fixed, (2 * width, channels, 16), per_piece, tile, pixels // 2 * mult * 4 * width,
             start=piece * per_piece, pixels=pixels, kept=kept,
         )
 
-    begun = first(0, z_own, z_over, m_pieces[0], ())
-    sent, zt = first(1, z_early, z_late, m_pieces[1], begun)
+    begun = first(0, z_own, [z_near], [(0, per_piece)], ())
+    sent, zt, mask = first(1, z_near, z_far, list(zip((0, *cuts), cuts)), begun)
     wide = 2 * tile
     steps = pixels // wide
 
     def gate_of(zt, u):
         return pixel_call(
-            functools.partial(gate_kernel, u), [(zt, 0, steps, False)], fixed, (channels,),
+            functools.partial(gate_kernel, u), [(zt, 0, steps)], fixed, (channels,),
             steps, wide, pixels * mult * channels,
         )[0]
 
@@ -396,10 +428,9 @@
 
     gate = gate_of(zt, 0)
     triangle = exchange(*triangle_call([exchange(sent)], 1, blocks, side, own, False))
-    mask = jnp.concatenate(m_pieces, axis=1)
     sent, zt = pixel_call(
         functools.partial(middle_kernel, peers),
-        [(a, 0, steps, False) for a in (triangle, zt, gate, mask)], fixed, (2 * width, channels),
+        [(a, 0, steps) for a in (triangle, zt, gate, mask)], fixed, (2 * width, channels),
         steps, wide, pixels * mult * 5 * width,
     )
     gate = gate_of(zt, 1)
@@ -409,7 +440,7 @@
         at = piece * steps // 2
         return pixel_call(
             last_kernel,
-            [(triangle, 0, steps // 2, False), (zt, at, steps, False), (gate, at, steps, False)],
+            [(triangle, 0, steps // 2), (zt, at, steps), (gate, at, steps)],
             fixed, (channels,), steps // 2, wide, pixels // 2 * mult * channels, row_major_out=True,
         )[0]
 
@@ -420,7 +451,6 @@
     there, waiting = lax.optimization_barrier((there, products[0]))
     here = finish(0, exchange(waiting))
     back = lax.ppermute(here, LINE, ((1, 3), (2, 0)))
-    place = jnp.stack([upper, home.astype(upper.dtype)])
     per_half = steps // 2
 
     def source(of_mine, at_home):

time: 374 us -> 354 us (0.947)
  the two profiles are of different devices: /device:TPU:4 before, /device:TPU:20 now
where the time goes in v7:
time: 354 us; the launch traced here: 349 us
  blocking collectives  128 us (36%)
  waiting for transfers between devices  127 us (36%)
  Pallas kernels  58.5 us (17%)
  starting transfers between devices  30.6 us (9%)
  local copies, waits for them, and re-layouts  3.58 us (1%)
    all_to_all x2, blocking collectives, exchange(): there = lax.all_to_all(array.reshape(peers, -1, array.shape[1]), CUBE, 0, 0)  128 us
    all_to_all x3, waiting for transfers between devices, exchange(): there = lax.all_to_all(array.reshape(peers, -1, array.shape[1]), CUBE, 0, 0)  52.8 us
    pallas_call x7, Pallas kernels, pixel_call(): pl.pallas_call(kernel, grid=(steps,), in_specs=in_specs, out_specs=[spec(...  32.5 us
    ppermute x2, waiting for transfers between devices, by_kernels(): lax.ppermute(there, LINE, pairs)  30.7 us
    ppermute x2, waiting for transfers between devices, by_kernels(): z_far.append(lax.ppermute(over, LINE, ((0, 1), (3, 2))))  20.9 us
    ppermute x2, waiting for transfers between devices, by_kernels(): over = lax.ppermute(part, LINE, ((1, 3), (2, 0)))  18.1 us
    pallas_call x2, Pallas kernels, triangle_call(): pl.pallas_call(functools.partial(triangle_kernel, blocks, side, own, inco...  15.8 us
    all_to_all x3, starting transfers between devices, exchange(): there = lax.all_to_all(array.reshape(peers, -1, array.shape[1]), CUBE, 0, 0)  15 us
  transfers between devices with their start and end apart: 12, of which 8 were waited for; matrix products, arithmetic and copies ran while one was open for 0% of the time, Pallas kernels for 4%

profile of v7, /device:TPU:20, one launch (start us, length us, event | category | flops | bytes accessed | tf_op | source)
XLA Modules:
  0.0 349.3 jit_solution(273780363970117406)
XLA Ops:
  2.1 5.1 %shard_map.91 = (bf16[1,1168,128]{2,1,0:T(8,128)(2,1)}, bf16[2,1168,128]{2,1,0:T(8,128)(2,1)}, bf16[1,1168,128]{2,1,0:T(8,128)(2,1)}, bf16[4,1168,128]{2,1,0:T(8,128)(2,1)}, bf16[4,1168,128]{2,1,0:T(8,128)(2,1)}) custom-call(s32[2]{0:T(128)} %pad_add_fusion.place_ref, bf16[9216,128]{1,0:T(8,128)(2,1)} %bitcast.32, ...), custom_call_target="tpu_custom_call" | custom-call | tf_op jit(solution)/shard_map/pallas_call | solution.py:351
  11.7 14.6 %collective-permute-done.3 = bf16[2,1168,128]{2,1,0:T(8,128)(2,1)S(1)} collective-permute-done((bf16[2,1168,128]{2,1,0:T(8,128)(2,1)}, bf16[2,1168,128]{2,1,0:T(8,128)(2,1)S(1)}, u32[]{:S(2)}, u32[]{:S(2)}) %collective-permute-start.3) | collective-permute-done | bytes 598048 | tf_op jit(solution)/shard_map/ppermute | solution.py:394
  32.9 4.8 %collective-permute-done.refs_1_.refs_0_ = bf16[4,1168,128]{2,1,0:T(8,128)(2,1)S(1)} collective-permute-done((bf16[4,1168,128]{2,1,0:T(8,128)(2,1)}, bf16[4,1168,128]{2,1,0:T(8,128)(2,1)S(1)}, u32[]{:S(2)}, u32[]{:S(2)}) %collective-permute-start) | collective-permute-done | bytes 1196064 | tf_op jit(solution)/shard_map/ppermute | solution.py:396
  39.0 4.1 %shard_map.92 = (bf16[256,9216]{1,0:T(8,128)(2,1)}, bf16[128,9216]{1,0:T(8,128)(2,1)}, bf16[16,9216]{1,0:T(8,128)(2,1)}) custom-call(bf16[4,1168,128]{2,1,0:T(8,128)(2,1)S(1)} %copy-done.2, bf16[4,1168,128]{2,1,0:T(8,128)(2,1)S(1)} %collective-permute-done.refs_1_.refs_0_, f32[128,8]{1,0:T(8,128)S(1)} %bitcast.24, ...), custom_call_target="tpu_custom_call" | custom-call | flops 603979776 | bytes 6045696 | tf_op jit(solution)/shard_map/pallas_call | solution.py:312
  43.0 20.8 %collective-permute-done.2.refs_1_ = bf16[1,1168,128]{2,1,0:T(8,128)(2,1)S(1)} collective-permute-done((bf16[1,1168,128]{2,1,0:T(8,128)(2,1)S(1)}, bf16[1,1168,128]{2,1,0:T(8,128)(2,1)S(1)}, u32[]{:S(2)}, u32[]{:S(2)}) %collective-permute-start.2) | collective-permute-done | bytes 299040 | tf_op jit(solution)/shard_map/ppermute | solution.py:395
  63.9 4.2 %shard_map.93 = (bf16[256,9216]{1,0:T(8,128)(2,1)}, bf16[128,9216]{1,0:T(8,128)(2,1)}, bf16[16,9216]{1,0:T(8,128)(2,1)}) custom-call(bf16[4,1168,128]{2,1,0:T(8,128)(2,1)S(1)} %collective-permute-done.refs_1_.refs_0_, bf16[1,1168,128]{2,1,0:T(8,128)(2,1)S(1)} %collective-permute-done.2.refs_1_, ...), custom_call_target="tpu_custom_call", output_to_operand_aliasing={{0}: (6, {}), {1}: (7, {}), {2}: (8, {})} | custom-call | flops 603979776 | bytes 6045696 | tf_op jit(solution)/shard_map/pallas_call | solution.py:312
  68.1 69.4 %all_to_all.25 = bf16[16,16,9216]{2,1,0:T(8,128)(2,1)S(1)} all-to-all(bf16[16,16,9216]{2,1,0:T(8,128)(2,1)} %bitcast.31), channel_id=1, replica_groups=mesh['groups'=2,'row'=4,'zh'=2,'zl'=2] {'groups','row','zl'}, dimensions={0} | all-to-all | bytes 9437184 | tf_op jit(solution)/shard_map/all_to_all | solution.py:426
  137.5 7.6 %shard_map.94 = bf16[128,9216]{1,0:T(8,128)(2,1)} custom-call(bf16[256,9216]{1,0:T(8,128)(2,1)S(1)} %bitcast.23), custom_call_target="tpu_custom_call" | custom-call | flops 905969664 | bytes 14155776 | tf_op jit(solution)/shard_map/pallas_call | solution.py:258
  145.1 4.9 %all-to-all-start.1 = ((bf16[16,8,9216]{2,1,0:T(8,128)(2,1)}), bf16[16,8,9216]{2,1,0:T(8,128)(2,1)}, u32[]{:S(2)}, u32[]{:S(2)}) async-start(bf16[16,8,9216]{2,1,0:T(8,128)(2,1)} %bitcast.34), calls=%async_computation.1 | async-start | bytes 4718592 | tf_op jit(solution)/shard_map/all_to_all | solution.py:426
  150.0 3.8 %shard_map.95.refs_2_ = bf16[128,9216]{1,0:T(8,128)(2,1)} custom-call(bf16[128,9216]{1,0:T(8,128)(2,1)S(1)} %copy-done.1, f32[128,8]{1,0:T(8,128)S(1)} %bitcast.26, bf16[2,768,128]{2,1,0:T(8,128)(2,1)S(1)} %maximum_bitcast_fusion.refs_3_.refs_5_.refs_2_.refs_4_), custom_call_target="tpu_custom_call" | custom-call | flops 301989888 | bytes 7077888 | tf_op jit(solution)/shard_map/pallas_call | solution.py:312
  153.8 26.5 %all-to-all-done.1 = bf16[16,8,9216]{2,1,0:T(8,128)(2,1)} async-done(((bf16[16,8,9216]{2,1,0:T(8,128)(2,1)}), bf16[16,8,9216]{2,1,0:T(8,128)(2,1)}, u32[]{:S(2)}, u32[]{:S(2)}) %all-to-all-start.1) | async-done | bytes 2359328 | tf_op jit(solution)/shard_map/all_to_all | solution.py:426
  180.3 9.3 %shard_map.96 = (bf16[256,9216]{1,0:T(8,128)(2,1)}, bf16[128,9216]{1,0:T(8,128)(2,1)}) custom-call(bf16[128,9216]{1,0:T(8,128)(2,1)} %bitcast.13.refs_0_, bf16[128,9216]{1,0:T(8,128)(2,1)S(1)} %copy-done.1, bf16[128,9216]{1,0:T(8,128)(2,1)} %shard_map.95.refs_2_, bf16[16,9216]{1,0:T(8,128)(2,1)S(1)} %copy-done.3, f32[128,8]{1,0:T(8,128)S(1)} %bitcast.27, ...), custom_call_target="tpu_custom_call" | custom-call | flops 1509949440 | bytes 11796480 | tf_op jit(solution)/shard_map/pallas_call | solution.py:312
  189.6 58.4 %all_to_all.26 = bf16[16,16,9216]{2,1,0:T(8,128)(2,1)S(1)} all-to-all(bf16[16,16,9216]{2,1,0:T(8,128)(2,1)} %bitcast.35), channel_id=1, replica_groups=mesh['groups'=2,'row'=4,'zh'=2,'zl'=2] {'groups','row','zl'}, dimensions={0} | all-to-all | bytes 9437184 | tf_op jit(solution)/shard_map/all_to_all | solution.py:426
  248.0 8.1 %shard_map.97 = (bf16[128,4608]{1,0:T(8,128)(2,1)}, bf16[128,4608]{1,0:T(8,128)(2,1)}) custom-call(bf16[256,9216]{1,0:T(8,128)(2,1)S(1)} %bitcast.22), custom_call_target="tpu_custom_call" | custom-call | flops 905969664 | bytes 14155776 | tf_op jit(solution)/shard_map/pallas_call | solution.py:258
  256.2 4.8 %all-to-all-start.3 = ((bf16[16,8,4608]{2,1,0:T(8,128)(2,1)}), bf16[16,8,4608]{2,1,0:T(8,128)(2,1)}, u32[]{:S(2)}, u32[]{:S(2)}) async-start(bf16[16,8,4608]{2,1,0:T(8,128)(2,1)} %bitcast.37), calls=%async_computation.3 | async-start | bytes 2359296 | tf_op jit(solution)/shard_map/all_to_all | solution.py:426
  261.0 3.8 %shard_map.98.refs_2_ = bf16[128,9216]{1,0:T(8,128)(2,1)} custom-call(bf16[128,9216]{1,0:T(8,128)(2,1)S(1)} %copy-done, f32[128,8]{1,0:T(8,128)S(1)} %bitcast.28, bf16[2,768,128]{2,1,0:T(8,128)(2,1)S(1)} %maximum_bitcast_fusion.refs_3_.refs_5_.refs_2_.refs_4_), custom_call_target="tpu_custom_call" | custom-call | flops 301989888 | bytes 7077888 | tf_op jit(solution)/shard_map/pallas_call | solution.py:312
  264.8 12.0 %all-to-all-done.3 = bf16[16,8,4608]{2,1,0:T(8,128)(2,1)} async-done(((bf16[16,8,4608]{2,1,0:T(8,128)(2,1)}), bf16[16,8,4608]{2,1,0:T(8,128)(2,1)}, u32[]{:S(2)}, u32[]{:S(2)}) %all-to-all-start.3) | async-done | bytes 1179680 | tf_op jit(solution)/shard_map/all_to_all | solution.py:426
  276.8 3.7 %shard_map.99 = bf16[4608,128]{1,0:T(8,128)(2,1)} custom-call(bf16[128,4608]{1,0:T(8,128)(2,1)} %bitcast.17.refs_0_, bf16[128,9216]{1,0:T(8,128)(2,1)S(1)} %copy-done, bf16[128,9216]{1,0:T(8,128)(2,1)} %shard_map.98.refs_2_, f32[128,8]{1,0:T(8,128)S(1)} %bitcast.29, bf16[2,768,128]{2,1,0:T(8,128)(2,1)S(1)} %maximum_bitcast_fusion.refs_3_.refs_5_.refs_2_.refs_4_), custom_call_target="tpu_custom_call" | custom-call | flops 150994944 | bytes 3538944 | tf_op jit(solution)/shard_map/pallas_call | solution.py:312
  280.5 5.3 %all-to-all-start.4 = ((bf16[16,8,4608]{2,1,0:T(8,128)(2,1)}), bf16[16,8,4608]{2,1,0:T(8,128)(2,1)}, u32[]{:S(2)}, u32[]{:S(2)}) async-start(bf16[16,8,4608]{2,1,0:T(8,128)(2,1)} %bitcast.36), calls=%async_computation.4 | async-start | bytes 2359296 | tf_op jit(solution)/shard_map/all_to_all | solution.py:426
  287.4 5.7 %collective-permute-start.6 = (bf16[4608,128]{1,0:T(8,128)(2,1)}, bf16[4608,128]{1,0:T(8,128)(2,1)}, u32[]{:S(2)}, u32[]{:S(2)}) collective-permute-start(bf16[4608,128]{1,0:T(8,128)(2,1)} %shard_map.99), channel_id=1, source_target_pairs={{0,2},{18,16},{1,3},{19,17},{4,6},{22,20},{5,7},{23,21},{8,10},{26... | collective-permute-start | bytes 3538952 | tf_op jit(solution)/shard_map/ppermute | solution.py:449
  293.2 14.3 %all-to-all-done.4 = bf16[16,8,4608]{2,1,0:T(8,128)(2,1)} async-done(((bf16[16,8,4608]{2,1,0:T(8,128)(2,1)}), bf16[16,8,4608]{2,1,0:T(8,128)(2,1)}, u32[]{:S(2)}, u32[]{:S(2)}) %all-to-all-start.4) | async-done | bytes 1179680 | tf_op jit(solution)/shard_map/all_to_all | solution.py:426
  307.5 3.7 %shard_map.100.here_ref = bf16[4608,128]{1,0:T(8,128)(2,1)} custom-call(bf16[128,4608]{1,0:T(8,128)(2,1)} %bitcast.19.refs_0_, bf16[128,9216]{1,0:T(8,128)(2,1)S(1)} %copy-done, bf16[128,9216]{1,0:T(8,128)(2,1)} %shard_map.98.refs_2_, f32[128,8]{1,0:T(8,128)S(1)} %bitcast.30, bf16[2,768,128]{2,1,0:T(8,128)(2,1)S(1)} %maximum_bitcast_fusion.refs_3_.refs_5_.refs_2_.refs_4_), custom_call_target="tpu_custom_call" | custom-call | flops 150994944 | bytes 3538944 | tf_op jit(solution)/shard_map/pallas_call | solution.py:312
  312.4 30.7 %collective-permute-done.6.beside_ref = bf16[4608,128]{1,0:T(8,128)(2,1)} collective-permute-done((bf16[4608,128]{1,0:T(8,128)(2,1)}, bf16[4608,128]{1,0:T(8,128)(2,1)}, u32[]{:S(2)}, u32[]{:S(2)}) %collective-permute-start.6) | collective-permute-done | bytes 1179680 | tf_op jit(solution)/shard_map/ppermute | solution.py:449
  344.2 5.1 %shard_map.101 = bf16[9216,128]{1,0:T(8,128)(2,1)} custom-call(s32[2]{0:T(128)} %pad_add_fusion.place_ref, bf16[4608,128]{1,0:T(8,128)(2,1)} %shard_map.100.here_ref, bf16[4608,128]{1,0:T(8,128)(2,1)} %collective-permute-done.6.beside_ref, bf16[4608,128]{1,0:T(8,128)(2,1)} %copy-done.4, bf16[4608,128]{1,0:T(8,128)(2,1)} %collective-permute-done.8.across_ref), custom_call_target="tpu_custom_call" | custom-call | tf_op jit(solution)/shard_map/pallas_call | solution.py:465
  (50 shorter events, 18.3 us)
Async XLA Ops:
  2.1 9.0 %copy-start.8 = (f32[2,128]{1,0:T(2,128)S(1)}, f32[2,128]{1,0:T(2,128)}, u32[]{:S(2)}) copy-start(f32[2,128]{1,0:T(2,128)} %param.16) | copy-start | bytes 3076
  2.1 9.0 %copy-start.9 = (f32[2,128]{1,0:T(2,128)S(1)}, f32[2,128]{1,0:T(2,128)}, u32[]{:S(2)}) copy-start(f32[2,128]{1,0:T(2,128)} %param.15) | copy-start | bytes 3076
  2.1 9.0 %copy-start.10 = (f32[2,128]{1,0:T(2,128)S(1)}, f32[2,128]{1,0:T(2,128)}, u32[]{:S(2)}) copy-start(f32[2,128]{1,0:T(2,128)} %param.12) | copy-start | bytes 3076
  2.1 9.0 %copy-start.11 = (f32[2,128]{1,0:T(2,128)S(1)}, f32[2,128]{1,0:T(2,128)}, u32[]{:S(2)}) copy-start(f32[2,128]{1,0:T(2,128)} %param.11) | copy-start | bytes 3076
  2.1 9.1 %copy-start.6 = (bf16[2,128,128]{2,1,0:T(8,128)(2,1)S(1)}, bf16[2,128,128]{2,1,0:T(8,128)(2,1)}, u32[]{:S(2)}) copy-start(bf16[2,128,128]{2,1,0:T(8,128)(2,1)} %param.14) | copy-start | bytes 196612
  2.1 9.2 %copy-start.7 = (bf16[2,128,128]{2,1,0:T(8,128)(2,1)S(1)}, bf16[2,128,128]{2,1,0:T(8,128)(2,1)}, u32[]{:S(2)}) copy-start(bf16[2,128,128]{2,1,0:T(8,128)(2,1)} %param.17) | copy-start | bytes 196612
  2.1 9.4 %copy-start.5 = (bf16[2,128,512]{2,1,0:T(8,128)(2,1)S(1)}, bf16[2,128,512]{2,1,0:T(8,128)(2,1)}, u32[]{:S(2)}) copy-start(bf16[2,128,512]{2,1,0:T(8,128)(2,1)} %param.13) | copy-start | bytes 786436
  7.2 30.5 %collective-permute-start = (bf16[4,1168,128]{2,1,0:T(8,128)(2,1)}, bf16[4,1168,128]{2,1,0:T(8,128)(2,1)S(1)}, u32[]{:S(2)}, u32[]{:S(2)}) collective-permute-start(bf16[4,1168,128]{2,1,0:T(8,128)(2,1)} %get-tuple-element.21), channel_id=1, source_target_pairs={{2,0},{16,18},{0,16},{18,2},{3,1},{17,19},{1,17},{19,3},{6,4},{20,... | collective-permute-start | bytes 3588104 | tf_op jit(solution)/shard_map/ppermute | solution.py:396
  7.8 18.5 %collective-permute-start.3 = (bf16[2,1168,128]{2,1,0:T(8,128)(2,1)}, bf16[2,1168,128]{2,1,0:T(8,128)(2,1)S(1)}, u32[]{:S(2)}, u32[]{:S(2)}) collective-permute-start(bf16[2,1168,128]{2,1,0:T(8,128)(2,1)} %get-tuple-element.23), channel_id=1, source_target_pairs={{2,18},{16,0},{3,19},{17,1},{6,22},{20,4},{7,23},{21,5},{10,26},{2... | collective-permute-start | bytes 1794056 | tf_op jit(solution)/shard_map/ppermute | solution.py:394
  9.1 22.2 %collective-permute-start.1 = (bf16[1,1168,128]{2,1,0:T(8,128)(2,1)}, bf16[1,1168,128]{2,1,0:T(8,128)(2,1)S(1)}, u32[]{:S(2)}, u32[]{:S(2)}) collective-permute-start(bf16[1,1168,128]{2,1,0:T(8,128)(2,1)} %get-tuple-element.22), channel_id=1, source_target_pairs={{2,18},{16,0},{3,19},{17,1},{6,22},{20,4},{7,23},{21,5},{10,26},{2... | collective-permute-start | bytes 897032 | tf_op jit(solution)/shard_map/ppermute | solution.py:394
  10.4 32.7 %collective-permute-start.5 = (bf16[1,1168,128]{2,1,0:T(8,128)(2,1)}, bf16[1,1168,128]{2,1,0:T(8,128)(2,1)S(1)}, u32[]{:S(2)}, u32[]{:S(2)}) collective-permute-start(bf16[1,1168,128]{2,1,0:T(8,128)(2,1)} %get-tuple-element.24), channel_id=1, source_target_pairs={{2,16},{16,2},{3,17},{17,3},{6,20},{20,6},{7,21},{21,7},{10,24},{2... | collective-permute-start | bytes 897032 | tf_op jit(solution)/shard_map/ppermute | solution.py:397
  26.3 37.6 %collective-permute-start.4 = (bf16[2,1168,128]{2,1,0:T(8,128)(2,1)S(1)}, bf16[2,1168,128]{2,1,0:T(8,128)(2,1)S(1)}, u32[]{:S(2)}, u32[]{:S(2)}) collective-permute-start(bf16[2,1168,128]{2,1,0:T(8,128)(2,1)S(1)} %collective-permute-done.3), channel_id=1, source_target_pairs={{0,2},{18,16},{1,3},{19,17},{4,6},{22,20},{5,7},{23,21},{8,10},{26... | collective-permute-start | bytes 1794056 | tf_op jit(solution)/shard_map/ppermute | solution.py:395
  31.2 32.7 %collective-permute-start.2 = (bf16[1,1168,128]{2,1,0:T(8,128)(2,1)S(1)}, bf16[1,1168,128]{2,1,0:T(8,128)(2,1)S(1)}, u32[]{:S(2)}, u32[]{:S(2)}) collective-permute-start(bf16[1,1168,128]{2,1,0:T(8,128)(2,1)S(1)} %collective-permute-done.1), channel_id=1, source_target_pairs={{0,2},{18,16},{1,3},{19,17},{4,6},{22,20},{5,7},{23,21},{8,10},{26... | collective-permute-start | bytes 897032 | tf_op jit(solution)/shard_map/ppermute | solution.py:395
  37.7 1.3 copy-start.2
  145.1 4.9 %copy-start.1 = (bf16[128,9216]{1,0:T(8,128)(2,1)S(1)}, bf16[128,9216]{1,0:T(8,128)(2,1)}, u32[]{:S(2)}) copy-start(bf16[128,9216]{1,0:T(8,128)(2,1)} %get-tuple-element.30.refs_0_.refs_1_) | copy-start | bytes 7077892
  145.1 35.3 %all-to-all-start.1 = ((bf16[16,8,9216]{2,1,0:T(8,128)(2,1)}), bf16[16,8,9216]{2,1,0:T(8,128)(2,1)}, u32[]{:S(2)}, u32[]{:S(2)}) async-start(bf16[16,8,9216]{2,1,0:T(8,128)(2,1)} %bitcast.34), calls=%async_computation.1 | async-start | bytes 4718592 | tf_op jit(solution)/shard_map/all_to_all | solution.py:426
  150.0 30.3 %copy-start.3 = (bf16[16,9216]{1,0:T(8,128)(2,1)S(1)}, bf16[16,9216]{1,0:T(8,128)(2,1)}, u32[]{:S(2)}) copy-start(bf16[16,9216]{1,0:T(8,128)(2,1)} %get-tuple-element.31.refs_3_) | copy-start | bytes 884740
  256.2 4.9 %copy-start = (bf16[128,9216]{1,0:T(8,128)(2,1)S(1)}, bf16[128,9216]{1,0:T(8,128)(2,1)}, u32[]{:S(2)}) copy-start(bf16[128,9216]{1,0:T(8,128)(2,1)} %get-tuple-element.34.refs_0_.refs_1_) | copy-start | bytes 7077892
  256.2 20.6 %all-to-all-start.3 = ((bf16[16,8,4608]{2,1,0:T(8,128)(2,1)}), bf16[16,8,4608]{2,1,0:T(8,128)(2,1)}, u32[]{:S(2)}, u32[]{:S(2)}) async-start(bf16[16,8,4608]{2,1,0:T(8,128)(2,1)} %bitcast.37), calls=%async_computation.3 | async-start | bytes 2359296 | tf_op jit(solution)/shard_map/all_to_all | solution.py:426
  280.5 27.0 %all-to-all-start.4 = ((bf16[16,8,4608]{2,1,0:T(8,128)(2,1)}), bf16[16,8,4608]{2,1,0:T(8,128)(2,1)}, u32[]{:S(2)}, u32[]{:S(2)}) async-start(bf16[16,8,4608]{2,1,0:T(8,128)(2,1)} %bitcast.36), calls=%async_computation.4 | async-start | bytes 2359296 | tf_op jit(solution)/shard_map/all_to_all | solution.py:426
  285.8 26.7 %collective-permute-start.8 = (bf16[4608,128]{1,0:T(8,128)(2,1)}, bf16[4608,128]{1,0:T(8,128)(2,1)}, u32[]{:S(2)}, u32[]{:S(2)}) collective-permute-start(bf16[4608,128]{1,0:T(8,128)(2,1)} %shard_map.99), channel_id=1, source_target_pairs={{2,16},{16,2},{3,17},{17,3},{6,20},{20,6},{7,21},{21,7},{10,24},{2... | collective-permute-start | bytes 3538952 | tf_op jit(solution)/shard_map/ppermute | solution.py:449
  287.4 55.7 %collective-permute-start.6 = (bf16[4608,128]{1,0:T(8,128)(2,1)}, bf16[4608,128]{1,0:T(8,128)(2,1)}, u32[]{:S(2)}, u32[]{:S(2)}) collective-permute-start(bf16[4608,128]{1,0:T(8,128)(2,1)} %shard_map.99), channel_id=1, source_target_pairs={{0,2},{18,16},{1,3},{19,17},{4,6},{22,20},{5,7},{23,21},{8,10},{26... | collective-permute-start | bytes 3538952 | tf_op jit(solution)/shard_map/ppermute | solution.py:449
  311.1 32.0 %collective-permute-start.7 = (bf16[4608,128]{1,0:T(8,128)(2,1)}, bf16[4608,128]{1,0:T(8,128)(2,1)S(1)}, u32[]{:S(2)}, u32[]{:S(2)}) collective-permute-start(bf16[4608,128]{1,0:T(8,128)(2,1)} %shard_map.100.here_ref), channel_id=1, source_target_pairs={{2,18},{16,0},{3,19},{17,1},{6,22},{20,4},{7,23},{21,5},{10,26},{2... | collective-permute-start | bytes 3538952 | tf_op jit(solution)/shard_map/ppermute | solution.py:453
  343.1 1.0 copy-start.4

commit v8 on v7

--- a/solution.py
+++ b/solution.py
@@ -44,22 +44,51 @@
     lr_ref[...] = both.reshape(2 * width, tile).astype(jnp.bfloat16)
 
 
-def pack_kernel(cuts, place_ref, own_ref, own_mask_ref, other_ref, other_mask_ref, *out_refs):
-    part_refs, (own_out_ref, next_ref) = out_refs[:-2], out_refs[-2:]
-    step = pl.program_id(0)
-    size = own_ref.shape[0]
-
-    def put(out_ref, ref, mask_ref):
-        out_ref[0, :size] = ref[...]
-        out_ref[0, size:] = mask_ref[0]
-
-    put(own_out_ref, own_ref, own_mask_ref)
-    pl.when(place_ref[1] == 1)(lambda: put(next_ref, other_ref, other_mask_ref))
-    pl.when(place_ref[1] != 1)(lambda: put(next_ref, own_ref, own_mask_ref))
-    for begin, end, part_ref in zip((0, *cuts), cuts, part_refs):
-        pl.when(jnp.logical_and(step >= begin, step < end))(
-            functools.partial(put, part_ref, other_ref, other_mask_ref)
-        )
+def pack_kernel(cuts, tile, z_ref, mask_ref, *refs):
+    out_refs, (held_ref, z_sems, mask_sems, out_sems) = refs[:-4], refs[-4:]
+    part_refs, (own_ref, next_ref) = out_refs[:-2], out_refs[-2:]
+    upper = lax.axis_index("groups")
+    home = upper == lax.axis_index("zh")
+    per_strip = cuts[-1]
+    rows = held_ref.shape[2]
+    fetches = []
+    for which in range(2):
+        strip = lax.rem(upper + 1 - which, 2)
+        for t in range(per_strip):
+            at = pl.multiple_of((strip * per_strip + t) * tile, tile)
+            fetches.append(
+                pltpu.make_async_copy(
+                    z_ref.at[pl.ds(at, tile)], held_ref.at[which, t, 0:tile], z_sems.at[which, t]
+                )
+            )
+            fetches.append(
+                pltpu.make_async_copy(
+                    mask_ref.at[strip * per_strip + t], held_ref.at[which, t, tile:rows],
+                    mask_sems.at[which, t],
+                )
+            )
+    stores = [
+        pltpu.make_async_copy(held_ref.at[0, begin:end], part_ref, out_sems.at[k])
+        for k, (begin, end, part_ref) in enumerate(zip((0, *cuts), cuts, part_refs))
+    ]
+    stores += [
+        pltpu.make_async_copy(held_ref.at[1], own_ref, out_sems.at[len(cuts)]),
+        pltpu.make_async_copy(
+            held_ref.at[1 - home.astype(jnp.int32)], next_ref, out_sems.at[len(cuts) + 1]
+        ),
+    ]
+    for fetch in fetches:
+        fetch.start()
+    for fetch in fetches[: 2 * per_strip]:
+        fetch.wait()
+    for store in stores[: len(cuts)]:
+        store.start()
+    for fetch in fetches[2 * per_strip :]:
+        fetch.wait()
+    for store in stores[len(cuts) :]:
+        store.start()
+    for store in stores:
+        store.wait()
 
 
 def first_kernel(peers, parts, own_ref, *refs):
@@ -114,19 +143,37 @@
     out_ref[...] = fresh.T.astype(jnp.bfloat16)
 
 
-def assemble_kernel(per_half, place_ref, here_ref, beside_ref, back_ref, across_ref, out_ref):
-    mine = pl.program_id(0) // per_half == place_ref[0]
-    home = place_ref[1] == 1
-    for side_of, whose, ref in (
-        (home, mine, here_ref),
-        (jnp.logical_not(home), mine, beside_ref),
-        (home, jnp.logical_not(mine), back_ref),
-        (jnp.logical_not(home), jnp.logical_not(mine), across_ref),
-    ):
-
-        @pl.when(jnp.logical_and(side_of, whose))
-        def _put(ref=ref):
-            out_ref[...] = ref[...]
+def assemble_kernel(here_ref, beside_ref, back_ref, across_ref, out_ref, held_ref, in_sems, out_sems):
+    upper = lax.axis_index("groups")
+    home = upper == lax.axis_index("zh")
+    parts = in_sems.shape[1]
+    size = here_ref.shape[0] // parts
+
+    def move(*sources):
+        pieces = [(which, k, slice(k * size, (k + 1) * size)) for k in range(parts) for which in range(2)]
+        fetches = [
+            pltpu.make_async_copy(
+                sources[which].at[rows], held_ref.at[which, rows], in_sems.at[which, k]
+            )
+            for which, k, rows in pieces
+        ]
+        stores = [
+            pltpu.make_async_copy(
+                held_ref.at[which, rows], out_ref.at[lax.rem(upper + which, 2), rows],
+                out_sems.at[which, k],
+            )
+            for which, k, rows in pieces
+        ]
+        for fetch in fetches:
+            fetch.start()
+        for fetch, store in zip(fetches, stores):
+            fetch.wait()
+            store.start()
+        for store in stores:
+            store.wait()
+
+    pl.when(home)(lambda: move(here_ref, back_ref))
+    pl.when(jnp.logical_not(home))(lambda: move(beside_ref, across_ref))
 
 
 def triangle_kernel(blocks, side, own, incoming, n_in, *refs):
@@ -331,33 +378,24 @@
 CUBE = ("groups", "row", "zl")
 
 
-def pack(pair_act, mask, place, cuts, tile):
+def pack(pair_act, mask, cuts, tile):
     per_strip = cuts[-1]
-    channels = pair_act.shape[1]
-    rows = tile + mask.shape[1]
-
-    def strip(other, blocks):
-        index = lambda i, place_ref: jnp.abs(other - place_ref[0]) * per_strip + i
-        if blocks:
-            return pl.BlockSpec((1, *mask.shape[1:]), lambda i, p: (index(i, p), 0, 0))
-        return pl.BlockSpec((tile, channels), lambda i, p: (index(i, p), 0))
-
-    def part(begin, end):
-        return pl.BlockSpec(
-            (1, rows, channels), lambda i, p: (jnp.clip(i - begin, 0, end - begin - 1), 0, 0)
-        )
-
-    outs = [*zip((0, *cuts), cuts), (0, per_strip), (0, per_strip)]
+    shape = (tile + mask.shape[1], pair_act.shape[1])
+    outs = [end - begin for begin, end in zip((0, *cuts), cuts)] + [per_strip, per_strip]
+    anywhere = pl.BlockSpec(memory_space=pltpu.HBM)
     return pl.pallas_call(
-        functools.partial(pack_kernel, cuts),
-        grid_spec=pltpu.PrefetchScalarGridSpec(
-            num_scalar_prefetch=1,
-            grid=(per_strip,),
-            in_specs=[strip(0, False), strip(0, True), strip(1, False), strip(1, True)],
-            out_specs=[part(*o) for o in outs],
-        ),
-        out_shape=[pltpu.HBM((end - begin, rows, channels), jnp.bfloat16) for begin, end in outs],
-    )(place, pair_act, mask, pair_act, mask)
+        functools.partial(pack_kernel, cuts, tile),
+        in_specs=[anywhere] * 2,
+        out_specs=[anywhere] * len(outs),
+        out_shape=[pltpu.HBM((n, *shape), jnp.bfloat16) for n in outs],
+        scratch_shapes=[
+            pltpu.VMEM((2, per_strip, *shape), jnp.bfloat16),
+            pltpu.SemaphoreType.DMA((2, per_strip)),
+            pltpu.SemaphoreType.DMA((2, per_strip)),
+            pltpu.SemaphoreType.DMA((len(outs),)),
+        ],
+        compiler_params=pltpu.CompilerParams(vmem_limit_bytes=48 * 1024 * 1024),
+    )(pair_act, mask)
 
 
 def by_kernels(
@@ -378,22 +416,20 @@
     own = width // peers
     pixels = side * side
     strip = side // 2
-    upper = lax.axis_index("groups")
-    home = upper == lax.axis_index("zh")
     mult = 2 * channels
 
-    place = jnp.stack([upper, home.astype(upper.dtype)])
     tile = 9 * LANES
     per_piece = pixels // 2 // tile
     cuts = (1, per_piece - 1, per_piece)
     marks = pair_mask.astype(jnp.bfloat16).reshape(2 * per_piece, tile // LANES, LANES)
     marks = jnp.pad(marks, ((0, 0), (0, 16 - tile // LANES), (0, 0)))
-    *z_parts, z_own, z_next = pack(pair_act.reshape(pixels, channels), marks, place, cuts, tile)
+    *z_parts, z_own, z_next = pack(pair_act.reshape(pixels, channels), marks, cuts, tile)
     z_far = []
     for part in z_parts[:-1]:
         over = lax.ppermute(part, LINE, ((1, 3), (2, 0)))
         z_far.append(lax.ppermute(over, LINE, ((0, 1), (3, 2))))
-    z_near = lax.ppermute(z_next, LINE, ((1, 0), (2, 3), (0, 2), (3, 1)))
+    z_over = lax.ppermute(z_next, LINE, ((0, 2), (3, 1)))
+    z_near = lax.ppermute(z_next, LINE, ((1, 0), (2, 3)))
     z_far.append(lax.ppermute(z_parts[-1], LINE, ((1, 2), (2, 1))))
     small = jnp.stack([input_gain, input_bias, output_gain, output_bias], axis=1)
     small = small.reshape(-1, channels).T
@@ -411,7 +447,7 @@
             start=piece * per_piece, pixels=pixels, kept=kept,
         )
 
-    begun = first(0, z_own, [z_near], [(0, per_piece)], ())
+    begun = first(0, z_own, [z_over], [(0, per_piece)], ())
     sent, zt, mask = first(1, z_near, z_far, list(zip((0, *cuts), cuts)), begun)
     wide = 2 * tile
     steps = pixels // wide
@@ -451,27 +487,18 @@
     there, waiting = lax.optimization_barrier((there, products[0]))
     here = finish(0, exchange(waiting))
     back = lax.ppermute(here, LINE, ((1, 3), (2, 0)))
-    per_half = steps // 2
-
-    def source(of_mine, at_home):
-        def index(i, place_ref):
-            wanted = jnp.logical_and(
-                (i // per_half == place_ref[0]) == of_mine, (place_ref[1] == 1) == at_home
-            )
-            return jnp.where(wanted, lax.rem(i, per_half), 0), 0
-
-        return pl.BlockSpec((wide, channels), index)
-
     return pl.pallas_call(
-        functools.partial(assemble_kernel, per_half),
-        grid_spec=pltpu.PrefetchScalarGridSpec(
-            num_scalar_prefetch=1,
-            grid=(steps,),
-            in_specs=[source(*w) for w in ((True, True), (True, False), (False, True), (False, False))],
-            out_specs=pl.BlockSpec((wide, channels), lambda i, place_ref: (i, 0)),
-        ),
-        out_shape=jax.ShapeDtypeStruct((pixels, channels), jnp.bfloat16),
-    )(place, here, beside, back, across).reshape(side, side, channels)
+        assemble_kernel,
+        in_specs=[pl.BlockSpec(memory_space=pl.ANY)] * 4,
+        out_specs=pl.BlockSpec(memory_space=pl.ANY),
+        out_shape=pltpu.HBM((2, *here.shape), here.dtype),
+        scratch_shapes=[
+            pltpu.VMEM((2, *here.shape), here.dtype),
+            pltpu.SemaphoreType.DMA((2, 2)),
+            pltpu.SemaphoreType.DMA((2, 2)),
+        ],
+        compiler_params=pltpu.CompilerParams(vmem_limit_bytes=48 * 1024 * 1024),
+    )(here, beside, back, across).reshape(side, side, channels)
 
 
 def layer_norm(values, gain, bias, axis):

time: 354 us -> 356 us (level)
  Pallas kernels: 58.5 us -> 54.1 us
  starting transfers between devices: 30.6 us -> 34.5 us
    pallas_call x2, Pallas kernels: 10.2 us -> 4.51 us  [the longest x1 2.56 us: pack(): pl.pallas_call(functools.partial(pack_kernel, cuts, tile), in_specs=[anyw...]
    ppermute x1 -> x2, waiting for transfers between devices: 4.76 us -> 0.01 us  [the longest x1 0.01 us: by_kernels(): z_over = lax.ppermute(z_next, LINE, ((0, 2), (3, 1)))]
    ppermute x1 -> x2, starting transfers between devices: 0.55 us -> 4.75 us  [the longest x1 3.46 us: by_kernels(): z_over = lax.ppermute(z_next, LINE, ((0, 2), (3, 1)))]
    all_to_all x2, blocking collectives: 128 us -> 131 us  [exchange(): there = lax.all_to_all(array.reshape(peers, -1, array.shape[1]), CUBE, 0, 0)]
  transfers between devices with their start and end apart: 12 -> 13, of which waited for: 8 -> 7; matrix products, arithmetic and copies ran while one was open for 0% -> 0% of each run, Pallas kernels for 4% -> 5%
where the time goes in v8:
time: 356 us; the launch traced here: 351 us
  blocking collectives  131 us (37%)
  waiting for transfers between devices  124 us (35%)
  Pallas kernels  54.1 us (15%)
  starting transfers between devices  34.5 us (10%)
  local copies, waits for them, and re-layouts  4.87 us (1%)
    all_to_all x2, blocking collectives, exchange(): there = lax.all_to_all(array.reshape(peers, -1, array.shape[1]), CUBE, 0, 0)  131 us
    all_to_all x3, waiting for transfers between devices, exchange(): there = lax.all_to_all(array.reshape(peers, -1, array.shape[1]), CUBE, 0, 0)  53.5 us
    pallas_call x7, Pallas kernels, pixel_call(): pl.pallas_call(kernel, grid=(steps,), in_specs=in_specs, out_specs=[spec(...  33.8 us
    ppermute x2, waiting for transfers between devices, by_kernels(): lax.ppermute(there, LINE, pairs)  30 us
    ppermute x2, waiting for transfers between devices, by_kernels(): z_far.append(lax.ppermute(over, LINE, ((0, 1), (3, 2))))  24.2 us
    ppermute x2, waiting for transfers between devices, by_kernels(): over = lax.ppermute(part, LINE, ((1, 3), (2, 0)))  16.8 us
    pallas_call x2, Pallas kernels, triangle_call(): pl.pallas_call(functools.partial(triangle_kernel, blocks, side, own, inco...  15.8 us
    all_to_all x3, starting transfers between devices, exchange(): there = lax.all_to_all(array.reshape(peers, -1, array.shape[1]), CUBE, 0, 0)  15 us
  transfers between devices with their start and end apart: 13, of which 7 were waited for; matrix products, arithmetic and copies ran while one was open for 0% of the time, Pallas kernels for 5%

profile of v8, /device:TPU:20, one launch (start us, length us, event | category | flops | bytes accessed | tf_op | source)
XLA Modules:
  0.0 350.9 jit_solution(4359735660564827119)
XLA Ops:
  2.7 2.6 shard_map.91
  5.3 3.5 collective-permute-start.6
  13.9 13.3 %collective-permute-done.3 = bf16[2,1168,128]{2,1,0:T(8,128)(2,1)S(1)} collective-permute-done((bf16[2,1168,128]{2,1,0:T(8,128)(2,1)}, bf16[2,1168,128]{2,1,0:T(8,128)(2,1)S(1)}, u32[]{:S(2)}, u32[]{:S(2)}) %collective-permute-start.3) | collective-permute-done | bytes 598048 | tf_op jit(solution)/shard_map/ppermute | solution.py:429
  28.7 3.5 collective-permute-done.1
  34.9 5.4 %shard_map.92 = (bf16[256,9216]{1,0:T(8,128)(2,1)}, bf16[128,9216]{1,0:T(8,128)(2,1)}, bf16[16,9216]{1,0:T(8,128)(2,1)}) custom-call(bf16[4,1168,128]{2,1,0:T(8,128)(2,1)S(1)} %copy-done.4, bf16[4,1168,128]{2,1,0:T(8,128)(2,1)} %collective-permute-done.6.refs_1_, f32[128,8]{1,0:T(8,128)S(1)} %bitcast.22, ...), custom_call_target="tpu_custom_call" | custom-call | flops 603979776 | bytes 6045696 | tf_op jit(solution)/shard_map/pallas_call | solution.py:359
  40.3 24.2 %collective-permute-done.2.refs_1_ = bf16[1,1168,128]{2,1,0:T(8,128)(2,1)S(1)} collective-permute-done((bf16[1,1168,128]{2,1,0:T(8,128)(2,1)S(1)}, bf16[1,1168,128]{2,1,0:T(8,128)(2,1)S(1)}, u32[]{:S(2)}, u32[]{:S(2)}) %collective-permute-start.2) | collective-permute-done | bytes 299040 | tf_op jit(solution)/shard_map/ppermute | solution.py:430
  64.5 4.2 %shard_map.93 = (bf16[256,9216]{1,0:T(8,128)(2,1)}, bf16[128,9216]{1,0:T(8,128)(2,1)}, bf16[16,9216]{1,0:T(8,128)(2,1)}) custom-call(bf16[4,1168,128]{2,1,0:T(8,128)(2,1)S(1)} %collective-permute-done.refs_0_, bf16[1,1168,128]{2,1,0:T(8,128)(2,1)S(1)} %collective-permute-done.2.refs_1_, ...), custom_call_target="tpu_custom_call", output_to_operand_aliasing={{0}: (6, {}), {1}: (7, {}), {2}: (8, {})} | custom-call | flops 603979776 | bytes 6045696 | tf_op jit(solution)/shard_map/pallas_call | solution.py:359
  68.7 73.1 %all_to_all.25 = bf16[16,16,9216]{2,1,0:T(8,128)(2,1)S(1)} all-to-all(bf16[16,16,9216]{2,1,0:T(8,128)(2,1)} %bitcast.30), channel_id=1, replica_groups=mesh['groups'=2,'row'=4,'zh'=2,'zl'=2] {'groups','row','zl'}, dimensions={0} | all-to-all | bytes 9437184 | tf_op jit(solution)/shard_map/all_to_all | solution.py:462
  141.8 7.6 %shard_map.94 = bf16[128,9216]{1,0:T(8,128)(2,1)} custom-call(bf16[256,9216]{1,0:T(8,128)(2,1)S(1)} %bitcast.21), custom_call_target="tpu_custom_call" | custom-call | flops 905969664 | bytes 14155776 | tf_op jit(solution)/shard_map/pallas_call | solution.py:305
  149.5 4.9 %all-to-all-start.1 = ((bf16[16,8,9216]{2,1,0:T(8,128)(2,1)}), bf16[16,8,9216]{2,1,0:T(8,128)(2,1)}, u32[]{:S(2)}, u32[]{:S(2)}) async-start(bf16[16,8,9216]{2,1,0:T(8,128)(2,1)} %bitcast.31), calls=%async_computation.1 | async-start | bytes 4718592 | tf_op jit(solution)/shard_map/all_to_all | solution.py:462
  154.4 3.8 %shard_map.95.refs_2_ = bf16[128,9216]{1,0:T(8,128)(2,1)} custom-call(bf16[128,9216]{1,0:T(8,128)(2,1)S(1)} %copy-done.1, f32[128,8]{1,0:T(8,128)S(1)} %bitcast.24, bf16[2,768,128]{2,1,0:T(8,128)(2,1)S(1)} %maximum_bitcast_fusion.refs_3_.refs_5_.refs_2_.refs_4_), custom_call_target="tpu_custom_call" | custom-call | flops 301989888 | bytes 7077888 | tf_op jit(solution)/shard_map/pallas_call | solution.py:359
  158.2 26.5 %all-to-all-done.1 = bf16[16,8,9216]{2,1,0:T(8,128)(2,1)} async-done(((bf16[16,8,9216]{2,1,0:T(8,128)(2,1)}), bf16[16,8,9216]{2,1,0:T(8,128)(2,1)}, u32[]{:S(2)}, u32[]{:S(2)}) %all-to-all-start.1) | async-done | bytes 2359328 | tf_op jit(solution)/shard_map/all_to_all | solution.py:462
  184.7 9.3 %shard_map.96 = (bf16[256,9216]{1,0:T(8,128)(2,1)}, bf16[128,9216]{1,0:T(8,128)(2,1)}) custom-call(bf16[128,9216]{1,0:T(8,128)(2,1)} %bitcast.11.refs_0_, bf16[128,9216]{1,0:T(8,128)(2,1)S(1)} %copy-done.1, bf16[128,9216]{1,0:T(8,128)(2,1)} %shard_map.95.refs_2_, bf16[16,9216]{1,0:T(8,128)(2,1)S(1)} %copy-done.5, f32[128,8]{1,0:T(8,128)S(1)} %bitcast.25, ...), custom_call_target="tpu_custom_call" | custom-call | flops 1509949440 | bytes 11796480 | tf_op jit(solution)/shard_map/pallas_call | solution.py:359
  194.0 58.4 %all_to_all.26 = bf16[16,16,9216]{2,1,0:T(8,128)(2,1)S(1)} all-to-all(bf16[16,16,9216]{2,1,0:T(8,128)(2,1)} %bitcast.32), channel_id=1, replica_groups=mesh['groups'=2,'row'=4,'zh'=2,'zl'=2] {'groups','row','zl'}, dimensions={0} | all-to-all | bytes 9437184 | tf_op jit(solution)/shard_map/all_to_all | solution.py:462
  252.4 8.2 %shard_map.97 = (bf16[128,4608]{1,0:T(8,128)(2,1)}, bf16[128,4608]{1,0:T(8,128)(2,1)}) custom-call(bf16[256,9216]{1,0:T(8,128)(2,1)S(1)} %bitcast.20), custom_call_target="tpu_custom_call" | custom-call | flops 905969664 | bytes 14155776 | tf_op jit(solution)/shard_map/pallas_call | solution.py:305
  260.6 4.8 %all-to-all-start.3 = ((bf16[16,8,4608]{2,1,0:T(8,128)(2,1)}), bf16[16,8,4608]{2,1,0:T(8,128)(2,1)}, u32[]{:S(2)}, u32[]{:S(2)}) async-start(bf16[16,8,4608]{2,1,0:T(8,128)(2,1)} %bitcast.34), calls=%async_computation.3 | async-start | bytes 2359296 | tf_op jit(solution)/shard_map/all_to_all | solution.py:462
  265.4 3.8 %shard_map.98.refs_2_ = bf16[128,9216]{1,0:T(8,128)(2,1)} custom-call(bf16[128,9216]{1,0:T(8,128)(2,1)S(1)} %copy-done, f32[128,8]{1,0:T(8,128)S(1)} %bitcast.26, bf16[2,768,128]{2,1,0:T(8,128)(2,1)S(1)} %maximum_bitcast_fusion.refs_3_.refs_5_.refs_2_.refs_4_), custom_call_target="tpu_custom_call" | custom-call | flops 301989888 | bytes 7077888 | tf_op jit(solution)/shard_map/pallas_call | solution.py:359
  269.2 12.0 %all-to-all-done.3 = bf16[16,8,4608]{2,1,0:T(8,128)(2,1)} async-done(((bf16[16,8,4608]{2,1,0:T(8,128)(2,1)}), bf16[16,8,4608]{2,1,0:T(8,128)(2,1)}, u32[]{:S(2)}, u32[]{:S(2)}) %all-to-all-start.3) | async-done | bytes 1179680 | tf_op jit(solution)/shard_map/all_to_all | solution.py:462
  281.2 3.7 %shard_map.99 = bf16[4608,128]{1,0:T(8,128)(2,1)} custom-call(bf16[128,4608]{1,0:T(8,128)(2,1)} %bitcast.15.refs_0_, bf16[128,9216]{1,0:T(8,128)(2,1)S(1)} %copy-done, bf16[128,9216]{1,0:T(8,128)(2,1)} %shard_map.98.refs_2_, f32[128,8]{1,0:T(8,128)S(1)} %bitcast.27, bf16[2,768,128]{2,1,0:T(8,128)(2,1)S(1)} %maximum_bitcast_fusion.refs_3_.refs_5_.refs_2_.refs_4_), custom_call_target="tpu_custom_call" | custom-call | flops 150994944 | bytes 3538944 | tf_op jit(solution)/shard_map/pallas_call | solution.py:359
  284.9 5.3 %all-to-all-start.4 = ((bf16[16,8,4608]{2,1,0:T(8,128)(2,1)}), bf16[16,8,4608]{2,1,0:T(8,128)(2,1)}, u32[]{:S(2)}, u32[]{:S(2)}) async-start(bf16[16,8,4608]{2,1,0:T(8,128)(2,1)} %bitcast.33), calls=%async_computation.4 | async-start | bytes 2359296 | tf_op jit(solution)/shard_map/all_to_all | solution.py:462
  291.8 5.8 %collective-permute-start.7 = (bf16[4608,128]{1,0:T(8,128)(2,1)}, bf16[4608,128]{1,0:T(8,128)(2,1)}, u32[]{:S(2)}, u32[]{:S(2)}) collective-permute-start(bf16[4608,128]{1,0:T(8,128)(2,1)} %shard_map.99), channel_id=1, source_target_pairs={{0,2},{18,16},{1,3},{19,17},{4,6},{22,20},{5,7},{23,21},{8,10},{26... | collective-permute-start | bytes 3538952 | tf_op jit(solution)/shard_map/ppermute | solution.py:485
  297.6 15.0 %all-to-all-done.4 = bf16[16,8,4608]{2,1,0:T(8,128)(2,1)} async-done(((bf16[16,8,4608]{2,1,0:T(8,128)(2,1)}), bf16[16,8,4608]{2,1,0:T(8,128)(2,1)}, u32[]{:S(2)}, u32[]{:S(2)}) %all-to-all-start.4) | async-done | bytes 1179680 | tf_op jit(solution)/shard_map/all_to_all | solution.py:462
  312.5 3.7 %shard_map.100.here_ref = bf16[4608,128]{1,0:T(8,128)(2,1)} custom-call(bf16[128,4608]{1,0:T(8,128)(2,1)} %bitcast.17.refs_0_, bf16[128,9216]{1,0:T(8,128)(2,1)S(1)} %copy-done, bf16[128,9216]{1,0:T(8,128)(2,1)} %shard_map.98.refs_2_, f32[128,8]{1,0:T(8,128)S(1)} %bitcast.28, bf16[2,768,128]{2,1,0:T(8,128)(2,1)S(1)} %maximum_bitcast_fusion.refs_3_.refs_5_.refs_2_.refs_4_), custom_call_target="tpu_custom_call" | custom-call | flops 150994944 | bytes 3538944 | tf_op jit(solution)/shard_map/pallas_call | solution.py:359
  317.5 30.0 %collective-permute-done.7.beside_ref = bf16[4608,128]{1,0:T(8,128)(2,1)} collective-permute-done((bf16[4608,128]{1,0:T(8,128)(2,1)}, bf16[4608,128]{1,0:T(8,128)(2,1)}, u32[]{:S(2)}, u32[]{:S(2)}) %collective-permute-start.7) | collective-permute-done | bytes 1179680 | tf_op jit(solution)/shard_map/ppermute | solution.py:485
  (53 shorter events, 18.1 us)
Async XLA Ops:
  0.0 13.3 %copy-start.9 = (f32[2,128]{1,0:T(2,128)S(1)}, f32[2,128]{1,0:T(2,128)}, u32[]{:S(2)}) copy-start(f32[2,128]{1,0:T(2,128)} %param.16) | copy-start | bytes 3076
  0.0 13.3 %copy-start.10 = (f32[2,128]{1,0:T(2,128)S(1)}, f32[2,128]{1,0:T(2,128)}, u32[]{:S(2)}) copy-start(f32[2,128]{1,0:T(2,128)} %param.15) | copy-start | bytes 3076
  0.0 13.3 %copy-start.11 = (f32[2,128]{1,0:T(2,128)S(1)}, f32[2,128]{1,0:T(2,128)}, u32[]{:S(2)}) copy-start(f32[2,128]{1,0:T(2,128)} %param.12) | copy-start | bytes 3076
  0.0 13.3 %copy-start.12 = (f32[2,128]{1,0:T(2,128)S(1)}, f32[2,128]{1,0:T(2,128)}, u32[]{:S(2)}) copy-start(f32[2,128]{1,0:T(2,128)} %param.11) | copy-start | bytes 3076
  0.0 13.5 %copy-start.7 = (bf16[2,128,128]{2,1,0:T(8,128)(2,1)S(1)}, bf16[2,128,128]{2,1,0:T(8,128)(2,1)}, u32[]{:S(2)}) copy-start(bf16[2,128,128]{2,1,0:T(8,128)(2,1)} %param.14) | copy-start | bytes 196612
  0.0 13.6 %copy-start.8 = (bf16[2,128,128]{2,1,0:T(8,128)(2,1)S(1)}, bf16[2,128,128]{2,1,0:T(8,128)(2,1)}, u32[]{:S(2)}) copy-start(bf16[2,128,128]{2,1,0:T(8,128)(2,1)} %param.17) | copy-start | bytes 196612
  1.0 1.7 copy-start.3
  2.7 11.0 %copy-start.6 = (bf16[2,128,512]{2,1,0:T(8,128)(2,1)S(1)}, bf16[2,128,512]{2,1,0:T(8,128)(2,1)}, u32[]{:S(2)}) copy-start(bf16[2,128,512]{2,1,0:T(8,128)(2,1)} %param.13) | copy-start | bytes 786436
  5.3 28.4 %collective-permute-start.6 = (bf16[4,1168,128]{2,1,0:T(8,128)(2,1)}, bf16[4,1168,128]{2,1,0:T(8,128)(2,1)}, u32[]{:S(2)}, u32[]{:S(2)}) collective-permute-start(bf16[4,1168,128]{2,1,0:T(8,128)(2,1)} %get-tuple-element.21), channel_id=1, source_target_pairs={{0,16},{18,2},{1,17},{19,3},{4,20},{22,6},{5,21},{23,7},{8,24},{26... | collective-permute-start | bytes 3588104 | tf_op jit(solution)/shard_map/ppermute | solution.py:431
  8.7 18.5 %collective-permute-start.3 = (bf16[2,1168,128]{2,1,0:T(8,128)(2,1)}, bf16[2,1168,128]{2,1,0:T(8,128)(2,1)S(1)}, u32[]{:S(2)}, u32[]{:S(2)}) collective-permute-start(bf16[2,1168,128]{2,1,0:T(8,128)(2,1)} %get-tuple-element.23), channel_id=1, source_target_pairs={{2,18},{16,0},{3,19},{17,1},{6,22},{20,4},{7,23},{21,5},{10,26},{2... | collective-permute-start | bytes 1794056 | tf_op jit(solution)/shard_map/ppermute | solution.py:429
  10.0 54.5 %collective-permute-start = (bf16[4,1168,128]{2,1,0:T(8,128)(2,1)}, bf16[4,1168,128]{2,1,0:T(8,128)(2,1)S(1)}, u32[]{:S(2)}, u32[]{:S(2)}) collective-permute-start(bf16[4,1168,128]{2,1,0:T(8,128)(2,1)} %get-tuple-element.21), channel_id=1, source_target_pairs={{2,0},{16,18},{3,1},{17,19},{6,4},{20,22},{7,5},{21,23},{10,8},{24... | collective-permute-start | bytes 3588104 | tf_op jit(solution)/shard_map/ppermute | solution.py:432
  11.3 20.9 %collective-permute-start.1 = (bf16[1,1168,128]{2,1,0:T(8,128)(2,1)}, bf16[1,1168,128]{2,1,0:T(8,128)(2,1)S(1)}, u32[]{:S(2)}, u32[]{:S(2)}) collective-permute-start(bf16[1,1168,128]{2,1,0:T(8,128)(2,1)} %get-tuple-element.22), channel_id=1, source_target_pairs={{2,18},{16,0},{3,19},{17,1},{6,22},{20,4},{7,23},{21,5},{10,26},{2... | collective-permute-start | bytes 897032 | tf_op jit(solution)/shard_map/ppermute | solution.py:429
  12.6 27.7 %collective-permute-start.5 = (bf16[1,1168,128]{2,1,0:T(8,128)(2,1)}, bf16[1,1168,128]{2,1,0:T(8,128)(2,1)S(1)}, u32[]{:S(2)}, u32[]{:S(2)}) collective-permute-start(bf16[1,1168,128]{2,1,0:T(8,128)(2,1)} %get-tuple-element.24), channel_id=1, source_target_pairs={{2,16},{16,2},{3,17},{17,3},{6,20},{20,6},{7,21},{21,7},{10,24},{2... | collective-permute-start | bytes 897032 | tf_op jit(solution)/shard_map/ppermute | solution.py:433
  27.3 37.3 %collective-permute-start.4 = (bf16[2,1168,128]{2,1,0:T(8,128)(2,1)S(1)}, bf16[2,1168,128]{2,1,0:T(8,128)(2,1)S(1)}, u32[]{:S(2)}, u32[]{:S(2)}) collective-permute-start(bf16[2,1168,128]{2,1,0:T(8,128)(2,1)S(1)} %collective-permute-done.3), channel_id=1, source_target_pairs={{0,2},{18,16},{1,3},{19,17},{4,6},{22,20},{5,7},{23,21},{8,10},{26... | collective-permute-start | bytes 1794056 | tf_op jit(solution)/shard_map/ppermute | solution.py:430
  32.2 32.3 %collective-permute-start.2 = (bf16[1,1168,128]{2,1,0:T(8,128)(2,1)S(1)}, bf16[1,1168,128]{2,1,0:T(8,128)(2,1)S(1)}, u32[]{:S(2)}, u32[]{:S(2)}) collective-permute-start(bf16[1,1168,128]{2,1,0:T(8,128)(2,1)S(1)} %collective-permute-done.1), channel_id=1, source_target_pairs={{0,2},{18,16},{1,3},{19,17},{4,6},{22,20},{5,7},{23,21},{8,10},{26... | collective-permute-start | bytes 897032 | tf_op jit(solution)/shard_map/ppermute | solution.py:430
  149.5 4.9 %copy-start.1 = (bf16[128,9216]{1,0:T(8,128)(2,1)S(1)}, bf16[128,9216]{1,0:T(8,128)(2,1)}, u32[]{:S(2)}) copy-start(bf16[128,9216]{1,0:T(8,128)(2,1)} %get-tuple-element.30.refs_0_.refs_1_) | copy-start | bytes 7077892
  149.5 35.3 %all-to-all-start.1 = ((bf16[16,8,9216]{2,1,0:T(8,128)(2,1)}), bf16[16,8,9216]{2,1,0:T(8,128)(2,1)}, u32[]{:S(2)}, u32[]{:S(2)}) async-start(bf16[16,8,9216]{2,1,0:T(8,128)(2,1)} %bitcast.31), calls=%async_computation.1 | async-start | bytes 4718592 | tf_op jit(solution)/shard_map/all_to_all | solution.py:462
  154.4 30.3 %copy-start.5 = (bf16[16,9216]{1,0:T(8,128)(2,1)S(1)}, bf16[16,9216]{1,0:T(8,128)(2,1)}, u32[]{:S(2)}) copy-start(bf16[16,9216]{1,0:T(8,128)(2,1)} %get-tuple-element.31.refs_3_) | copy-start | bytes 884740
  260.5 4.9 %copy-start = (bf16[128,9216]{1,0:T(8,128)(2,1)S(1)}, bf16[128,9216]{1,0:T(8,128)(2,1)}, u32[]{:S(2)}) copy-start(bf16[128,9216]{1,0:T(8,128)(2,1)} %get-tuple-element.34.refs_0_.refs_1_) | copy-start | bytes 7077892
  260.6 20.6 %all-to-all-start.3 = ((bf16[16,8,4608]{2,1,0:T(8,128)(2,1)}), bf16[16,8,4608]{2,1,0:T(8,128)(2,1)}, u32[]{:S(2)}, u32[]{:S(2)}) async-start(bf16[16,8,4608]{2,1,0:T(8,128)(2,1)} %bitcast.34), calls=%async_computation.3 | async-start | bytes 2359296 | tf_op jit(solution)/shard_map/all_to_all | solution.py:462
  284.9 27.7 %all-to-all-start.4 = ((bf16[16,8,4608]{2,1,0:T(8,128)(2,1)}), bf16[16,8,4608]{2,1,0:T(8,128)(2,1)}, u32[]{:S(2)}, u32[]{:S(2)}) async-start(bf16[16,8,4608]{2,1,0:T(8,128)(2,1)} %bitcast.33), calls=%async_computation.4 | async-start | bytes 2359296 | tf_op jit(solution)/shard_map/all_to_all | solution.py:462
  290.1 27.4 %collective-permute-start.9 = (bf16[4608,128]{1,0:T(8,128)(2,1)}, bf16[4608,128]{1,0:T(8,128)(2,1)}, u32[]{:S(2)}, u32[]{:S(2)}) collective-permute-start(bf16[4608,128]{1,0:T(8,128)(2,1)} %shard_map.99), channel_id=1, source_target_pairs={{2,16},{16,2},{3,17},{17,3},{6,20},{20,6},{7,21},{21,7},{10,24},{2... | collective-permute-start | bytes 3538952 | tf_op jit(solution)/shard_map/ppermute | solution.py:485
  291.8 55.7 %collective-permute-start.7 = (bf16[4608,128]{1,0:T(8,128)(2,1)}, bf16[4608,128]{1,0:T(8,128)(2,1)}, u32[]{:S(2)}, u32[]{:S(2)}) collective-permute-start(bf16[4608,128]{1,0:T(8,128)(2,1)} %shard_map.99), channel_id=1, source_target_pairs={{0,2},{18,16},{1,3},{19,17},{4,6},{22,20},{5,7},{23,21},{8,10},{26... | collective-permute-start | bytes 3538952 | tf_op jit(solution)/shard_map/ppermute | solution.py:485
  316.2 31.3 %collective-permute-start.8 = (bf16[4608,128]{1,0:T(8,128)(2,1)}, bf16[4608,128]{1,0:T(8,128)(2,1)S(1)}, u32[]{:S(2)}, u32[]{:S(2)}) collective-permute-start(bf16[4608,128]{1,0:T(8,128)(2,1)} %shard_map.100.here_ref), channel_id=1, source_target_pairs={{2,18},{16,0},{3,19},{17,1},{6,22},{20,4},{7,23},{21,5},{10,26},{2... | collective-permute-start | bytes 3538952 | tf_op jit(solution)/shard_map/ppermute | solution.py:489
  (2 other events, 2.6 us)

commit v9 on v8

--- a/solution.py
+++ b/solution.py
@@ -428,8 +428,7 @@
     for part in z_parts[:-1]:
         over = lax.ppermute(part, LINE, ((1, 3), (2, 0)))
         z_far.append(lax.ppermute(over, LINE, ((0, 1), (3, 2))))
-    z_over = lax.ppermute(z_next, LINE, ((0, 2), (3, 1)))
-    z_near = lax.ppermute(z_next, LINE, ((1, 0), (2, 3)))
+    z_near = lax.ppermute(z_next, LINE, ((1, 0), (2, 3), (0, 2), (3, 1)))
     z_far.append(lax.ppermute(z_parts[-1], LINE, ((1, 2), (2, 1))))
     small = jnp.stack([input_gain, input_bias, output_gain, output_bias], axis=1)
     small = small.reshape(-1, channels).T
@@ -447,7 +446,7 @@
             start=piece * per_piece, pixels=pixels, kept=kept,
         )
 
-    begun = first(0, z_own, [z_over], [(0, per_piece)], ())
+    begun = first(0, z_own, [z_near], [(0, per_piece)], ())
     sent, zt, mask = first(1, z_near, z_far, list(zip((0, *cuts), cuts)), begun)
     wide = 2 * tile
     steps = pixels // wide
@@ -480,12 +479,13 @@
             fixed, (channels,), steps // 2, wide, pixels // 2 * mult * channels, row_major_out=True,
         )[0]
 
-    there = finish(1, exchange(products[1]))
+    arrived = [exchange(product) for product in products[::-1]]
+    there = finish(1, arrived[0])
     beside, across = (
         lax.ppermute(there, LINE, pairs) for pairs in (((0, 1), (3, 2)), ((1, 2), (2, 1)))
     )
-    there, waiting = lax.optimization_barrier((there, products[0]))
-    here = finish(0, exchange(waiting))
+    there, waiting = lax.optimization_barrier((there, arrived[1]))
+    here = finish(0, waiting)
     back = lax.ppermute(here, LINE, ((1, 3), (2, 0)))
     return pl.pallas_call(
         assemble_kernel,

time: 356 us -> 368 us (1.034)
  blocking collectives: 131 us -> 149 us
  starting transfers between devices: 34.5 us -> 27.2 us
  waiting for transfers between devices: 124 us -> 129 us
    ppermute x1, waiting for transfers between devices: 0.01 us -> 19.8 us  [by_kernels(): back = lax.ppermute(here, LINE, ((1, 3), (2, 0)))]
    all_to_all x3 -> x2, waiting for transfers between devices: 53.5 us -> 34.9 us  [exchange(): there = lax.all_to_all(array.reshape(peers, -1, array.shape[1]), CUBE, 0, 0)]
    all_to_all x2 -> x3, blocking collectives: 131 us -> 149 us  [exchange(): there = lax.all_to_all(array.reshape(peers, -1, array.shape[1]), CUBE, 0, 0)]
    all_to_all x3 -> x2, starting transfers between devices: 15 us -> 10.1 us  [exchange(): there = lax.all_to_all(array.reshape(peers, -1, array.shape[1]), CUBE, 0, 0)]
    ppermute x2 -> x1, waiting for transfers between devices: 0.01 us -> 4.76 us  [by_kernels(): z_near = lax.ppermute(z_next, LINE, ((1, 0), (2, 3), (0, 2), (3, 1)))]
    ppermute x2 -> x1, starting transfers between devices: 4.75 us -> 0.56 us  [by_kernels(): z_near = lax.ppermute(z_next, LINE, ((1, 0), (2, 3), (0, 2), (3, 1)))]
  transfers between devices with their start and end apart: 13 -> 11, of which waited for: 7 -> 8; matrix products, arithmetic and copies ran while one was open for 0% -> 0% of each run, Pallas kernels for 5% -> 4%
where the time goes in v9:
time: 368 us; the launch traced here: 364 us
  blocking collectives  149 us (40%)
  waiting for transfers between devices  129 us (35%)
  Pallas kernels  52.7 us (14%)
  starting transfers between devices  27.2 us (7%)
  local copies, waits for them, and re-layouts  4.88 us (1%)
    all_to_all x3, blocking collectives, exchange(): there = lax.all_to_all(array.reshape(peers, -1, array.shape[1]), CUBE, 0, 0)  149 us
    all_to_all x2, waiting for transfers between devices, exchange(): there = lax.all_to_all(array.reshape(peers, -1, array.shape[1]), CUBE, 0, 0)  34.9 us
    pallas_call x7, Pallas kernels, pixel_call(): pl.pallas_call(kernel, grid=(steps,), in_specs=in_specs, out_specs=[spec(...  32.4 us
    ppermute x2, waiting for transfers between devices, by_kernels(): lax.ppermute(there, LINE, pairs)  30.3 us
    ppermute x2, waiting for transfers between devices, by_kernels(): z_far.append(lax.ppermute(over, LINE, ((0, 1), (3, 2))))  20.8 us
    ppermute x1, waiting for transfers between devices, by_kernels(): back = lax.ppermute(here, LINE, ((1, 3), (2, 0)))  19.8 us
    ppermute x2, waiting for transfers between devices, by_kernels(): over = lax.ppermute(part, LINE, ((1, 3), (2, 0)))  18.1 us
    pallas_call x2, Pallas kernels, triangle_call(): pl.pallas_call(functools.partial(triangle_kernel, blocks, side, own, inco...  15.8 us
  transfers between devices with their start and end apart: 11, of which 8 were waited for; matrix products, arithmetic and copies ran while one was open for 0% of the time, Pallas kernels for 4%

profile of v9, /device:TPU:20, one launch (start us, length us, event | category | flops | bytes accessed | tf_op | source)
XLA Modules:
  0.0 363.8 jit_solution(4387038632125692825)
XLA Ops:
  2.7 2.5 shard_map.91
  9.7 14.6 %collective-permute-done.3 = bf16[2,1168,128]{2,1,0:T(8,128)(2,1)S(1)} collective-permute-done((bf16[2,1168,128]{2,1,0:T(8,128)(2,1)}, bf16[2,1168,128]{2,1,0:T(8,128)(2,1)S(1)}, u32[]{:S(2)}, u32[]{:S(2)}) %collective-permute-start.3) | collective-permute-done | bytes 598048 | tf_op jit(solution)/shard_map/ppermute | solution.py:429
  25.8 3.5 collective-permute-done.1
  31.0 4.8 %collective-permute-done.refs_1_.refs_0_ = bf16[4,1168,128]{2,1,0:T(8,128)(2,1)S(1)} collective-permute-done((bf16[4,1168,128]{2,1,0:T(8,128)(2,1)}, bf16[4,1168,128]{2,1,0:T(8,128)(2,1)S(1)}, u32[]{:S(2)}, u32[]{:S(2)}) %collective-permute-start) | collective-permute-done | bytes 1196064 | tf_op jit(solution)/shard_map/ppermute | solution.py:431
  37.0 4.1 %shard_map.92 = (bf16[256,9216]{1,0:T(8,128)(2,1)}, bf16[128,9216]{1,0:T(8,128)(2,1)}, bf16[16,9216]{1,0:T(8,128)(2,1)}) custom-call(bf16[4,1168,128]{2,1,0:T(8,128)(2,1)S(1)} %copy-done.5, bf16[4,1168,128]{2,1,0:T(8,128)(2,1)S(1)} %collective-permute-done.refs_1_.refs_0_, f32[128,8]{1,0:T(8,128)S(1)} %bitcast.23, ...), custom_call_target="tpu_custom_call" | custom-call | flops 603979776 | bytes 6045696 | tf_op jit(solution)/shard_map/pallas_call | solution.py:359
  41.1 20.8 %collective-permute-done.2.refs_1_ = bf16[1,1168,128]{2,1,0:T(8,128)(2,1)S(1)} collective-permute-done((bf16[1,1168,128]{2,1,0:T(8,128)(2,1)S(1)}, bf16[1,1168,128]{2,1,0:T(8,128)(2,1)S(1)}, u32[]{:S(2)}, u32[]{:S(2)}) %collective-permute-start.2) | collective-permute-done | bytes 299040 | tf_op jit(solution)/shard_map/ppermute | solution.py:430
  61.9 4.1 %shard_map.93 = (bf16[256,9216]{1,0:T(8,128)(2,1)}, bf16[128,9216]{1,0:T(8,128)(2,1)}, bf16[16,9216]{1,0:T(8,128)(2,1)}) custom-call(bf16[4,1168,128]{2,1,0:T(8,128)(2,1)S(1)} %collective-permute-done.refs_1_.refs_0_, bf16[1,1168,128]{2,1,0:T(8,128)(2,1)S(1)} %collective-permute-done.2.refs_1_, ...), custom_call_target="tpu_custom_call", output_to_operand_aliasing={{0}: (6, {}), {1}: (7, {}), {2}: (8, {})} | custom-call | flops 603979776 | bytes 6045696 | tf_op jit(solution)/shard_map/pallas_call | solution.py:359
  66.1 69.4 %all_to_all.25 = bf16[16,16,9216]{2,1,0:T(8,128)(2,1)S(1)} all-to-all(bf16[16,16,9216]{2,1,0:T(8,128)(2,1)} %bitcast.31), channel_id=1, replica_groups=mesh['groups'=2,'row'=4,'zh'=2,'zl'=2] {'groups','row','zl'}, dimensions={0} | all-to-all | bytes 9437184 | tf_op jit(solution)/shard_map/all_to_all | solution.py:461
  135.5 7.6 %shard_map.94 = bf16[128,9216]{1,0:T(8,128)(2,1)} custom-call(bf16[256,9216]{1,0:T(8,128)(2,1)S(1)} %bitcast.21), custom_call_target="tpu_custom_call" | custom-call | flops 905969664 | bytes 14155776 | tf_op jit(solution)/shard_map/pallas_call | solution.py:305
  143.1 4.9 %all-to-all-start.1 = ((bf16[16,8,9216]{2,1,0:T(8,128)(2,1)}), bf16[16,8,9216]{2,1,0:T(8,128)(2,1)}, u32[]{:S(2)}, u32[]{:S(2)}) async-start(bf16[16,8,9216]{2,1,0:T(8,128)(2,1)} %bitcast.32), calls=%async_computation.1 | async-start | bytes 4718592 | tf_op jit(solution)/shard_map/all_to_all | solution.py:461
  148.1 3.8 %shard_map.95.refs_2_ = bf16[128,9216]{1,0:T(8,128)(2,1)} custom-call(bf16[128,9216]{1,0:T(8,128)(2,1)S(1)} %copy-done.1, f32[128,8]{1,0:T(8,128)S(1)} %bitcast.25, bf16[2,768,128]{2,1,0:T(8,128)(2,1)S(1)} %maximum_bitcast_fusion.refs_3_.refs_5_.refs_2_.refs_4_), custom_call_target="tpu_custom_call" | custom-call | flops 301989888 | bytes 7077888 | tf_op jit(solution)/shard_map/pallas_call | solution.py:359
  151.9 26.5 %all-to-all-done.1 = bf16[16,8,9216]{2,1,0:T(8,128)(2,1)} async-done(((bf16[16,8,9216]{2,1,0:T(8,128)(2,1)}), bf16[16,8,9216]{2,1,0:T(8,128)(2,1)}, u32[]{:S(2)}, u32[]{:S(2)}) %all-to-all-start.1) | async-done | bytes 2359328 | tf_op jit(solution)/shard_map/all_to_all | solution.py:461
  178.4 9.3 %shard_map.96 = (bf16[256,9216]{1,0:T(8,128)(2,1)}, bf16[128,9216]{1,0:T(8,128)(2,1)}) custom-call(bf16[128,9216]{1,0:T(8,128)(2,1)} %bitcast.11.refs_0_, bf16[128,9216]{1,0:T(8,128)(2,1)S(1)} %copy-done.1, bf16[128,9216]{1,0:T(8,128)(2,1)} %shard_map.95.refs_2_, bf16[16,9216]{1,0:T(8,128)(2,1)S(1)} %copy-done.6, f32[128,8]{1,0:T(8,128)S(1)} %bitcast.26, ...), custom_call_target="tpu_custom_call" | custom-call | flops 1509949440 | bytes 11796480 | tf_op jit(solution)/shard_map/pallas_call | solution.py:359
  187.7 58.4 %all_to_all.26 = bf16[16,16,9216]{2,1,0:T(8,128)(2,1)S(1)} all-to-all(bf16[16,16,9216]{2,1,0:T(8,128)(2,1)} %bitcast.33), channel_id=1, replica_groups=mesh['groups'=2,'row'=4,'zh'=2,'zl'=2] {'groups','row','zl'}, dimensions={0} | all-to-all | bytes 9437184 | tf_op jit(solution)/shard_map/all_to_all | solution.py:461
  246.1 8.1 %shard_map.97 = (bf16[128,4608]{1,0:T(8,128)(2,1)}, bf16[128,4608]{1,0:T(8,128)(2,1)}) custom-call(bf16[256,9216]{1,0:T(8,128)(2,1)S(1)} %bitcast.20), custom_call_target="tpu_custom_call" | custom-call | flops 905969664 | bytes 14155776 | tf_op jit(solution)/shard_map/pallas_call | solution.py:305
  254.2 21.0 %all_to_all.27 = bf16[16,8,4608]{2,1,0:T(8,128)(2,1)} all-to-all(bf16[16,8,4608]{2,1,0:T(8,128)(2,1)} %bitcast.35), channel_id=1, replica_groups=mesh['groups'=2,'row'=4,'zh'=2,'zl'=2] {'groups','row','zl'}, dimensions={0} | all-to-all | bytes 2359296 | tf_op jit(solution)/shard_map/all_to_all | solution.py:461
  275.2 5.2 %all-to-all-start.4 = ((bf16[16,8,4608]{2,1,0:T(8,128)(2,1)}), bf16[16,8,4608]{2,1,0:T(8,128)(2,1)}, u32[]{:S(2)}, u32[]{:S(2)}) async-start(bf16[16,8,4608]{2,1,0:T(8,128)(2,1)} %bitcast.34), calls=%async_computation.4 | async-start | bytes 2359296 | tf_op jit(solution)/shard_map/all_to_all | solution.py:461
  280.4 3.8 %shard_map.98.refs_2_ = bf16[128,9216]{1,0:T(8,128)(2,1)} custom-call(bf16[128,9216]{1,0:T(8,128)(2,1)S(1)} %copy-done, f32[128,8]{1,0:T(8,128)S(1)} %bitcast.27, bf16[2,768,128]{2,1,0:T(8,128)(2,1)S(1)} %maximum_bitcast_fusion.refs_3_.refs_5_.refs_2_.refs_4_), custom_call_target="tpu_custom_call" | custom-call | flops 301989888 | bytes 7077888 | tf_op jit(solution)/shard_map/pallas_call | solution.py:359
  284.2 3.6 shard_map.99
  287.8 8.4 %all-to-all-done.4 = bf16[16,8,4608]{2,1,0:T(8,128)(2,1)} async-done(((bf16[16,8,4608]{2,1,0:T(8,128)(2,1)}), bf16[16,8,4608]{2,1,0:T(8,128)(2,1)}, u32[]{:S(2)}, u32[]{:S(2)}) %all-to-all-start.4) | async-done | bytes 1179680 | tf_op jit(solution)/shard_map/all_to_all | solution.py:461
  296.2 3.8 %shard_map.100.here_ref = bf16[4608,128]{1,0:T(8,128)(2,1)} custom-call(bf16[128,4608]{1,0:T(8,128)(2,1)} %bitcast.17.refs_0_, bf16[128,9216]{1,0:T(8,128)(2,1)S(1)} %copy-done, bf16[128,9216]{1,0:T(8,128)(2,1)} %shard_map.98.refs_2_, f32[128,8]{1,0:T(8,128)S(1)} %bitcast.29, bf16[2,768,128]{2,1,0:T(8,128)(2,1)S(1)} %maximum_bitcast_fusion.refs_3_.refs_5_.refs_2_.refs_4_), custom_call_target="tpu_custom_call" | custom-call | flops 150994944 | bytes 3538944 | tf_op jit(solution)/shard_map/pallas_call | solution.py:359
  302.0 8.2 %collective-permute-start.6 = (bf16[4608,128]{1,0:T(8,128)(2,1)S(1)}, bf16[4608,128]{1,0:T(8,128)(2,1)S(1)}, u32[]{:S(2)}, u32[]{:S(2)}) collective-permute-start(bf16[4608,128]{1,0:T(8,128)(2,1)S(1)} %copy-done.7), channel_id=1, source_target_pairs={{0,2},{18,16},{1,3},{19,17},{4,6},{22,20},{5,7},{23,21},{8,10},{26... | collective-permute-start | bytes 3538952 | tf_op jit(solution)/shard_map/ppermute | solution.py:485
  310.3 19.8 %collective-permute-done.7.back_ref = bf16[4608,128]{1,0:T(8,128)(2,1)S(1)} collective-permute-done((bf16[4608,128]{1,0:T(8,128)(2,1)}, bf16[4608,128]{1,0:T(8,128)(2,1)S(1)}, u32[]{:S(2)}, u32[]{:S(2)}) %collective-permute-start.7) | collective-permute-done | bytes 1179680 | tf_op jit(solution)/shard_map/ppermute | solution.py:489
  330.1 30.3 %collective-permute-done.6.beside_ref = bf16[4608,128]{1,0:T(8,128)(2,1)S(1)} collective-permute-done((bf16[4608,128]{1,0:T(8,128)(2,1)S(1)}, bf16[4608,128]{1,0:T(8,128)(2,1)S(1)}, u32[]{:S(2)}, u32[]{:S(2)}) %collective-permute-start.6) | collective-permute-done | bytes 1179680 | tf_op jit(solution)/shard_map/ppermute | solution.py:485
  (54 shorter events, 16.6 us)
Async XLA Ops:
  0.0 9.1 %copy-start.11 = (f32[2,128]{1,0:T(2,128)S(1)}, f32[2,128]{1,0:T(2,128)}, u32[]{:S(2)}) copy-start(f32[2,128]{1,0:T(2,128)} %param.16) | copy-start | bytes 3076
  0.0 9.1 %copy-start.12 = (f32[2,128]{1,0:T(2,128)S(1)}, f32[2,128]{1,0:T(2,128)}, u32[]{:S(2)}) copy-start(f32[2,128]{1,0:T(2,128)} %param.15) | copy-start | bytes 3076
  0.0 9.1 %copy-start.13 = (f32[2,128]{1,0:T(2,128)S(1)}, f32[2,128]{1,0:T(2,128)}, u32[]{:S(2)}) copy-start(f32[2,128]{1,0:T(2,128)} %param.12) | copy-start | bytes 3076
  0.0 9.1 %copy-start.14 = (f32[2,128]{1,0:T(2,128)S(1)}, f32[2,128]{1,0:T(2,128)}, u32[]{:S(2)}) copy-start(f32[2,128]{1,0:T(2,128)} %param.11) | copy-start | bytes 3076
  0.0 9.2 %copy-start.9 = (bf16[2,128,128]{2,1,0:T(8,128)(2,1)S(1)}, bf16[2,128,128]{2,1,0:T(8,128)(2,1)}, u32[]{:S(2)}) copy-start(bf16[2,128,128]{2,1,0:T(8,128)(2,1)} %param.14) | copy-start | bytes 196612
  0.0 9.4 %copy-start.10 = (bf16[2,128,128]{2,1,0:T(8,128)(2,1)S(1)}, bf16[2,128,128]{2,1,0:T(8,128)(2,1)}, u32[]{:S(2)}) copy-start(bf16[2,128,128]{2,1,0:T(8,128)(2,1)} %param.17) | copy-start | bytes 196612
  1.0 1.7 copy-start.4
  2.7 6.8 %copy-start.8 = (bf16[2,128,512]{2,1,0:T(8,128)(2,1)S(1)}, bf16[2,128,512]{2,1,0:T(8,128)(2,1)}, u32[]{:S(2)}) copy-start(bf16[2,128,512]{2,1,0:T(8,128)(2,1)} %param.13) | copy-start | bytes 786436
  5.3 30.5 %collective-permute-start = (bf16[4,1168,128]{2,1,0:T(8,128)(2,1)}, bf16[4,1168,128]{2,1,0:T(8,128)(2,1)S(1)}, u32[]{:S(2)}, u32[]{:S(2)}) collective-permute-start(bf16[4,1168,128]{2,1,0:T(8,128)(2,1)} %get-tuple-element.21), channel_id=1, source_target_pairs={{2,0},{16,18},{0,16},{18,2},{3,1},{17,19},{1,17},{19,3},{6,4},{20,... | collective-permute-start | bytes 3588104 | tf_op jit(solution)/shard_map/ppermute | solution.py:431
  5.8 18.5 %collective-permute-start.3 = (bf16[2,1168,128]{2,1,0:T(8,128)(2,1)}, bf16[2,1168,128]{2,1,0:T(8,128)(2,1)S(1)}, u32[]{:S(2)}, u32[]{:S(2)}) collective-permute-start(bf16[2,1168,128]{2,1,0:T(8,128)(2,1)} %get-tuple-element.23), channel_id=1, source_target_pairs={{2,18},{16,0},{3,19},{17,1},{6,22},{20,4},{7,23},{21,5},{10,26},{2... | collective-permute-start | bytes 1794056 | tf_op jit(solution)/shard_map/ppermute | solution.py:429
  7.1 22.2 %collective-permute-start.1 = (bf16[1,1168,128]{2,1,0:T(8,128)(2,1)}, bf16[1,1168,128]{2,1,0:T(8,128)(2,1)S(1)}, u32[]{:S(2)}, u32[]{:S(2)}) collective-permute-start(bf16[1,1168,128]{2,1,0:T(8,128)(2,1)} %get-tuple-element.22), channel_id=1, source_target_pairs={{2,18},{16,0},{3,19},{17,1},{6,22},{20,4},{7,23},{21,5},{10,26},{2... | collective-permute-start | bytes 897032 | tf_op jit(solution)/shard_map/ppermute | solution.py:429
  8.4 32.7 %collective-permute-start.5 = (bf16[1,1168,128]{2,1,0:T(8,128)(2,1)}, bf16[1,1168,128]{2,1,0:T(8,128)(2,1)S(1)}, u32[]{:S(2)}, u32[]{:S(2)}) collective-permute-start(bf16[1,1168,128]{2,1,0:T(8,128)(2,1)} %get-tuple-element.24), channel_id=1, source_target_pairs={{2,16},{16,2},{3,17},{17,3},{6,20},{20,6},{7,21},{21,7},{10,24},{2... | collective-permute-start | bytes 897032 | tf_op jit(solution)/shard_map/ppermute | solution.py:432
  24.3 37.6 %collective-permute-start.4 = (bf16[2,1168,128]{2,1,0:T(8,128)(2,1)S(1)}, bf16[2,1168,128]{2,1,0:T(8,128)(2,1)S(1)}, u32[]{:S(2)}, u32[]{:S(2)}) collective-permute-start(bf16[2,1168,128]{2,1,0:T(8,128)(2,1)S(1)} %collective-permute-done.3), channel_id=1, source_target_pairs={{0,2},{18,16},{1,3},{19,17},{4,6},{22,20},{5,7},{23,21},{8,10},{26... | collective-permute-start | bytes 1794056 | tf_op jit(solution)/shard_map/ppermute | solution.py:430
  29.3 32.6 %collective-permute-start.2 = (bf16[1,1168,128]{2,1,0:T(8,128)(2,1)S(1)}, bf16[1,1168,128]{2,1,0:T(8,128)(2,1)S(1)}, u32[]{:S(2)}, u32[]{:S(2)}) collective-permute-start(bf16[1,1168,128]{2,1,0:T(8,128)(2,1)S(1)} %collective-permute-done.1), channel_id=1, source_target_pairs={{0,2},{18,16},{1,3},{19,17},{4,6},{22,20},{5,7},{23,21},{8,10},{26... | collective-permute-start | bytes 897032 | tf_op jit(solution)/shard_map/ppermute | solution.py:430
  143.1 4.9 %copy-start.1 = (bf16[128,9216]{1,0:T(8,128)(2,1)S(1)}, bf16[128,9216]{1,0:T(8,128)(2,1)}, u32[]{:S(2)}) copy-start(bf16[128,9216]{1,0:T(8,128)(2,1)} %get-tuple-element.30.refs_0_.refs_1_) | copy-start | bytes 7077892
  143.1 35.3 %all-to-all-start.1 = ((bf16[16,8,9216]{2,1,0:T(8,128)(2,1)}), bf16[16,8,9216]{2,1,0:T(8,128)(2,1)}, u32[]{:S(2)}, u32[]{:S(2)}) async-start(bf16[16,8,9216]{2,1,0:T(8,128)(2,1)} %bitcast.32), calls=%async_computation.1 | async-start | bytes 4718592 | tf_op jit(solution)/shard_map/all_to_all | solution.py:461
  148.0 30.3 %copy-start.6 = (bf16[16,9216]{1,0:T(8,128)(2,1)S(1)}, bf16[16,9216]{1,0:T(8,128)(2,1)}, u32[]{:S(2)}) copy-start(bf16[16,9216]{1,0:T(8,128)(2,1)} %get-tuple-element.31.refs_3_) | copy-start | bytes 884740
  254.2 26.2 %copy-start = (bf16[128,9216]{1,0:T(8,128)(2,1)S(1)}, bf16[128,9216]{1,0:T(8,128)(2,1)}, u32[]{:S(2)}) copy-start(bf16[128,9216]{1,0:T(8,128)(2,1)} %get-tuple-element.34.refs_0_.refs_1_) | copy-start | bytes 7077892
  275.2 21.0 %all-to-all-start.4 = ((bf16[16,8,4608]{2,1,0:T(8,128)(2,1)}), bf16[16,8,4608]{2,1,0:T(8,128)(2,1)}, u32[]{:S(2)}, u32[]{:S(2)}) async-start(bf16[16,8,4608]{2,1,0:T(8,128)(2,1)} %bitcast.34), calls=%async_computation.4 | async-start | bytes 2359296 | tf_op jit(solution)/shard_map/all_to_all | solution.py:461
  280.4 3.8 %copy-start.3 = (bf16[16,8,4608]{2,1,0:T(8,128)(2,1)S(1)}, bf16[16,8,4608]{2,1,0:T(8,128)(2,1)}, u32[]{:S(2)}) copy-start(bf16[16,8,4608]{2,1,0:T(8,128)(2,1)} %all_to_all.27) | copy-start | bytes 3538948
  296.2 5.1 %copy-start.7 = (bf16[4608,128]{1,0:T(8,128)(2,1)S(1)}, bf16[4608,128]{1,0:T(8,128)(2,1)}, u32[]{:S(2)}) copy-start(bf16[4608,128]{1,0:T(8,128)(2,1)} %shard_map.99) | copy-start | bytes 3538948
  300.0 30.1 %collective-permute-start.7 = (bf16[4608,128]{1,0:T(8,128)(2,1)}, bf16[4608,128]{1,0:T(8,128)(2,1)S(1)}, u32[]{:S(2)}, u32[]{:S(2)}) collective-permute-start(bf16[4608,128]{1,0:T(8,128)(2,1)} %shard_map.100.here_ref), channel_id=1, source_target_pairs={{2,18},{16,0},{3,19},{17,1},{6,22},{20,4},{7,23},{21,5},{10,26},{2... | collective-permute-start | bytes 3538952 | tf_op jit(solution)/shard_map/ppermute | solution.py:489
  301.3 28.8 %collective-permute-start.8 = (bf16[4608,128]{1,0:T(8,128)(2,1)S(1)}, bf16[4608,128]{1,0:T(8,128)(2,1)S(1)}, u32[]{:S(2)}, u32[]{:S(2)}) collective-permute-start(bf16[4608,128]{1,0:T(8,128)(2,1)S(1)} %copy-done.7), channel_id=1, source_target_pairs={{2,16},{16,2},{3,17},{17,3},{6,20},{20,6},{7,21},{21,7},{10,24},{2... | collective-permute-start | bytes 3538952 | tf_op jit(solution)/shard_map/ppermute | solution.py:485
  302.0 58.4 %collective-permute-start.6 = (bf16[4608,128]{1,0:T(8,128)(2,1)S(1)}, bf16[4608,128]{1,0:T(8,128)(2,1)S(1)}, u32[]{:S(2)}, u32[]{:S(2)}) collective-permute-start(bf16[4608,128]{1,0:T(8,128)(2,1)S(1)} %copy-done.7), channel_id=1, source_target_pairs={{0,2},{18,16},{1,3},{19,17},{4,6},{22,20},{5,7},{23,21},{8,10},{26... | collective-permute-start | bytes 3538952 | tf_op jit(solution)/shard_map/ppermute | solution.py:485
  (2 other events, 2.5 us)

commit v10 on v9

--- a/solution.py
+++ b/solution.py
@@ -176,8 +176,7 @@
     pl.when(jnp.logical_not(home))(lambda: move(beside_ref, across_ref))
 
 
-def triangle_kernel(blocks, side, own, incoming, n_in, *refs):
-    x_refs, y_refs, (left_ref, right_ref, rows_ref, tiles_ref) = refs[:n_in], refs[n_in:-4], refs[-4:]
+def triangle_kernel(blocks, side, own, incoming, made, x_ref, y_ref, left_ref, right_ref, rows_ref, tiles_ref):
     step = pl.program_id(0)
     zh = lax.axis_index("zh")
     pair = 2 * own
@@ -188,10 +187,7 @@
     lane = lax.broadcasted_iota(jnp.int32, (pair, LANES), 1)
     inside = lane < side
 
-    def piece_of(piece_refs, piece):
-        if len(piece_refs) == 1:
-            return piece_refs[0], piece * strip * side
-        return piece_refs[piece], 0
+    wanted = range(blocks) if len(made) == 2 else range(made[0] * half, (made[0] + 1) * half)
 
     @pl.when(step < blocks)
     def _unpack():
@@ -205,7 +201,7 @@
                 at_right = pl.multiple_of((mirror * 2 + r) * LANES + upper * strip, 16)
             for zl in range(half):
                 for piece in range(2):
-                    x_ref, first = piece_of(x_refs, piece)
+                    first = piece * strip * side
                     for group in range(strip // 4):
                         x = x_ref[
                             (r * half + zl) * pair : (r * half + zl + 1) * pair,
@@ -227,6 +223,8 @@
                         left_ref[ch, pl.ds(at, strip), lanes] = rows_ref[
                             pl.ds(ch, strip, stride=pitch_rows), :
                         ].astype(jnp.bfloat16)
+                        if incoming and piece not in made:
+                            continue
                         right_ref[ch, pl.ds(at_right, strip), lanes] = rows_ref[
                             pl.ds(own + ch, strip, stride=pitch_rows), :
                         ].astype(jnp.bfloat16)
@@ -235,8 +233,11 @@
     def _multiply():
         contract = ((0,), (0,)) if incoming else ((1,), (1,))
         for ch in range(own):
+            right = right_ref[ch]
+            if incoming:
+                right = right[:, wanted[0] * LANES : (wanted[-1] + 1) * LANES]
             product = lax.dot_general(
-                left_ref[ch], right_ref[ch], (contract, ((), ())), preferred_element_type=jnp.float32
+                left_ref[ch], right, (contract, ((), ())), preferred_element_type=jnp.float32
             )
             for place in range(blocks):
                 if incoming:
@@ -244,7 +245,7 @@
                 else:
                     row, pitch = place, side
                 for upper in range(2):
-                    for col in range(blocks):
+                    for col in range(len(wanted)):
                         tiles_ref[
                             col // half,
                             upper * blocks + row,
@@ -259,8 +260,8 @@
     def _repack():
         for r in range(2):
             place = (step - blocks) * 2 + r
-            for piece in range(2):
-                y_ref, first = piece_of(y_refs, piece)
+            for piece in range(len(made)):
+                first = piece * strip * side
                 for group in range(strip // 4):
                     p, q, t, s = (
                         tiles_ref[piece, place, pl.ds((group * 4 + k) * pitch_rows, pair), :]
@@ -295,7 +296,7 @@
     return pl.BlockSpec(array.shape, lambda i: (0,) * array.ndim)
 
 
-def triangle_call(received, n_out, blocks, side, own, incoming):
+def triangle_call(received, made, blocks, side, own, incoming):
     pair = 2 * own
     pixels = side * side
     padded = blocks * LANES
@@ -303,31 +304,28 @@
     left_rows = blocks * side
     right_rows = left_rows if incoming else padded
     return pl.pallas_call(
-        functools.partial(triangle_kernel, blocks, side, own, incoming, len(received)),
+        functools.partial(triangle_kernel, blocks, side, own, incoming, made),
         grid=(2 * blocks,),
         in_specs=[
-            pl.BlockSpec((blocks * pair, a.shape[1]), lambda i: (jnp.minimum(i, blocks - 1), 0))
-            for a in received
+            pl.BlockSpec((blocks * pair, pixels), lambda i: (jnp.minimum(i, blocks - 1), 0))
         ],
-        out_specs=[
-            pl.BlockSpec((2 * pair, pixels // n_out), lambda i: (jnp.maximum(i - blocks, 0), 0))
-        ] * n_out,
-        out_shape=[
-            pltpu.HBM((blocks * blocks * own, pixels // n_out), jnp.bfloat16)
-        ] * n_out,
+        out_specs=pl.BlockSpec(
+            (2 * pair, pixels // 2 * len(made)), lambda i: (jnp.maximum(i - blocks, 0), 0)
+        ),
+        out_shape=pltpu.HBM((blocks * blocks * own, pixels // 2 * len(made)), jnp.bfloat16),
         scratch_shapes=[
             pltpu.VMEM((own, left_rows, padded), jnp.bfloat16),
             pltpu.VMEM((own, right_rows, padded), jnp.bfloat16),
             pltpu.VMEM((strip * (pair + 1), LANES), jnp.float32),
-            pltpu.VMEM((2, 2 * blocks, strip * (pair + 1), LANES), jnp.float32),
+            pltpu.VMEM((len(made), 2 * blocks, strip * (pair + 1), LANES), jnp.float32),
         ],
         compiler_params=pltpu.CompilerParams(vmem_limit_bytes=48 * 1024 * 1024),
         cost_estimate=pl.CostEstimate(
-            flops=2 * own * (blocks * side) ** 3,
+            flops=own * (blocks * side) ** 3 * len(made),
             bytes_accessed=12 * blocks * blocks * pair * pixels // 2,
             transcendentals=0,
         ),
-    )(*received)
+    )(received)
 
 
 def pixel_call(body, tiled, fixed, outs, steps, tile, flops, start=0, pixels=None, kept=(), scratch=(), row_major_out=False):
@@ -462,14 +460,15 @@
         return there.reshape(array.shape)
 
     gate = gate_of(zt, 0)
-    triangle = exchange(*triangle_call([exchange(sent)], 1, blocks, side, own, False))
+    triangle = exchange(triangle_call(exchange(sent), (0, 1), blocks, side, own, False))
     sent, zt = pixel_call(
         functools.partial(middle_kernel, peers),
         [(a, 0, steps) for a in (triangle, zt, gate, mask)], fixed, (2 * width, channels),
         steps, wide, pixels * mult * 5 * width,
     )
     gate = gate_of(zt, 1)
-    products = triangle_call([exchange(sent)], 2, blocks, side, own, True)
+    received = exchange(sent)
+    product = lambda piece: triangle_call(received, (piece,), blocks, side, own, True)
 
     def finish(piece, triangle):
         at = piece * steps // 2
@@ -479,13 +478,12 @@
             fixed, (channels,), steps // 2, wide, pixels // 2 * mult * channels, row_major_out=True,
         )[0]
 
-    arrived = [exchange(product) for product in products[::-1]]
-    there = finish(1, arrived[0])
+    there = finish(1, exchange(product(1)))
     beside, across = (
         lax.ppermute(there, LINE, pairs) for pairs in (((0, 1), (3, 2)), ((1, 2), (2, 1)))
     )
-    there, waiting = lax.optimization_barrier((there, arrived[1]))
-    here = finish(0, waiting)
+    there, waiting = lax.optimization_barrier((there, product(0)))
+    here = finish(0, exchange(waiting))
     back = lax.ppermute(here, LINE, ((1, 3), (2, 0)))
     return pl.pallas_call(
         assemble_kernel,

time: 368 us -> 347 us (0.943)
  blocking collectives: 149 us -> 128 us
  waiting for transfers between devices: 129 us -> 121 us
  Pallas kernels: 52.7 us -> 56.6 us
    all_to_all x3 -> x2, blocking collectives: 149 us -> 128 us  [exchange(): there = lax.all_to_all(array.reshape(peers, -1, array.shape[1]), CUBE, 0, 0)]
    ppermute x1, waiting for transfers between devices: 19.8 us -> 0.01 us  [by_kernels(): back = lax.ppermute(here, LINE, ((1, 3), (2, 0)))]
    all_to_all x2 -> x3, waiting for transfers between devices: 34.9 us -> 46.8 us  [exchange(): there = lax.all_to_all(array.reshape(peers, -1, array.shape[1]), CUBE, 0, 0)]
    all_to_all x2 -> x3, starting transfers between devices: 10.1 us -> 15 us  [exchange(): there = lax.all_to_all(array.reshape(peers, -1, array.shape[1]), CUBE, 0, 0)]
    pallas_call x2 -> x3, Pallas kernels: 15.8 us -> 19.6 us  [triangle_call(): pl.pallas_call(functools.partial(triangle_kernel, blocks, side, own, inco...]
  transfers between devices with their start and end apart: 11 -> 12, of which waited for: 8 -> 8; matrix products, arithmetic and copies ran while one was open for 0% -> 0% of each run, Pallas kernels for 4% -> 6%
where the time goes in v10:
time: 347 us; the launch traced here: 342 us
  blocking collectives  128 us (37%)
  waiting for transfers between devices  121 us (35%)
  Pallas kernels  56.6 us (16%)
  starting transfers between devices  30.5 us (9%)
  local copies, waits for them, and re-layouts  4.88 us (1%)
    all_to_all x2, blocking collectives, exchange(): there = lax.all_to_all(array.reshape(peers, -1, array.shape[1]), CUBE, 0, 0)  128 us
    all_to_all x3, waiting for transfers between devices, exchange(): there = lax.all_to_all(array.reshape(peers, -1, array.shape[1]), CUBE, 0, 0)  46.8 us
    pallas_call x7, Pallas kernels, pixel_call(): pl.pallas_call(kernel, grid=(steps,), in_specs=in_specs, out_specs=[spec(...  32.5 us
    ppermute x2, waiting for transfers between devices, by_kernels(): lax.ppermute(there, LINE, pairs)  30.7 us
    ppermute x2, waiting for transfers between devices, by_kernels(): z_far.append(lax.ppermute(over, LINE, ((0, 1), (3, 2))))  20.9 us
    pallas_call x3, Pallas kernels, triangle_call(): pl.pallas_call(functools.partial(triangle_kernel, blocks, side, own, inco...  19.6 us
    ppermute x2, waiting for transfers between devices, by_kernels(): over = lax.ppermute(part, LINE, ((1, 3), (2, 0)))  18.3 us
    all_to_all x3, starting transfers between devices, exchange(): there = lax.all_to_all(array.reshape(peers, -1, array.shape[1]), CUBE, 0, 0)  15 us
  transfers between devices with their start and end apart: 12, of which 8 were waited for; matrix products, arithmetic and copies ran while one was open for 0% of the time, Pallas kernels for 6%

profile of v10, /device:TPU:20, one launch (start us, length us, event | category | flops | bytes accessed | tf_op | source)
XLA Modules:
  0.0 342.4 jit_solution(14201139090375896325)
XLA Ops:
  9.7 14.6 %collective-permute-done.3 = bf16[2,1168,128]{2,1,0:T(8,128)(2,1)S(1)} collective-permute-done((bf16[2,1168,128]{2,1,0:T(8,128)(2,1)}, bf16[2,1168,128]{2,1,0:T(8,128)(2,1)S(1)}, u32[]{:S(2)}, u32[]{:S(2)}) %collective-permute-start.3) | collective-permute-done | bytes 598048 | tf_op jit(solution)/shard_map/ppermute | solution.py:427
  25.8 3.6 %collective-permute-done.1 = bf16[1,1168,128]{2,1,0:T(8,128)(2,1)} collective-permute-done((bf16[1,1168,128]{2,1,0:T(8,128)(2,1)}, bf16[1,1168,128]{2,1,0:T(8,128)(2,1)}, u32[]{:S(2)}, u32[]{:S(2)}) %collective-permute-start.1) | collective-permute-done | bytes 299040 | tf_op jit(solution)/shard_map/ppermute | solution.py:427
  31.0 4.8 %collective-permute-done.refs_1_.refs_0_ = bf16[4,1168,128]{2,1,0:T(8,128)(2,1)S(1)} collective-permute-done((bf16[4,1168,128]{2,1,0:T(8,128)(2,1)}, bf16[4,1168,128]{2,1,0:T(8,128)(2,1)S(1)}, u32[]{:S(2)}, u32[]{:S(2)}) %collective-permute-start) | collective-permute-done | bytes 1196064 | tf_op jit(solution)/shard_map/ppermute | solution.py:429
  37.0 4.1 %shard_map.92 = (bf16[256,9216]{1,0:T(8,128)(2,1)}, bf16[128,9216]{1,0:T(8,128)(2,1)}, bf16[16,9216]{1,0:T(8,128)(2,1)}) custom-call(bf16[4,1168,128]{2,1,0:T(8,128)(2,1)S(1)} %copy-done.6, bf16[4,1168,128]{2,1,0:T(8,128)(2,1)S(1)} %collective-permute-done.refs_1_.refs_0_, f32[128,8]{1,0:T(8,128)S(1)} %bitcast.23, ...), custom_call_target="tpu_custom_call" | custom-call | flops 603979776 | bytes 6045696 | tf_op jit(solution)/shard_map/pallas_call | solution.py:357
  41.1 20.9 %collective-permute-done.2.refs_1_ = bf16[1,1168,128]{2,1,0:T(8,128)(2,1)S(1)} collective-permute-done((bf16[1,1168,128]{2,1,0:T(8,128)(2,1)}, bf16[1,1168,128]{2,1,0:T(8,128)(2,1)S(1)}, u32[]{:S(2)}, u32[]{:S(2)}) %collective-permute-start.2) | collective-permute-done | bytes 299040 | tf_op jit(solution)/shard_map/ppermute | solution.py:428
  62.0 4.1 %shard_map.93 = (bf16[256,9216]{1,0:T(8,128)(2,1)}, bf16[128,9216]{1,0:T(8,128)(2,1)}, bf16[16,9216]{1,0:T(8,128)(2,1)}) custom-call(bf16[4,1168,128]{2,1,0:T(8,128)(2,1)S(1)} %collective-permute-done.refs_1_.refs_0_, bf16[1,1168,128]{2,1,0:T(8,128)(2,1)S(1)} %collective-permute-done.2.refs_1_, ...), custom_call_target="tpu_custom_call", output_to_operand_aliasing={{0}: (6, {}), {1}: (7, {}), {2}: (8, {})} | custom-call | flops 603979776 | bytes 6045696 | tf_op jit(solution)/shard_map/pallas_call | solution.py:357
  66.2 69.3 %all_to_all.25 = bf16[16,16,9216]{2,1,0:T(8,128)(2,1)S(1)} all-to-all(bf16[16,16,9216]{2,1,0:T(8,128)(2,1)} %bitcast.31), channel_id=1, replica_groups=mesh['groups'=2,'row'=4,'zh'=2,'zl'=2] {'groups','row','zl'}, dimensions={0} | all-to-all | bytes 9437184 | tf_op jit(solution)/shard_map/all_to_all | solution.py:459
  135.5 7.6 %shard_map.94 = bf16[128,9216]{1,0:T(8,128)(2,1)} custom-call(bf16[256,9216]{1,0:T(8,128)(2,1)S(1)} %bitcast.22), custom_call_target="tpu_custom_call" | custom-call | flops 905969664 | bytes 14155776 | tf_op jit(solution)/shard_map/pallas_call | solution.py:306
  143.1 4.9 %all-to-all-start.1 = ((bf16[16,8,9216]{2,1,0:T(8,128)(2,1)}), bf16[16,8,9216]{2,1,0:T(8,128)(2,1)}, u32[]{:S(2)}, u32[]{:S(2)}) async-start(bf16[16,8,9216]{2,1,0:T(8,128)(2,1)} %bitcast.32), calls=%async_computation.1 | async-start | bytes 4718592 | tf_op jit(solution)/shard_map/all_to_all | solution.py:459
  148.0 3.8 %shard_map.95.refs_2_ = bf16[128,9216]{1,0:T(8,128)(2,1)} custom-call(bf16[128,9216]{1,0:T(8,128)(2,1)S(1)} %copy-done.3, f32[128,8]{1,0:T(8,128)S(1)} %bitcast.25, bf16[2,768,128]{2,1,0:T(8,128)(2,1)S(1)} %maximum_bitcast_fusion.refs_3_.refs_5_.refs_2_.refs_4_), custom_call_target="tpu_custom_call" | custom-call | flops 301989888 | bytes 7077888 | tf_op jit(solution)/shard_map/pallas_call | solution.py:357
  151.9 26.5 %all-to-all-done.1 = bf16[16,8,9216]{2,1,0:T(8,128)(2,1)} async-done(((bf16[16,8,9216]{2,1,0:T(8,128)(2,1)}), bf16[16,8,9216]{2,1,0:T(8,128)(2,1)}, u32[]{:S(2)}, u32[]{:S(2)}) %all-to-all-start.1) | async-done | bytes 2359328 | tf_op jit(solution)/shard_map/all_to_all | solution.py:459
  178.4 9.3 %shard_map.96 = (bf16[256,9216]{1,0:T(8,128)(2,1)}, bf16[128,9216]{1,0:T(8,128)(2,1)}) custom-call(bf16[128,9216]{1,0:T(8,128)(2,1)} %bitcast.11.refs_0_, bf16[128,9216]{1,0:T(8,128)(2,1)S(1)} %copy-done.3, bf16[128,9216]{1,0:T(8,128)(2,1)} %shard_map.95.refs_2_, bf16[16,9216]{1,0:T(8,128)(2,1)S(1)} %copy-done.7, f32[128,8]{1,0:T(8,128)S(1)} %bitcast.26, ...), custom_call_target="tpu_custom_call" | custom-call | flops 1509949440 | bytes 11796480 | tf_op jit(solution)/shard_map/pallas_call | solution.py:357
  187.6 58.4 %all_to_all.26 = bf16[16,16,9216]{2,1,0:T(8,128)(2,1)S(1)} all-to-all(bf16[16,16,9216]{2,1,0:T(8,128)(2,1)} %bitcast.33), channel_id=1, replica_groups=mesh['groups'=2,'row'=4,'zh'=2,'zl'=2] {'groups','row','zl'}, dimensions={0} | all-to-all | bytes 9437184 | tf_op jit(solution)/shard_map/all_to_all | solution.py:459
  246.0 6.0 %shard_map.97 = bf16[128,4608]{1,0:T(8,128)(2,1)} custom-call(bf16[256,9216]{1,0:T(8,128)(2,1)S(1)} %bitcast.20), custom_call_target="tpu_custom_call" | custom-call | flops 452984832 | bytes 14155776 | tf_op jit(solution)/shard_map/pallas_call | solution.py:306
  252.0 4.9 %all-to-all-start.3 = ((bf16[16,8,4608]{2,1,0:T(8,128)(2,1)}), bf16[16,8,4608]{2,1,0:T(8,128)(2,1)}, u32[]{:S(2)}, u32[]{:S(2)}) async-start(bf16[16,8,4608]{2,1,0:T(8,128)(2,1)} %bitcast.35), calls=%async_computation.3 | async-start | bytes 2359296 | tf_op jit(solution)/shard_map/all_to_all | solution.py:459
  256.9 3.8 %shard_map.98.refs_2_ = bf16[128,9216]{1,0:T(8,128)(2,1)} custom-call(bf16[128,9216]{1,0:T(8,128)(2,1)S(1)} %copy-done.2, f32[128,8]{1,0:T(8,128)S(1)} %bitcast.27, bf16[2,768,128]{2,1,0:T(8,128)(2,1)S(1)} %maximum_bitcast_fusion.refs_3_.refs_5_.refs_2_.refs_4_), custom_call_target="tpu_custom_call" | custom-call | flops 301989888 | bytes 7077888 | tf_op jit(solution)/shard_map/pallas_call | solution.py:357
  260.7 6.0 %shard_map.100 = bf16[128,4608]{1,0:T(8,128)(2,1)} custom-call(bf16[256,9216]{1,0:T(8,128)(2,1)S(1)} %bitcast.21), custom_call_target="tpu_custom_call" | custom-call | flops 452984832 | bytes 14155776 | tf_op jit(solution)/shard_map/pallas_call | solution.py:306
  266.7 6.0 %all-to-all-done.3 = bf16[16,8,4608]{2,1,0:T(8,128)(2,1)} async-done(((bf16[16,8,4608]{2,1,0:T(8,128)(2,1)}), bf16[16,8,4608]{2,1,0:T(8,128)(2,1)}, u32[]{:S(2)}, u32[]{:S(2)}) %all-to-all-start.3) | async-done | bytes 1179680 | tf_op jit(solution)/shard_map/all_to_all | solution.py:459
  272.7 3.7 %shard_map.99 = bf16[4608,128]{1,0:T(8,128)(2,1)} custom-call(bf16[128,4608]{1,0:T(8,128)(2,1)} %bitcast.15.refs_0_, bf16[128,9216]{1,0:T(8,128)(2,1)S(1)} %copy-done.2, bf16[128,9216]{1,0:T(8,128)(2,1)} %shard_map.98.refs_2_, f32[128,8]{1,0:T(8,128)S(1)} %bitcast.28, bf16[2,768,128]{2,1,0:T(8,128)(2,1)S(1)} %maximum_bitcast_fusion.refs_3_.refs_5_.refs_2_.refs_4_), custom_call_target="tpu_custom_call" | custom-call | flops 150994944 | bytes 3538944 | tf_op jit(solution)/shard_map/pallas_call | solution.py:357
  276.3 5.3 %all-to-all-start.4 = ((bf16[16,8,4608]{2,1,0:T(8,128)(2,1)}), bf16[16,8,4608]{2,1,0:T(8,128)(2,1)}, u32[]{:S(2)}, u32[]{:S(2)}) async-start(bf16[16,8,4608]{2,1,0:T(8,128)(2,1)} %bitcast.34), calls=%async_computation.4 | async-start | bytes 2359296 | tf_op jit(solution)/shard_map/all_to_all | solution.py:459
  283.3 5.8 %collective-permute-start.6 = (bf16[4608,128]{1,0:T(8,128)(2,1)}, bf16[4608,128]{1,0:T(8,128)(2,1)}, u32[]{:S(2)}, u32[]{:S(2)}) collective-permute-start(bf16[4608,128]{1,0:T(8,128)(2,1)} %shard_map.99), channel_id=1, source_target_pairs={{0,2},{18,16},{1,3},{19,17},{4,6},{22,20},{5,7},{23,21},{8,10},{26... | collective-permute-start | bytes 3538952 | tf_op jit(solution)/shard_map/ppermute | solution.py:483
  289.0 14.3 %all-to-all-done.4 = bf16[16,8,4608]{2,1,0:T(8,128)(2,1)} async-done(((bf16[16,8,4608]{2,1,0:T(8,128)(2,1)}), bf16[16,8,4608]{2,1,0:T(8,128)(2,1)}, u32[]{:S(2)}, u32[]{:S(2)}) %all-to-all-start.4) | async-done | bytes 1179680 | tf_op jit(solution)/shard_map/all_to_all | solution.py:459
  303.3 3.7 %shard_map.101.here_ref = bf16[4608,128]{1,0:T(8,128)(2,1)} custom-call(bf16[128,4608]{1,0:T(8,128)(2,1)} %bitcast.17.refs_0_, bf16[128,9216]{1,0:T(8,128)(2,1)S(1)} %copy-done.2, bf16[128,9216]{1,0:T(8,128)(2,1)} %shard_map.98.refs_2_, f32[128,8]{1,0:T(8,128)S(1)} %bitcast.29, bf16[2,768,128]{2,1,0:T(8,128)(2,1)S(1)} %maximum_bitcast_fusion.refs_3_.refs_5_.refs_2_.refs_4_), custom_call_target="tpu_custom_call" | custom-call | flops 150994944 | bytes 3538944 | tf_op jit(solution)/shard_map/pallas_call | solution.py:357
  308.3 30.7 %collective-permute-done.6.beside_ref = bf16[4608,128]{1,0:T(8,128)(2,1)} collective-permute-done((bf16[4608,128]{1,0:T(8,128)(2,1)}, bf16[4608,128]{1,0:T(8,128)(2,1)}, u32[]{:S(2)}, u32[]{:S(2)}) %collective-permute-start.6) | collective-permute-done | bytes 1179680 | tf_op jit(solution)/shard_map/ppermute | solution.py:483
  (56 shorter events, 20.0 us)
Async XLA Ops:
  0.0 9.1 %copy-start.11 = (f32[2,128]{1,0:T(2,128)S(1)}, f32[2,128]{1,0:T(2,128)}, u32[]{:S(2)}) copy-start(f32[2,128]{1,0:T(2,128)} %param.16) | copy-start | bytes 3076
  0.0 9.1 %copy-start.12 = (f32[2,128]{1,0:T(2,128)S(1)}, f32[2,128]{1,0:T(2,128)}, u32[]{:S(2)}) copy-start(f32[2,128]{1,0:T(2,128)} %param.15) | copy-start | bytes 3076
  0.0 9.1 %copy-start.13 = (f32[2,128]{1,0:T(2,128)S(1)}, f32[2,128]{1,0:T(2,128)}, u32[]{:S(2)}) copy-start(f32[2,128]{1,0:T(2,128)} %param.12) | copy-start | bytes 3076
  0.0 9.1 %copy-start.14 = (f32[2,128]{1,0:T(2,128)S(1)}, f32[2,128]{1,0:T(2,128)}, u32[]{:S(2)}) copy-start(f32[2,128]{1,0:T(2,128)} %param.11) | copy-start | bytes 3076
  0.0 9.3 %copy-start.9 = (bf16[2,128,128]{2,1,0:T(8,128)(2,1)S(1)}, bf16[2,128,128]{2,1,0:T(8,128)(2,1)}, u32[]{:S(2)}) copy-start(bf16[2,128,128]{2,1,0:T(8,128)(2,1)} %param.14) | copy-start | bytes 196612
  0.0 9.4 %copy-start.10 = (bf16[2,128,128]{2,1,0:T(8,128)(2,1)S(1)}, bf16[2,128,128]{2,1,0:T(8,128)(2,1)}, u32[]{:S(2)}) copy-start(bf16[2,128,128]{2,1,0:T(8,128)(2,1)} %param.17) | copy-start | bytes 196612
  2.7 6.8 %copy-start.8 = (bf16[2,128,512]{2,1,0:T(8,128)(2,1)S(1)}, bf16[2,128,512]{2,1,0:T(8,128)(2,1)}, u32[]{:S(2)}) copy-start(bf16[2,128,512]{2,1,0:T(8,128)(2,1)} %param.13) | copy-start | bytes 786436
  5.3 30.5 %collective-permute-start = (bf16[4,1168,128]{2,1,0:T(8,128)(2,1)}, bf16[4,1168,128]{2,1,0:T(8,128)(2,1)S(1)}, u32[]{:S(2)}, u32[]{:S(2)}) collective-permute-start(bf16[4,1168,128]{2,1,0:T(8,128)(2,1)} %get-tuple-element.19), channel_id=1, source_target_pairs={{2,0},{16,18},{0,16},{18,2},{3,1},{17,19},{1,17},{19,3},{6,4},{20,... | collective-permute-start | bytes 3588104 | tf_op jit(solution)/shard_map/ppermute | solution.py:429
  5.8 18.5 %collective-permute-start.3 = (bf16[2,1168,128]{2,1,0:T(8,128)(2,1)}, bf16[2,1168,128]{2,1,0:T(8,128)(2,1)S(1)}, u32[]{:S(2)}, u32[]{:S(2)}) collective-permute-start(bf16[2,1168,128]{2,1,0:T(8,128)(2,1)} %get-tuple-element.21), channel_id=1, source_target_pairs={{2,18},{16,0},{3,19},{17,1},{6,22},{20,4},{7,23},{21,5},{10,26},{2... | collective-permute-start | bytes 1794056 | tf_op jit(solution)/shard_map/ppermute | solution.py:427
  7.1 22.3 %collective-permute-start.1 = (bf16[1,1168,128]{2,1,0:T(8,128)(2,1)}, bf16[1,1168,128]{2,1,0:T(8,128)(2,1)}, u32[]{:S(2)}, u32[]{:S(2)}) collective-permute-start(bf16[1,1168,128]{2,1,0:T(8,128)(2,1)} %get-tuple-element.20), channel_id=1, source_target_pairs={{2,18},{16,0},{3,19},{17,1},{6,22},{20,4},{7,23},{21,5},{10,26},{2... | collective-permute-start | bytes 897032 | tf_op jit(solution)/shard_map/ppermute | solution.py:427
  8.4 32.7 %collective-permute-start.5 = (bf16[1,1168,128]{2,1,0:T(8,128)(2,1)}, bf16[1,1168,128]{2,1,0:T(8,128)(2,1)S(1)}, u32[]{:S(2)}, u32[]{:S(2)}) collective-permute-start(bf16[1,1168,128]{2,1,0:T(8,128)(2,1)} %get-tuple-element.22), channel_id=1, source_target_pairs={{2,16},{16,2},{3,17},{17,3},{6,20},{20,6},{7,21},{21,7},{10,24},{2... | collective-permute-start | bytes 897032 | tf_op jit(solution)/shard_map/ppermute | solution.py:430
  24.3 37.7 %collective-permute-start.4 = (bf16[2,1168,128]{2,1,0:T(8,128)(2,1)S(1)}, bf16[2,1168,128]{2,1,0:T(8,128)(2,1)S(1)}, u32[]{:S(2)}, u32[]{:S(2)}) collective-permute-start(bf16[2,1168,128]{2,1,0:T(8,128)(2,1)S(1)} %collective-permute-done.3), channel_id=1, source_target_pairs={{0,2},{18,16},{1,3},{19,17},{4,6},{22,20},{5,7},{23,21},{8,10},{26... | collective-permute-start | bytes 1794056 | tf_op jit(solution)/shard_map/ppermute | solution.py:428
  29.4 32.6 %collective-permute-start.2 = (bf16[1,1168,128]{2,1,0:T(8,128)(2,1)}, bf16[1,1168,128]{2,1,0:T(8,128)(2,1)S(1)}, u32[]{:S(2)}, u32[]{:S(2)}) collective-permute-start(bf16[1,1168,128]{2,1,0:T(8,128)(2,1)} %collective-permute-done.1), channel_id=1, source_target_pairs={{0,2},{18,16},{1,3},{19,17},{4,6},{22,20},{5,7},{23,21},{8,10},{26... | collective-permute-start | bytes 897032 | tf_op jit(solution)/shard_map/ppermute | solution.py:428
  143.1 4.9 %copy-start.3 = (bf16[128,9216]{1,0:T(8,128)(2,1)S(1)}, bf16[128,9216]{1,0:T(8,128)(2,1)}, u32[]{:S(2)}) copy-start(bf16[128,9216]{1,0:T(8,128)(2,1)} %get-tuple-element.28.refs_0_.refs_1_) | copy-start | bytes 7077892
  143.1 35.3 %all-to-all-start.1 = ((bf16[16,8,9216]{2,1,0:T(8,128)(2,1)}), bf16[16,8,9216]{2,1,0:T(8,128)(2,1)}, u32[]{:S(2)}, u32[]{:S(2)}) async-start(bf16[16,8,9216]{2,1,0:T(8,128)(2,1)} %bitcast.32), calls=%async_computation.1 | async-start | bytes 4718592 | tf_op jit(solution)/shard_map/all_to_all | solution.py:459
  148.0 30.3 %copy-start.7 = (bf16[16,9216]{1,0:T(8,128)(2,1)S(1)}, bf16[16,9216]{1,0:T(8,128)(2,1)}, u32[]{:S(2)}) copy-start(bf16[16,9216]{1,0:T(8,128)(2,1)} %get-tuple-element.29.refs_3_) | copy-start | bytes 884740
  246.0 6.0 %copy-start = (bf16[16,16,9216]{2,1,0:T(8,128)(2,1)}, bf16[16,16,9216]{2,1,0:T(8,128)(2,1)S(1)}, u32[]{:S(2)}) copy-start(bf16[16,16,9216]{2,1,0:T(8,128)(2,1)S(1)} %all_to_all.26) | copy-start | bytes 14155780
  252.0 4.9 %copy-start.2 = (bf16[128,9216]{1,0:T(8,128)(2,1)S(1)}, bf16[128,9216]{1,0:T(8,128)(2,1)}, u32[]{:S(2)}) copy-start(bf16[128,9216]{1,0:T(8,128)(2,1)} %get-tuple-element.31.refs_0_.refs_1_) | copy-start | bytes 7077892
  252.0 20.6 %all-to-all-start.3 = ((bf16[16,8,4608]{2,1,0:T(8,128)(2,1)}), bf16[16,8,4608]{2,1,0:T(8,128)(2,1)}, u32[]{:S(2)}, u32[]{:S(2)}) async-start(bf16[16,8,4608]{2,1,0:T(8,128)(2,1)} %bitcast.35), calls=%async_computation.3 | async-start | bytes 2359296 | tf_op jit(solution)/shard_map/all_to_all | solution.py:459
  256.9 3.8 %copy-start.1 = (bf16[16,16,9216]{2,1,0:T(8,128)(2,1)S(1)}, bf16[16,16,9216]{2,1,0:T(8,128)(2,1)}, u32[]{:S(2)}) copy-start(bf16[16,16,9216]{2,1,0:T(8,128)(2,1)} %copy-done) | copy-start | bytes 14155780
  276.3 27.0 %all-to-all-start.4 = ((bf16[16,8,4608]{2,1,0:T(8,128)(2,1)}), bf16[16,8,4608]{2,1,0:T(8,128)(2,1)}, u32[]{:S(2)}, u32[]{:S(2)}) async-start(bf16[16,8,4608]{2,1,0:T(8,128)(2,1)} %bitcast.34), calls=%async_computation.4 | async-start | bytes 2359296 | tf_op jit(solution)/shard_map/all_to_all | solution.py:459
  281.6 26.7 %collective-permute-start.8 = (bf16[4608,128]{1,0:T(8,128)(2,1)}, bf16[4608,128]{1,0:T(8,128)(2,1)}, u32[]{:S(2)}, u32[]{:S(2)}) collective-permute-start(bf16[4608,128]{1,0:T(8,128)(2,1)} %shard_map.99), channel_id=1, source_target_pairs={{2,16},{16,2},{3,17},{17,3},{6,20},{20,6},{7,21},{21,7},{10,24},{2... | collective-permute-start | bytes 3538952 | tf_op jit(solution)/shard_map/ppermute | solution.py:483
  283.3 55.7 %collective-permute-start.6 = (bf16[4608,128]{1,0:T(8,128)(2,1)}, bf16[4608,128]{1,0:T(8,128)(2,1)}, u32[]{:S(2)}, u32[]{:S(2)}) collective-permute-start(bf16[4608,128]{1,0:T(8,128)(2,1)} %shard_map.99), channel_id=1, source_target_pairs={{0,2},{18,16},{1,3},{19,17},{4,6},{22,20},{5,7},{23,21},{8,10},{26... | collective-permute-start | bytes 3538952 | tf_op jit(solution)/shard_map/ppermute | solution.py:483
  307.0 32.0 %collective-permute-start.7 = (bf16[4608,128]{1,0:T(8,128)(2,1)}, bf16[4608,128]{1,0:T(8,128)(2,1)S(1)}, u32[]{:S(2)}, u32[]{:S(2)}) collective-permute-start(bf16[4608,128]{1,0:T(8,128)(2,1)} %shard_map.101.here_ref), channel_id=1, source_target_pairs={{2,18},{16,0},{3,19},{17,1},{6,22},{20,4},{7,23},{21,5},{10,26},{2... | collective-permute-start | bytes 3538952 | tf_op jit(solution)/shard_map/ppermute | solution.py:487
  (3 other events, 4.2 us)

commit v11 on v10

--- a/solution.py
+++ b/solution.py
@@ -292,6 +292,10 @@
     )
 
 
+def in_hbm(array):
+    return pltpu.with_memory_space_constraint(array, pltpu.HBM)
+
+
 def whole_spec(array):
     return pl.BlockSpec(array.shape, lambda i: (0,) * array.ndim)
 
@@ -393,7 +397,7 @@
             pltpu.SemaphoreType.DMA((len(outs),)),
         ],
         compiler_params=pltpu.CompilerParams(vmem_limit_bytes=48 * 1024 * 1024),
-    )(pair_act, mask)
+    )(in_hbm(pair_act), mask)
 
 
 def by_kernels(
@@ -444,6 +448,7 @@
             start=piece * per_piece, pixels=pixels, kept=kept,
         )
 
+    z_near = in_hbm(z_near)
     begun = first(0, z_own, [z_near], [(0, per_piece)], ())
     sent, zt, mask = first(1, z_near, z_far, list(zip((0, *cuts), cuts)), begun)
     wide = 2 * tile
@@ -496,7 +501,7 @@
             pltpu.SemaphoreType.DMA((2, 2)),
         ],
         compiler_params=pltpu.CompilerParams(vmem_limit_bytes=48 * 1024 * 1024),
-    )(here, beside, back, across).reshape(side, side, channels)
+    )(*map(in_hbm, (here, beside, back, across))).reshape(side, side, channels)
 
 
 def layer_norm(values, gain, bias, axis):

time: 347 us -> 359 us (1.035); the launches traced: 342 us -> 358 us
  waiting for transfers between devices: 121 us -> 137 us
  Pallas kernels: 56.6 us -> 60.5 us
    ppermute x2, waiting for transfers between devices: 30.7 us -> 13.6 us  [by_kernels(): lax.ppermute(there, LINE, pairs)]
    all_to_all x3, waiting for transfers between devices: 46.8 us -> 63.8 us  [exchange(): there = lax.all_to_all(array.reshape(peers, -1, array.shape[1]), CUBE, 0, 0)]
    ppermute x1, waiting for transfers between devices: 0.01 us -> 15 us  [by_kernels(): back = lax.ppermute(here, LINE, ((1, 3), (2, 0)))]
  transfers between devices with their start and end apart: 12 -> 12, of which waited for: 8 -> 9; matrix products, arithmetic and copies ran while one was open for 0% -> 0% of each run, Pallas kernels for 6% -> 6%
where the time goes in v11:
time: 359 us; the launch traced here: 358 us
  waiting for transfers between devices  137 us (38%)
  blocking collectives  128 us (36%)
  Pallas kernels  60.5 us (17%)
  starting transfers between devices  30.4 us (8%)
    all_to_all x2, blocking collectives, exchange(): there = lax.all_to_all(array.reshape(peers, -1, array.shape[1]), CUBE, 0, 0)  128 us
    all_to_all x3, waiting for transfers between devices, exchange(): there = lax.all_to_all(array.reshape(peers, -1, array.shape[1]), CUBE, 0, 0)  63.8 us
    pallas_call x7, Pallas kernels, pixel_call(): pl.pallas_call(kernel, grid=(steps,), in_specs=in_specs, out_specs=[spec(...  35.1 us
    ppermute x2, waiting for transfers between devices, by_kernels(): z_far.append(lax.ppermute(over, LINE, ((0, 1), (3, 2))))  20.9 us
    pallas_call x3, Pallas kernels, triangle_call(): pl.pallas_call(functools.partial(triangle_kernel, blocks, side, own, inco...  19.6 us
    ppermute x2, waiting for transfers between devices, by_kernels(): over = lax.ppermute(part, LINE, ((1, 3), (2, 0)))  18.4 us
    all_to_all x3, starting transfers between devices, exchange(): there = lax.all_to_all(array.reshape(peers, -1, array.shape[1]), CUBE, 0, 0)  15 us
    ppermute x1, waiting for transfers between devices, by_kernels(): back = lax.ppermute(here, LINE, ((1, 3), (2, 0)))  15 us
  transfers between devices with their start and end apart: 12, of which 9 were waited for; matrix products, arithmetic and copies ran while one was open for 0% of the time, Pallas kernels for 6%

profile of v11, /device:TPU:20, one launch (start us, length us, event | category | flops | bytes accessed | tf_op | source)
XLA Modules:
  0.0 358.0 jit_solution(9238083241693492590)
XLA Ops:
  8.8 14.6 %collective-permute-done.3 = bf16[2,1168,128]{2,1,0:T(8,128)(2,1)S(1)} collective-permute-done((bf16[2,1168,128]{2,1,0:T(8,128)(2,1)}, bf16[2,1168,128]{2,1,0:T(8,128)(2,1)S(1)}, u32[]{:S(2)}, u32[]{:S(2)}) %collective-permute-start.3) | collective-permute-done | bytes 598048 | tf_op jit(solution)/shard_map/ppermute | solution.py:431
  24.8 3.8 %collective-permute-done.1 = bf16[1,1168,128]{2,1,0:T(8,128)(2,1)} collective-permute-done((bf16[1,1168,128]{2,1,0:T(8,128)(2,1)}, bf16[1,1168,128]{2,1,0:T(8,128)(2,1)}, u32[]{:S(2)}, u32[]{:S(2)}) %collective-permute-start.1) | collective-permute-done | bytes 299040 | tf_op jit(solution)/shard_map/ppermute | solution.py:431
  30.0 4.9 %collective-permute-done.refs_1_.refs_0_ = bf16[4,1168,128]{2,1,0:T(8,128)(2,1)} collective-permute-done((bf16[4,1168,128]{2,1,0:T(8,128)(2,1)}, bf16[4,1168,128]{2,1,0:T(8,128)(2,1)}, u32[]{:S(2)}, u32[]{:S(2)}) %collective-permute-start) | collective-permute-done | bytes 1196064 | tf_op jit(solution)/shard_map/ppermute | solution.py:433
  34.9 5.4 %shard_map.92 = (bf16[256,9216]{1,0:T(8,128)(2,1)}, bf16[128,9216]{1,0:T(8,128)(2,1)}, bf16[16,9216]{1,0:T(8,128)(2,1)}) custom-call(bf16[4,1168,128]{2,1,0:T(8,128)(2,1)S(1)} %copy-done.4, bf16[4,1168,128]{2,1,0:T(8,128)(2,1)} %collective-permute-done.refs_1_.refs_0_, f32[128,8]{1,0:T(8,128)S(1)} %bitcast.23, ...), custom_call_target="tpu_custom_call" | custom-call | flops 603979776 | bytes 6045696 | tf_op jit(solution)/shard_map/pallas_call | solution.py:361
  40.3 20.8 %collective-permute-done.2.refs_1_ = bf16[1,1168,128]{2,1,0:T(8,128)(2,1)S(1)} collective-permute-done((bf16[1,1168,128]{2,1,0:T(8,128)(2,1)}, bf16[1,1168,128]{2,1,0:T(8,128)(2,1)S(1)}, u32[]{:S(2)}, u32[]{:S(2)}) %collective-permute-start.2) | collective-permute-done | bytes 299040 | tf_op jit(solution)/shard_map/ppermute | solution.py:432
  61.2 5.4 %shard_map.93 = (bf16[256,9216]{1,0:T(8,128)(2,1)}, bf16[128,9216]{1,0:T(8,128)(2,1)}, bf16[16,9216]{1,0:T(8,128)(2,1)}) custom-call(bf16[4,1168,128]{2,1,0:T(8,128)(2,1)} %collective-permute-done.refs_1_.refs_0_, bf16[1,1168,128]{2,1,0:T(8,128)(2,1)S(1)} %collective-permute-done.2.refs_1_, ...), custom_call_target="tpu_custom_call", output_to_operand_aliasing={{0}: (6, {}), {1}: (7, {}), {2}: (8, {})} | custom-call | flops 603979776 | bytes 6045696 | tf_op jit(solution)/shard_map/pallas_call | solution.py:361
  66.6 69.2 %all_to_all.25 = bf16[16,16,9216]{2,1,0:T(8,128)(2,1)S(1)} all-to-all(bf16[16,16,9216]{2,1,0:T(8,128)(2,1)} %bitcast.30), channel_id=1, replica_groups=mesh['groups'=2,'row'=4,'zh'=2,'zl'=2] {'groups','row','zl'}, dimensions={0} | all-to-all | bytes 9437184 | tf_op jit(solution)/shard_map/all_to_all | solution.py:464
  135.8 7.6 %shard_map.94 = bf16[128,9216]{1,0:T(8,128)(2,1)} custom-call(bf16[256,9216]{1,0:T(8,128)(2,1)S(1)} %bitcast.22), custom_call_target="tpu_custom_call" | custom-call | flops 905969664 | bytes 14155776 | tf_op jit(solution)/shard_map/pallas_call | solution.py:310
  143.4 4.9 %all-to-all-start.1 = ((bf16[16,8,9216]{2,1,0:T(8,128)(2,1)}), bf16[16,8,9216]{2,1,0:T(8,128)(2,1)}, u32[]{:S(2)}, u32[]{:S(2)}) async-start(bf16[16,8,9216]{2,1,0:T(8,128)(2,1)} %bitcast.31), calls=%async_computation.1 | async-start | bytes 4718592 | tf_op jit(solution)/shard_map/all_to_all | solution.py:464
  148.4 3.8 %shard_map.95.refs_2_ = bf16[128,9216]{1,0:T(8,128)(2,1)} custom-call(bf16[128,9216]{1,0:T(8,128)(2,1)S(1)} %copy-done.3, f32[128,8]{1,0:T(8,128)S(1)} %bitcast.25, bf16[2,768,128]{2,1,0:T(8,128)(2,1)S(1)} %maximum_bitcast_fusion.refs_3_.refs_5_.refs_2_.refs_4_), custom_call_target="tpu_custom_call" | custom-call | flops 301989888 | bytes 7077888 | tf_op jit(solution)/shard_map/pallas_call | solution.py:361
  152.2 26.5 %all-to-all-done.1 = bf16[16,8,9216]{2,1,0:T(8,128)(2,1)} async-done(((bf16[16,8,9216]{2,1,0:T(8,128)(2,1)}), bf16[16,8,9216]{2,1,0:T(8,128)(2,1)}, u32[]{:S(2)}, u32[]{:S(2)}) %all-to-all-start.1) | async-done | bytes 2359328 | tf_op jit(solution)/shard_map/all_to_all | solution.py:464
  178.7 9.3 %shard_map.96 = (bf16[256,9216]{1,0:T(8,128)(2,1)}, bf16[128,9216]{1,0:T(8,128)(2,1)}) custom-call(bf16[128,9216]{1,0:T(8,128)(2,1)} %bitcast.11.refs_0_, bf16[128,9216]{1,0:T(8,128)(2,1)S(1)} %copy-done.3, bf16[128,9216]{1,0:T(8,128)(2,1)} %shard_map.95.refs_2_, bf16[16,9216]{1,0:T(8,128)(2,1)S(1)} %copy-done.5, f32[128,8]{1,0:T(8,128)S(1)} %bitcast.26, ...), custom_call_target="tpu_custom_call" | custom-call | flops 1509949440 | bytes 11796480 | tf_op jit(solution)/shard_map/pallas_call | solution.py:361
  188.0 58.4 %all_to_all.26 = bf16[16,16,9216]{2,1,0:T(8,128)(2,1)S(1)} all-to-all(bf16[16,16,9216]{2,1,0:T(8,128)(2,1)} %bitcast.32), channel_id=1, replica_groups=mesh['groups'=2,'row'=4,'zh'=2,'zl'=2] {'groups','row','zl'}, dimensions={0} | all-to-all | bytes 9437184 | tf_op jit(solution)/shard_map/all_to_all | solution.py:464
  246.4 6.0 %shard_map.97 = bf16[128,4608]{1,0:T(8,128)(2,1)} custom-call(bf16[256,9216]{1,0:T(8,128)(2,1)S(1)} %bitcast.20), custom_call_target="tpu_custom_call" | custom-call | flops 452984832 | bytes 14155776 | tf_op jit(solution)/shard_map/pallas_call | solution.py:310
  252.4 4.9 %all-to-all-start.3 = ((bf16[16,8,4608]{2,1,0:T(8,128)(2,1)}), bf16[16,8,4608]{2,1,0:T(8,128)(2,1)}, u32[]{:S(2)}, u32[]{:S(2)}) async-start(bf16[16,8,4608]{2,1,0:T(8,128)(2,1)} %bitcast.34), calls=%async_computation.3 | async-start | bytes 2359296 | tf_op jit(solution)/shard_map/all_to_all | solution.py:464
  257.2 3.8 %shard_map.98.refs_2_ = bf16[128,9216]{1,0:T(8,128)(2,1)} custom-call(bf16[128,9216]{1,0:T(8,128)(2,1)S(1)} %copy-done.2, f32[128,8]{1,0:T(8,128)S(1)} %bitcast.27, bf16[2,768,128]{2,1,0:T(8,128)(2,1)S(1)} %maximum_bitcast_fusion.refs_3_.refs_5_.refs_2_.refs_4_), custom_call_target="tpu_custom_call" | custom-call | flops 301989888 | bytes 7077888 | tf_op jit(solution)/shard_map/pallas_call | solution.py:361
  261.0 6.0 %shard_map.100 = bf16[128,4608]{1,0:T(8,128)(2,1)} custom-call(bf16[256,9216]{1,0:T(8,128)(2,1)S(1)} %bitcast.21), custom_call_target="tpu_custom_call" | custom-call | flops 452984832 | bytes 14155776 | tf_op jit(solution)/shard_map/pallas_call | solution.py:310
  267.0 6.0 %all-to-all-done.3 = bf16[16,8,4608]{2,1,0:T(8,128)(2,1)} async-done(((bf16[16,8,4608]{2,1,0:T(8,128)(2,1)}), bf16[16,8,4608]{2,1,0:T(8,128)(2,1)}, u32[]{:S(2)}, u32[]{:S(2)}) %all-to-all-start.3) | async-done | bytes 1179680 | tf_op jit(solution)/shard_map/all_to_all | solution.py:464
  276.7 5.3 %all-to-all-start.4 = ((bf16[16,8,4608]{2,1,0:T(8,128)(2,1)}), bf16[16,8,4608]{2,1,0:T(8,128)(2,1)}, u32[]{:S(2)}, u32[]{:S(2)}) async-start(bf16[16,8,4608]{2,1,0:T(8,128)(2,1)} %bitcast.33), calls=%async_computation.4 | async-start | bytes 2359296 | tf_op jit(solution)/shard_map/all_to_all | solution.py:464
  283.6 5.8 %collective-permute-start.6 = (bf16[4608,128]{1,0:T(8,128)(2,1)}, bf16[4608,128]{1,0:T(8,128)(2,1)}, u32[]{:S(2)}, u32[]{:S(2)}) collective-permute-start(bf16[4608,128]{1,0:T(8,128)(2,1)} %shard_map.99), channel_id=1, source_target_pairs={{0,2},{18,16},{1,3},{19,17},{4,6},{22,20},{5,7},{23,21},{8,10},{26... | collective-permute-start | bytes 3538952 | tf_op jit(solution)/shard_map/ppermute | solution.py:488
  289.4 31.4 %all-to-all-done.4 = bf16[16,8,4608]{2,1,0:T(8,128)(2,1)} async-done(((bf16[16,8,4608]{2,1,0:T(8,128)(2,1)}), bf16[16,8,4608]{2,1,0:T(8,128)(2,1)}, u32[]{:S(2)}, u32[]{:S(2)}) %all-to-all-start.4) | async-done | bytes 1179680 | tf_op jit(solution)/shard_map/all_to_all | solution.py:464
  320.7 3.7 %shard_map.101.here_ref = bf16[4608,128]{1,0:T(8,128)(2,1)} custom-call(bf16[128,4608]{1,0:T(8,128)(2,1)} %bitcast.17.refs_0_, bf16[128,9216]{1,0:T(8,128)(2,1)S(1)} %copy-done.2, bf16[128,9216]{1,0:T(8,128)(2,1)} %shard_map.98.refs_2_, f32[128,8]{1,0:T(8,128)S(1)} %bitcast.29, bf16[2,768,128]{2,1,0:T(8,128)(2,1)S(1)} %maximum_bitcast_fusion.refs_3_.refs_5_.refs_2_.refs_4_), custom_call_target="tpu_custom_call" | custom-call | flops 150994944 | bytes 3538944 | tf_op jit(solution)/shard_map/pallas_call | solution.py:361
  325.7 13.6 %collective-permute-done.6.beside_ref = bf16[4608,128]{1,0:T(8,128)(2,1)} collective-permute-done((bf16[4608,128]{1,0:T(8,128)(2,1)}, bf16[4608,128]{1,0:T(8,128)(2,1)}, u32[]{:S(2)}, u32[]{:S(2)}) %collective-permute-start.6) | collective-permute-done | bytes 1179680 | tf_op jit(solution)/shard_map/ppermute | solution.py:488
  339.3 15.0 %collective-permute-done.7.back_ref = bf16[4608,128]{1,0:T(8,128)(2,1)S(1)} collective-permute-done((bf16[4608,128]{1,0:T(8,128)(2,1)}, bf16[4608,128]{1,0:T(8,128)(2,1)S(1)}, u32[]{:S(2)}, u32[]{:S(2)}) %collective-permute-start.7) | collective-permute-done | bytes 1179680 | tf_op jit(solution)/shard_map/ppermute | solution.py:492
  (54 shorter events, 21.7 us)
Async XLA Ops:
  0.0 8.2 %copy-start.10 = (f32[2,128]{1,0:T(2,128)S(1)}, f32[2,128]{1,0:T(2,128)}, u32[]{:S(2)}) copy-start(f32[2,128]{1,0:T(2,128)} %param.16) | copy-start | bytes 3076
  0.0 8.2 %copy-start.11 = (f32[2,128]{1,0:T(2,128)S(1)}, f32[2,128]{1,0:T(2,128)}, u32[]{:S(2)}) copy-start(f32[2,128]{1,0:T(2,128)} %param.15) | copy-start | bytes 3076
  0.0 8.2 %copy-start.12 = (f32[2,128]{1,0:T(2,128)S(1)}, f32[2,128]{1,0:T(2,128)}, u32[]{:S(2)}) copy-start(f32[2,128]{1,0:T(2,128)} %param.12) | copy-start | bytes 3076
  0.0 8.2 %copy-start.13 = (f32[2,128]{1,0:T(2,128)S(1)}, f32[2,128]{1,0:T(2,128)}, u32[]{:S(2)}) copy-start(f32[2,128]{1,0:T(2,128)} %param.11) | copy-start | bytes 3076
  0.0 8.3 %copy-start.8 = (bf16[2,128,128]{2,1,0:T(8,128)(2,1)S(1)}, bf16[2,128,128]{2,1,0:T(8,128)(2,1)}, u32[]{:S(2)}) copy-start(bf16[2,128,128]{2,1,0:T(8,128)(2,1)} %param.14) | copy-start | bytes 196612
  0.0 8.4 %copy-start.9 = (bf16[2,128,128]{2,1,0:T(8,128)(2,1)S(1)}, bf16[2,128,128]{2,1,0:T(8,128)(2,1)}, u32[]{:S(2)}) copy-start(bf16[2,128,128]{2,1,0:T(8,128)(2,1)} %param.17) | copy-start | bytes 196612
  0.0 8.6 %copy-start.7 = (bf16[2,128,512]{2,1,0:T(8,128)(2,1)S(1)}, bf16[2,128,512]{2,1,0:T(8,128)(2,1)}, u32[]{:S(2)}) copy-start(bf16[2,128,512]{2,1,0:T(8,128)(2,1)} %param.13) | copy-start | bytes 786436
  4.3 30.6 %copy-start.4 = (bf16[4,1168,128]{2,1,0:T(8,128)(2,1)S(1)}, bf16[4,1168,128]{2,1,0:T(8,128)(2,1)}, u32[]{:S(2)}) copy-start(bf16[4,1168,128]{2,1,0:T(8,128)(2,1)} %get-tuple-element.23.refs_0_) | copy-start | bytes 3588100
  4.3 30.6 %collective-permute-start = (bf16[4,1168,128]{2,1,0:T(8,128)(2,1)}, bf16[4,1168,128]{2,1,0:T(8,128)(2,1)}, u32[]{:S(2)}, u32[]{:S(2)}) collective-permute-start(bf16[4,1168,128]{2,1,0:T(8,128)(2,1)} %get-tuple-element.19), channel_id=1, source_target_pairs={{2,0},{16,18},{0,16},{18,2},{3,1},{17,19},{1,17},{19,3},{6,4},{20,... | collective-permute-start | bytes 3588104 | tf_op jit(solution)/shard_map/ppermute | solution.py:433
  4.9 18.5 %collective-permute-start.3 = (bf16[2,1168,128]{2,1,0:T(8,128)(2,1)}, bf16[2,1168,128]{2,1,0:T(8,128)(2,1)S(1)}, u32[]{:S(2)}, u32[]{:S(2)}) collective-permute-start(bf16[2,1168,128]{2,1,0:T(8,128)(2,1)} %get-tuple-element.21), channel_id=1, source_target_pairs={{2,18},{16,0},{3,19},{17,1},{6,22},{20,4},{7,23},{21,5},{10,26},{2... | collective-permute-start | bytes 1794056 | tf_op jit(solution)/shard_map/ppermute | solution.py:431
  6.2 22.4 %collective-permute-start.1 = (bf16[1,1168,128]{2,1,0:T(8,128)(2,1)}, bf16[1,1168,128]{2,1,0:T(8,128)(2,1)}, u32[]{:S(2)}, u32[]{:S(2)}) collective-permute-start(bf16[1,1168,128]{2,1,0:T(8,128)(2,1)} %get-tuple-element.20), channel_id=1, source_target_pairs={{2,18},{16,0},{3,19},{17,1},{6,22},{20,4},{7,23},{21,5},{10,26},{2... | collective-permute-start | bytes 897032 | tf_op jit(solution)/shard_map/ppermute | solution.py:431
  7.5 32.9 %collective-permute-start.5 = (bf16[1,1168,128]{2,1,0:T(8,128)(2,1)}, bf16[1,1168,128]{2,1,0:T(8,128)(2,1)S(1)}, u32[]{:S(2)}, u32[]{:S(2)}) collective-permute-start(bf16[1,1168,128]{2,1,0:T(8,128)(2,1)} %get-tuple-element.22), channel_id=1, source_target_pairs={{2,16},{16,2},{3,17},{17,3},{6,20},{20,6},{7,21},{21,7},{10,24},{2... | collective-permute-start | bytes 897032 | tf_op jit(solution)/shard_map/ppermute | solution.py:434
  23.4 37.8 %collective-permute-start.4 = (bf16[2,1168,128]{2,1,0:T(8,128)(2,1)S(1)}, bf16[2,1168,128]{2,1,0:T(8,128)(2,1)S(1)}, u32[]{:S(2)}, u32[]{:S(2)}) collective-permute-start(bf16[2,1168,128]{2,1,0:T(8,128)(2,1)S(1)} %collective-permute-done.3), channel_id=1, source_target_pairs={{0,2},{18,16},{1,3},{19,17},{4,6},{22,20},{5,7},{23,21},{8,10},{26... | collective-permute-start | bytes 1794056 | tf_op jit(solution)/shard_map/ppermute | solution.py:432
  28.6 32.6 %collective-permute-start.2 = (bf16[1,1168,128]{2,1,0:T(8,128)(2,1)}, bf16[1,1168,128]{2,1,0:T(8,128)(2,1)S(1)}, u32[]{:S(2)}, u32[]{:S(2)}) collective-permute-start(bf16[1,1168,128]{2,1,0:T(8,128)(2,1)} %collective-permute-done.1), channel_id=1, source_target_pairs={{0,2},{18,16},{1,3},{19,17},{4,6},{22,20},{5,7},{23,21},{8,10},{26... | collective-permute-start | bytes 897032 | tf_op jit(solution)/shard_map/ppermute | solution.py:432
  143.4 4.9 %copy-start.3 = (bf16[128,9216]{1,0:T(8,128)(2,1)S(1)}, bf16[128,9216]{1,0:T(8,128)(2,1)}, u32[]{:S(2)}) copy-start(bf16[128,9216]{1,0:T(8,128)(2,1)} %get-tuple-element.28.refs_0_.refs_1_) | copy-start | bytes 7077892
  143.4 35.3 %all-to-all-start.1 = ((bf16[16,8,9216]{2,1,0:T(8,128)(2,1)}), bf16[16,8,9216]{2,1,0:T(8,128)(2,1)}, u32[]{:S(2)}, u32[]{:S(2)}) async-start(bf16[16,8,9216]{2,1,0:T(8,128)(2,1)} %bitcast.31), calls=%async_computation.1 | async-start | bytes 4718592 | tf_op jit(solution)/shard_map/all_to_all | solution.py:464
  148.4 30.3 %copy-start.5 = (bf16[16,9216]{1,0:T(8,128)(2,1)S(1)}, bf16[16,9216]{1,0:T(8,128)(2,1)}, u32[]{:S(2)}) copy-start(bf16[16,9216]{1,0:T(8,128)(2,1)} %get-tuple-element.29.refs_3_) | copy-start | bytes 884740
  246.4 6.0 %copy-start = (bf16[16,16,9216]{2,1,0:T(8,128)(2,1)}, bf16[16,16,9216]{2,1,0:T(8,128)(2,1)S(1)}, u32[]{:S(2)}) copy-start(bf16[16,16,9216]{2,1,0:T(8,128)(2,1)S(1)} %all_to_all.26) | copy-start | bytes 14155780
  252.4 4.9 %copy-start.2 = (bf16[128,9216]{1,0:T(8,128)(2,1)S(1)}, bf16[128,9216]{1,0:T(8,128)(2,1)}, u32[]{:S(2)}) copy-start(bf16[128,9216]{1,0:T(8,128)(2,1)} %get-tuple-element.31.refs_0_.refs_1_) | copy-start | bytes 7077892
  252.4 20.6 %all-to-all-start.3 = ((bf16[16,8,4608]{2,1,0:T(8,128)(2,1)}), bf16[16,8,4608]{2,1,0:T(8,128)(2,1)}, u32[]{:S(2)}, u32[]{:S(2)}) async-start(bf16[16,8,4608]{2,1,0:T(8,128)(2,1)} %bitcast.34), calls=%async_computation.3 | async-start | bytes 2359296 | tf_op jit(solution)/shard_map/all_to_all | solution.py:464
  276.7 44.1 %all-to-all-start.4 = ((bf16[16,8,4608]{2,1,0:T(8,128)(2,1)}), bf16[16,8,4608]{2,1,0:T(8,128)(2,1)}, u32[]{:S(2)}, u32[]{:S(2)}) async-start(bf16[16,8,4608]{2,1,0:T(8,128)(2,1)} %bitcast.33), calls=%async_computation.4 | async-start | bytes 2359296 | tf_op jit(solution)/shard_map/all_to_all | solution.py:464
  281.9 43.8 %collective-permute-start.8 = (bf16[4608,128]{1,0:T(8,128)(2,1)}, bf16[4608,128]{1,0:T(8,128)(2,1)}, u32[]{:S(2)}, u32[]{:S(2)}) collective-permute-start(bf16[4608,128]{1,0:T(8,128)(2,1)} %shard_map.99), channel_id=1, source_target_pairs={{2,16},{16,2},{3,17},{17,3},{6,20},{20,6},{7,21},{21,7},{10,24},{2... | collective-permute-start | bytes 3538952 | tf_op jit(solution)/shard_map/ppermute | solution.py:488
  283.6 55.7 %collective-permute-start.6 = (bf16[4608,128]{1,0:T(8,128)(2,1)}, bf16[4608,128]{1,0:T(8,128)(2,1)}, u32[]{:S(2)}, u32[]{:S(2)}) collective-permute-start(bf16[4608,128]{1,0:T(8,128)(2,1)} %shard_map.99), channel_id=1, source_target_pairs={{0,2},{18,16},{1,3},{19,17},{4,6},{22,20},{5,7},{23,21},{8,10},{26... | collective-permute-start | bytes 3538952 | tf_op jit(solution)/shard_map/ppermute | solution.py:488
  324.4 29.9 %collective-permute-start.7 = (bf16[4608,128]{1,0:T(8,128)(2,1)}, bf16[4608,128]{1,0:T(8,128)(2,1)S(1)}, u32[]{:S(2)}, u32[]{:S(2)}) collective-permute-start(bf16[4608,128]{1,0:T(8,128)(2,1)} %shard_map.101.here_ref), channel_id=1, source_target_pairs={{2,18},{16,0},{3,19},{17,1},{6,22},{20,4},{7,23},{21,5},{10,26},{2... | collective-permute-start | bytes 3538952 | tf_op jit(solution)/shard_map/ppermute | solution.py:492
  (2 other events, 4.8 us)

commit v12 on v10

--- a/solution.py
+++ b/solution.py
@@ -46,7 +46,7 @@
 
 def pack_kernel(cuts, tile, z_ref, mask_ref, *refs):
     out_refs, (held_ref, z_sems, mask_sems, out_sems) = refs[:-4], refs[-4:]
-    part_refs, (own_ref, next_ref) = out_refs[:-2], out_refs[-2:]
+    part_refs, (*next_refs, own_ref) = out_refs[: len(cuts)], out_refs[len(cuts) :]
     upper = lax.axis_index("groups")
     home = upper == lax.axis_index("zh")
     per_strip = cuts[-1]
@@ -72,11 +72,14 @@
         for k, (begin, end, part_ref) in enumerate(zip((0, *cuts), cuts, part_refs))
     ]
     stores += [
-        pltpu.make_async_copy(held_ref.at[1], own_ref, out_sems.at[len(cuts)]),
         pltpu.make_async_copy(
-            held_ref.at[1 - home.astype(jnp.int32)], next_ref, out_sems.at[len(cuts) + 1]
-        ),
+            held_ref.at[1 - home.astype(jnp.int32), begin:end], next_ref, out_sems.at[len(cuts) + k]
+        )
+        for k, (begin, end, next_ref) in enumerate(
+            zip((0, per_strip - 1), (per_strip - 1, per_strip), next_refs)
+        )
     ]
+    stores.append(pltpu.make_async_copy(held_ref.at[1], own_ref, out_sems.at[len(cuts) + 2]))
     for fetch in fetches:
         fetch.start()
     for fetch in fetches[: 2 * per_strip]:
@@ -91,9 +94,9 @@
         store.wait()
 
 
-def first_kernel(peers, parts, own_ref, *refs):
-    far_refs, (small_ref, weight_ref), (lr_ref, zt_ref, mask_ref) = (
-        refs[: len(parts)], refs[len(parts) : -3], refs[-3:],
+def first_kernel(peers, sources, *refs):
+    z_refs, (small_ref, weight_ref), (lr_ref, zt_ref, mask_ref) = (
+        refs[: len(sources)], refs[len(sources) : -3], refs[-3:],
     )
     home = lax.axis_index("groups") == lax.axis_index("zh")
     step = pl.program_id(0)
@@ -105,10 +108,10 @@
         flat = jnp.concatenate([marks[k : k + 1] for k in range(tile // LANES)], axis=1)
         mask_ref[...] = jnp.broadcast_to(flat, mask_ref.shape).astype(jnp.bfloat16)
 
-    pl.when(home)(lambda: put(own_ref))
-    for (begin, end), far_ref in zip(parts, far_refs):
+    for (begin, end, at_home), z_ref in zip(sources, z_refs):
         here = jnp.logical_and(step >= begin, step < end)
-        pl.when(jnp.logical_and(jnp.logical_not(home), here))(functools.partial(put, far_ref))
+        whose = home if at_home else jnp.logical_not(home)
+        pl.when(jnp.logical_and(whose, here))(functools.partial(put, z_ref))
     zt = zt_ref[...].astype(jnp.float32)
     mask = mask_ref[...].astype(jnp.float32)[:1]
     emit_projections(peers, 0, zt, mask, small_ref, weight_ref, lr_ref)
@@ -379,7 +382,7 @@
 def pack(pair_act, mask, cuts, tile):
     per_strip = cuts[-1]
     shape = (tile + mask.shape[1], pair_act.shape[1])
-    outs = [end - begin for begin, end in zip((0, *cuts), cuts)] + [per_strip, per_strip]
+    outs = [end - begin for begin, end in zip((0, *cuts), cuts)] + [per_strip - 1, 1, per_strip]
     anywhere = pl.BlockSpec(memory_space=pltpu.HBM)
     return pl.pallas_call(
         functools.partial(pack_kernel, cuts, tile),
@@ -421,12 +424,14 @@
     cuts = (1, per_piece - 1, per_piece)
     marks = pair_mask.astype(jnp.bfloat16).reshape(2 * per_piece, tile // LANES, LANES)
     marks = jnp.pad(marks, ((0, 0), (0, 16 - tile // LANES), (0, 0)))
-    *z_parts, z_own, z_next = pack(pair_act.reshape(pixels, channels), marks, cuts, tile)
+    *z_parts, z_next, z_last, z_own = pack(pair_act.reshape(pixels, channels), marks, cuts, tile)
     z_far = []
     for part in z_parts[:-1]:
         over = lax.ppermute(part, LINE, ((1, 3), (2, 0)))
         z_far.append(lax.ppermute(over, LINE, ((0, 1), (3, 2))))
-    z_near = lax.ppermute(z_next, LINE, ((1, 0), (2, 3), (0, 2), (3, 1)))
+    z_near, z_rest = (
+        lax.ppermute(part, LINE, ((1, 0), (2, 3), (0, 2), (3, 1))) for part in (z_next, z_last)
+    )
     z_far.append(lax.ppermute(z_parts[-1], LINE, ((1, 2), (2, 1))))
     small = jnp.stack([input_gain, input_bias, output_gain, output_bias], axis=1)
     small = small.reshape(-1, channels).T
@@ -435,17 +440,22 @@
     ).transpose(0, 2, 1)
     fixed = (small, weights)
 
-    def first(piece, ours, far, parts, kept):
-        tiled = [(ours, 0, per_piece)]
-        tiled += [(part, -begin, end - begin) for part, (begin, end) in zip(far, parts)]
+    def first(start, steps, sources, kept):
         return pixel_call(
-            functools.partial(first_kernel, peers, parts),
-            tiled, fixed, (2 * width, channels, 16), per_piece, tile, pixels // 2 * mult * 4 * width,
-            start=piece * per_piece, pixels=pixels, kept=kept,
+            functools.partial(first_kernel, peers, [served for _, _, *served in sources]),
+            [(a, at - begin, a.shape[0]) for a, at, begin, *_ in sources],
+            fixed, (2 * width, channels, 16), steps, tile, steps * tile * mult * 4 * width,
+            start=start, pixels=pixels, kept=kept,
         )
 
-    begun = first(0, z_own, [z_near], [(0, per_piece)], ())
-    sent, zt, mask = first(1, z_near, z_far, list(zip((0, *cuts), cuts)), begun)
+    soon = per_piece - 1
+    begun = first(0, soon, [(z_own, 0, 0, soon, True), (z_near, 0, 0, soon, False)], ())
+    sources = [(z_own, soon, 0, 1, True), (z_near, 0, 1, per_piece, True), (z_rest, 0, per_piece, per_piece + 1, True)]
+    sources += [(z_rest, 0, 0, 1, False)]
+    sources += [
+        (part, 0, 1 + begin, 1 + end, False) for part, begin, end in zip(z_far, (0, *cuts), cuts)
+    ]
+    sent, zt, mask = first(soon, per_piece + 1, sources, begun)
     wide = 2 * tile
     steps = pixels // wide
 

time: 347 us -> 350 us (level)
    ppermute x1 -> x2, waiting for transfers between devices: 4.76 us -> 8.31 us  [by_kernels(): lax.ppermute(part, LINE, ((1, 0), (2, 3), (0, 2), (3, 1)))]
  transfers between devices with their start and end apart: 12 -> 13, of which waited for: 8 -> 9; matrix products, arithmetic and copies ran while one was open for 0% -> 0% of each run, Pallas kernels for 6% -> 6%
where the time goes in v12:
time: 350 us; the launch traced here: 345 us
  blocking collectives  129 us (37%)
  waiting for transfers between devices  121 us (35%)
  Pallas kernels  56.7 us (16%)
  starting transfers between devices  33.3 us (10%)
  local copies, waits for them, and re-layouts  3.61 us (1%)
    all_to_all x2, blocking collectives, exchange(): there = lax.all_to_all(array.reshape(peers, -1, array.shape[1]), CUBE, 0, 0)  129 us
    all_to_all x3, waiting for transfers between devices, exchange(): there = lax.all_to_all(array.reshape(peers, -1, array.shape[1]), CUBE, 0, 0)  48.8 us
    pallas_call x7, Pallas kernels, pixel_call(): pl.pallas_call(kernel, grid=(steps,), in_specs=in_specs, out_specs=[spec(...  32.7 us
    ppermute x2, waiting for transfers between devices, by_kernels(): lax.ppermute(there, LINE, pairs)  28.6 us
    ppermute x2, waiting for transfers between devices, by_kernels(): z_far.append(lax.ppermute(over, LINE, ((0, 1), (3, 2))))  20 us
    pallas_call x3, Pallas kernels, triangle_call(): pl.pallas_call(functools.partial(triangle_kernel, blocks, side, own, inco...  19.6 us
    ppermute x2, waiting for transfers between devices, by_kernels(): over = lax.ppermute(part, LINE, ((1, 3), (2, 0)))  15.1 us
    all_to_all x3, starting transfers between devices, exchange(): there = lax.all_to_all(array.reshape(peers, -1, array.shape[1]), CUBE, 0, 0)  15 us
  transfers between devices with their start and end apart: 13, of which 9 were waited for; matrix products, arithmetic and copies ran while one was open for 0% of the time, Pallas kernels for 6%

profile of v12, /device:TPU:20, one launch (start us, length us, event | category | flops | bytes accessed | tf_op | source)
XLA Modules:
  0.0 344.8 jit_solution(14987355363658718158)
XLA Ops:
  6.7 3.5 %collective-permute-start = (bf16[3,1168,128]{2,1,0:T(8,128)(2,1)}, bf16[3,1168,128]{2,1,0:T(8,128)(2,1)S(1)}, u32[]{:S(2)}, u32[]{:S(2)}) collective-permute-start(bf16[3,1168,128]{2,1,0:T(8,128)(2,1)} %get-tuple-element.21), channel_id=1, source_target_pairs={{2,0},{16,18},{0,16},{18,2},{3,1},{17,19},{1,17},{19,3},{6,4},{20,... | collective-permute-start | bytes 2691080 | tf_op jit(solution)/shard_map/ppermute | solution.py:433
  12.8 11.2 %collective-permute-done.4 = bf16[2,1168,128]{2,1,0:T(8,128)(2,1)} collective-permute-done((bf16[2,1168,128]{2,1,0:T(8,128)(2,1)}, bf16[2,1168,128]{2,1,0:T(8,128)(2,1)}, u32[]{:S(2)}, u32[]{:S(2)}) %collective-permute-start.4) | collective-permute-done | bytes 598048 | tf_op jit(solution)/shard_map/ppermute | solution.py:430
  25.4 3.9 %collective-permute-done.2 = bf16[1,1168,128]{2,1,0:T(8,128)(2,1)} collective-permute-done((bf16[1,1168,128]{2,1,0:T(8,128)(2,1)}, bf16[1,1168,128]{2,1,0:T(8,128)(2,1)}, u32[]{:S(2)}, u32[]{:S(2)}) %collective-permute-start.2) | collective-permute-done | bytes 299040 | tf_op jit(solution)/shard_map/ppermute | solution.py:430
  34.1 8.1 %collective-permute-done.1.refs_2_.refs_3_ = bf16[1,1168,128]{2,1,0:T(8,128)(2,1)S(1)} collective-permute-done((bf16[1,1168,128]{2,1,0:T(8,128)(2,1)}, bf16[1,1168,128]{2,1,0:T(8,128)(2,1)S(1)}, u32[]{:S(2)}, u32[]{:S(2)}) %collective-permute-start.1) | collective-permute-done | bytes 299040 | tf_op jit(solution)/shard_map/ppermute | solution.py:433
  42.2 20.0 %collective-permute-done.3.refs_4_ = bf16[1,1168,128]{2,1,0:T(8,128)(2,1)S(1)} collective-permute-done((bf16[1,1168,128]{2,1,0:T(8,128)(2,1)}, bf16[1,1168,128]{2,1,0:T(8,128)(2,1)S(1)}, u32[]{:S(2)}, u32[]{:S(2)}) %collective-permute-start.3) | collective-permute-done | bytes 299040 | tf_op jit(solution)/shard_map/ppermute | solution.py:431
  62.2 5.0 %shard_map.93 = (bf16[256,9216]{1,0:T(8,128)(2,1)}, bf16[128,9216]{1,0:T(8,128)(2,1)}, bf16[16,9216]{1,0:T(8,128)(2,1)}) custom-call(bf16[4,1168,128]{2,1,0:T(8,128)(2,1)S(1)} %copy-done.4, bf16[3,1168,128]{2,1,0:T(8,128)(2,1)S(1)} %collective-permute-done.refs_1_, ...), custom_call_target="tpu_custom_call", output_to_operand_aliasing={{0}: (9, {}), {1}: (10, {}), {2}: (11, {})} | custom-call | flops 754974720 | bytes 7557120 | tf_op jit(solution)/shard_map/pallas_call | solution.py:360
  67.3 70.6 %all_to_all.25 = bf16[16,16,9216]{2,1,0:T(8,128)(2,1)S(1)} all-to-all(bf16[16,16,9216]{2,1,0:T(8,128)(2,1)} %bitcast.31), channel_id=1, replica_groups=mesh['groups'=2,'row'=4,'zh'=2,'zl'=2] {'groups','row','zl'}, dimensions={0} | all-to-all | bytes 9437184 | tf_op jit(solution)/shard_map/all_to_all | solution.py:469
  137.8 7.7 %shard_map.94 = bf16[128,9216]{1,0:T(8,128)(2,1)} custom-call(bf16[256,9216]{1,0:T(8,128)(2,1)S(1)} %bitcast.22), custom_call_target="tpu_custom_call" | custom-call | flops 905969664 | bytes 14155776 | tf_op jit(solution)/shard_map/pallas_call | solution.py:309
  145.5 4.9 %all-to-all-start.1 = ((bf16[16,8,9216]{2,1,0:T(8,128)(2,1)}), bf16[16,8,9216]{2,1,0:T(8,128)(2,1)}, u32[]{:S(2)}, u32[]{:S(2)}) async-start(bf16[16,8,9216]{2,1,0:T(8,128)(2,1)} %bitcast.32), calls=%async_computation.1 | async-start | bytes 4718592 | tf_op jit(solution)/shard_map/all_to_all | solution.py:469
  150.4 3.8 %shard_map.95.refs_2_ = bf16[128,9216]{1,0:T(8,128)(2,1)} custom-call(bf16[128,9216]{1,0:T(8,128)(2,1)S(1)} %copy-done.3, f32[128,8]{1,0:T(8,128)S(1)} %bitcast.25, bf16[2,768,128]{2,1,0:T(8,128)(2,1)S(1)} %maximum_bitcast_fusion.refs_3_.refs_8_.refs_2_.refs_5_.refs_4_), custom_call_target="tpu_custom_call" | custom-call | flops 301989888 | bytes 7077888 | tf_op jit(solution)/shard_map/pallas_call | solution.py:360
  154.2 26.5 %all-to-all-done.1 = bf16[16,8,9216]{2,1,0:T(8,128)(2,1)} async-done(((bf16[16,8,9216]{2,1,0:T(8,128)(2,1)}), bf16[16,8,9216]{2,1,0:T(8,128)(2,1)}, u32[]{:S(2)}, u32[]{:S(2)}) %all-to-all-start.1) | async-done | bytes 2359328 | tf_op jit(solution)/shard_map/all_to_all | solution.py:469
  180.8 9.3 %shard_map.96 = (bf16[256,9216]{1,0:T(8,128)(2,1)}, bf16[128,9216]{1,0:T(8,128)(2,1)}) custom-call(bf16[128,9216]{1,0:T(8,128)(2,1)} %bitcast.11.refs_0_, bf16[128,9216]{1,0:T(8,128)(2,1)S(1)} %copy-done.3, bf16[128,9216]{1,0:T(8,128)(2,1)} %shard_map.95.refs_2_, bf16[16,9216]{1,0:T(8,128)(2,1)S(1)} %copy-done.7, f32[128,8]{1,0:T(8,128)S(1)} %bitcast.26, ...), custom_call_target="tpu_custom_call" | custom-call | flops 1509949440 | bytes 11796480 | tf_op jit(solution)/shard_map/pallas_call | solution.py:360
  190.1 58.4 %all_to_all.26 = bf16[16,16,9216]{2,1,0:T(8,128)(2,1)S(1)} all-to-all(bf16[16,16,9216]{2,1,0:T(8,128)(2,1)} %bitcast.33), channel_id=1, replica_groups=mesh['groups'=2,'row'=4,'zh'=2,'zl'=2] {'groups','row','zl'}, dimensions={0} | all-to-all | bytes 9437184 | tf_op jit(solution)/shard_map/all_to_all | solution.py:469
  248.5 6.0 %shard_map.97 = bf16[128,4608]{1,0:T(8,128)(2,1)} custom-call(bf16[256,9216]{1,0:T(8,128)(2,1)S(1)} %bitcast.20), custom_call_target="tpu_custom_call" | custom-call | flops 452984832 | bytes 14155776 | tf_op jit(solution)/shard_map/pallas_call | solution.py:309
  254.5 4.9 %all-to-all-start.3 = ((bf16[16,8,4608]{2,1,0:T(8,128)(2,1)}), bf16[16,8,4608]{2,1,0:T(8,128)(2,1)}, u32[]{:S(2)}, u32[]{:S(2)}) async-start(bf16[16,8,4608]{2,1,0:T(8,128)(2,1)} %bitcast.35), calls=%async_computation.3 | async-start | bytes 2359296 | tf_op jit(solution)/shard_map/all_to_all | solution.py:469
  259.3 3.8 %shard_map.98.refs_2_ = bf16[128,9216]{1,0:T(8,128)(2,1)} custom-call(bf16[128,9216]{1,0:T(8,128)(2,1)S(1)} %copy-done.2, f32[128,8]{1,0:T(8,128)S(1)} %bitcast.27, bf16[2,768,128]{2,1,0:T(8,128)(2,1)S(1)} %maximum_bitcast_fusion.refs_3_.refs_8_.refs_2_.refs_5_.refs_4_), custom_call_target="tpu_custom_call" | custom-call | flops 301989888 | bytes 7077888 | tf_op jit(solution)/shard_map/pallas_call | solution.py:360
  263.1 6.0 %shard_map.100 = bf16[128,4608]{1,0:T(8,128)(2,1)} custom-call(bf16[256,9216]{1,0:T(8,128)(2,1)S(1)} %bitcast.21), custom_call_target="tpu_custom_call" | custom-call | flops 452984832 | bytes 14155776 | tf_op jit(solution)/shard_map/pallas_call | solution.py:309
  269.1 6.0 %all-to-all-done.3 = bf16[16,8,4608]{2,1,0:T(8,128)(2,1)} async-done(((bf16[16,8,4608]{2,1,0:T(8,128)(2,1)}), bf16[16,8,4608]{2,1,0:T(8,128)(2,1)}, u32[]{:S(2)}, u32[]{:S(2)}) %all-to-all-start.3) | async-done | bytes 1179680 | tf_op jit(solution)/shard_map/all_to_all | solution.py:469
  275.1 3.7 %shard_map.99 = bf16[4608,128]{1,0:T(8,128)(2,1)} custom-call(bf16[128,4608]{1,0:T(8,128)(2,1)} %bitcast.15.refs_0_, bf16[128,9216]{1,0:T(8,128)(2,1)S(1)} %copy-done.2, bf16[128,9216]{1,0:T(8,128)(2,1)} %shard_map.98.refs_2_, f32[128,8]{1,0:T(8,128)S(1)} %bitcast.28, bf16[2,768,128]{2,1,0:T(8,128)(2,1)S(1)} %maximum_bitcast_fusion.refs_3_.refs_8_.refs_2_.refs_5_.refs_4_), custom_call_target="tpu_custom_call" | custom-call | flops 150994944 | bytes 3538944 | tf_op jit(solution)/shard_map/pallas_call | solution.py:360
  278.8 5.3 %all-to-all-start.4 = ((bf16[16,8,4608]{2,1,0:T(8,128)(2,1)}), bf16[16,8,4608]{2,1,0:T(8,128)(2,1)}, u32[]{:S(2)}, u32[]{:S(2)}) async-start(bf16[16,8,4608]{2,1,0:T(8,128)(2,1)} %bitcast.34), calls=%async_computation.4 | async-start | bytes 2359296 | tf_op jit(solution)/shard_map/all_to_all | solution.py:469
  285.7 5.8 %collective-permute-start.7 = (bf16[4608,128]{1,0:T(8,128)(2,1)}, bf16[4608,128]{1,0:T(8,128)(2,1)}, u32[]{:S(2)}, u32[]{:S(2)}) collective-permute-start(bf16[4608,128]{1,0:T(8,128)(2,1)} %shard_map.99), channel_id=1, source_target_pairs={{0,2},{18,16},{1,3},{19,17},{4,6},{22,20},{5,7},{23,21},{8,10},{26... | collective-permute-start | bytes 3538952 | tf_op jit(solution)/shard_map/ppermute | solution.py:493
  291.5 16.3 %all-to-all-done.4 = bf16[16,8,4608]{2,1,0:T(8,128)(2,1)} async-done(((bf16[16,8,4608]{2,1,0:T(8,128)(2,1)}), bf16[16,8,4608]{2,1,0:T(8,128)(2,1)}, u32[]{:S(2)}, u32[]{:S(2)}) %all-to-all-start.4) | async-done | bytes 1179680 | tf_op jit(solution)/shard_map/all_to_all | solution.py:469
  307.8 3.7 %shard_map.101.here_ref = bf16[4608,128]{1,0:T(8,128)(2,1)} custom-call(bf16[128,4608]{1,0:T(8,128)(2,1)} %bitcast.17.refs_0_, bf16[128,9216]{1,0:T(8,128)(2,1)S(1)} %copy-done.2, bf16[128,9216]{1,0:T(8,128)(2,1)} %shard_map.98.refs_2_, f32[128,8]{1,0:T(8,128)S(1)} %bitcast.29, ...), custom_call_target="tpu_custom_call" | custom-call | flops 150994944 | bytes 3538944 | tf_op jit(solution)/shard_map/pallas_call | solution.py:360
  312.8 28.6 %collective-permute-done.7.beside_ref = bf16[4608,128]{1,0:T(8,128)(2,1)} collective-permute-done((bf16[4608,128]{1,0:T(8,128)(2,1)}, bf16[4608,128]{1,0:T(8,128)(2,1)}, u32[]{:S(2)}, u32[]{:S(2)}) %collective-permute-start.7) | collective-permute-done | bytes 1179680 | tf_op jit(solution)/shard_map/ppermute | solution.py:493
  (58 shorter events, 21.5 us)
Async XLA Ops:
  0.0 12.2 %copy-start.11 = (f32[2,128]{1,0:T(2,128)S(1)}, f32[2,128]{1,0:T(2,128)}, u32[]{:S(2)}) copy-start(f32[2,128]{1,0:T(2,128)} %param.16) | copy-start | bytes 3076
  0.0 12.2 %copy-start.12 = (f32[2,128]{1,0:T(2,128)S(1)}, f32[2,128]{1,0:T(2,128)}, u32[]{:S(2)}) copy-start(f32[2,128]{1,0:T(2,128)} %param.15) | copy-start | bytes 3076
  0.0 12.2 %copy-start.13 = (f32[2,128]{1,0:T(2,128)S(1)}, f32[2,128]{1,0:T(2,128)}, u32[]{:S(2)}) copy-start(f32[2,128]{1,0:T(2,128)} %param.12) | copy-start | bytes 3076
  0.0 12.2 %copy-start.14 = (f32[2,128]{1,0:T(2,128)S(1)}, f32[2,128]{1,0:T(2,128)}, u32[]{:S(2)}) copy-start(f32[2,128]{1,0:T(2,128)} %param.11) | copy-start | bytes 3076
  0.0 12.3 %copy-start.9 = (bf16[2,128,128]{2,1,0:T(8,128)(2,1)S(1)}, bf16[2,128,128]{2,1,0:T(8,128)(2,1)}, u32[]{:S(2)}) copy-start(bf16[2,128,128]{2,1,0:T(8,128)(2,1)} %param.14) | copy-start | bytes 196612
  0.0 12.4 %copy-start.10 = (bf16[2,128,128]{2,1,0:T(8,128)(2,1)S(1)}, bf16[2,128,128]{2,1,0:T(8,128)(2,1)}, u32[]{:S(2)}) copy-start(bf16[2,128,128]{2,1,0:T(8,128)(2,1)} %param.17) | copy-start | bytes 196612
  2.7 9.9 %copy-start.8 = (bf16[2,128,512]{2,1,0:T(8,128)(2,1)S(1)}, bf16[2,128,512]{2,1,0:T(8,128)(2,1)}, u32[]{:S(2)}) copy-start(bf16[2,128,512]{2,1,0:T(8,128)(2,1)} %param.13) | copy-start | bytes 786436
  5.3 25.6 %copy-start.4 = (bf16[4,1168,128]{2,1,0:T(8,128)(2,1)S(1)}, bf16[4,1168,128]{2,1,0:T(8,128)(2,1)}, u32[]{:S(2)}) copy-start(bf16[4,1168,128]{2,1,0:T(8,128)(2,1)} %get-tuple-element.20.refs_0_) | copy-start | bytes 3588100
  5.3 18.7 %collective-permute-start.4 = (bf16[2,1168,128]{2,1,0:T(8,128)(2,1)}, bf16[2,1168,128]{2,1,0:T(8,128)(2,1)}, u32[]{:S(2)}, u32[]{:S(2)}) collective-permute-start(bf16[2,1168,128]{2,1,0:T(8,128)(2,1)} %get-tuple-element.24), channel_id=1, source_target_pairs={{2,18},{16,0},{3,19},{17,1},{6,22},{20,4},{7,23},{21,5},{10,26},{2... | collective-permute-start | bytes 1794056 | tf_op jit(solution)/shard_map/ppermute | solution.py:430
  6.7 24.1 %collective-permute-start = (bf16[3,1168,128]{2,1,0:T(8,128)(2,1)}, bf16[3,1168,128]{2,1,0:T(8,128)(2,1)S(1)}, u32[]{:S(2)}, u32[]{:S(2)}) collective-permute-start(bf16[3,1168,128]{2,1,0:T(8,128)(2,1)} %get-tuple-element.21), channel_id=1, source_target_pairs={{2,0},{16,18},{0,16},{18,2},{3,1},{17,19},{1,17},{19,3},{6,4},{20,... | collective-permute-start | bytes 2691080 | tf_op jit(solution)/shard_map/ppermute | solution.py:433
  10.2 32.1 %collective-permute-start.1 = (bf16[1,1168,128]{2,1,0:T(8,128)(2,1)}, bf16[1,1168,128]{2,1,0:T(8,128)(2,1)S(1)}, u32[]{:S(2)}, u32[]{:S(2)}) collective-permute-start(bf16[1,1168,128]{2,1,0:T(8,128)(2,1)} %get-tuple-element.22), channel_id=1, source_target_pairs={{2,0},{16,18},{0,16},{18,2},{3,1},{17,19},{1,17},{19,3},{6,4},{20,... | collective-permute-start | bytes 897032 | tf_op jit(solution)/shard_map/ppermute | solution.py:433
  10.2 19.1 %collective-permute-start.2 = (bf16[1,1168,128]{2,1,0:T(8,128)(2,1)}, bf16[1,1168,128]{2,1,0:T(8,128)(2,1)}, u32[]{:S(2)}, u32[]{:S(2)}) collective-permute-start(bf16[1,1168,128]{2,1,0:T(8,128)(2,1)} %get-tuple-element.23), channel_id=1, source_target_pairs={{2,18},{16,0},{3,19},{17,1},{6,22},{20,4},{7,23},{21,5},{10,26},{2... | collective-permute-start | bytes 897032 | tf_op jit(solution)/shard_map/ppermute | solution.py:430
  11.5 30.7 %collective-permute-start.6 = (bf16[1,1168,128]{2,1,0:T(8,128)(2,1)}, bf16[1,1168,128]{2,1,0:T(8,128)(2,1)S(1)}, u32[]{:S(2)}, u32[]{:S(2)}) collective-permute-start(bf16[1,1168,128]{2,1,0:T(8,128)(2,1)} %get-tuple-element.25), channel_id=1, source_target_pairs={{2,16},{16,2},{3,17},{17,3},{6,20},{20,6},{7,21},{21,7},{10,24},{2... | collective-permute-start | bytes 897032 | tf_op jit(solution)/shard_map/ppermute | solution.py:435
  24.0 38.2 %collective-permute-start.5 = (bf16[2,1168,128]{2,1,0:T(8,128)(2,1)}, bf16[2,1168,128]{2,1,0:T(8,128)(2,1)S(1)}, u32[]{:S(2)}, u32[]{:S(2)}) collective-permute-start(bf16[2,1168,128]{2,1,0:T(8,128)(2,1)} %collective-permute-done.4), channel_id=1, source_target_pairs={{0,2},{18,16},{1,3},{19,17},{4,6},{22,20},{5,7},{23,21},{8,10},{26... | collective-permute-start | bytes 1794056 | tf_op jit(solution)/shard_map/ppermute | solution.py:431
  29.3 33.0 %collective-permute-start.3 = (bf16[1,1168,128]{2,1,0:T(8,128)(2,1)}, bf16[1,1168,128]{2,1,0:T(8,128)(2,1)S(1)}, u32[]{:S(2)}, u32[]{:S(2)}) collective-permute-start(bf16[1,1168,128]{2,1,0:T(8,128)(2,1)} %collective-permute-done.2), channel_id=1, source_target_pairs={{0,2},{18,16},{1,3},{19,17},{4,6},{22,20},{5,7},{23,21},{8,10},{26... | collective-permute-start | bytes 897032 | tf_op jit(solution)/shard_map/ppermute | solution.py:431
  145.5 4.9 %copy-start.3 = (bf16[128,9216]{1,0:T(8,128)(2,1)S(1)}, bf16[128,9216]{1,0:T(8,128)(2,1)}, u32[]{:S(2)}) copy-start(bf16[128,9216]{1,0:T(8,128)(2,1)} %get-tuple-element.30.refs_0_.refs_1_) | copy-start | bytes 7077892
  145.5 35.3 %all-to-all-start.1 = ((bf16[16,8,9216]{2,1,0:T(8,128)(2,1)}), bf16[16,8,9216]{2,1,0:T(8,128)(2,1)}, u32[]{:S(2)}, u32[]{:S(2)}) async-start(bf16[16,8,9216]{2,1,0:T(8,128)(2,1)} %bitcast.32), calls=%async_computation.1 | async-start | bytes 4718592 | tf_op jit(solution)/shard_map/all_to_all | solution.py:469
  150.4 30.3 %copy-start.7 = (bf16[16,9216]{1,0:T(8,128)(2,1)S(1)}, bf16[16,9216]{1,0:T(8,128)(2,1)}, u32[]{:S(2)}) copy-start(bf16[16,9216]{1,0:T(8,128)(2,1)} %get-tuple-element.31.refs_3_) | copy-start | bytes 884740
  248.5 6.0 %copy-start = (bf16[16,16,9216]{2,1,0:T(8,128)(2,1)}, bf16[16,16,9216]{2,1,0:T(8,128)(2,1)S(1)}, u32[]{:S(2)}) copy-start(bf16[16,16,9216]{2,1,0:T(8,128)(2,1)S(1)} %all_to_all.26) | copy-start | bytes 14155780
  254.5 20.6 %all-to-all-start.3 = ((bf16[16,8,4608]{2,1,0:T(8,128)(2,1)}), bf16[16,8,4608]{2,1,0:T(8,128)(2,1)}, u32[]{:S(2)}, u32[]{:S(2)}) async-start(bf16[16,8,4608]{2,1,0:T(8,128)(2,1)} %bitcast.35), calls=%async_computation.3 | async-start | bytes 2359296 | tf_op jit(solution)/shard_map/all_to_all | solution.py:469
  278.8 29.0 %all-to-all-start.4 = ((bf16[16,8,4608]{2,1,0:T(8,128)(2,1)}), bf16[16,8,4608]{2,1,0:T(8,128)(2,1)}, u32[]{:S(2)}, u32[]{:S(2)}) async-start(bf16[16,8,4608]{2,1,0:T(8,128)(2,1)} %bitcast.34), calls=%async_computation.4 | async-start | bytes 2359296 | tf_op jit(solution)/shard_map/all_to_all | solution.py:469
  284.1 28.8 %collective-permute-start.9 = (bf16[4608,128]{1,0:T(8,128)(2,1)}, bf16[4608,128]{1,0:T(8,128)(2,1)}, u32[]{:S(2)}, u32[]{:S(2)}) collective-permute-start(bf16[4608,128]{1,0:T(8,128)(2,1)} %shard_map.99), channel_id=1, source_target_pairs={{2,16},{16,2},{3,17},{17,3},{6,20},{20,6},{7,21},{21,7},{10,24},{2... | collective-permute-start | bytes 3538952 | tf_op jit(solution)/shard_map/ppermute | solution.py:493
  285.7 55.7 %collective-permute-start.7 = (bf16[4608,128]{1,0:T(8,128)(2,1)}, bf16[4608,128]{1,0:T(8,128)(2,1)}, u32[]{:S(2)}, u32[]{:S(2)}) collective-permute-start(bf16[4608,128]{1,0:T(8,128)(2,1)} %shard_map.99), channel_id=1, source_target_pairs={{0,2},{18,16},{1,3},{19,17},{4,6},{22,20},{5,7},{23,21},{8,10},{26... | collective-permute-start | bytes 3538952 | tf_op jit(solution)/shard_map/ppermute | solution.py:493
  311.5 29.9 %collective-permute-start.8 = (bf16[4608,128]{1,0:T(8,128)(2,1)}, bf16[4608,128]{1,0:T(8,128)(2,1)S(1)}, u32[]{:S(2)}, u32[]{:S(2)}) collective-permute-start(bf16[4608,128]{1,0:T(8,128)(2,1)} %shard_map.101.here_ref), channel_id=1, source_target_pairs={{2,18},{16,0},{3,19},{17,1},{6,22},{20,4},{7,23},{21,5},{10,26},{2... | collective-permute-start | bytes 3538952 | tf_op jit(solution)/shard_map/ppermute | solution.py:497
  (4 other events, 11.6 us)

commit v13 on v12

--- a/solution.py
+++ b/solution.py
@@ -46,7 +46,7 @@
 
 def pack_kernel(cuts, tile, z_ref, mask_ref, *refs):
     out_refs, (held_ref, z_sems, mask_sems, out_sems) = refs[:-4], refs[-4:]
-    part_refs, (*next_refs, own_ref) = out_refs[: len(cuts)], out_refs[len(cuts) :]
+    part_refs, (next_ref, own_ref) = out_refs[:-2], out_refs[-2:]
     upper = lax.axis_index("groups")
     home = upper == lax.axis_index("zh")
     per_strip = cuts[-1]
@@ -73,13 +73,10 @@
     ]
     stores += [
         pltpu.make_async_copy(
-            held_ref.at[1 - home.astype(jnp.int32), begin:end], next_ref, out_sems.at[len(cuts) + k]
-        )
-        for k, (begin, end, next_ref) in enumerate(
-            zip((0, per_strip - 1), (per_strip - 1, per_strip), next_refs)
-        )
+            held_ref.at[1 - home.astype(jnp.int32)], next_ref, out_sems.at[len(cuts)]
+        ),
+        pltpu.make_async_copy(held_ref.at[1], own_ref, out_sems.at[len(cuts) + 1]),
     ]
-    stores.append(pltpu.make_async_copy(held_ref.at[1], own_ref, out_sems.at[len(cuts) + 2]))
     for fetch in fetches:
         fetch.start()
     for fetch in fetches[: 2 * per_strip]:
@@ -382,7 +379,7 @@
 def pack(pair_act, mask, cuts, tile):
     per_strip = cuts[-1]
     shape = (tile + mask.shape[1], pair_act.shape[1])
-    outs = [end - begin for begin, end in zip((0, *cuts), cuts)] + [per_strip - 1, 1, per_strip]
+    outs = [end - begin for begin, end in zip((0, *cuts), cuts)] + [per_strip, per_strip]
     anywhere = pl.BlockSpec(memory_space=pltpu.HBM)
     return pl.pallas_call(
         functools.partial(pack_kernel, cuts, tile),
@@ -424,14 +421,12 @@
     cuts = (1, per_piece - 1, per_piece)
     marks = pair_mask.astype(jnp.bfloat16).reshape(2 * per_piece, tile // LANES, LANES)
     marks = jnp.pad(marks, ((0, 0), (0, 16 - tile // LANES), (0, 0)))
-    *z_parts, z_next, z_last, z_own = pack(pair_act.reshape(pixels, channels), marks, cuts, tile)
+    *z_parts, z_next, z_own = pack(pair_act.reshape(pixels, channels), marks, cuts, tile)
     z_far = []
     for part in z_parts[:-1]:
         over = lax.ppermute(part, LINE, ((1, 3), (2, 0)))
         z_far.append(lax.ppermute(over, LINE, ((0, 1), (3, 2))))
-    z_near, z_rest = (
-        lax.ppermute(part, LINE, ((1, 0), (2, 3), (0, 2), (3, 1))) for part in (z_next, z_last)
-    )
+    z_near = lax.ppermute(z_next, LINE, ((1, 0), (2, 3), (0, 2), (3, 1)))
     z_far.append(lax.ppermute(z_parts[-1], LINE, ((1, 2), (2, 1))))
     small = jnp.stack([input_gain, input_bias, output_gain, output_bias], axis=1)
     small = small.reshape(-1, channels).T
@@ -440,22 +435,17 @@
     ).transpose(0, 2, 1)
     fixed = (small, weights)
 
-    def first(start, steps, sources, kept):
-        return pixel_call(
-            functools.partial(first_kernel, peers, [served for _, _, *served in sources]),
-            [(a, at - begin, a.shape[0]) for a, at, begin, *_ in sources],
-            fixed, (2 * width, channels, 16), steps, tile, steps * tile * mult * 4 * width,
-            start=start, pixels=pixels, kept=kept,
-        )
-
-    soon = per_piece - 1
-    begun = first(0, soon, [(z_own, 0, 0, soon, True), (z_near, 0, 0, soon, False)], ())
-    sources = [(z_own, soon, 0, 1, True), (z_near, 0, 1, per_piece, True), (z_rest, 0, per_piece, per_piece + 1, True)]
-    sources += [(z_rest, 0, 0, 1, False)]
+    sources = [(z_own, 0, per_piece, True), (z_near, per_piece, 2 * per_piece, True)]
+    sources += [(z_near, 0, per_piece, False)]
     sources += [
-        (part, 0, 1 + begin, 1 + end, False) for part, begin, end in zip(z_far, (0, *cuts), cuts)
+        (part, per_piece + begin, per_piece + end, False)
+        for part, begin, end in zip(z_far, (0, *cuts), cuts)
     ]
-    sent, zt, mask = first(soon, per_piece + 1, sources, begun)
+    sent, zt, mask = pixel_call(
+        functools.partial(first_kernel, peers, [served for _, *served in sources]),
+        [(a, -begin, a.shape[0]) for a, begin, *_ in sources],
+        fixed, (2 * width, channels, 16), 2 * per_piece, tile, pixels * mult * 4 * width,
+    )
     wide = 2 * tile
     steps = pixels // wide
 

time: 350 us -> 353 us (level)
  waiting for transfers between devices: 121 us -> 125 us
    ppermute x2, waiting for transfers between devices: 20 us -> 31.3 us  [by_kernels(): z_far.append(lax.ppermute(over, LINE, ((0, 1), (3, 2))))]
    ppermute x2 -> x1, waiting for transfers between devices: 8.31 us -> 0.01 us  [by_kernels(): z_near = lax.ppermute(z_next, LINE, ((1, 0), (2, 3), (0, 2), (3, 1)))]
    pallas_call x7 -> x6, Pallas kernels: 32.7 us -> 31.8 us  [pixel_call(): pl.pallas_call(kernel, grid=(steps,), in_specs=in_specs, out_specs=[spec(...]
  transfers between devices with their start and end apart: 13 -> 12, of which waited for: 9 -> 7; matrix products, arithmetic and copies ran while one was open for 0% -> 0% of each run, Pallas kernels for 6% -> 5%
where the time goes in v13:
time: 353 us; the launch traced here: 348 us
  blocking collectives  129 us (37%)
  waiting for transfers between devices  125 us (35%)
  Pallas kernels  55.9 us (16%)
  starting transfers between devices  32.4 us (9%)
  local copies, waits for them, and re-layouts  4.88 us (1%)
    all_to_all x2, blocking collectives, exchange(): there = lax.all_to_all(array.reshape(peers, -1, array.shape[1]), CUBE, 0, 0)  129 us
    all_to_all x3, waiting for transfers between devices, exchange(): there = lax.all_to_all(array.reshape(peers, -1, array.shape[1]), CUBE, 0, 0)  48.1 us
    pallas_call x6, Pallas kernels, pixel_call(): pl.pallas_call(kernel, grid=(steps,), in_specs=in_specs, out_specs=[spec(...  31.8 us
    ppermute x2, waiting for transfers between devices, by_kernels(): z_far.append(lax.ppermute(over, LINE, ((0, 1), (3, 2))))  31.3 us
    ppermute x2, waiting for transfers between devices, by_kernels(): lax.ppermute(there, LINE, pairs)  29.4 us
    pallas_call x3, Pallas kernels, triangle_call(): pl.pallas_call(functools.partial(triangle_kernel, blocks, side, own, inco...  19.6 us
    ppermute x2, waiting for transfers between devices, by_kernels(): over = lax.ppermute(part, LINE, ((1, 3), (2, 0)))  15.9 us
    all_to_all x3, starting transfers between devices, exchange(): there = lax.all_to_all(array.reshape(peers, -1, array.shape[1]), CUBE, 0, 0)  15 us
  transfers between devices with their start and end apart: 12, of which 7 were waited for; matrix products, arithmetic and copies ran while one was open for 0% of the time, Pallas kernels for 5%

profile of v13, /device:TPU:20, one launch (start us, length us, event | category | flops | bytes accessed | tf_op | source)
XLA Modules:
  0.0 348.3 jit_solution(4230705865646014385)
XLA Ops:
  2.7 2.5 shard_map.91
  6.6 2.7 collective-permute-start
  11.3 12.5 %collective-permute-done.3 = bf16[2,1168,128]{2,1,0:T(8,128)(2,1)S(1)} collective-permute-done((bf16[2,1168,128]{2,1,0:T(8,128)(2,1)}, bf16[2,1168,128]{2,1,0:T(8,128)(2,1)S(1)}, u32[]{:S(2)}, u32[]{:S(2)}) %collective-permute-start.3) | collective-permute-done | bytes 598048 | tf_op jit(solution)/shard_map/ppermute | solution.py:427
  25.7 3.4 collective-permute-done.1
  30.5 31.3 %collective-permute-done.2.refs_3_ = bf16[1,1168,128]{2,1,0:T(8,128)(2,1)S(1)} collective-permute-done((bf16[1,1168,128]{2,1,0:T(8,128)(2,1)}, bf16[1,1168,128]{2,1,0:T(8,128)(2,1)S(1)}, u32[]{:S(2)}, u32[]{:S(2)}) %collective-permute-start.2) | collective-permute-done | bytes 299040 | tf_op jit(solution)/shard_map/ppermute | solution.py:428
  63.1 7.5 %shard_map.92 = (bf16[256,9216]{1,0:T(8,128)(2,1)}, bf16[128,9216]{1,0:T(8,128)(2,1)}, bf16[16,9216]{1,0:T(8,128)(2,1)}) custom-call(bf16[4,1168,128]{2,1,0:T(8,128)(2,1)S(1)} %copy-done.6, bf16[4,1168,128]{2,1,0:T(8,128)(2,1)S(1)} %collective-permute-done.refs_1_.refs_2_, bf16[4,1168,128]{2,1,0:T(8,128)(2,1)S(1)} %collective-permute-done.refs_1_.refs_2_, ...), custom_call_target="tpu_custom_call" | custom-call | flops 1207959552 | bytes 12091392 | tf_op jit(solution)/shard_map/pallas_call | solution.py:357
  70.6 70.8 %all_to_all.25 = bf16[16,16,9216]{2,1,0:T(8,128)(2,1)S(1)} all-to-all(bf16[16,16,9216]{2,1,0:T(8,128)(2,1)} %bitcast.31), channel_id=1, replica_groups=mesh['groups'=2,'row'=4,'zh'=2,'zl'=2] {'groups','row','zl'}, dimensions={0} | all-to-all | bytes 9437184 | tf_op jit(solution)/shard_map/all_to_all | solution.py:459
  141.4 7.6 %shard_map.93 = bf16[128,9216]{1,0:T(8,128)(2,1)} custom-call(bf16[256,9216]{1,0:T(8,128)(2,1)S(1)} %bitcast.22), custom_call_target="tpu_custom_call" | custom-call | flops 905969664 | bytes 14155776 | tf_op jit(solution)/shard_map/pallas_call | solution.py:306
  149.1 4.9 %all-to-all-start.1 = ((bf16[16,8,9216]{2,1,0:T(8,128)(2,1)}), bf16[16,8,9216]{2,1,0:T(8,128)(2,1)}, u32[]{:S(2)}, u32[]{:S(2)}) async-start(bf16[16,8,9216]{2,1,0:T(8,128)(2,1)} %bitcast.30), calls=%async_computation.1 | async-start | bytes 4718592 | tf_op jit(solution)/shard_map/all_to_all | solution.py:459
  154.0 3.8 %shard_map.94.refs_2_ = bf16[128,9216]{1,0:T(8,128)(2,1)} custom-call(bf16[128,9216]{1,0:T(8,128)(2,1)S(1)} %copy-done.3, f32[128,8]{1,0:T(8,128)S(1)} %bitcast.24, bf16[2,768,128]{2,1,0:T(8,128)(2,1)S(1)} %maximum_bitcast_fusion.refs_7_.refs_2_.refs_5_.refs_4_), custom_call_target="tpu_custom_call" | custom-call | flops 301989888 | bytes 7077888 | tf_op jit(solution)/shard_map/pallas_call | solution.py:357
  157.8 26.5 %all-to-all-done.1 = bf16[16,8,9216]{2,1,0:T(8,128)(2,1)} async-done(((bf16[16,8,9216]{2,1,0:T(8,128)(2,1)}), bf16[16,8,9216]{2,1,0:T(8,128)(2,1)}, u32[]{:S(2)}, u32[]{:S(2)}) %all-to-all-start.1) | async-done | bytes 2359328 | tf_op jit(solution)/shard_map/all_to_all | solution.py:459
  184.3 9.3 %shard_map.95 = (bf16[256,9216]{1,0:T(8,128)(2,1)}, bf16[128,9216]{1,0:T(8,128)(2,1)}) custom-call(bf16[128,9216]{1,0:T(8,128)(2,1)} %bitcast.11.refs_0_, bf16[128,9216]{1,0:T(8,128)(2,1)S(1)} %copy-done.3, bf16[128,9216]{1,0:T(8,128)(2,1)} %shard_map.94.refs_2_, bf16[16,9216]{1,0:T(8,128)(2,1)S(1)} %copy-done.7, f32[128,8]{1,0:T(8,128)S(1)} %bitcast.25, ...), custom_call_target="tpu_custom_call" | custom-call | flops 1509949440 | bytes 11796480 | tf_op jit(solution)/shard_map/pallas_call | solution.py:357
  193.6 58.4 %all_to_all.26 = bf16[16,16,9216]{2,1,0:T(8,128)(2,1)S(1)} all-to-all(bf16[16,16,9216]{2,1,0:T(8,128)(2,1)} %bitcast.32), channel_id=1, replica_groups=mesh['groups'=2,'row'=4,'zh'=2,'zl'=2] {'groups','row','zl'}, dimensions={0} | all-to-all | bytes 9437184 | tf_op jit(solution)/shard_map/all_to_all | solution.py:459
  252.0 6.0 %shard_map.96 = bf16[128,4608]{1,0:T(8,128)(2,1)} custom-call(bf16[256,9216]{1,0:T(8,128)(2,1)S(1)} %bitcast.20), custom_call_target="tpu_custom_call" | custom-call | flops 452984832 | bytes 14155776 | tf_op jit(solution)/shard_map/pallas_call | solution.py:306
  258.0 4.9 %all-to-all-start.3 = ((bf16[16,8,4608]{2,1,0:T(8,128)(2,1)}), bf16[16,8,4608]{2,1,0:T(8,128)(2,1)}, u32[]{:S(2)}, u32[]{:S(2)}) async-start(bf16[16,8,4608]{2,1,0:T(8,128)(2,1)} %bitcast.34), calls=%async_computation.3 | async-start | bytes 2359296 | tf_op jit(solution)/shard_map/all_to_all | solution.py:459
  262.8 3.8 %shard_map.97.refs_2_ = bf16[128,9216]{1,0:T(8,128)(2,1)} custom-call(bf16[128,9216]{1,0:T(8,128)(2,1)S(1)} %copy-done.2, f32[128,8]{1,0:T(8,128)S(1)} %bitcast.26, bf16[2,768,128]{2,1,0:T(8,128)(2,1)S(1)} %maximum_bitcast_fusion.refs_7_.refs_2_.refs_5_.refs_4_), custom_call_target="tpu_custom_call" | custom-call | flops 301989888 | bytes 7077888 | tf_op jit(solution)/shard_map/pallas_call | solution.py:357
  266.6 6.0 %shard_map.99 = bf16[128,4608]{1,0:T(8,128)(2,1)} custom-call(bf16[256,9216]{1,0:T(8,128)(2,1)S(1)} %bitcast.21), custom_call_target="tpu_custom_call" | custom-call | flops 452984832 | bytes 14155776 | tf_op jit(solution)/shard_map/pallas_call | solution.py:306
  272.6 6.0 %all-to-all-done.3 = bf16[16,8,4608]{2,1,0:T(8,128)(2,1)} async-done(((bf16[16,8,4608]{2,1,0:T(8,128)(2,1)}), bf16[16,8,4608]{2,1,0:T(8,128)(2,1)}, u32[]{:S(2)}, u32[]{:S(2)}) %all-to-all-start.3) | async-done | bytes 1179680 | tf_op jit(solution)/shard_map/all_to_all | solution.py:459
  278.6 3.7 %shard_map.98 = bf16[4608,128]{1,0:T(8,128)(2,1)} custom-call(bf16[128,4608]{1,0:T(8,128)(2,1)} %bitcast.15.refs_0_, bf16[128,9216]{1,0:T(8,128)(2,1)S(1)} %copy-done.2, bf16[128,9216]{1,0:T(8,128)(2,1)} %shard_map.97.refs_2_, f32[128,8]{1,0:T(8,128)S(1)} %bitcast.27, bf16[2,768,128]{2,1,0:T(8,128)(2,1)S(1)} %maximum_bitcast_fusion.refs_7_.refs_2_.refs_5_.refs_4_), custom_call_target="tpu_custom_call" | custom-call | flops 150994944 | bytes 3538944 | tf_op jit(solution)/shard_map/pallas_call | solution.py:357
  282.3 5.3 %all-to-all-start.4 = ((bf16[16,8,4608]{2,1,0:T(8,128)(2,1)}), bf16[16,8,4608]{2,1,0:T(8,128)(2,1)}, u32[]{:S(2)}, u32[]{:S(2)}) async-start(bf16[16,8,4608]{2,1,0:T(8,128)(2,1)} %bitcast.33), calls=%async_computation.4 | async-start | bytes 2359296 | tf_op jit(solution)/shard_map/all_to_all | solution.py:459
  289.2 5.8 %collective-permute-start.6 = (bf16[4608,128]{1,0:T(8,128)(2,1)}, bf16[4608,128]{1,0:T(8,128)(2,1)}, u32[]{:S(2)}, u32[]{:S(2)}) collective-permute-start(bf16[4608,128]{1,0:T(8,128)(2,1)} %shard_map.98), channel_id=1, source_target_pairs={{0,2},{18,16},{1,3},{19,17},{4,6},{22,20},{5,7},{23,21},{8,10},{26... | collective-permute-start | bytes 3538952 | tf_op jit(solution)/shard_map/ppermute | solution.py:483
  295.0 15.6 %all-to-all-done.4 = bf16[16,8,4608]{2,1,0:T(8,128)(2,1)} async-done(((bf16[16,8,4608]{2,1,0:T(8,128)(2,1)}), bf16[16,8,4608]{2,1,0:T(8,128)(2,1)}, u32[]{:S(2)}, u32[]{:S(2)}) %all-to-all-start.4) | async-done | bytes 1179680 | tf_op jit(solution)/shard_map/all_to_all | solution.py:459
  310.6 3.7 %shard_map.100.here_ref = bf16[4608,128]{1,0:T(8,128)(2,1)} custom-call(bf16[128,4608]{1,0:T(8,128)(2,1)} %bitcast.17.refs_0_, bf16[128,9216]{1,0:T(8,128)(2,1)S(1)} %copy-done.2, bf16[128,9216]{1,0:T(8,128)(2,1)} %shard_map.97.refs_2_, f32[128,8]{1,0:T(8,128)S(1)} %bitcast.28, bf16[2,768,128]{2,1,0:T(8,128)(2,1)S(1)} %maximum_bitcast_fusion.refs_7_.refs_2_.refs_5_.refs_4_), custom_call_target="tpu_custom_call" | custom-call | flops 150994944 | bytes 3538944 | tf_op jit(solution)/shard_map/pallas_call | solution.py:357
  315.6 29.4 %collective-permute-done.6.beside_ref = bf16[4608,128]{1,0:T(8,128)(2,1)} collective-permute-done((bf16[4608,128]{1,0:T(8,128)(2,1)}, bf16[4608,128]{1,0:T(8,128)(2,1)}, u32[]{:S(2)}, u32[]{:S(2)}) %collective-permute-start.6) | collective-permute-done | bytes 1179680 | tf_op jit(solution)/shard_map/ppermute | solution.py:483
  (55 shorter events, 16.6 us)
Async XLA Ops:
  0.0 25.1 %copy-start.11 = (f32[2,128]{1,0:T(2,128)S(1)}, f32[2,128]{1,0:T(2,128)}, u32[]{:S(2)}) copy-start(f32[2,128]{1,0:T(2,128)} %param.16) | copy-start | bytes 3076
  0.0 25.1 %copy-start.12 = (f32[2,128]{1,0:T(2,128)S(1)}, f32[2,128]{1,0:T(2,128)}, u32[]{:S(2)}) copy-start(f32[2,128]{1,0:T(2,128)} %param.15) | copy-start | bytes 3076
  0.0 25.1 %copy-start.13 = (f32[2,128]{1,0:T(2,128)S(1)}, f32[2,128]{1,0:T(2,128)}, u32[]{:S(2)}) copy-start(f32[2,128]{1,0:T(2,128)} %param.12) | copy-start | bytes 3076
  0.0 25.1 %copy-start.14 = (f32[2,128]{1,0:T(2,128)S(1)}, f32[2,128]{1,0:T(2,128)}, u32[]{:S(2)}) copy-start(f32[2,128]{1,0:T(2,128)} %param.11) | copy-start | bytes 3076
  0.0 25.2 %copy-start.9 = (bf16[2,128,128]{2,1,0:T(8,128)(2,1)S(1)}, bf16[2,128,128]{2,1,0:T(8,128)(2,1)}, u32[]{:S(2)}) copy-start(bf16[2,128,128]{2,1,0:T(8,128)(2,1)} %param.14) | copy-start | bytes 196612
  0.0 25.3 %copy-start.10 = (bf16[2,128,128]{2,1,0:T(8,128)(2,1)S(1)}, bf16[2,128,128]{2,1,0:T(8,128)(2,1)}, u32[]{:S(2)}) copy-start(bf16[2,128,128]{2,1,0:T(8,128)(2,1)} %param.17) | copy-start | bytes 196612
  2.7 22.8 %copy-start.8 = (bf16[2,128,512]{2,1,0:T(8,128)(2,1)S(1)}, bf16[2,128,512]{2,1,0:T(8,128)(2,1)}, u32[]{:S(2)}) copy-start(bf16[2,128,512]{2,1,0:T(8,128)(2,1)} %param.13) | copy-start | bytes 786436
  5.3 18.5 %collective-permute-start.3 = (bf16[2,1168,128]{2,1,0:T(8,128)(2,1)}, bf16[2,1168,128]{2,1,0:T(8,128)(2,1)S(1)}, u32[]{:S(2)}, u32[]{:S(2)}) collective-permute-start(bf16[2,1168,128]{2,1,0:T(8,128)(2,1)} %get-tuple-element.19), channel_id=1, source_target_pairs={{2,18},{16,0},{3,19},{17,1},{6,22},{20,4},{7,23},{21,5},{10,26},{2... | collective-permute-start | bytes 1794056 | tf_op jit(solution)/shard_map/ppermute | solution.py:427
  6.6 55.2 %collective-permute-start = (bf16[4,1168,128]{2,1,0:T(8,128)(2,1)}, bf16[4,1168,128]{2,1,0:T(8,128)(2,1)S(1)}, u32[]{:S(2)}, u32[]{:S(2)}) collective-permute-start(bf16[4,1168,128]{2,1,0:T(8,128)(2,1)} %get-tuple-element.17), channel_id=1, source_target_pairs={{2,0},{16,18},{0,16},{18,2},{3,1},{17,19},{1,17},{19,3},{6,4},{20,... | collective-permute-start | bytes 3588104 | tf_op jit(solution)/shard_map/ppermute | solution.py:429
  9.3 19.8 %collective-permute-start.1 = (bf16[1,1168,128]{2,1,0:T(8,128)(2,1)}, bf16[1,1168,128]{2,1,0:T(8,128)(2,1)}, u32[]{:S(2)}, u32[]{:S(2)}) collective-permute-start(bf16[1,1168,128]{2,1,0:T(8,128)(2,1)} %get-tuple-element.18), channel_id=1, source_target_pairs={{2,18},{16,0},{3,19},{17,1},{6,22},{20,4},{7,23},{21,5},{10,26},{2... | collective-permute-start | bytes 897032 | tf_op jit(solution)/shard_map/ppermute | solution.py:427
  10.6 19.9 %collective-permute-start.5 = (bf16[1,1168,128]{2,1,0:T(8,128)(2,1)}, bf16[1,1168,128]{2,1,0:T(8,128)(2,1)S(1)}, u32[]{:S(2)}, u32[]{:S(2)}) collective-permute-start(bf16[1,1168,128]{2,1,0:T(8,128)(2,1)} %get-tuple-element.20), channel_id=1, source_target_pairs={{2,16},{16,2},{3,17},{17,3},{6,20},{20,6},{7,21},{21,7},{10,24},{2... | collective-permute-start | bytes 897032 | tf_op jit(solution)/shard_map/ppermute | solution.py:430
  23.8 38.0 %collective-permute-start.4 = (bf16[2,1168,128]{2,1,0:T(8,128)(2,1)S(1)}, bf16[2,1168,128]{2,1,0:T(8,128)(2,1)S(1)}, u32[]{:S(2)}, u32[]{:S(2)}) collective-permute-start(bf16[2,1168,128]{2,1,0:T(8,128)(2,1)S(1)} %collective-permute-done.3), channel_id=1, source_target_pairs={{0,2},{18,16},{1,3},{19,17},{4,6},{22,20},{5,7},{23,21},{8,10},{26... | collective-permute-start | bytes 1794056 | tf_op jit(solution)/shard_map/ppermute | solution.py:428
  29.1 32.7 %collective-permute-start.2 = (bf16[1,1168,128]{2,1,0:T(8,128)(2,1)}, bf16[1,1168,128]{2,1,0:T(8,128)(2,1)S(1)}, u32[]{:S(2)}, u32[]{:S(2)}) collective-permute-start(bf16[1,1168,128]{2,1,0:T(8,128)(2,1)} %collective-permute-done.1), channel_id=1, source_target_pairs={{0,2},{18,16},{1,3},{19,17},{4,6},{22,20},{5,7},{23,21},{8,10},{26... | collective-permute-start | bytes 897032 | tf_op jit(solution)/shard_map/ppermute | solution.py:428
  149.1 4.9 %copy-start.3 = (bf16[128,9216]{1,0:T(8,128)(2,1)S(1)}, bf16[128,9216]{1,0:T(8,128)(2,1)}, u32[]{:S(2)}) copy-start(bf16[128,9216]{1,0:T(8,128)(2,1)} %get-tuple-element.22.refs_0_.refs_1_) | copy-start | bytes 7077892
  149.1 35.3 %all-to-all-start.1 = ((bf16[16,8,9216]{2,1,0:T(8,128)(2,1)}), bf16[16,8,9216]{2,1,0:T(8,128)(2,1)}, u32[]{:S(2)}, u32[]{:S(2)}) async-start(bf16[16,8,9216]{2,1,0:T(8,128)(2,1)} %bitcast.30), calls=%async_computation.1 | async-start | bytes 4718592 | tf_op jit(solution)/shard_map/all_to_all | solution.py:459
  154.0 30.3 %copy-start.7 = (bf16[16,9216]{1,0:T(8,128)(2,1)S(1)}, bf16[16,9216]{1,0:T(8,128)(2,1)}, u32[]{:S(2)}) copy-start(bf16[16,9216]{1,0:T(8,128)(2,1)} %get-tuple-element.23.refs_3_) | copy-start | bytes 884740
  252.0 6.0 %copy-start = (bf16[16,16,9216]{2,1,0:T(8,128)(2,1)}, bf16[16,16,9216]{2,1,0:T(8,128)(2,1)S(1)}, u32[]{:S(2)}) copy-start(bf16[16,16,9216]{2,1,0:T(8,128)(2,1)S(1)} %all_to_all.26) | copy-start | bytes 14155780
  258.0 4.9 %copy-start.2 = (bf16[128,9216]{1,0:T(8,128)(2,1)S(1)}, bf16[128,9216]{1,0:T(8,128)(2,1)}, u32[]{:S(2)}) copy-start(bf16[128,9216]{1,0:T(8,128)(2,1)} %get-tuple-element.25.refs_0_.refs_1_) | copy-start | bytes 7077892
  258.0 20.6 %all-to-all-start.3 = ((bf16[16,8,4608]{2,1,0:T(8,128)(2,1)}), bf16[16,8,4608]{2,1,0:T(8,128)(2,1)}, u32[]{:S(2)}, u32[]{:S(2)}) async-start(bf16[16,8,4608]{2,1,0:T(8,128)(2,1)} %bitcast.34), calls=%async_computation.3 | async-start | bytes 2359296 | tf_op jit(solution)/shard_map/all_to_all | solution.py:459
  262.8 3.8 %copy-start.1 = (bf16[16,16,9216]{2,1,0:T(8,128)(2,1)S(1)}, bf16[16,16,9216]{2,1,0:T(8,128)(2,1)}, u32[]{:S(2)}) copy-start(bf16[16,16,9216]{2,1,0:T(8,128)(2,1)} %copy-done) | copy-start | bytes 14155780
  282.3 28.3 %all-to-all-start.4 = ((bf16[16,8,4608]{2,1,0:T(8,128)(2,1)}), bf16[16,8,4608]{2,1,0:T(8,128)(2,1)}, u32[]{:S(2)}, u32[]{:S(2)}) async-start(bf16[16,8,4608]{2,1,0:T(8,128)(2,1)} %bitcast.33), calls=%async_computation.4 | async-start | bytes 2359296 | tf_op jit(solution)/shard_map/all_to_all | solution.py:459
  287.6 28.0 %collective-permute-start.8 = (bf16[4608,128]{1,0:T(8,128)(2,1)}, bf16[4608,128]{1,0:T(8,128)(2,1)}, u32[]{:S(2)}, u32[]{:S(2)}) collective-permute-start(bf16[4608,128]{1,0:T(8,128)(2,1)} %shard_map.98), channel_id=1, source_target_pairs={{2,16},{16,2},{3,17},{17,3},{6,20},{20,6},{7,21},{21,7},{10,24},{2... | collective-permute-start | bytes 3538952 | tf_op jit(solution)/shard_map/ppermute | solution.py:483
  289.2 55.7 %collective-permute-start.6 = (bf16[4608,128]{1,0:T(8,128)(2,1)}, bf16[4608,128]{1,0:T(8,128)(2,1)}, u32[]{:S(2)}, u32[]{:S(2)}) collective-permute-start(bf16[4608,128]{1,0:T(8,128)(2,1)} %shard_map.98), channel_id=1, source_target_pairs={{0,2},{18,16},{1,3},{19,17},{4,6},{22,20},{5,7},{23,21},{8,10},{26... | collective-permute-start | bytes 3538952 | tf_op jit(solution)/shard_map/ppermute | solution.py:483
  314.3 30.7 %collective-permute-start.7 = (bf16[4608,128]{1,0:T(8,128)(2,1)}, bf16[4608,128]{1,0:T(8,128)(2,1)S(1)}, u32[]{:S(2)}, u32[]{:S(2)}) collective-permute-start(bf16[4608,128]{1,0:T(8,128)(2,1)} %shard_map.100.here_ref), channel_id=1, source_target_pairs={{2,18},{16,0},{3,19},{17,1},{6,22},{20,4},{7,23},{21,5},{10,26},{2... | collective-permute-start | bytes 3538952 | tf_op jit(solution)/shard_map/ppermute | solution.py:487
  (3 other events, 4.2 us)

commit v14 on v10

--- a/solution.py
+++ b/solution.py
@@ -1,4 +1,5 @@
 import functools
+import itertools
 
 import jax
 import jax.numpy as jnp
@@ -9,6 +10,7 @@
 
 GRID = ("row", "col")
 LANES = 128
+FOLD = 2
 
 
 IN_GAIN, IN_BIAS, OUT_GAIN, OUT_BIAS = range(4)
@@ -189,11 +191,12 @@
 
     wanted = range(blocks) if len(made) == 2 else range(made[0] * half, (made[0] + 1) * half)
 
-    @pl.when(step < blocks)
+    @pl.when(step < blocks // FOLD)
     def _unpack():
-        upper, row_pair = step // half, lax.rem(step, half)
-        mirror = lax.rem(row_pair + zh, 2)
-        for r in range(2):
+        for fold, r in itertools.product(range(FOLD), range(2)):
+            upper, row_pair = (step * FOLD + fold) // half, lax.rem(step * FOLD + fold, half)
+            mirror = lax.rem(row_pair + zh, 2)
+            source = (fold * 2 + r) * half
             at = pl.multiple_of((row_pair * 2 + r) * side + upper * strip, 16)
             if incoming:
                 at_right = at
@@ -204,7 +207,7 @@
                     first = piece * strip * side
                     for group in range(strip // 4):
                         x = x_ref[
-                            (r * half + zl) * pair : (r * half + zl + 1) * pair,
+                            (source + zl) * pair : (source + zl + 1) * pair,
                             first + group * span : first + (group + 1) * span,
                         ].astype(jnp.float32)
                         a, b, c = x[:, :LANES], x[:, LANES : 2 * LANES], x[:, 2 * LANES :]
@@ -229,7 +232,7 @@
                             pl.ds(own + ch, strip, stride=pitch_rows), :
                         ].astype(jnp.bfloat16)
 
-    @pl.when(step == blocks - 1)
+    @pl.when(step == blocks // FOLD - 1)
     def _multiply():
         contract = ((0,), (0,)) if incoming else ((1,), (1,))
         for ch in range(own):
@@ -256,10 +259,10 @@
                             col * LANES : (col + 1) * LANES,
                         ]
 
-    @pl.when(step >= blocks)
+    @pl.when(step >= blocks // FOLD)
     def _repack():
-        for r in range(2):
-            place = (step - blocks) * 2 + r
+        for r in range(2 * FOLD):
+            place = (step - blocks // FOLD) * 2 * FOLD + r
             for piece in range(len(made)):
                 first = piece * strip * side
                 for group in range(strip // 4):
@@ -305,12 +308,15 @@
     right_rows = left_rows if incoming else padded
     return pl.pallas_call(
         functools.partial(triangle_kernel, blocks, side, own, incoming, made),
-        grid=(2 * blocks,),
+        grid=(2 * blocks // FOLD,),
         in_specs=[
-            pl.BlockSpec((blocks * pair, pixels), lambda i: (jnp.minimum(i, blocks - 1), 0))
+            pl.BlockSpec(
+                (FOLD * blocks * pair, pixels), lambda i: (jnp.minimum(i, blocks // FOLD - 1), 0)
+            )
         ],
         out_specs=pl.BlockSpec(
-            (2 * pair, pixels // 2 * len(made)), lambda i: (jnp.maximum(i - blocks, 0), 0)
+            (2 * FOLD * pair, pixels // 2 * len(made)),
+            lambda i: (jnp.maximum(i - blocks // FOLD, 0), 0),
         ),
         out_shape=pltpu.HBM((blocks * blocks * own, pixels // 2 * len(made)), jnp.bfloat16),
         scratch_shapes=[

time: 347 us -> 357 us (1.029); the launches traced: 342 us -> 356 us
  waiting for transfers between devices: 121 us -> 137 us
    all_to_all x3, waiting for transfers between devices: 46.8 us -> 64.6 us  [exchange(): there = lax.all_to_all(array.reshape(peers, -1, array.shape[1]), CUBE, 0, 0)]
    ppermute x2, waiting for transfers between devices: 30.7 us -> 13.6 us  [by_kernels(): lax.ppermute(there, LINE, pairs)]
    ppermute x1, waiting for transfers between devices: 0.01 us -> 15 us  [by_kernels(): back = lax.ppermute(here, LINE, ((1, 3), (2, 0)))]
  transfers between devices with their start and end apart: 12 -> 12, of which waited for: 8 -> 9; matrix products, arithmetic and copies ran while one was open for 0% -> 0% of each run, Pallas kernels for 6% -> 6%
where the time goes in v14:
time: 357 us; the launch traced here: 356 us
  waiting for transfers between devices  137 us (38%)
  blocking collectives  128 us (36%)
  Pallas kernels  54.5 us (15%)
  starting transfers between devices  30.5 us (9%)
  local copies, waits for them, and re-layouts  4.88 us (1%)
    all_to_all x2, blocking collectives, exchange(): there = lax.all_to_all(array.reshape(peers, -1, array.shape[1]), CUBE, 0, 0)  128 us
    all_to_all x3, waiting for transfers between devices, exchange(): there = lax.all_to_all(array.reshape(peers, -1, array.shape[1]), CUBE, 0, 0)  64.6 us
    pallas_call x7, Pallas kernels, pixel_call(): pl.pallas_call(kernel, grid=(steps,), in_specs=in_specs, out_specs=[spec(...  32.5 us
    ppermute x2, waiting for transfers between devices, by_kernels(): z_far.append(lax.ppermute(over, LINE, ((0, 1), (3, 2))))  20.9 us
    ppermute x2, waiting for transfers between devices, by_kernels(): over = lax.ppermute(part, LINE, ((1, 3), (2, 0)))  18.3 us
    pallas_call x3, Pallas kernels, triangle_call(): pl.pallas_call(functools.partial(triangle_kernel, blocks, side, own, inco...  17.6 us
    all_to_all x3, starting transfers between devices, exchange(): there = lax.all_to_all(array.reshape(peers, -1, array.shape[1]), CUBE, 0, 0)  15 us
    ppermute x1, waiting for transfers between devices, by_kernels(): back = lax.ppermute(here, LINE, ((1, 3), (2, 0)))  15 us
  transfers between devices with their start and end apart: 12, of which 9 were waited for; matrix products, arithmetic and copies ran while one was open for 0% of the time, Pallas kernels for 6%

profile of v14, /device:TPU:20, one launch (start us, length us, event | category | flops | bytes accessed | tf_op | source)
XLA Modules:
  0.0 356.0 jit_solution(16401853488534448735)
XLA Ops:
  9.7 14.6 %collective-permute-done.3 = bf16[2,1168,128]{2,1,0:T(8,128)(2,1)S(1)} collective-permute-done((bf16[2,1168,128]{2,1,0:T(8,128)(2,1)}, bf16[2,1168,128]{2,1,0:T(8,128)(2,1)S(1)}, u32[]{:S(2)}, u32[]{:S(2)}) %collective-permute-start.3) | collective-permute-done | bytes 598048 | tf_op jit(solution)/shard_map/ppermute | solution.py:433
  31.0 4.8 %collective-permute-done.refs_1_.refs_0_ = bf16[4,1168,128]{2,1,0:T(8,128)(2,1)S(1)} collective-permute-done((bf16[4,1168,128]{2,1,0:T(8,128)(2,1)}, bf16[4,1168,128]{2,1,0:T(8,128)(2,1)S(1)}, u32[]{:S(2)}, u32[]{:S(2)}) %collective-permute-start) | collective-permute-done | bytes 1196064 | tf_op jit(solution)/shard_map/ppermute | solution.py:435
  37.0 4.1 %shard_map.92 = (bf16[256,9216]{1,0:T(8,128)(2,1)}, bf16[128,9216]{1,0:T(8,128)(2,1)}, bf16[16,9216]{1,0:T(8,128)(2,1)}) custom-call(bf16[4,1168,128]{2,1,0:T(8,128)(2,1)S(1)} %copy-done.6, bf16[4,1168,128]{2,1,0:T(8,128)(2,1)S(1)} %collective-permute-done.refs_1_.refs_0_, f32[128,8]{1,0:T(8,128)S(1)} %bitcast.23, ...), custom_call_target="tpu_custom_call" | custom-call | flops 603979776 | bytes 6045696 | tf_op jit(solution)/shard_map/pallas_call | solution.py:363
  41.1 20.9 %collective-permute-done.2.refs_1_ = bf16[1,1168,128]{2,1,0:T(8,128)(2,1)S(1)} collective-permute-done((bf16[1,1168,128]{2,1,0:T(8,128)(2,1)}, bf16[1,1168,128]{2,1,0:T(8,128)(2,1)S(1)}, u32[]{:S(2)}, u32[]{:S(2)}) %collective-permute-start.2) | collective-permute-done | bytes 299040 | tf_op jit(solution)/shard_map/ppermute | solution.py:434
  62.0 4.1 %shard_map.93 = (bf16[256,9216]{1,0:T(8,128)(2,1)}, bf16[128,9216]{1,0:T(8,128)(2,1)}, bf16[16,9216]{1,0:T(8,128)(2,1)}) custom-call(bf16[4,1168,128]{2,1,0:T(8,128)(2,1)S(1)} %collective-permute-done.refs_1_.refs_0_, bf16[1,1168,128]{2,1,0:T(8,128)(2,1)S(1)} %collective-permute-done.2.refs_1_, ...), custom_call_target="tpu_custom_call", output_to_operand_aliasing={{0}: (6, {}), {1}: (7, {}), {2}: (8, {})} | custom-call | flops 603979776 | bytes 6045696 | tf_op jit(solution)/shard_map/pallas_call | solution.py:363
  66.2 69.3 %all_to_all.25 = bf16[16,16,9216]{2,1,0:T(8,128)(2,1)S(1)} all-to-all(bf16[16,16,9216]{2,1,0:T(8,128)(2,1)} %bitcast.31), channel_id=1, replica_groups=mesh['groups'=2,'row'=4,'zh'=2,'zl'=2] {'groups','row','zl'}, dimensions={0} | all-to-all | bytes 9437184 | tf_op jit(solution)/shard_map/all_to_all | solution.py:465
  135.5 7.0 %shard_map.94 = bf16[128,9216]{1,0:T(8,128)(2,1)} custom-call(bf16[256,9216]{1,0:T(8,128)(2,1)S(1)} %bitcast.22), custom_call_target="tpu_custom_call" | custom-call | flops 905969664 | bytes 14155776 | tf_op jit(solution)/shard_map/pallas_call | solution.py:309
  142.5 4.9 %all-to-all-start.1 = ((bf16[16,8,9216]{2,1,0:T(8,128)(2,1)}), bf16[16,8,9216]{2,1,0:T(8,128)(2,1)}, u32[]{:S(2)}, u32[]{:S(2)}) async-start(bf16[16,8,9216]{2,1,0:T(8,128)(2,1)} %bitcast.32), calls=%async_computation.1 | async-start | bytes 4718592 | tf_op jit(solution)/shard_map/all_to_all | solution.py:465
  147.4 3.8 %shard_map.95.refs_2_ = bf16[128,9216]{1,0:T(8,128)(2,1)} custom-call(bf16[128,9216]{1,0:T(8,128)(2,1)S(1)} %copy-done.3, f32[128,8]{1,0:T(8,128)S(1)} %bitcast.25, bf16[2,768,128]{2,1,0:T(8,128)(2,1)S(1)} %maximum_bitcast_fusion.refs_3_.refs_5_.refs_2_.refs_4_), custom_call_target="tpu_custom_call" | custom-call | flops 301989888 | bytes 7077888 | tf_op jit(solution)/shard_map/pallas_call | solution.py:363
  151.2 26.5 %all-to-all-done.1 = bf16[16,8,9216]{2,1,0:T(8,128)(2,1)} async-done(((bf16[16,8,9216]{2,1,0:T(8,128)(2,1)}), bf16[16,8,9216]{2,1,0:T(8,128)(2,1)}, u32[]{:S(2)}, u32[]{:S(2)}) %all-to-all-start.1) | async-done | bytes 2359328 | tf_op jit(solution)/shard_map/all_to_all | solution.py:465
  177.8 9.3 %shard_map.96 = (bf16[256,9216]{1,0:T(8,128)(2,1)}, bf16[128,9216]{1,0:T(8,128)(2,1)}) custom-call(bf16[128,9216]{1,0:T(8,128)(2,1)} %bitcast.11.refs_0_, bf16[128,9216]{1,0:T(8,128)(2,1)S(1)} %copy-done.3, bf16[128,9216]{1,0:T(8,128)(2,1)} %shard_map.95.refs_2_, bf16[16,9216]{1,0:T(8,128)(2,1)S(1)} %copy-done.7, f32[128,8]{1,0:T(8,128)S(1)} %bitcast.26, ...), custom_call_target="tpu_custom_call" | custom-call | flops 1509949440 | bytes 11796480 | tf_op jit(solution)/shard_map/pallas_call | solution.py:363
  187.0 58.4 %all_to_all.26 = bf16[16,16,9216]{2,1,0:T(8,128)(2,1)S(1)} all-to-all(bf16[16,16,9216]{2,1,0:T(8,128)(2,1)} %bitcast.33), channel_id=1, replica_groups=mesh['groups'=2,'row'=4,'zh'=2,'zl'=2] {'groups','row','zl'}, dimensions={0} | all-to-all | bytes 9437184 | tf_op jit(solution)/shard_map/all_to_all | solution.py:465
  245.4 5.3 %shard_map.97 = bf16[128,4608]{1,0:T(8,128)(2,1)} custom-call(bf16[256,9216]{1,0:T(8,128)(2,1)S(1)} %bitcast.20), custom_call_target="tpu_custom_call" | custom-call | flops 452984832 | bytes 14155776 | tf_op jit(solution)/shard_map/pallas_call | solution.py:309
  250.7 4.9 %all-to-all-start.3 = ((bf16[16,8,4608]{2,1,0:T(8,128)(2,1)}), bf16[16,8,4608]{2,1,0:T(8,128)(2,1)}, u32[]{:S(2)}, u32[]{:S(2)}) async-start(bf16[16,8,4608]{2,1,0:T(8,128)(2,1)} %bitcast.35), calls=%async_computation.3 | async-start | bytes 2359296 | tf_op jit(solution)/shard_map/all_to_all | solution.py:465
  255.6 3.8 %shard_map.98.refs_2_ = bf16[128,9216]{1,0:T(8,128)(2,1)} custom-call(bf16[128,9216]{1,0:T(8,128)(2,1)S(1)} %copy-done.2, f32[128,8]{1,0:T(8,128)S(1)} %bitcast.27, bf16[2,768,128]{2,1,0:T(8,128)(2,1)S(1)} %maximum_bitcast_fusion.refs_3_.refs_5_.refs_2_.refs_4_), custom_call_target="tpu_custom_call" | custom-call | flops 301989888 | bytes 7077888 | tf_op jit(solution)/shard_map/pallas_call | solution.py:363
  259.4 5.3 %shard_map.100 = bf16[128,4608]{1,0:T(8,128)(2,1)} custom-call(bf16[256,9216]{1,0:T(8,128)(2,1)S(1)} %bitcast.21), custom_call_target="tpu_custom_call" | custom-call | flops 452984832 | bytes 14155776 | tf_op jit(solution)/shard_map/pallas_call | solution.py:309
  264.6 6.7 %all-to-all-done.3 = bf16[16,8,4608]{2,1,0:T(8,128)(2,1)} async-done(((bf16[16,8,4608]{2,1,0:T(8,128)(2,1)}), bf16[16,8,4608]{2,1,0:T(8,128)(2,1)}, u32[]{:S(2)}, u32[]{:S(2)}) %all-to-all-start.3) | async-done | bytes 1179680 | tf_op jit(solution)/shard_map/all_to_all | solution.py:465
  271.3 3.7 %shard_map.99 = bf16[4608,128]{1,0:T(8,128)(2,1)} custom-call(bf16[128,4608]{1,0:T(8,128)(2,1)} %bitcast.15.refs_0_, bf16[128,9216]{1,0:T(8,128)(2,1)S(1)} %copy-done.2, bf16[128,9216]{1,0:T(8,128)(2,1)} %shard_map.98.refs_2_, f32[128,8]{1,0:T(8,128)S(1)} %bitcast.28, bf16[2,768,128]{2,1,0:T(8,128)(2,1)S(1)} %maximum_bitcast_fusion.refs_3_.refs_5_.refs_2_.refs_4_), custom_call_target="tpu_custom_call" | custom-call | flops 150994944 | bytes 3538944 | tf_op jit(solution)/shard_map/pallas_call | solution.py:363
  275.0 5.3 %all-to-all-start.4 = ((bf16[16,8,4608]{2,1,0:T(8,128)(2,1)}), bf16[16,8,4608]{2,1,0:T(8,128)(2,1)}, u32[]{:S(2)}, u32[]{:S(2)}) async-start(bf16[16,8,4608]{2,1,0:T(8,128)(2,1)} %bitcast.34), calls=%async_computation.4 | async-start | bytes 2359296 | tf_op jit(solution)/shard_map/all_to_all | solution.py:465
  282.0 5.8 %collective-permute-start.6 = (bf16[4608,128]{1,0:T(8,128)(2,1)}, bf16[4608,128]{1,0:T(8,128)(2,1)}, u32[]{:S(2)}, u32[]{:S(2)}) collective-permute-start(bf16[4608,128]{1,0:T(8,128)(2,1)} %shard_map.99), channel_id=1, source_target_pairs={{0,2},{18,16},{1,3},{19,17},{4,6},{22,20},{5,7},{23,21},{8,10},{26... | collective-permute-start | bytes 3538952 | tf_op jit(solution)/shard_map/ppermute | solution.py:489
  287.7 31.4 %all-to-all-done.4 = bf16[16,8,4608]{2,1,0:T(8,128)(2,1)} async-done(((bf16[16,8,4608]{2,1,0:T(8,128)(2,1)}), bf16[16,8,4608]{2,1,0:T(8,128)(2,1)}, u32[]{:S(2)}, u32[]{:S(2)}) %all-to-all-start.4) | async-done | bytes 1179680 | tf_op jit(solution)/shard_map/all_to_all | solution.py:465
  319.1 3.7 %shard_map.101.here_ref = bf16[4608,128]{1,0:T(8,128)(2,1)} custom-call(bf16[128,4608]{1,0:T(8,128)(2,1)} %bitcast.17.refs_0_, bf16[128,9216]{1,0:T(8,128)(2,1)S(1)} %copy-done.2, bf16[128,9216]{1,0:T(8,128)(2,1)} %shard_map.98.refs_2_, f32[128,8]{1,0:T(8,128)S(1)} %bitcast.29, bf16[2,768,128]{2,1,0:T(8,128)(2,1)S(1)} %maximum_bitcast_fusion.refs_3_.refs_5_.refs_2_.refs_4_), custom_call_target="tpu_custom_call" | custom-call | flops 150994944 | bytes 3538944 | tf_op jit(solution)/shard_map/pallas_call | solution.py:363
  324.1 13.6 %collective-permute-done.6.beside_ref = bf16[4608,128]{1,0:T(8,128)(2,1)} collective-permute-done((bf16[4608,128]{1,0:T(8,128)(2,1)}, bf16[4608,128]{1,0:T(8,128)(2,1)}, u32[]{:S(2)}, u32[]{:S(2)}) %collective-permute-start.6) | collective-permute-done | bytes 1179680 | tf_op jit(solution)/shard_map/ppermute | solution.py:489
  337.7 15.0 %collective-permute-done.7.back_ref = bf16[4608,128]{1,0:T(8,128)(2,1)S(1)} collective-permute-done((bf16[4608,128]{1,0:T(8,128)(2,1)}, bf16[4608,128]{1,0:T(8,128)(2,1)S(1)}, u32[]{:S(2)}, u32[]{:S(2)}) %collective-permute-start.7) | collective-permute-done | bytes 1179680 | tf_op jit(solution)/shard_map/ppermute | solution.py:493
  (56 shorter events, 23.6 us)
Async XLA Ops:
  0.0 9.1 %copy-start.11 = (f32[2,128]{1,0:T(2,128)S(1)}, f32[2,128]{1,0:T(2,128)}, u32[]{:S(2)}) copy-start(f32[2,128]{1,0:T(2,128)} %param.16) | copy-start | bytes 3076
  0.0 9.1 %copy-start.12 = (f32[2,128]{1,0:T(2,128)S(1)}, f32[2,128]{1,0:T(2,128)}, u32[]{:S(2)}) copy-start(f32[2,128]{1,0:T(2,128)} %param.15) | copy-start | bytes 3076
  0.0 9.1 %copy-start.13 = (f32[2,128]{1,0:T(2,128)S(1)}, f32[2,128]{1,0:T(2,128)}, u32[]{:S(2)}) copy-start(f32[2,128]{1,0:T(2,128)} %param.12) | copy-start | bytes 3076
  0.0 9.1 %copy-start.14 = (f32[2,128]{1,0:T(2,128)S(1)}, f32[2,128]{1,0:T(2,128)}, u32[]{:S(2)}) copy-start(f32[2,128]{1,0:T(2,128)} %param.11) | copy-start | bytes 3076
  0.0 9.3 %copy-start.9 = (bf16[2,128,128]{2,1,0:T(8,128)(2,1)S(1)}, bf16[2,128,128]{2,1,0:T(8,128)(2,1)}, u32[]{:S(2)}) copy-start(bf16[2,128,128]{2,1,0:T(8,128)(2,1)} %param.14) | copy-start | bytes 196612
  0.0 9.4 %copy-start.10 = (bf16[2,128,128]{2,1,0:T(8,128)(2,1)S(1)}, bf16[2,128,128]{2,1,0:T(8,128)(2,1)}, u32[]{:S(2)}) copy-start(bf16[2,128,128]{2,1,0:T(8,128)(2,1)} %param.17) | copy-start | bytes 196612
  2.7 6.8 %copy-start.8 = (bf16[2,128,512]{2,1,0:T(8,128)(2,1)S(1)}, bf16[2,128,512]{2,1,0:T(8,128)(2,1)}, u32[]{:S(2)}) copy-start(bf16[2,128,512]{2,1,0:T(8,128)(2,1)} %param.13) | copy-start | bytes 786436
  5.3 30.5 %collective-permute-start = (bf16[4,1168,128]{2,1,0:T(8,128)(2,1)}, bf16[4,1168,128]{2,1,0:T(8,128)(2,1)S(1)}, u32[]{:S(2)}, u32[]{:S(2)}) collective-permute-start(bf16[4,1168,128]{2,1,0:T(8,128)(2,1)} %get-tuple-element.19), channel_id=1, source_target_pairs={{2,0},{16,18},{0,16},{18,2},{3,1},{17,19},{1,17},{19,3},{6,4},{20,... | collective-permute-start | bytes 3588104 | tf_op jit(solution)/shard_map/ppermute | solution.py:435
  5.8 18.5 %collective-permute-start.3 = (bf16[2,1168,128]{2,1,0:T(8,128)(2,1)}, bf16[2,1168,128]{2,1,0:T(8,128)(2,1)S(1)}, u32[]{:S(2)}, u32[]{:S(2)}) collective-permute-start(bf16[2,1168,128]{2,1,0:T(8,128)(2,1)} %get-tuple-element.21), channel_id=1, source_target_pairs={{2,18},{16,0},{3,19},{17,1},{6,22},{20,4},{7,23},{21,5},{10,26},{2... | collective-permute-start | bytes 1794056 | tf_op jit(solution)/shard_map/ppermute | solution.py:433
  7.1 22.3 %collective-permute-start.1 = (bf16[1,1168,128]{2,1,0:T(8,128)(2,1)}, bf16[1,1168,128]{2,1,0:T(8,128)(2,1)}, u32[]{:S(2)}, u32[]{:S(2)}) collective-permute-start(bf16[1,1168,128]{2,1,0:T(8,128)(2,1)} %get-tuple-element.20), channel_id=1, source_target_pairs={{2,18},{16,0},{3,19},{17,1},{6,22},{20,4},{7,23},{21,5},{10,26},{2... | collective-permute-start | bytes 897032 | tf_op jit(solution)/shard_map/ppermute | solution.py:433
  8.4 32.7 %collective-permute-start.5 = (bf16[1,1168,128]{2,1,0:T(8,128)(2,1)}, bf16[1,1168,128]{2,1,0:T(8,128)(2,1)S(1)}, u32[]{:S(2)}, u32[]{:S(2)}) collective-permute-start(bf16[1,1168,128]{2,1,0:T(8,128)(2,1)} %get-tuple-element.22), channel_id=1, source_target_pairs={{2,16},{16,2},{3,17},{17,3},{6,20},{20,6},{7,21},{21,7},{10,24},{2... | collective-permute-start | bytes 897032 | tf_op jit(solution)/shard_map/ppermute | solution.py:436
  24.3 37.7 %collective-permute-start.4 = (bf16[2,1168,128]{2,1,0:T(8,128)(2,1)S(1)}, bf16[2,1168,128]{2,1,0:T(8,128)(2,1)S(1)}, u32[]{:S(2)}, u32[]{:S(2)}) collective-permute-start(bf16[2,1168,128]{2,1,0:T(8,128)(2,1)S(1)} %collective-permute-done.3), channel_id=1, source_target_pairs={{0,2},{18,16},{1,3},{19,17},{4,6},{22,20},{5,7},{23,21},{8,10},{26... | collective-permute-start | bytes 1794056 | tf_op jit(solution)/shard_map/ppermute | solution.py:434
  29.4 32.6 %collective-permute-start.2 = (bf16[1,1168,128]{2,1,0:T(8,128)(2,1)}, bf16[1,1168,128]{2,1,0:T(8,128)(2,1)S(1)}, u32[]{:S(2)}, u32[]{:S(2)}) collective-permute-start(bf16[1,1168,128]{2,1,0:T(8,128)(2,1)} %collective-permute-done.1), channel_id=1, source_target_pairs={{0,2},{18,16},{1,3},{19,17},{4,6},{22,20},{5,7},{23,21},{8,10},{26... | collective-permute-start | bytes 897032 | tf_op jit(solution)/shard_map/ppermute | solution.py:434
  142.5 4.9 %copy-start.3 = (bf16[128,9216]{1,0:T(8,128)(2,1)S(1)}, bf16[128,9216]{1,0:T(8,128)(2,1)}, u32[]{:S(2)}) copy-start(bf16[128,9216]{1,0:T(8,128)(2,1)} %get-tuple-element.28.refs_0_.refs_1_) | copy-start | bytes 7077892
  142.5 35.3 %all-to-all-start.1 = ((bf16[16,8,9216]{2,1,0:T(8,128)(2,1)}), bf16[16,8,9216]{2,1,0:T(8,128)(2,1)}, u32[]{:S(2)}, u32[]{:S(2)}) async-start(bf16[16,8,9216]{2,1,0:T(8,128)(2,1)} %bitcast.32), calls=%async_computation.1 | async-start | bytes 4718592 | tf_op jit(solution)/shard_map/all_to_all | solution.py:465
  147.4 30.3 %copy-start.7 = (bf16[16,9216]{1,0:T(8,128)(2,1)S(1)}, bf16[16,9216]{1,0:T(8,128)(2,1)}, u32[]{:S(2)}) copy-start(bf16[16,9216]{1,0:T(8,128)(2,1)} %get-tuple-element.29.refs_3_) | copy-start | bytes 884740
  245.4 5.3 %copy-start = (bf16[16,16,9216]{2,1,0:T(8,128)(2,1)}, bf16[16,16,9216]{2,1,0:T(8,128)(2,1)S(1)}, u32[]{:S(2)}) copy-start(bf16[16,16,9216]{2,1,0:T(8,128)(2,1)S(1)} %all_to_all.26) | copy-start | bytes 14155780
  250.7 4.9 %copy-start.2 = (bf16[128,9216]{1,0:T(8,128)(2,1)S(1)}, bf16[128,9216]{1,0:T(8,128)(2,1)}, u32[]{:S(2)}) copy-start(bf16[128,9216]{1,0:T(8,128)(2,1)} %get-tuple-element.31.refs_0_.refs_1_) | copy-start | bytes 7077892
  250.7 20.6 %all-to-all-start.3 = ((bf16[16,8,4608]{2,1,0:T(8,128)(2,1)}), bf16[16,8,4608]{2,1,0:T(8,128)(2,1)}, u32[]{:S(2)}, u32[]{:S(2)}) async-start(bf16[16,8,4608]{2,1,0:T(8,128)(2,1)} %bitcast.35), calls=%async_computation.3 | async-start | bytes 2359296 | tf_op jit(solution)/shard_map/all_to_all | solution.py:465
  255.6 3.8 %copy-start.1 = (bf16[16,16,9216]{2,1,0:T(8,128)(2,1)S(1)}, bf16[16,16,9216]{2,1,0:T(8,128)(2,1)}, u32[]{:S(2)}) copy-start(bf16[16,16,9216]{2,1,0:T(8,128)(2,1)} %copy-done) | copy-start | bytes 14155780
  275.0 44.1 %all-to-all-start.4 = ((bf16[16,8,4608]{2,1,0:T(8,128)(2,1)}), bf16[16,8,4608]{2,1,0:T(8,128)(2,1)}, u32[]{:S(2)}, u32[]{:S(2)}) async-start(bf16[16,8,4608]{2,1,0:T(8,128)(2,1)} %bitcast.34), calls=%async_computation.4 | async-start | bytes 2359296 | tf_op jit(solution)/shard_map/all_to_all | solution.py:465
  280.3 43.8 %collective-permute-start.8 = (bf16[4608,128]{1,0:T(8,128)(2,1)}, bf16[4608,128]{1,0:T(8,128)(2,1)}, u32[]{:S(2)}, u32[]{:S(2)}) collective-permute-start(bf16[4608,128]{1,0:T(8,128)(2,1)} %shard_map.99), channel_id=1, source_target_pairs={{2,16},{16,2},{3,17},{17,3},{6,20},{20,6},{7,21},{21,7},{10,24},{2... | collective-permute-start | bytes 3538952 | tf_op jit(solution)/shard_map/ppermute | solution.py:489
  282.0 55.7 %collective-permute-start.6 = (bf16[4608,128]{1,0:T(8,128)(2,1)}, bf16[4608,128]{1,0:T(8,128)(2,1)}, u32[]{:S(2)}, u32[]{:S(2)}) collective-permute-start(bf16[4608,128]{1,0:T(8,128)(2,1)} %shard_map.99), channel_id=1, source_target_pairs={{0,2},{18,16},{1,3},{19,17},{4,6},{22,20},{5,7},{23,21},{8,10},{26... | collective-permute-start | bytes 3538952 | tf_op jit(solution)/shard_map/ppermute | solution.py:489
  322.8 29.9 %collective-permute-start.7 = (bf16[4608,128]{1,0:T(8,128)(2,1)}, bf16[4608,128]{1,0:T(8,128)(2,1)S(1)}, u32[]{:S(2)}, u32[]{:S(2)}) collective-permute-start(bf16[4608,128]{1,0:T(8,128)(2,1)} %shard_map.101.here_ref), channel_id=1, source_target_pairs={{2,18},{16,0},{3,19},{17,1},{6,22},{20,4},{7,23},{21,5},{10,26},{2... | collective-permute-start | bytes 3538952 | tf_op jit(solution)/shard_map/ppermute | solution.py:493
  (3 other events, 4.2 us)

commit v15 on v14

--- a/solution.py
+++ b/solution.py
@@ -10,7 +10,6 @@
 
 GRID = ("row", "col")
 LANES = 128
-FOLD = 2
 
 
 IN_GAIN, IN_BIAS, OUT_GAIN, OUT_BIAS = range(4)
@@ -178,7 +177,7 @@
     pl.when(jnp.logical_not(home))(lambda: move(beside_ref, across_ref))
 
 
-def triangle_kernel(blocks, side, own, incoming, made, x_ref, y_ref, left_ref, right_ref, rows_ref, tiles_ref):
+def triangle_kernel(blocks, side, own, incoming, made, folded, x_ref, y_ref, left_ref, right_ref, rows_ref, tiles_ref):
     step = pl.program_id(0)
     zh = lax.axis_index("zh")
     pair = 2 * own
@@ -191,10 +190,10 @@
 
     wanted = range(blocks) if len(made) == 2 else range(made[0] * half, (made[0] + 1) * half)
 
-    @pl.when(step < blocks // FOLD)
+    @pl.when(step < blocks // folded)
     def _unpack():
-        for fold, r in itertools.product(range(FOLD), range(2)):
-            upper, row_pair = (step * FOLD + fold) // half, lax.rem(step * FOLD + fold, half)
+        for fold, r in itertools.product(range(folded), range(2)):
+            upper, row_pair = (step * folded + fold) // half, lax.rem(step * folded + fold, half)
             mirror = lax.rem(row_pair + zh, 2)
             source = (fold * 2 + r) * half
             at = pl.multiple_of((row_pair * 2 + r) * side + upper * strip, 16)
@@ -232,7 +231,7 @@
                             pl.ds(own + ch, strip, stride=pitch_rows), :
                         ].astype(jnp.bfloat16)
 
-    @pl.when(step == blocks // FOLD - 1)
+    @pl.when(step == blocks // folded - 1)
     def _multiply():
         contract = ((0,), (0,)) if incoming else ((1,), (1,))
         for ch in range(own):
@@ -259,10 +258,10 @@
                             col * LANES : (col + 1) * LANES,
                         ]
 
-    @pl.when(step >= blocks // FOLD)
+    @pl.when(step >= blocks // folded)
     def _repack():
-        for r in range(2 * FOLD):
-            place = (step - blocks // FOLD) * 2 * FOLD + r
+        for r in range(2 * folded):
+            place = (step - blocks // folded) * 2 * folded + r
             for piece in range(len(made)):
                 first = piece * strip * side
                 for group in range(strip // 4):
@@ -300,6 +299,7 @@
 
 
 def triangle_call(received, made, blocks, side, own, incoming):
+    folded = 1 if incoming else 2
     pair = 2 * own
     pixels = side * side
     padded = blocks * LANES
@@ -307,16 +307,16 @@
     left_rows = blocks * side
     right_rows = left_rows if incoming else padded
     return pl.pallas_call(
-        functools.partial(triangle_kernel, blocks, side, own, incoming, made),
-        grid=(2 * blocks // FOLD,),
+        functools.partial(triangle_kernel, blocks, side, own, incoming, made, folded),
+        grid=(2 * blocks // folded,),
         in_specs=[
             pl.BlockSpec(
-                (FOLD * blocks * pair, pixels), lambda i: (jnp.minimum(i, blocks // FOLD - 1), 0)
+                (folded * blocks * pair, pixels), lambda i: (jnp.minimum(i, blocks // folded - 1), 0)
             )
         ],
         out_specs=pl.BlockSpec(
-            (2 * FOLD * pair, pixels // 2 * len(made)),
-            lambda i: (jnp.maximum(i - blocks // FOLD, 0), 0),
+            (2 * folded * pair, pixels // 2 * len(made)),
+            lambda i: (jnp.maximum(i - blocks // folded, 0), 0),
         ),
         out_shape=pltpu.HBM((blocks * blocks * own, pixels // 2 * len(made)), jnp.bfloat16),
         scratch_shapes=[

time: 357 us -> 358 us (level)
  no operation moved by 1% of the time
where the time goes in v15:
time: 358 us; the launch traced here: 357 us
  waiting for transfers between devices  136 us (38%)
  blocking collectives  128 us (36%)
  Pallas kernels  55.9 us (16%)
  starting transfers between devices  30.5 us (9%)
  local copies, waits for them, and re-layouts  4.88 us (1%)
    all_to_all x2, blocking collectives, exchange(): there = lax.all_to_all(array.reshape(peers, -1, array.shape[1]), CUBE, 0, 0)  128 us
    all_to_all x3, waiting for transfers between devices, exchange(): there = lax.all_to_all(array.reshape(peers, -1, array.shape[1]), CUBE, 0, 0)  63.8 us
    pallas_call x7, Pallas kernels, pixel_call(): pl.pallas_call(kernel, grid=(steps,), in_specs=in_specs, out_specs=[spec(...  32.5 us
    ppermute x2, waiting for transfers between devices, by_kernels(): z_far.append(lax.ppermute(over, LINE, ((0, 1), (3, 2))))  20.9 us
    pallas_call x3, Pallas kernels, triangle_call(): pl.pallas_call(functools.partial(triangle_kernel, blocks, side, own, inco...  19 us
    ppermute x2, waiting for transfers between devices, by_kernels(): over = lax.ppermute(part, LINE, ((1, 3), (2, 0)))  18.3 us
    all_to_all x3, starting transfers between devices, exchange(): there = lax.all_to_all(array.reshape(peers, -1, array.shape[1]), CUBE, 0, 0)  15 us
    ppermute x1, waiting for transfers between devices, by_kernels(): back = lax.ppermute(here, LINE, ((1, 3), (2, 0)))  15 us
  transfers between devices with their start and end apart: 12, of which 9 were waited for; matrix products, arithmetic and copies ran while one was open for 0% of the time, Pallas kernels for 6%

profile of v15, /device:TPU:20, one launch (start us, length us, event | category | flops | bytes accessed | tf_op | source)
XLA Modules:
  0.0 356.7 jit_solution(10732281374277874760)
XLA Ops:
  9.7 14.6 %collective-permute-done.3 = bf16[2,1168,128]{2,1,0:T(8,128)(2,1)S(1)} collective-permute-done((bf16[2,1168,128]{2,1,0:T(8,128)(2,1)}, bf16[2,1168,128]{2,1,0:T(8,128)(2,1)S(1)}, u32[]{:S(2)}, u32[]{:S(2)}) %collective-permute-start.3) | collective-permute-done | bytes 598048 | tf_op jit(solution)/shard_map/ppermute | solution.py:433
  31.0 4.8 %collective-permute-done.refs_1_.refs_0_ = bf16[4,1168,128]{2,1,0:T(8,128)(2,1)S(1)} collective-permute-done((bf16[4,1168,128]{2,1,0:T(8,128)(2,1)}, bf16[4,1168,128]{2,1,0:T(8,128)(2,1)S(1)}, u32[]{:S(2)}, u32[]{:S(2)}) %collective-permute-start) | collective-permute-done | bytes 1196064 | tf_op jit(solution)/shard_map/ppermute | solution.py:435
  37.0 4.1 %shard_map.92 = (bf16[256,9216]{1,0:T(8,128)(2,1)}, bf16[128,9216]{1,0:T(8,128)(2,1)}, bf16[16,9216]{1,0:T(8,128)(2,1)}) custom-call(bf16[4,1168,128]{2,1,0:T(8,128)(2,1)S(1)} %copy-done.6, bf16[4,1168,128]{2,1,0:T(8,128)(2,1)S(1)} %collective-permute-done.refs_1_.refs_0_, f32[128,8]{1,0:T(8,128)S(1)} %bitcast.23, ...), custom_call_target="tpu_custom_call" | custom-call | flops 603979776 | bytes 6045696 | tf_op jit(solution)/shard_map/pallas_call | solution.py:363
  41.1 20.9 %collective-permute-done.2.refs_1_ = bf16[1,1168,128]{2,1,0:T(8,128)(2,1)S(1)} collective-permute-done((bf16[1,1168,128]{2,1,0:T(8,128)(2,1)}, bf16[1,1168,128]{2,1,0:T(8,128)(2,1)S(1)}, u32[]{:S(2)}, u32[]{:S(2)}) %collective-permute-start.2) | collective-permute-done | bytes 299040 | tf_op jit(solution)/shard_map/ppermute | solution.py:434
  62.0 4.1 %shard_map.93 = (bf16[256,9216]{1,0:T(8,128)(2,1)}, bf16[128,9216]{1,0:T(8,128)(2,1)}, bf16[16,9216]{1,0:T(8,128)(2,1)}) custom-call(bf16[4,1168,128]{2,1,0:T(8,128)(2,1)S(1)} %collective-permute-done.refs_1_.refs_0_, bf16[1,1168,128]{2,1,0:T(8,128)(2,1)S(1)} %collective-permute-done.2.refs_1_, ...), custom_call_target="tpu_custom_call", output_to_operand_aliasing={{0}: (6, {}), {1}: (7, {}), {2}: (8, {})} | custom-call | flops 603979776 | bytes 6045696 | tf_op jit(solution)/shard_map/pallas_call | solution.py:363
  66.2 69.3 %all_to_all.25 = bf16[16,16,9216]{2,1,0:T(8,128)(2,1)S(1)} all-to-all(bf16[16,16,9216]{2,1,0:T(8,128)(2,1)} %bitcast.31), channel_id=1, replica_groups=mesh['groups'=2,'row'=4,'zh'=2,'zl'=2] {'groups','row','zl'}, dimensions={0} | all-to-all | bytes 9437184 | tf_op jit(solution)/shard_map/all_to_all | solution.py:465
  135.5 7.0 %shard_map.94 = bf16[128,9216]{1,0:T(8,128)(2,1)} custom-call(bf16[256,9216]{1,0:T(8,128)(2,1)S(1)} %bitcast.22), custom_call_target="tpu_custom_call" | custom-call | flops 905969664 | bytes 14155776 | tf_op jit(solution)/shard_map/pallas_call | solution.py:309
  142.5 4.9 %all-to-all-start.1 = ((bf16[16,8,9216]{2,1,0:T(8,128)(2,1)}), bf16[16,8,9216]{2,1,0:T(8,128)(2,1)}, u32[]{:S(2)}, u32[]{:S(2)}) async-start(bf16[16,8,9216]{2,1,0:T(8,128)(2,1)} %bitcast.32), calls=%async_computation.1 | async-start | bytes 4718592 | tf_op jit(solution)/shard_map/all_to_all | solution.py:465
  147.4 3.8 %shard_map.95.refs_2_ = bf16[128,9216]{1,0:T(8,128)(2,1)} custom-call(bf16[128,9216]{1,0:T(8,128)(2,1)S(1)} %copy-done.3, f32[128,8]{1,0:T(8,128)S(1)} %bitcast.25, bf16[2,768,128]{2,1,0:T(8,128)(2,1)S(1)} %maximum_bitcast_fusion.refs_3_.refs_5_.refs_2_.refs_4_), custom_call_target="tpu_custom_call" | custom-call | flops 301989888 | bytes 7077888 | tf_op jit(solution)/shard_map/pallas_call | solution.py:363
  151.2 26.5 %all-to-all-done.1 = bf16[16,8,9216]{2,1,0:T(8,128)(2,1)} async-done(((bf16[16,8,9216]{2,1,0:T(8,128)(2,1)}), bf16[16,8,9216]{2,1,0:T(8,128)(2,1)}, u32[]{:S(2)}, u32[]{:S(2)}) %all-to-all-start.1) | async-done | bytes 2359328 | tf_op jit(solution)/shard_map/all_to_all | solution.py:465
  177.8 9.3 %shard_map.96 = (bf16[256,9216]{1,0:T(8,128)(2,1)}, bf16[128,9216]{1,0:T(8,128)(2,1)}) custom-call(bf16[128,9216]{1,0:T(8,128)(2,1)} %bitcast.11.refs_0_, bf16[128,9216]{1,0:T(8,128)(2,1)S(1)} %copy-done.3, bf16[128,9216]{1,0:T(8,128)(2,1)} %shard_map.95.refs_2_, bf16[16,9216]{1,0:T(8,128)(2,1)S(1)} %copy-done.7, f32[128,8]{1,0:T(8,128)S(1)} %bitcast.26, ...), custom_call_target="tpu_custom_call" | custom-call | flops 1509949440 | bytes 11796480 | tf_op jit(solution)/shard_map/pallas_call | solution.py:363
  187.0 58.4 %all_to_all.26 = bf16[16,16,9216]{2,1,0:T(8,128)(2,1)S(1)} all-to-all(bf16[16,16,9216]{2,1,0:T(8,128)(2,1)} %bitcast.33), channel_id=1, replica_groups=mesh['groups'=2,'row'=4,'zh'=2,'zl'=2] {'groups','row','zl'}, dimensions={0} | all-to-all | bytes 9437184 | tf_op jit(solution)/shard_map/all_to_all | solution.py:465
  245.4 6.0 %shard_map.97 = bf16[128,4608]{1,0:T(8,128)(2,1)} custom-call(bf16[256,9216]{1,0:T(8,128)(2,1)S(1)} %bitcast.20), custom_call_target="tpu_custom_call" | custom-call | flops 452984832 | bytes 14155776 | tf_op jit(solution)/shard_map/pallas_call | solution.py:309
  251.4 4.9 %all-to-all-start.3 = ((bf16[16,8,4608]{2,1,0:T(8,128)(2,1)}), bf16[16,8,4608]{2,1,0:T(8,128)(2,1)}, u32[]{:S(2)}, u32[]{:S(2)}) async-start(bf16[16,8,4608]{2,1,0:T(8,128)(2,1)} %bitcast.35), calls=%async_computation.3 | async-start | bytes 2359296 | tf_op jit(solution)/shard_map/all_to_all | solution.py:465
  256.3 3.8 %shard_map.98.refs_2_ = bf16[128,9216]{1,0:T(8,128)(2,1)} custom-call(bf16[128,9216]{1,0:T(8,128)(2,1)S(1)} %copy-done.2, f32[128,8]{1,0:T(8,128)S(1)} %bitcast.27, bf16[2,768,128]{2,1,0:T(8,128)(2,1)S(1)} %maximum_bitcast_fusion.refs_3_.refs_5_.refs_2_.refs_4_), custom_call_target="tpu_custom_call" | custom-call | flops 301989888 | bytes 7077888 | tf_op jit(solution)/shard_map/pallas_call | solution.py:363
  260.1 6.0 %shard_map.100 = bf16[128,4608]{1,0:T(8,128)(2,1)} custom-call(bf16[256,9216]{1,0:T(8,128)(2,1)S(1)} %bitcast.21), custom_call_target="tpu_custom_call" | custom-call | flops 452984832 | bytes 14155776 | tf_op jit(solution)/shard_map/pallas_call | solution.py:309
  266.1 6.0 %all-to-all-done.3 = bf16[16,8,4608]{2,1,0:T(8,128)(2,1)} async-done(((bf16[16,8,4608]{2,1,0:T(8,128)(2,1)}), bf16[16,8,4608]{2,1,0:T(8,128)(2,1)}, u32[]{:S(2)}, u32[]{:S(2)}) %all-to-all-start.3) | async-done | bytes 1179680 | tf_op jit(solution)/shard_map/all_to_all | solution.py:465
  272.0 3.7 %shard_map.99 = bf16[4608,128]{1,0:T(8,128)(2,1)} custom-call(bf16[128,4608]{1,0:T(8,128)(2,1)} %bitcast.15.refs_0_, bf16[128,9216]{1,0:T(8,128)(2,1)S(1)} %copy-done.2, bf16[128,9216]{1,0:T(8,128)(2,1)} %shard_map.98.refs_2_, f32[128,8]{1,0:T(8,128)S(1)} %bitcast.28, bf16[2,768,128]{2,1,0:T(8,128)(2,1)S(1)} %maximum_bitcast_fusion.refs_3_.refs_5_.refs_2_.refs_4_), custom_call_target="tpu_custom_call" | custom-call | flops 150994944 | bytes 3538944 | tf_op jit(solution)/shard_map/pallas_call | solution.py:363
  275.7 5.3 %all-to-all-start.4 = ((bf16[16,8,4608]{2,1,0:T(8,128)(2,1)}), bf16[16,8,4608]{2,1,0:T(8,128)(2,1)}, u32[]{:S(2)}, u32[]{:S(2)}) async-start(bf16[16,8,4608]{2,1,0:T(8,128)(2,1)} %bitcast.34), calls=%async_computation.4 | async-start | bytes 2359296 | tf_op jit(solution)/shard_map/all_to_all | solution.py:465
  282.7 5.8 %collective-permute-start.6 = (bf16[4608,128]{1,0:T(8,128)(2,1)}, bf16[4608,128]{1,0:T(8,128)(2,1)}, u32[]{:S(2)}, u32[]{:S(2)}) collective-permute-start(bf16[4608,128]{1,0:T(8,128)(2,1)} %shard_map.99), channel_id=1, source_target_pairs={{0,2},{18,16},{1,3},{19,17},{4,6},{22,20},{5,7},{23,21},{8,10},{26... | collective-permute-start | bytes 3538952 | tf_op jit(solution)/shard_map/ppermute | solution.py:489
  288.4 31.4 %all-to-all-done.4 = bf16[16,8,4608]{2,1,0:T(8,128)(2,1)} async-done(((bf16[16,8,4608]{2,1,0:T(8,128)(2,1)}), bf16[16,8,4608]{2,1,0:T(8,128)(2,1)}, u32[]{:S(2)}, u32[]{:S(2)}) %all-to-all-start.4) | async-done | bytes 1179680 | tf_op jit(solution)/shard_map/all_to_all | solution.py:465
  319.8 3.7 %shard_map.101.here_ref = bf16[4608,128]{1,0:T(8,128)(2,1)} custom-call(bf16[128,4608]{1,0:T(8,128)(2,1)} %bitcast.17.refs_0_, bf16[128,9216]{1,0:T(8,128)(2,1)S(1)} %copy-done.2, bf16[128,9216]{1,0:T(8,128)(2,1)} %shard_map.98.refs_2_, f32[128,8]{1,0:T(8,128)S(1)} %bitcast.29, bf16[2,768,128]{2,1,0:T(8,128)(2,1)S(1)} %maximum_bitcast_fusion.refs_3_.refs_5_.refs_2_.refs_4_), custom_call_target="tpu_custom_call" | custom-call | flops 150994944 | bytes 3538944 | tf_op jit(solution)/shard_map/pallas_call | solution.py:363
  324.8 13.6 %collective-permute-done.6.beside_ref = bf16[4608,128]{1,0:T(8,128)(2,1)} collective-permute-done((bf16[4608,128]{1,0:T(8,128)(2,1)}, bf16[4608,128]{1,0:T(8,128)(2,1)}, u32[]{:S(2)}, u32[]{:S(2)}) %collective-permute-start.6) | collective-permute-done | bytes 1179680 | tf_op jit(solution)/shard_map/ppermute | solution.py:489
  338.4 15.0 %collective-permute-done.7.back_ref = bf16[4608,128]{1,0:T(8,128)(2,1)S(1)} collective-permute-done((bf16[4608,128]{1,0:T(8,128)(2,1)}, bf16[4608,128]{1,0:T(8,128)(2,1)S(1)}, u32[]{:S(2)}, u32[]{:S(2)}) %collective-permute-start.7) | collective-permute-done | bytes 1179680 | tf_op jit(solution)/shard_map/ppermute | solution.py:493
  (56 shorter events, 23.6 us)
Async XLA Ops:
  0.0 9.1 %copy-start.11 = (f32[2,128]{1,0:T(2,128)S(1)}, f32[2,128]{1,0:T(2,128)}, u32[]{:S(2)}) copy-start(f32[2,128]{1,0:T(2,128)} %param.16) | copy-start | bytes 3076
  0.0 9.1 %copy-start.12 = (f32[2,128]{1,0:T(2,128)S(1)}, f32[2,128]{1,0:T(2,128)}, u32[]{:S(2)}) copy-start(f32[2,128]{1,0:T(2,128)} %param.15) | copy-start | bytes 3076
  0.0 9.1 %copy-start.13 = (f32[2,128]{1,0:T(2,128)S(1)}, f32[2,128]{1,0:T(2,128)}, u32[]{:S(2)}) copy-start(f32[2,128]{1,0:T(2,128)} %param.12) | copy-start | bytes 3076
  0.0 9.1 %copy-start.14 = (f32[2,128]{1,0:T(2,128)S(1)}, f32[2,128]{1,0:T(2,128)}, u32[]{:S(2)}) copy-start(f32[2,128]{1,0:T(2,128)} %param.11) | copy-start | bytes 3076
  0.0 9.3 %copy-start.9 = (bf16[2,128,128]{2,1,0:T(8,128)(2,1)S(1)}, bf16[2,128,128]{2,1,0:T(8,128)(2,1)}, u32[]{:S(2)}) copy-start(bf16[2,128,128]{2,1,0:T(8,128)(2,1)} %param.14) | copy-start | bytes 196612
  0.0 9.4 %copy-start.10 = (bf16[2,128,128]{2,1,0:T(8,128)(2,1)S(1)}, bf16[2,128,128]{2,1,0:T(8,128)(2,1)}, u32[]{:S(2)}) copy-start(bf16[2,128,128]{2,1,0:T(8,128)(2,1)} %param.17) | copy-start | bytes 196612
  2.7 6.8 %copy-start.8 = (bf16[2,128,512]{2,1,0:T(8,128)(2,1)S(1)}, bf16[2,128,512]{2,1,0:T(8,128)(2,1)}, u32[]{:S(2)}) copy-start(bf16[2,128,512]{2,1,0:T(8,128)(2,1)} %param.13) | copy-start | bytes 786436
  5.3 30.5 %collective-permute-start = (bf16[4,1168,128]{2,1,0:T(8,128)(2,1)}, bf16[4,1168,128]{2,1,0:T(8,128)(2,1)S(1)}, u32[]{:S(2)}, u32[]{:S(2)}) collective-permute-start(bf16[4,1168,128]{2,1,0:T(8,128)(2,1)} %get-tuple-element.19), channel_id=1, source_target_pairs={{2,0},{16,18},{0,16},{18,2},{3,1},{17,19},{1,17},{19,3},{6,4},{20,... | collective-permute-start | bytes 3588104 | tf_op jit(solution)/shard_map/ppermute | solution.py:435
  5.8 18.5 %collective-permute-start.3 = (bf16[2,1168,128]{2,1,0:T(8,128)(2,1)}, bf16[2,1168,128]{2,1,0:T(8,128)(2,1)S(1)}, u32[]{:S(2)}, u32[]{:S(2)}) collective-permute-start(bf16[2,1168,128]{2,1,0:T(8,128)(2,1)} %get-tuple-element.21), channel_id=1, source_target_pairs={{2,18},{16,0},{3,19},{17,1},{6,22},{20,4},{7,23},{21,5},{10,26},{2... | collective-permute-start | bytes 1794056 | tf_op jit(solution)/shard_map/ppermute | solution.py:433
  7.1 22.3 %collective-permute-start.1 = (bf16[1,1168,128]{2,1,0:T(8,128)(2,1)}, bf16[1,1168,128]{2,1,0:T(8,128)(2,1)}, u32[]{:S(2)}, u32[]{:S(2)}) collective-permute-start(bf16[1,1168,128]{2,1,0:T(8,128)(2,1)} %get-tuple-element.20), channel_id=1, source_target_pairs={{2,18},{16,0},{3,19},{17,1},{6,22},{20,4},{7,23},{21,5},{10,26},{2... | collective-permute-start | bytes 897032 | tf_op jit(solution)/shard_map/ppermute | solution.py:433
  8.4 32.7 %collective-permute-start.5 = (bf16[1,1168,128]{2,1,0:T(8,128)(2,1)}, bf16[1,1168,128]{2,1,0:T(8,128)(2,1)S(1)}, u32[]{:S(2)}, u32[]{:S(2)}) collective-permute-start(bf16[1,1168,128]{2,1,0:T(8,128)(2,1)} %get-tuple-element.22), channel_id=1, source_target_pairs={{2,16},{16,2},{3,17},{17,3},{6,20},{20,6},{7,21},{21,7},{10,24},{2... | collective-permute-start | bytes 897032 | tf_op jit(solution)/shard_map/ppermute | solution.py:436
  24.3 37.7 %collective-permute-start.4 = (bf16[2,1168,128]{2,1,0:T(8,128)(2,1)S(1)}, bf16[2,1168,128]{2,1,0:T(8,128)(2,1)S(1)}, u32[]{:S(2)}, u32[]{:S(2)}) collective-permute-start(bf16[2,1168,128]{2,1,0:T(8,128)(2,1)S(1)} %collective-permute-done.3), channel_id=1, source_target_pairs={{0,2},{18,16},{1,3},{19,17},{4,6},{22,20},{5,7},{23,21},{8,10},{26... | collective-permute-start | bytes 1794056 | tf_op jit(solution)/shard_map/ppermute | solution.py:434
  29.4 32.6 %collective-permute-start.2 = (bf16[1,1168,128]{2,1,0:T(8,128)(2,1)}, bf16[1,1168,128]{2,1,0:T(8,128)(2,1)S(1)}, u32[]{:S(2)}, u32[]{:S(2)}) collective-permute-start(bf16[1,1168,128]{2,1,0:T(8,128)(2,1)} %collective-permute-done.1), channel_id=1, source_target_pairs={{0,2},{18,16},{1,3},{19,17},{4,6},{22,20},{5,7},{23,21},{8,10},{26... | collective-permute-start | bytes 897032 | tf_op jit(solution)/shard_map/ppermute | solution.py:434
  142.5 4.9 %copy-start.3 = (bf16[128,9216]{1,0:T(8,128)(2,1)S(1)}, bf16[128,9216]{1,0:T(8,128)(2,1)}, u32[]{:S(2)}) copy-start(bf16[128,9216]{1,0:T(8,128)(2,1)} %get-tuple-element.28.refs_0_.refs_1_) | copy-start | bytes 7077892
  142.5 35.3 %all-to-all-start.1 = ((bf16[16,8,9216]{2,1,0:T(8,128)(2,1)}), bf16[16,8,9216]{2,1,0:T(8,128)(2,1)}, u32[]{:S(2)}, u32[]{:S(2)}) async-start(bf16[16,8,9216]{2,1,0:T(8,128)(2,1)} %bitcast.32), calls=%async_computation.1 | async-start | bytes 4718592 | tf_op jit(solution)/shard_map/all_to_all | solution.py:465
  147.4 30.3 %copy-start.7 = (bf16[16,9216]{1,0:T(8,128)(2,1)S(1)}, bf16[16,9216]{1,0:T(8,128)(2,1)}, u32[]{:S(2)}) copy-start(bf16[16,9216]{1,0:T(8,128)(2,1)} %get-tuple-element.29.refs_3_) | copy-start | bytes 884740
  245.4 6.0 %copy-start = (bf16[16,16,9216]{2,1,0:T(8,128)(2,1)}, bf16[16,16,9216]{2,1,0:T(8,128)(2,1)S(1)}, u32[]{:S(2)}) copy-start(bf16[16,16,9216]{2,1,0:T(8,128)(2,1)S(1)} %all_to_all.26) | copy-start | bytes 14155780
  251.4 4.9 %copy-start.2 = (bf16[128,9216]{1,0:T(8,128)(2,1)S(1)}, bf16[128,9216]{1,0:T(8,128)(2,1)}, u32[]{:S(2)}) copy-start(bf16[128,9216]{1,0:T(8,128)(2,1)} %get-tuple-element.31.refs_0_.refs_1_) | copy-start | bytes 7077892
  251.4 20.6 %all-to-all-start.3 = ((bf16[16,8,4608]{2,1,0:T(8,128)(2,1)}), bf16[16,8,4608]{2,1,0:T(8,128)(2,1)}, u32[]{:S(2)}, u32[]{:S(2)}) async-start(bf16[16,8,4608]{2,1,0:T(8,128)(2,1)} %bitcast.35), calls=%async_computation.3 | async-start | bytes 2359296 | tf_op jit(solution)/shard_map/all_to_all | solution.py:465
  256.3 3.8 %copy-start.1 = (bf16[16,16,9216]{2,1,0:T(8,128)(2,1)S(1)}, bf16[16,16,9216]{2,1,0:T(8,128)(2,1)}, u32[]{:S(2)}) copy-start(bf16[16,16,9216]{2,1,0:T(8,128)(2,1)} %copy-done) | copy-start | bytes 14155780
  275.7 44.1 %all-to-all-start.4 = ((bf16[16,8,4608]{2,1,0:T(8,128)(2,1)}), bf16[16,8,4608]{2,1,0:T(8,128)(2,1)}, u32[]{:S(2)}, u32[]{:S(2)}) async-start(bf16[16,8,4608]{2,1,0:T(8,128)(2,1)} %bitcast.34), calls=%async_computation.4 | async-start | bytes 2359296 | tf_op jit(solution)/shard_map/all_to_all | solution.py:465
  281.0 43.8 %collective-permute-start.8 = (bf16[4608,128]{1,0:T(8,128)(2,1)}, bf16[4608,128]{1,0:T(8,128)(2,1)}, u32[]{:S(2)}, u32[]{:S(2)}) collective-permute-start(bf16[4608,128]{1,0:T(8,128)(2,1)} %shard_map.99), channel_id=1, source_target_pairs={{2,16},{16,2},{3,17},{17,3},{6,20},{20,6},{7,21},{21,7},{10,24},{2... | collective-permute-start | bytes 3538952 | tf_op jit(solution)/shard_map/ppermute | solution.py:489
  282.7 55.7 %collective-permute-start.6 = (bf16[4608,128]{1,0:T(8,128)(2,1)}, bf16[4608,128]{1,0:T(8,128)(2,1)}, u32[]{:S(2)}, u32[]{:S(2)}) collective-permute-start(bf16[4608,128]{1,0:T(8,128)(2,1)} %shard_map.99), channel_id=1, source_target_pairs={{0,2},{18,16},{1,3},{19,17},{4,6},{22,20},{5,7},{23,21},{8,10},{26... | collective-permute-start | bytes 3538952 | tf_op jit(solution)/shard_map/ppermute | solution.py:489
  323.5 29.9 %collective-permute-start.7 = (bf16[4608,128]{1,0:T(8,128)(2,1)}, bf16[4608,128]{1,0:T(8,128)(2,1)S(1)}, u32[]{:S(2)}, u32[]{:S(2)}) collective-permute-start(bf16[4608,128]{1,0:T(8,128)(2,1)} %shard_map.101.here_ref), channel_id=1, source_target_pairs={{2,18},{16,0},{3,19},{17,1},{6,22},{20,4},{7,23},{21,5},{10,26},{2... | collective-permute-start | bytes 3538952 | tf_op jit(solution)/shard_map/ppermute | solution.py:493
  (3 other events, 4.2 us)

commit v16 on v10

--- a/solution.py
+++ b/solution.py
@@ -463,8 +463,8 @@
     triangle = exchange(triangle_call(exchange(sent), (0, 1), blocks, side, own, False))
     sent, zt = pixel_call(
         functools.partial(middle_kernel, peers),
-        [(a, 0, steps) for a in (triangle, zt, gate, mask)], fixed, (2 * width, channels),
-        steps, wide, pixels * mult * 5 * width,
+        [(a, 0, steps // 2) for a in (triangle, zt, gate, mask)], fixed, (2 * width, channels),
+        steps // 2, 2 * wide, pixels * mult * 5 * width,
     )
     gate = gate_of(zt, 1)
     received = exchange(sent)

time: 347 us -> 348 us (level)
  no operation moved by 1% of the time
where the time goes in v16:
time: 348 us; the launch traced here: 343 us
  blocking collectives  128 us (37%)
  waiting for transfers between devices  121 us (35%)
  Pallas kernels  57.1 us (16%)
  starting transfers between devices  30.5 us (9%)
  local copies, waits for them, and re-layouts  4.88 us (1%)
    all_to_all x2, blocking collectives, exchange(): there = lax.all_to_all(array.reshape(peers, -1, array.shape[1]), CUBE, 0, 0)  128 us
    all_to_all x3, waiting for transfers between devices, exchange(): there = lax.all_to_all(array.reshape(peers, -1, array.shape[1]), CUBE, 0, 0)  46.8 us
    pallas_call x7, Pallas kernels, pixel_call(): pl.pallas_call(kernel, grid=(steps,), in_specs=in_specs, out_specs=[spec(...  33 us
    ppermute x2, waiting for transfers between devices, by_kernels(): lax.ppermute(there, LINE, pairs)  30.7 us
    ppermute x2, waiting for transfers between devices, by_kernels(): z_far.append(lax.ppermute(over, LINE, ((0, 1), (3, 2))))  20.9 us
    pallas_call x3, Pallas kernels, triangle_call(): pl.pallas_call(functools.partial(triangle_kernel, blocks, side, own, inco...  19.6 us
    ppermute x2, waiting for transfers between devices, by_kernels(): over = lax.ppermute(part, LINE, ((1, 3), (2, 0)))  18.3 us
    all_to_all x3, starting transfers between devices, exchange(): there = lax.all_to_all(array.reshape(peers, -1, array.shape[1]), CUBE, 0, 0)  15 us
  transfers between devices with their start and end apart: 12, of which 8 were waited for; matrix products, arithmetic and copies ran while one was open for 0% of the time, Pallas kernels for 6%

profile of v16, /device:TPU:20, one launch (start us, length us, event | category | flops | bytes accessed | tf_op | source)
XLA Modules:
  0.0 342.9 jit_solution(15795134803184582045)
XLA Ops:
  9.7 14.6 %collective-permute-done.3 = bf16[2,1168,128]{2,1,0:T(8,128)(2,1)S(1)} collective-permute-done((bf16[2,1168,128]{2,1,0:T(8,128)(2,1)}, bf16[2,1168,128]{2,1,0:T(8,128)(2,1)S(1)}, u32[]{:S(2)}, u32[]{:S(2)}) %collective-permute-start.3) | collective-permute-done | bytes 598048 | tf_op jit(solution)/shard_map/ppermute | solution.py:427
  25.8 3.6 %collective-permute-done.1 = bf16[1,1168,128]{2,1,0:T(8,128)(2,1)} collective-permute-done((bf16[1,1168,128]{2,1,0:T(8,128)(2,1)}, bf16[1,1168,128]{2,1,0:T(8,128)(2,1)}, u32[]{:S(2)}, u32[]{:S(2)}) %collective-permute-start.1) | collective-permute-done | bytes 299040 | tf_op jit(solution)/shard_map/ppermute | solution.py:427
  31.0 4.8 %collective-permute-done.refs_1_.refs_0_ = bf16[4,1168,128]{2,1,0:T(8,128)(2,1)S(1)} collective-permute-done((bf16[4,1168,128]{2,1,0:T(8,128)(2,1)}, bf16[4,1168,128]{2,1,0:T(8,128)(2,1)S(1)}, u32[]{:S(2)}, u32[]{:S(2)}) %collective-permute-start) | collective-permute-done | bytes 1196064 | tf_op jit(solution)/shard_map/ppermute | solution.py:429
  37.0 4.1 %shard_map.92 = (bf16[256,9216]{1,0:T(8,128)(2,1)}, bf16[128,9216]{1,0:T(8,128)(2,1)}, bf16[16,9216]{1,0:T(8,128)(2,1)}) custom-call(bf16[4,1168,128]{2,1,0:T(8,128)(2,1)S(1)} %copy-done.6, bf16[4,1168,128]{2,1,0:T(8,128)(2,1)S(1)} %collective-permute-done.refs_1_.refs_0_, f32[128,8]{1,0:T(8,128)S(1)} %bitcast.23, ...), custom_call_target="tpu_custom_call" | custom-call | flops 603979776 | bytes 6045696 | tf_op jit(solution)/shard_map/pallas_call | solution.py:357
  41.1 20.9 %collective-permute-done.2.refs_1_ = bf16[1,1168,128]{2,1,0:T(8,128)(2,1)S(1)} collective-permute-done((bf16[1,1168,128]{2,1,0:T(8,128)(2,1)}, bf16[1,1168,128]{2,1,0:T(8,128)(2,1)S(1)}, u32[]{:S(2)}, u32[]{:S(2)}) %collective-permute-start.2) | collective-permute-done | bytes 299040 | tf_op jit(solution)/shard_map/ppermute | solution.py:428
  62.0 4.1 %shard_map.93 = (bf16[256,9216]{1,0:T(8,128)(2,1)}, bf16[128,9216]{1,0:T(8,128)(2,1)}, bf16[16,9216]{1,0:T(8,128)(2,1)}) custom-call(bf16[4,1168,128]{2,1,0:T(8,128)(2,1)S(1)} %collective-permute-done.refs_1_.refs_0_, bf16[1,1168,128]{2,1,0:T(8,128)(2,1)S(1)} %collective-permute-done.2.refs_1_, ...), custom_call_target="tpu_custom_call", output_to_operand_aliasing={{0}: (6, {}), {1}: (7, {}), {2}: (8, {})} | custom-call | flops 603979776 | bytes 6045696 | tf_op jit(solution)/shard_map/pallas_call | solution.py:357
  66.2 69.3 %all_to_all.25 = bf16[16,16,9216]{2,1,0:T(8,128)(2,1)S(1)} all-to-all(bf16[16,16,9216]{2,1,0:T(8,128)(2,1)} %bitcast.31), channel_id=1, replica_groups=mesh['groups'=2,'row'=4,'zh'=2,'zl'=2] {'groups','row','zl'}, dimensions={0} | all-to-all | bytes 9437184 | tf_op jit(solution)/shard_map/all_to_all | solution.py:459
  135.5 7.6 %shard_map.94 = bf16[128,9216]{1,0:T(8,128)(2,1)} custom-call(bf16[256,9216]{1,0:T(8,128)(2,1)S(1)} %bitcast.22), custom_call_target="tpu_custom_call" | custom-call | flops 905969664 | bytes 14155776 | tf_op jit(solution)/shard_map/pallas_call | solution.py:306
  143.1 4.9 %all-to-all-start.1 = ((bf16[16,8,9216]{2,1,0:T(8,128)(2,1)}), bf16[16,8,9216]{2,1,0:T(8,128)(2,1)}, u32[]{:S(2)}, u32[]{:S(2)}) async-start(bf16[16,8,9216]{2,1,0:T(8,128)(2,1)} %bitcast.32), calls=%async_computation.1 | async-start | bytes 4718592 | tf_op jit(solution)/shard_map/all_to_all | solution.py:459
  148.0 3.8 %shard_map.95.refs_2_ = bf16[128,9216]{1,0:T(8,128)(2,1)} custom-call(bf16[128,9216]{1,0:T(8,128)(2,1)S(1)} %copy-done.3, f32[128,8]{1,0:T(8,128)S(1)} %bitcast.25, bf16[2,768,128]{2,1,0:T(8,128)(2,1)S(1)} %maximum_bitcast_fusion.refs_3_.refs_5_.refs_2_.refs_4_), custom_call_target="tpu_custom_call" | custom-call | flops 301989888 | bytes 7077888 | tf_op jit(solution)/shard_map/pallas_call | solution.py:357
  151.9 26.5 %all-to-all-done.1 = bf16[16,8,9216]{2,1,0:T(8,128)(2,1)} async-done(((bf16[16,8,9216]{2,1,0:T(8,128)(2,1)}), bf16[16,8,9216]{2,1,0:T(8,128)(2,1)}, u32[]{:S(2)}, u32[]{:S(2)}) %all-to-all-start.1) | async-done | bytes 2359328 | tf_op jit(solution)/shard_map/all_to_all | solution.py:459
  178.4 9.8 %shard_map.96 = (bf16[256,9216]{1,0:T(8,128)(2,1)}, bf16[128,9216]{1,0:T(8,128)(2,1)}) custom-call(bf16[128,9216]{1,0:T(8,128)(2,1)} %bitcast.11.refs_0_, bf16[128,9216]{1,0:T(8,128)(2,1)S(1)} %copy-done.3, bf16[128,9216]{1,0:T(8,128)(2,1)} %shard_map.95.refs_2_, bf16[16,9216]{1,0:T(8,128)(2,1)S(1)} %copy-done.7, f32[128,8]{1,0:T(8,128)S(1)} %bitcast.26, ...), custom_call_target="tpu_custom_call" | custom-call | flops 1509949440 | bytes 11796480 | tf_op jit(solution)/shard_map/pallas_call | solution.py:357
  188.2 58.4 %all_to_all.26 = bf16[16,16,9216]{2,1,0:T(8,128)(2,1)S(1)} all-to-all(bf16[16,16,9216]{2,1,0:T(8,128)(2,1)} %bitcast.33), channel_id=1, replica_groups=mesh['groups'=2,'row'=4,'zh'=2,'zl'=2] {'groups','row','zl'}, dimensions={0} | all-to-all | bytes 9437184 | tf_op jit(solution)/shard_map/all_to_all | solution.py:459
  246.6 6.0 %shard_map.97 = bf16[128,4608]{1,0:T(8,128)(2,1)} custom-call(bf16[256,9216]{1,0:T(8,128)(2,1)S(1)} %bitcast.20), custom_call_target="tpu_custom_call" | custom-call | flops 452984832 | bytes 14155776 | tf_op jit(solution)/shard_map/pallas_call | solution.py:306
  252.5 4.9 %all-to-all-start.3 = ((bf16[16,8,4608]{2,1,0:T(8,128)(2,1)}), bf16[16,8,4608]{2,1,0:T(8,128)(2,1)}, u32[]{:S(2)}, u32[]{:S(2)}) async-start(bf16[16,8,4608]{2,1,0:T(8,128)(2,1)} %bitcast.35), calls=%async_computation.3 | async-start | bytes 2359296 | tf_op jit(solution)/shard_map/all_to_all | solution.py:459
  257.4 3.8 %shard_map.98.refs_2_ = bf16[128,9216]{1,0:T(8,128)(2,1)} custom-call(bf16[128,9216]{1,0:T(8,128)(2,1)S(1)} %copy-done.2, f32[128,8]{1,0:T(8,128)S(1)} %bitcast.27, bf16[2,768,128]{2,1,0:T(8,128)(2,1)S(1)} %maximum_bitcast_fusion.refs_3_.refs_5_.refs_2_.refs_4_), custom_call_target="tpu_custom_call" | custom-call | flops 301989888 | bytes 7077888 | tf_op jit(solution)/shard_map/pallas_call | solution.py:357
  261.2 6.0 %shard_map.100 = bf16[128,4608]{1,0:T(8,128)(2,1)} custom-call(bf16[256,9216]{1,0:T(8,128)(2,1)S(1)} %bitcast.21), custom_call_target="tpu_custom_call" | custom-call | flops 452984832 | bytes 14155776 | tf_op jit(solution)/shard_map/pallas_call | solution.py:306
  267.2 6.0 %all-to-all-done.3 = bf16[16,8,4608]{2,1,0:T(8,128)(2,1)} async-done(((bf16[16,8,4608]{2,1,0:T(8,128)(2,1)}), bf16[16,8,4608]{2,1,0:T(8,128)(2,1)}, u32[]{:S(2)}, u32[]{:S(2)}) %all-to-all-start.3) | async-done | bytes 1179680 | tf_op jit(solution)/shard_map/all_to_all | solution.py:459
  273.2 3.7 %shard_map.99 = bf16[4608,128]{1,0:T(8,128)(2,1)} custom-call(bf16[128,4608]{1,0:T(8,128)(2,1)} %bitcast.15.refs_0_, bf16[128,9216]{1,0:T(8,128)(2,1)S(1)} %copy-done.2, bf16[128,9216]{1,0:T(8,128)(2,1)} %shard_map.98.refs_2_, f32[128,8]{1,0:T(8,128)S(1)} %bitcast.28, bf16[2,768,128]{2,1,0:T(8,128)(2,1)S(1)} %maximum_bitcast_fusion.refs_3_.refs_5_.refs_2_.refs_4_), custom_call_target="tpu_custom_call" | custom-call | flops 150994944 | bytes 3538944 | tf_op jit(solution)/shard_map/pallas_call | solution.py:357
  276.9 5.3 %all-to-all-start.4 = ((bf16[16,8,4608]{2,1,0:T(8,128)(2,1)}), bf16[16,8,4608]{2,1,0:T(8,128)(2,1)}, u32[]{:S(2)}, u32[]{:S(2)}) async-start(bf16[16,8,4608]{2,1,0:T(8,128)(2,1)} %bitcast.34), calls=%async_computation.4 | async-start | bytes 2359296 | tf_op jit(solution)/shard_map/all_to_all | solution.py:459
  283.8 5.8 %collective-permute-start.6 = (bf16[4608,128]{1,0:T(8,128)(2,1)}, bf16[4608,128]{1,0:T(8,128)(2,1)}, u32[]{:S(2)}, u32[]{:S(2)}) collective-permute-start(bf16[4608,128]{1,0:T(8,128)(2,1)} %shard_map.99), channel_id=1, source_target_pairs={{0,2},{18,16},{1,3},{19,17},{4,6},{22,20},{5,7},{23,21},{8,10},{26... | collective-permute-start | bytes 3538952 | tf_op jit(solution)/shard_map/ppermute | solution.py:483
  289.6 14.3 %all-to-all-done.4 = bf16[16,8,4608]{2,1,0:T(8,128)(2,1)} async-done(((bf16[16,8,4608]{2,1,0:T(8,128)(2,1)}), bf16[16,8,4608]{2,1,0:T(8,128)(2,1)}, u32[]{:S(2)}, u32[]{:S(2)}) %all-to-all-start.4) | async-done | bytes 1179680 | tf_op jit(solution)/shard_map/all_to_all | solution.py:459
  303.8 3.7 %shard_map.101.here_ref = bf16[4608,128]{1,0:T(8,128)(2,1)} custom-call(bf16[128,4608]{1,0:T(8,128)(2,1)} %bitcast.17.refs_0_, bf16[128,9216]{1,0:T(8,128)(2,1)S(1)} %copy-done.2, bf16[128,9216]{1,0:T(8,128)(2,1)} %shard_map.98.refs_2_, f32[128,8]{1,0:T(8,128)S(1)} %bitcast.29, bf16[2,768,128]{2,1,0:T(8,128)(2,1)S(1)} %maximum_bitcast_fusion.refs_3_.refs_5_.refs_2_.refs_4_), custom_call_target="tpu_custom_call" | custom-call | flops 150994944 | bytes 3538944 | tf_op jit(solution)/shard_map/pallas_call | solution.py:357
  308.8 30.7 %collective-permute-done.6.beside_ref = bf16[4608,128]{1,0:T(8,128)(2,1)} collective-permute-done((bf16[4608,128]{1,0:T(8,128)(2,1)}, bf16[4608,128]{1,0:T(8,128)(2,1)}, u32[]{:S(2)}, u32[]{:S(2)}) %collective-permute-start.6) | collective-permute-done | bytes 1179680 | tf_op jit(solution)/shard_map/ppermute | solution.py:483
  (56 shorter events, 20.0 us)
Async XLA Ops:
  0.0 9.1 %copy-start.11 = (f32[2,128]{1,0:T(2,128)S(1)}, f32[2,128]{1,0:T(2,128)}, u32[]{:S(2)}) copy-start(f32[2,128]{1,0:T(2,128)} %param.16) | copy-start | bytes 3076
  0.0 9.1 %copy-start.12 = (f32[2,128]{1,0:T(2,128)S(1)}, f32[2,128]{1,0:T(2,128)}, u32[]{:S(2)}) copy-start(f32[2,128]{1,0:T(2,128)} %param.15) | copy-start | bytes 3076
  0.0 9.1 %copy-start.13 = (f32[2,128]{1,0:T(2,128)S(1)}, f32[2,128]{1,0:T(2,128)}, u32[]{:S(2)}) copy-start(f32[2,128]{1,0:T(2,128)} %param.12) | copy-start | bytes 3076
  0.0 9.1 %copy-start.14 = (f32[2,128]{1,0:T(2,128)S(1)}, f32[2,128]{1,0:T(2,128)}, u32[]{:S(2)}) copy-start(f32[2,128]{1,0:T(2,128)} %param.11) | copy-start | bytes 3076
  0.0 9.3 %copy-start.9 = (bf16[2,128,128]{2,1,0:T(8,128)(2,1)S(1)}, bf16[2,128,128]{2,1,0:T(8,128)(2,1)}, u32[]{:S(2)}) copy-start(bf16[2,128,128]{2,1,0:T(8,128)(2,1)} %param.14) | copy-start | bytes 196612
  0.0 9.4 %copy-start.10 = (bf16[2,128,128]{2,1,0:T(8,128)(2,1)S(1)}, bf16[2,128,128]{2,1,0:T(8,128)(2,1)}, u32[]{:S(2)}) copy-start(bf16[2,128,128]{2,1,0:T(8,128)(2,1)} %param.17) | copy-start | bytes 196612
  2.7 6.8 %copy-start.8 = (bf16[2,128,512]{2,1,0:T(8,128)(2,1)S(1)}, bf16[2,128,512]{2,1,0:T(8,128)(2,1)}, u32[]{:S(2)}) copy-start(bf16[2,128,512]{2,1,0:T(8,128)(2,1)} %param.13) | copy-start | bytes 786436
  5.3 30.5 %collective-permute-start = (bf16[4,1168,128]{2,1,0:T(8,128)(2,1)}, bf16[4,1168,128]{2,1,0:T(8,128)(2,1)S(1)}, u32[]{:S(2)}, u32[]{:S(2)}) collective-permute-start(bf16[4,1168,128]{2,1,0:T(8,128)(2,1)} %get-tuple-element.19), channel_id=1, source_target_pairs={{2,0},{16,18},{0,16},{18,2},{3,1},{17,19},{1,17},{19,3},{6,4},{20,... | collective-permute-start | bytes 3588104 | tf_op jit(solution)/shard_map/ppermute | solution.py:429
  5.8 18.5 %collective-permute-start.3 = (bf16[2,1168,128]{2,1,0:T(8,128)(2,1)}, bf16[2,1168,128]{2,1,0:T(8,128)(2,1)S(1)}, u32[]{:S(2)}, u32[]{:S(2)}) collective-permute-start(bf16[2,1168,128]{2,1,0:T(8,128)(2,1)} %get-tuple-element.21), channel_id=1, source_target_pairs={{2,18},{16,0},{3,19},{17,1},{6,22},{20,4},{7,23},{21,5},{10,26},{2... | collective-permute-start | bytes 1794056 | tf_op jit(solution)/shard_map/ppermute | solution.py:427
  7.1 22.3 %collective-permute-start.1 = (bf16[1,1168,128]{2,1,0:T(8,128)(2,1)}, bf16[1,1168,128]{2,1,0:T(8,128)(2,1)}, u32[]{:S(2)}, u32[]{:S(2)}) collective-permute-start(bf16[1,1168,128]{2,1,0:T(8,128)(2,1)} %get-tuple-element.20), channel_id=1, source_target_pairs={{2,18},{16,0},{3,19},{17,1},{6,22},{20,4},{7,23},{21,5},{10,26},{2... | collective-permute-start | bytes 897032 | tf_op jit(solution)/shard_map/ppermute | solution.py:427
  8.4 32.7 %collective-permute-start.5 = (bf16[1,1168,128]{2,1,0:T(8,128)(2,1)}, bf16[1,1168,128]{2,1,0:T(8,128)(2,1)S(1)}, u32[]{:S(2)}, u32[]{:S(2)}) collective-permute-start(bf16[1,1168,128]{2,1,0:T(8,128)(2,1)} %get-tuple-element.22), channel_id=1, source_target_pairs={{2,16},{16,2},{3,17},{17,3},{6,20},{20,6},{7,21},{21,7},{10,24},{2... | collective-permute-start | bytes 897032 | tf_op jit(solution)/shard_map/ppermute | solution.py:430
  24.3 37.7 %collective-permute-start.4 = (bf16[2,1168,128]{2,1,0:T(8,128)(2,1)S(1)}, bf16[2,1168,128]{2,1,0:T(8,128)(2,1)S(1)}, u32[]{:S(2)}, u32[]{:S(2)}) collective-permute-start(bf16[2,1168,128]{2,1,0:T(8,128)(2,1)S(1)} %collective-permute-done.3), channel_id=1, source_target_pairs={{0,2},{18,16},{1,3},{19,17},{4,6},{22,20},{5,7},{23,21},{8,10},{26... | collective-permute-start | bytes 1794056 | tf_op jit(solution)/shard_map/ppermute | solution.py:428
  29.4 32.6 %collective-permute-start.2 = (bf16[1,1168,128]{2,1,0:T(8,128)(2,1)}, bf16[1,1168,128]{2,1,0:T(8,128)(2,1)S(1)}, u32[]{:S(2)}, u32[]{:S(2)}) collective-permute-start(bf16[1,1168,128]{2,1,0:T(8,128)(2,1)} %collective-permute-done.1), channel_id=1, source_target_pairs={{0,2},{18,16},{1,3},{19,17},{4,6},{22,20},{5,7},{23,21},{8,10},{26... | collective-permute-start | bytes 897032 | tf_op jit(solution)/shard_map/ppermute | solution.py:428
  143.1 4.9 %copy-start.3 = (bf16[128,9216]{1,0:T(8,128)(2,1)S(1)}, bf16[128,9216]{1,0:T(8,128)(2,1)}, u32[]{:S(2)}) copy-start(bf16[128,9216]{1,0:T(8,128)(2,1)} %get-tuple-element.28.refs_0_.refs_1_) | copy-start | bytes 7077892
  143.1 35.3 %all-to-all-start.1 = ((bf16[16,8,9216]{2,1,0:T(8,128)(2,1)}), bf16[16,8,9216]{2,1,0:T(8,128)(2,1)}, u32[]{:S(2)}, u32[]{:S(2)}) async-start(bf16[16,8,9216]{2,1,0:T(8,128)(2,1)} %bitcast.32), calls=%async_computation.1 | async-start | bytes 4718592 | tf_op jit(solution)/shard_map/all_to_all | solution.py:459
  148.0 30.3 %copy-start.7 = (bf16[16,9216]{1,0:T(8,128)(2,1)S(1)}, bf16[16,9216]{1,0:T(8,128)(2,1)}, u32[]{:S(2)}) copy-start(bf16[16,9216]{1,0:T(8,128)(2,1)} %get-tuple-element.29.refs_3_) | copy-start | bytes 884740
  246.6 6.0 %copy-start = (bf16[16,16,9216]{2,1,0:T(8,128)(2,1)}, bf16[16,16,9216]{2,1,0:T(8,128)(2,1)S(1)}, u32[]{:S(2)}) copy-start(bf16[16,16,9216]{2,1,0:T(8,128)(2,1)S(1)} %all_to_all.26) | copy-start | bytes 14155780
  252.5 4.9 %copy-start.2 = (bf16[128,9216]{1,0:T(8,128)(2,1)S(1)}, bf16[128,9216]{1,0:T(8,128)(2,1)}, u32[]{:S(2)}) copy-start(bf16[128,9216]{1,0:T(8,128)(2,1)} %get-tuple-element.31.refs_0_.refs_1_) | copy-start | bytes 7077892
  252.5 20.6 %all-to-all-start.3 = ((bf16[16,8,4608]{2,1,0:T(8,128)(2,1)}), bf16[16,8,4608]{2,1,0:T(8,128)(2,1)}, u32[]{:S(2)}, u32[]{:S(2)}) async-start(bf16[16,8,4608]{2,1,0:T(8,128)(2,1)} %bitcast.35), calls=%async_computation.3 | async-start | bytes 2359296 | tf_op jit(solution)/shard_map/all_to_all | solution.py:459
  257.4 3.8 %copy-start.1 = (bf16[16,16,9216]{2,1,0:T(8,128)(2,1)S(1)}, bf16[16,16,9216]{2,1,0:T(8,128)(2,1)}, u32[]{:S(2)}) copy-start(bf16[16,16,9216]{2,1,0:T(8,128)(2,1)} %copy-done) | copy-start | bytes 14155780
  276.9 27.0 %all-to-all-start.4 = ((bf16[16,8,4608]{2,1,0:T(8,128)(2,1)}), bf16[16,8,4608]{2,1,0:T(8,128)(2,1)}, u32[]{:S(2)}, u32[]{:S(2)}) async-start(bf16[16,8,4608]{2,1,0:T(8,128)(2,1)} %bitcast.34), calls=%async_computation.4 | async-start | bytes 2359296 | tf_op jit(solution)/shard_map/all_to_all | solution.py:459
  282.1 26.7 %collective-permute-start.8 = (bf16[4608,128]{1,0:T(8,128)(2,1)}, bf16[4608,128]{1,0:T(8,128)(2,1)}, u32[]{:S(2)}, u32[]{:S(2)}) collective-permute-start(bf16[4608,128]{1,0:T(8,128)(2,1)} %shard_map.99), channel_id=1, source_target_pairs={{2,16},{16,2},{3,17},{17,3},{6,20},{20,6},{7,21},{21,7},{10,24},{2... | collective-permute-start | bytes 3538952 | tf_op jit(solution)/shard_map/ppermute | solution.py:483
  283.8 55.7 %collective-permute-start.6 = (bf16[4608,128]{1,0:T(8,128)(2,1)}, bf16[4608,128]{1,0:T(8,128)(2,1)}, u32[]{:S(2)}, u32[]{:S(2)}) collective-permute-start(bf16[4608,128]{1,0:T(8,128)(2,1)} %shard_map.99), channel_id=1, source_target_pairs={{0,2},{18,16},{1,3},{19,17},{4,6},{22,20},{5,7},{23,21},{8,10},{26... | collective-permute-start | bytes 3538952 | tf_op jit(solution)/shard_map/ppermute | solution.py:483
  307.5 32.0 %collective-permute-start.7 = (bf16[4608,128]{1,0:T(8,128)(2,1)}, bf16[4608,128]{1,0:T(8,128)(2,1)S(1)}, u32[]{:S(2)}, u32[]{:S(2)}) collective-permute-start(bf16[4608,128]{1,0:T(8,128)(2,1)} %shard_map.101.here_ref), channel_id=1, source_target_pairs={{2,18},{16,0},{3,19},{17,1},{6,22},{20,4},{7,23},{21,5},{10,26},{2... | collective-permute-start | bytes 3538952 | tf_op jit(solution)/shard_map/ppermute | solution.py:487
  (3 other events, 4.2 us)
